TPU v7x, 32 devices: a whole 2x2x4 slice. The times are simulated.
32 devices in a mesh: gx: 4 (over z), gy: 8 (over y, x, core).
Axes of the slice: x: 2, y: 2, z: 4, core: 2. Of those that a mesh axis runs over, the one named last changes fastest.
Arguments:
- fine_state: float32 [9, 16, 256, 1024], P(None, None, 'gx', 'gy'), may hold values from -6 to 6
- fine_medium: float32 [3, 16, 256, 1024], P(None, None, 'gx', 'gy'), may hold values from 0.5 to 2
- coarse_state: float32 [9, 8, 128, 512], P(None, None, 'gy', 'gx'), may hold values from -6 to 6
- coarse_medium: float32 [3, 8, 128, 512], P(None, None, 'gy', 'gx'), may hold values from 0.5 to 2
- coarse_past: float32 [9, 2, 128, 512], P(None, None, 'gy', 'gx'), may hold values from -6 to 6
- parent_rows: int32 [256], P('gx'), may hold values from 0 to 127, as said below
- parent_cols: int32 [1024], P('gy'), may hold values from 0 to 511, as said below
Outputs:
- fine_out: float32 [9, 16, 256, 1024], P(None, None, 'gx', 'gy')
- coarse_out: float32 [9, 8, 128, 512], P(None, None, 'gy', 'gx')
Inputs may be any that keep to these rules, and one draw needn't show every extreme that they name: parent_rows[x] is x / 2 - 1 for x a positive multiple of 4, 0 for x = 0, x / 2 for x of remainder 2 by 4, (x - 1) / 2 or (x + 1) / 2 for remainder 1, and (x + 1) / 2 for remainder 3, never past the last coarse row. parent_cols[y] follows the same rule along columns, never past the last coarse column.
All inputs are finite; a program needn't handle non-finite values.
Results may differ from a plain program's by a relative error of at most 0.00002.
Values sent between devices are 32-bit elements; how exact they have to be, the bound alone decides.
No kernel may reach another device: no remote copies, remote signals or barrier semaphores. Data moves between devices by JAX's collectives and lax.ppermute only.
A program may use at most 192 MiB of HBM per device.

v0:
```python
import jax
import jax.numpy as jnp
from jax import lax
from jax.sharding import PartitionSpec as P

COEFFS = (1225.0 / 1024.0, -245.0 / 3072.0, 49.0 / 5120.0, -5.0 / 7168.0)
STEP = 0.1


def extended_2(x, sides, width):
    for axis, dim in sides:
        peers, length = (lax.axis_size(axis), x.shape[dim])
        up = [(i, (i + 1) % peers) for i in range(peers - 1)]
        down = [(j, i) for i, j in up]
        last = lax.slice_in_dim(x, length - width, length, axis=dim)
        leading = lax.slice_in_dim(x, 0, width, axis=dim)
        before = lax.ppermute(last, axis, up)
        after = lax.ppermute(leading, axis, down)
        x = jnp.concatenate([before, x, after], axis=dim)
    return x


def derivative(values, dimension, forward, inv_spacing):
    rank_count = values.ndim
    dimension = dimension % rank_count
    cropped = values
    for other_dim in range(rank_count - 3, rank_count):
        if other_dim != dimension:
            cropped = lax.slice_in_dim(cropped, 4, cropped.shape[other_dim] - 4, axis=other_dim)
    length = cropped.shape[dimension] - 8
    result = None
    for tap_index in range(1, 5):
        upper_start = 4 + tap_index if forward else 3 + tap_index
        lower_start = 5 - tap_index if forward else 4 - tap_index
        upper_part = lax.slice_in_dim(cropped, upper_start, upper_start + length, axis=dimension)
        lower_part = lax.slice_in_dim(cropped, lower_start, lower_start + length, axis=dimension)
        tap_term = COEFFS[tap_index - 1] * (upper_part - lower_part)
        result = tap_term if result is None else result + tap_term
    return result * inv_spacing


def velocity_step(velocity, stress_pad, buoyancy, step_size, inv_spacing):
    first_rate = (
        derivative(stress_pad[0], -2, True, inv_spacing)
        + derivative(stress_pad[3], -1, False, inv_spacing)
        + derivative(stress_pad[4], -3, False, inv_spacing)
    )
    second_rate = (
        derivative(stress_pad[3], -2, False, inv_spacing)
        + derivative(stress_pad[1], -1, True, inv_spacing)
        + derivative(stress_pad[5], -3, False, inv_spacing)
    )
    third_rate = (
        derivative(stress_pad[4], -2, False, inv_spacing)
        + derivative(stress_pad[5], -1, False, inv_spacing)
        + derivative(stress_pad[2], -3, True, inv_spacing)
    )
    return velocity + step_size * buoyancy * jnp.stack([first_rate, second_rate, third_rate])


def stress_step(stress, velocity_pad, lame_first, shear_modulus, step_size, inv_spacing):
    strain_first = derivative(velocity_pad[0], -2, False, inv_spacing)
    strain_second = derivative(velocity_pad[1], -1, False, inv_spacing)
    strain_third = derivative(velocity_pad[2], -3, False, inv_spacing)
    dilation = strain_first + strain_second + strain_third
    rate_list = [
        lame_first * dilation + 2.0 * shear_modulus * strain_first,
        lame_first * dilation + 2.0 * shear_modulus * strain_second,
        lame_first * dilation + 2.0 * shear_modulus * strain_third,
        shear_modulus
        * (
            derivative(velocity_pad[0], -1, True, inv_spacing)
            + derivative(velocity_pad[1], -2, True, inv_spacing)
        ),
        shear_modulus
        * (
            derivative(velocity_pad[0], -3, True, inv_spacing)
            + derivative(velocity_pad[2], -2, True, inv_spacing)
        ),
        shear_modulus
        * (
            derivative(velocity_pad[1], -3, True, inv_spacing)
            + derivative(velocity_pad[2], -1, True, inv_spacing)
        ),
    ]
    return stress + step_size * jnp.stack(rate_list)


def zero_layers(values, layer_count):
    return jnp.zeros((values.shape[0], layer_count) + values.shape[2:], values.dtype)


def widen_ghost(widened, ghost_cells):
    margin = (widened.shape[-1] - ghost_cells.shape[-1]) // 2
    return jnp.pad(ghost_cells, ((0, 0), (0, 0), (margin, margin), (margin, margin)))


def above_pad(widened, ghost_cells):
    return jnp.concatenate(
        [widen_ghost(widened, ghost_cells), widened, zero_layers(widened, 4)], axis=1
    )


def coarse_rim(values):
    return extended_2(values, (("gx", 3), ("gy", 2)), 4)


def regrid(planes):
    devices_x = lax.axis_size("gx")
    ratio_xy = lax.axis_size("gy") // devices_x
    lead_count, rows_in, cols_in = planes.shape
    piece_cols = cols_in // ratio_xy // devices_x
    sectioned = planes.reshape(lead_count, 1, rows_in, ratio_xy, devices_x, piece_cols)
    moved_pair = lax.all_to_all(
        lax.all_to_all(sectioned, "gx", split_axis=4, concat_axis=3, tiled=True),
        "gy",
        split_axis=3,
        concat_axis=1,
        tiled=True,
    )
    settled = lax.all_to_all(moved_pair, "gx", split_axis=1, concat_axis=4, tiled=True)
    return settled.reshape(lead_count, ratio_xy * rows_in, cols_in // ratio_xy)


def body(
    fine_state, fine_medium, coarse_state, coarse_medium, coarse_past, parent_rows, parent_cols
):
    fine_depth = fine_state.shape[1]
    rows_half = fine_state.shape[2] // 2
    cols_half = fine_state.shape[3] // 2
    coarse_top = coarse_state[:, :2]
    plane_rows = coarse_top.shape[2]
    plane_cols = coarse_top.shape[3]
    moved_top = regrid(coarse_top.reshape(-1, plane_rows, plane_cols))
    moved_past = regrid(coarse_past.reshape(-1, plane_rows, plane_cols))
    moved_planes = jnp.concatenate([moved_top, 1.5 * moved_top - 0.5 * moved_past], axis=0)
    widened = extended_2(moved_planes, (("gx", 1), ("gy", 2)), 1)
    local_rows = parent_rows - lax.axis_index("gx") * rows_half + 1
    local_cols = parent_cols - lax.axis_index("gy") * cols_half + 1
    picked = jnp.take(jnp.take(widened, local_rows, axis=1), local_cols, axis=2)
    picked = picked.reshape((2, 9, 2) + picked.shape[1:])
    ghosts = jnp.repeat(picked, 2, axis=2)
    lame_first = fine_medium[1]
    shear_modulus = fine_medium[2]
    fine_now = fine_state
    buoyancy_wide = extended_2(fine_medium[0:1], (("gx", 2), ("gy", 3)), 4)[0]
    for level_index in range(2):
        ghost_cells = ghosts[level_index]
        extended = jnp.concatenate([fine_now, ghost_cells], axis=1)
        widened_all = extended_2(extended, (("gx", 2), ("gy", 3)), 8)
        padded = jnp.concatenate([zero_layers(widened_all, 4), widened_all], axis=1)
        velocity_wide = velocity_step(
            padded[:3, 4 : 4 + fine_depth, 4:-4, 4:-4], padded[3:], buoyancy_wide, STEP, 1.0
        )
        velocity_pad = jnp.concatenate(
            [
                zero_layers(velocity_wide, 4),
                velocity_wide,
                padded[:3, 4 + fine_depth :, 4:-4, 4:-4],
            ],
            axis=1,
        )
        stress = stress_step(fine_now[3:], velocity_pad, lame_first, shear_modulus, STEP, 1.0)
        fine_now = jnp.concatenate([velocity_wide[:, :, 4:-4, 4:-4], stress], axis=0)
    blended = 0.5 * (fine_state[:, fine_depth - 8 :] + fine_now[:, fine_depth - 8 :])
    restricted = blended.reshape(9, 4, 2, rows_half, 2, cols_half, 2).mean(axis=(2, 4, 6))
    flipped = jnp.swapaxes(restricted, 2, 3).reshape(36, cols_half, rows_half)
    lifted = regrid(flipped)
    coarse_ghost = jnp.swapaxes(lifted.reshape(9, 4, lifted.shape[1], lifted.shape[2]), 2, 3)
    stress_pad = above_pad(coarse_rim(coarse_state[3:]), coarse_ghost[3:])
    velocity = velocity_step(coarse_state[:3], stress_pad, coarse_medium[0], 2.0 * STEP, 0.5)
    velocity_pad = above_pad(coarse_rim(velocity), coarse_ghost[:3])
    stress = stress_step(
        coarse_state[3:], velocity_pad, coarse_medium[1], coarse_medium[2], 2.0 * STEP, 0.5
    )
    coarse_out = jnp.concatenate([velocity, stress], axis=0)
    return (fine_now, coarse_out)


def solution(mesh):
    placed = (
        P(None, None, "gx", "gy"),
        P(None, None, "gx", "gy"),
        P(None, None, "gy", "gx"),
        P(None, None, "gy", "gx"),
        P(None, None, "gy", "gx"),
        P("gx"),
        P("gy"),
    )
    return jax.shard_map(
        body,
        mesh=mesh,
        in_specs=placed,
        out_specs=(P(None, None, "gx", "gy"), P(None, None, "gy", "gx")),
        check_vma=False,
    )
```

profile of v0, /device:TPU:1, one launch (start us, length us, event | category | flops | bytes accessed | tf_op | source)
XLA Modules:
  0.0 570.0 jit_solution(8905549922004579306)
XLA Ops:
  5.0 5.4 all-to-all-start
  23.8 6.8 %all-to-all-start.1 = ((f32[8,1,4608]{2,1,0:T(1,128)}), f32[8,1,4608]{2,1,0:T(1,128)S(1)}, u32[]{:S(2)}, u32[]{:S(2)}) async-start(f32[8,1,4608]{2,1,0:T(1,128)} %reshape.107), calls=%async_computation.1 | async-start | bytes 294912 | tf_op jit(solution)/shard_map/all_to_all | solution.py:114
  73.9 7.0 %collective-permute-start.2 = (f32[36,34,1]{0,2,1:T(1,128)S(1)}, f32[36,34,1]{0,2,1:T(1,128)S(1)}, u32[]{:S(2)}, u32[]{:S(2)}) collective-permute-start(f32[36,34,1]{0,2,1:T(1,128)S(1)} %copy.127), channel_id=1, source_target_pairs={{0,1},{1,2},{2,3},{3,4},{4,5},{5,6},{6,7},{8,9},{9,10},{10,11},{11... | collective-permute-start | bytes 14696 | tf_op jit(solution)/shard_map/ppermute | solution.py:17
  107.7 12.1 %collective-permute-start.9 = (f32[1,16,4,128]{3,1,2,0:T(8,128)S(1)}, f32[1,16,4,128]{3,1,2,0:T(8,128)S(1)}, u32[]{:S(2)}, u32[]{:S(2)}) collective-permute-start(f32[1,16,4,128]{3,1,2,0:T(8,128)S(1)} %copy.158), channel_id=1, source_target_pairs={{8,0},{16,8},{24,16},{9,1},{17,9},{25,17},{10,2},{18,10},{26,18},{... | collective-permute-start | bytes 98312 | tf_op jit(solution)/shard_map/ppermute | solution.py:18
  126.6 5.5 pad_maximum_fusion.2
  132.0 12.4 %fusion.470 = (f32[9,20,80,8]{3,2,1,0:T(8,128)}, f32[9,20,80,8]{3,2,1,0:T(8,128)}) fusion(f32[9,20,80,128]{3,2,1,0:T(8,128)} %pad_maximum_fusion.2), kind=kLoop, calls=%fused_computation.795 | loop fusion | bytes 1843200 | tf_op jit(solution)/shard_map/slice | solution.py:15
  144.4 5.6 copy.134
  153.4 5.6 copy.135
  175.3 5.3 copy.136
  180.7 5.3 copy.137
  186.0 14.7 %pad_maximum_fusion = f32[9,20,80,144]{3,2,1,0:T(8,128)S(1)} fusion(f32[9,20,80,8]{3,2,1,0:T(8,128)} %copy.137, f32[9,20,8,128]{3,2,1,0:T(8,128)} %collective-permute-done.5, f32[9,4,64,128]{3,2,1,0:T(8,128)S(1)} %bitcast.328, f32[9,16,64,128]{3,2,1,0:T(8,128)} %param.7, f32[9,20,8,128]{3,2,1,0:T(8,128)} %collective-permute-done.4, f32[9,20,80,8]{3,2,1,0:T(8,128)} %copy.136), kind=kLoop, calls=%fused_computation.8 | loop fusion | flops 10368000 | bytes 16588800 | tf_op jit(solution)/shard_map/concatenate | solution.py:19
  204.1 11.4 %fusion.134 = f32[1,16,72,136]{3,2,1,0:T(8,128)} fusion(f32[24,80,144]{2,1,0:T(8,128)} %get-tuple-element.33, f32[16,80,144]{2,1,0:T(8,128)S(1)} %get-tuple-element.32, f32[16,80,144]{2,1,0:T(8,128)S(1)} %get-tuple-element.28), kind=kLoop, calls=%fused_computation.246 | loop fusion | flops 5483520 | bytes 15667200 | tf_op jit(solution)/shard_map/stack | solution.py:58
  215.5 11.8 %fusion.110 = f32[1,16,72,136]{3,2,1,0:T(8,128)} fusion(f32[24,80,144]{2,1,0:T(8,128)} %get-tuple-element.34, f32[16,80,144]{2,1,0:T(8,128)S(1)} %get-tuple-element.31, f32[16,80,144]{2,1,0:T(8,128)S(1)} %get-tuple-element.32), kind=kLoop, calls=%fused_computation.210 | loop fusion | flops 5483520 | bytes 15667200 | tf_op jit(solution)/shard_map/stack | solution.py:58
  227.4 8.1 %fusion.86 = f32[1,16,72,136]{3,2,1,0:T(8,128)} fusion(f32[24,80,144]{2,1,0:T(8,128)S(1)} %get-tuple-element.35, f32[16,80,144]{2,1,0:T(8,128)S(1)} %get-tuple-element.29, f32[16,80,144]{2,1,0:T(8,128)S(1)} %get-tuple-element.30), kind=kLoop, calls=%fused_computation.174 | loop fusion | flops 5483520 | bytes 15667200 | tf_op jit(solution)/shard_map/stack | solution.py:58
  261.8 10.8 %collective-permute-done.12 = f32[9,20,8,128]{3,2,1,0:T(8,128)S(1)} collective-permute-done((f32[9,20,8,128]{3,2,1,0:T(8,128)S(1)}, f32[9,20,8,128]{3,2,1,0:T(8,128)S(1)}, u32[]{:S(2)}, u32[]{:S(2)}) %collective-permute-start.12) | collective-permute-done | bytes 737312 | tf_op jit(solution)/shard_map/ppermute | solution.py:17
  281.3 12.4 %fusion.469 = (f32[9,20,80,8]{3,2,1,0:T(8,128)}, f32[9,20,80,8]{3,2,1,0:T(8,128)}) fusion(f32[9,20,80,128]{3,2,1,0:T(8,128)} %pad_maximum_fusion.3), kind=kLoop, calls=%fused_computation.794 | loop fusion | bytes 1843200 | tf_op jit(solution)/shard_map/slice | solution.py:15
  293.7 5.6 copy.144
  304.4 5.6 copy.145
  313.1 5.3 copy.146
  318.5 5.6 collective-permute-done.15
  324.1 5.3 copy.147
  329.4 15.4 %pad_maximum_fusion.1 = f32[9,20,80,144]{3,2,1,0:T(8,128)S(1)} fusion(f32[9,20,80,8]{3,2,1,0:T(8,128)} %copy.147, f32[9,20,8,128]{3,2,1,0:T(8,128)} %copy-done.24, f32[9,4,64,128]{3,2,1,0:T(8,128)} %bitcast.331, f32[6,16,64,128]{3,2,1,0:T(8,128)S(1)} %multiply_add_fusion.1, f32[3,16,64,128]{3,2,1,0:T(8,128)} %copy-done.5, f32[9,20,8,128]{3,2,1,0:T(8,128)} %copy-done.23, ...), kind=kLoop, calls=%fused_computation.9 | loop fusion | flops 12441600 | bytes 16588800 | tf_op jit(solution)/shard_map/concatenate | solution.py:19
  348.2 11.2 %fusion.62 = f32[1,16,72,136]{3,2,1,0:T(8,128)} fusion(f32[24,80,144]{2,1,0:T(8,128)} %get-tuple-element.25, f32[16,80,144]{2,1,0:T(8,128)S(1)} %get-tuple-element.24, f32[16,80,144]{2,1,0:T(8,128)S(1)} %get-tuple-element.20), kind=kLoop, calls=%fused_computation.135 | loop fusion | flops 5483520 | bytes 15667200 | tf_op jit(solution)/shard_map/stack | solution.py:58
  359.4 11.8 %fusion.38 = f32[1,16,72,136]{3,2,1,0:T(8,128)} fusion(f32[24,80,144]{2,1,0:T(8,128)} %get-tuple-element.26, f32[16,80,144]{2,1,0:T(8,128)S(1)} %get-tuple-element.23, f32[16,80,144]{2,1,0:T(8,128)S(1)} %get-tuple-element.24), kind=kLoop, calls=%fused_computation.99 | loop fusion | flops 5483520 | bytes 15667200 | tf_op jit(solution)/shard_map/stack | solution.py:58
  371.2 8.1 %fusion.14 = f32[1,16,72,136]{3,2,1,0:T(8,128)} fusion(f32[24,80,144]{2,1,0:T(8,128)S(1)} %get-tuple-element.27, f32[16,80,144]{2,1,0:T(8,128)S(1)} %get-tuple-element.21, f32[16,80,144]{2,1,0:T(8,128)S(1)} %get-tuple-element.22), kind=kLoop, calls=%fused_computation.63 | loop fusion | flops 5483520 | bytes 15667200 | tf_op jit(solution)/shard_map/stack | solution.py:58
  405.1 18.3 %copy.148 = f32[9,8,64,128]{0,3,2,1:T(8,128)} copy(f32[9,8,64,128]{3,2,1,0:T(8,128)} %fusion.2) | data formatting | bytes 4718592 | tf_op jit(solution)/shard_map/mul | solution.py:165
  423.4 24.3 %reduce_sum.9 = f32[9,4,32,64]{0,3,2,1:T(8,128)} reduce(f32[9,4,2,32,2,64,2]{0,6,5,4,3,2,1:T(2,128)} %bitcast.321, f32[]{:T(128)} %constant.40.clone.1), dimensions={2,4,6}, to_apply=%region_0.1 | reduce | flops 516096 | bytes 2654212 | tf_op jit(solution)/shard_map/reduce_sum | solution.py:166
  459.9 9.9 %all_to_all.147 = f32[4,1,18432]{2,1,0:T(1,128)} all-to-all(f32[4,1,18432]{2,1,0:T(1,128)S(1)} %reshape.111), channel_id=1, replica_groups=mesh['gx'=4,'gy'=8] {'gx'}, dimensions={0} | all-to-all | bytes 589824 | tf_op jit(solution)/shard_map/all_to_all | solution.py:115
  478.2 5.3 all-to-all-start.7
  488.4 7.2 %collective-permute-done.16 = f32[6,8,16,4]{3,2,1,0:T(8,128)S(1)} collective-permute-done((f32[6,8,16,4]{3,2,1,0:T(8,128)S(1)}, f32[6,8,16,4]{3,2,1,0:T(8,128)S(1)}, u32[]{:S(2)}, u32[]{:S(2)}) %collective-permute-start.16) | collective-permute-done | bytes 12320 | tf_op jit(solution)/shard_map/ppermute | solution.py:17
  500.5 5.2 collective-permute-start.18
  554.5 5.2 collective-permute-start.22
  (294 shorter events, 278.2 us)
Async XLA Ops:
  5.0 10.3 %all-to-all-start = ((f32[4,1,9216]{2,1,0:T(1,128)}), f32[4,1,9216]{2,1,0:T(1,128)S(1)}, u32[]{:S(2)}, u32[]{:S(2)}) async-start(f32[4,1,9216]{2,1,0:T(1,128)} %reshape.105), calls=%async_computation | async-start | bytes 294912 | tf_op jit(solution)/shard_map/all_to_all | solution.py:115
  15.2 8.5 %all-to-all-start.3 = ((f32[4,1,9216]{2,1,0:T(1,128)}), f32[4,1,9216]{2,1,0:T(1,128)S(1)}, u32[]{:S(2)}, u32[]{:S(2)}) async-start(f32[4,1,9216]{2,1,0:T(1,128)} %reshape.99), calls=%async_computation.3 | async-start | bytes 294912 | tf_op jit(solution)/shard_map/all_to_all | solution.py:115
  23.8 11.7 %all-to-all-start.1 = ((f32[8,1,4608]{2,1,0:T(1,128)}), f32[8,1,4608]{2,1,0:T(1,128)S(1)}, u32[]{:S(2)}, u32[]{:S(2)}) async-start(f32[8,1,4608]{2,1,0:T(1,128)} %reshape.107), calls=%async_computation.1 | async-start | bytes 294912 | tf_op jit(solution)/shard_map/all_to_all | solution.py:114
  35.4 9.0 %all-to-all-start.4 = ((f32[8,1,4608]{2,1,0:T(1,128)}), f32[8,1,4608]{2,1,0:T(1,128)S(1)}, u32[]{:S(2)}, u32[]{:S(2)}) async-start(f32[8,1,4608]{2,1,0:T(1,128)} %reshape.101), calls=%async_computation.4 | async-start | bytes 294912 | tf_op jit(solution)/shard_map/all_to_all | solution.py:114
  44.5 8.4 %all-to-all-start.2 = ((f32[4,1,9216]{2,1,0:T(1,128)}), f32[4,1,9216]{2,1,0:T(1,128)S(1)}, u32[]{:S(2)}, u32[]{:S(2)}) async-start(f32[4,1,9216]{2,1,0:T(1,128)} %reshape.109), calls=%async_computation.2 | async-start | bytes 294912 | tf_op jit(solution)/shard_map/all_to_all | solution.py:121
  52.9 8.4 %all-to-all-start.5 = ((f32[4,1,9216]{2,1,0:T(1,128)}), f32[4,1,9216]{2,1,0:T(1,128)S(1)}, u32[]{:S(2)}, u32[]{:S(2)}) async-start(f32[4,1,9216]{2,1,0:T(1,128)} %reshape.103), calls=%async_computation.5 | async-start | bytes 294912 | tf_op jit(solution)/shard_map/all_to_all | solution.py:121
  65.7 4.3 collective-permute-start
  68.7 4.5 collective-permute-start.1
  73.9 9.2 %collective-permute-start.2 = (f32[36,34,1]{0,2,1:T(1,128)S(1)}, f32[36,34,1]{0,2,1:T(1,128)S(1)}, u32[]{:S(2)}, u32[]{:S(2)}) collective-permute-start(f32[36,34,1]{0,2,1:T(1,128)S(1)} %copy.127), channel_id=1, source_target_pairs={{0,1},{1,2},{2,3},{3,4},{4,5},{5,6},{6,7},{8,9},{9,10},{10,11},{11... | collective-permute-start | bytes 14696 | tf_op jit(solution)/shard_map/ppermute | solution.py:17
  81.2 5.1 collective-permute-start.3
  99.2 27.3 %collective-permute-start.4 = (f32[9,20,8,128]{3,2,1,0:T(8,128)}, f32[9,20,8,128]{3,2,1,0:T(8,128)}, u32[]{:S(2)}, u32[]{:S(2)}) collective-permute-start(f32[9,20,8,128]{3,2,1,0:T(8,128)} %get-tuple-element.42), channel_id=1, source_target_pairs={{0,8},{8,16},{16,24},{1,9},{9,17},{17,25},{2,10},{10,18},{18,26},{... | collective-permute-start | bytes 2211848 | tf_op jit(solution)/shard_map/ppermute | solution.py:17
  102.4 24.2 %collective-permute-start.5 = (f32[9,20,8,128]{3,2,1,0:T(8,128)}, f32[9,20,8,128]{3,2,1,0:T(8,128)}, u32[]{:S(2)}, u32[]{:S(2)}) collective-permute-start(f32[9,20,8,128]{3,2,1,0:T(8,128)} %get-tuple-element.43), channel_id=1, source_target_pairs={{8,0},{16,8},{24,16},{9,1},{17,9},{25,17},{10,2},{18,10},{26,18},{... | collective-permute-start | bytes 2211848 | tf_op jit(solution)/shard_map/ppermute | solution.py:18
  103.7 17.1 %collective-permute-start.8 = (f32[1,16,4,128]{3,1,2,0:T(8,128)S(1)}, f32[1,16,4,128]{3,1,2,0:T(8,128)S(1)}, u32[]{:S(2)}, u32[]{:S(2)}) collective-permute-start(f32[1,16,4,128]{3,1,2,0:T(8,128)S(1)} %copy.156), channel_id=1, source_target_pairs={{0,8},{8,16},{16,24},{1,9},{9,17},{17,25},{2,10},{10,18},{18,26},{... | collective-permute-start | bytes 98312 | tf_op jit(solution)/shard_map/ppermute | solution.py:17
  107.7 14.4 %collective-permute-start.9 = (f32[1,16,4,128]{3,1,2,0:T(8,128)S(1)}, f32[1,16,4,128]{3,1,2,0:T(8,128)S(1)}, u32[]{:S(2)}, u32[]{:S(2)}) collective-permute-start(f32[1,16,4,128]{3,1,2,0:T(8,128)S(1)} %copy.158), channel_id=1, source_target_pairs={{8,0},{16,8},{24,16},{9,1},{17,9},{25,17},{10,2},{18,10},{26,18},{... | collective-permute-start | bytes 98312 | tf_op jit(solution)/shard_map/ppermute | solution.py:18
  150.0 25.3 %collective-permute-start.6 = (f32[9,20,80,8]{2,3,1,0:T(8,128)}, f32[9,20,80,8]{2,3,1,0:T(8,128)}, u32[]{:S(2)}, u32[]{:S(2)}) collective-permute-start(f32[9,20,80,8]{2,3,1,0:T(8,128)} %copy.134), channel_id=1, source_target_pairs={{0,1},{1,2},{2,3},{3,4},{4,5},{5,6},{6,7},{8,9},{9,10},{10,11},{11... | collective-permute-start | bytes 1382408 | tf_op jit(solution)/shard_map/ppermute | solution.py:17
  159.1 21.6 %collective-permute-start.7 = (f32[9,20,80,8]{2,3,1,0:T(8,128)}, f32[9,20,80,8]{2,3,1,0:T(8,128)}, u32[]{:S(2)}, u32[]{:S(2)}) collective-permute-start(f32[9,20,80,8]{2,3,1,0:T(8,128)} %copy.135), channel_id=1, source_target_pairs={{1,0},{2,1},{3,2},{4,3},{5,4},{6,5},{7,6},{9,8},{10,9},{11,10},{12... | collective-permute-start | bytes 1382408 | tf_op jit(solution)/shard_map/ppermute | solution.py:18
  161.8 7.4 %collective-permute-start.10 = (f32[1,16,72,4]{2,1,3,0:T(8,128)S(1)}, f32[1,16,72,4]{2,1,3,0:T(8,128)S(1)}, u32[]{:S(2)}, u32[]{:S(2)}) collective-permute-start(f32[1,16,72,4]{2,1,3,0:T(8,128)S(1)} %get-tuple-element.73), channel_id=1, source_target_pairs={{0,1},{1,2},{2,3},{3,4},{4,5},{5,6},{6,7},{8,9},{9,10},{10,11},{11... | collective-permute-start | bytes 55304 | tf_op jit(solution)/shard_map/ppermute | solution.py:17
  165.4 8.1 %collective-permute-start.11 = (f32[1,16,72,4]{2,1,3,0:T(8,128)S(1)}, f32[1,16,72,4]{2,1,3,0:T(8,128)S(1)}, u32[]{:S(2)}, u32[]{:S(2)}) collective-permute-start(f32[1,16,72,4]{2,1,3,0:T(8,128)S(1)} %get-tuple-element.74), channel_id=1, source_target_pairs={{1,0},{2,1},{3,2},{4,3},{5,4},{6,5},{7,6},{9,8},{10,9},{11,10},{12... | collective-permute-start | bytes 55304 | tf_op jit(solution)/shard_map/ppermute | solution.py:18
  257.8 14.7 %collective-permute-start.12 = (f32[9,20,8,128]{3,2,1,0:T(8,128)S(1)}, f32[9,20,8,128]{3,2,1,0:T(8,128)S(1)}, u32[]{:S(2)}, u32[]{:S(2)}) collective-permute-start(f32[9,20,8,128]{3,2,1,0:T(8,128)S(1)} %get-tuple-element.40), channel_id=1, source_target_pairs={{0,8},{8,16},{16,24},{1,9},{9,17},{17,25},{2,10},{10,18},{18,26},{... | collective-permute-start | bytes 2211848 | tf_op jit(solution)/shard_map/ppermute | solution.py:17
  260.5 16.2 %collective-permute-start.13 = (f32[9,20,8,128]{3,2,1,0:T(8,128)S(1)}, f32[9,20,8,128]{3,2,1,0:T(8,128)S(1)}, u32[]{:S(2)}, u32[]{:S(2)}) collective-permute-start(f32[9,20,8,128]{3,2,1,0:T(8,128)S(1)} %get-tuple-element.41), channel_id=1, source_target_pairs={{8,0},{16,8},{24,16},{9,1},{17,9},{25,17},{10,2},{18,10},{26,18},{... | collective-permute-start | bytes 2211848 | tf_op jit(solution)/shard_map/ppermute | solution.py:18
  299.3 13.8 %collective-permute-start.14 = (f32[9,20,80,8]{2,3,1,0:T(8,128)}, f32[9,20,80,8]{2,3,1,0:T(8,128)}, u32[]{:S(2)}, u32[]{:S(2)}) collective-permute-start(f32[9,20,80,8]{2,3,1,0:T(8,128)} %copy.144), channel_id=1, source_target_pairs={{0,1},{1,2},{2,3},{3,4},{4,5},{5,6},{6,7},{8,9},{9,10},{10,11},{11... | collective-permute-start | bytes 1382408 | tf_op jit(solution)/shard_map/ppermute | solution.py:17
  310.1 14.0 %collective-permute-start.15 = (f32[9,20,80,8]{2,3,1,0:T(8,128)}, f32[9,20,80,8]{2,3,1,0:T(8,128)}, u32[]{:S(2)}, u32[]{:S(2)}) collective-permute-start(f32[9,20,80,8]{2,3,1,0:T(8,128)} %copy.145), channel_id=1, source_target_pairs={{1,0},{2,1},{3,2},{4,3},{5,4},{6,5},{7,6},{9,8},{10,9},{11,10},{12... | collective-permute-start | bytes 1382408 | tf_op jit(solution)/shard_map/ppermute | solution.py:18
  478.2 29.4 %all-to-all-start.7 = ((f32[8,1,9216]{2,1,0:T(1,128)}), f32[8,1,9216]{2,1,0:T(1,128)}, u32[]{:S(2)}, u32[]{:S(2)}) async-start(f32[8,1,9216]{2,1,0:T(1,128)} %reshape.113), calls=%async_computation.7 | async-start | bytes 589824 | tf_op jit(solution)/shard_map/all_to_all | solution.py:114
  484.9 10.6 %collective-permute-start.16 = (f32[6,8,16,4]{3,2,1,0:T(8,128)S(1)}, f32[6,8,16,4]{3,2,1,0:T(8,128)S(1)}, u32[]{:S(2)}, u32[]{:S(2)}) collective-permute-start(f32[6,8,16,4]{3,2,1,0:T(8,128)S(1)} %get-tuple-element.82), channel_id=1, source_target_pairs={{0,8},{8,16},{16,24},{1,9},{9,17},{17,25},{2,10},{10,18},{18,26},{... | collective-permute-start | bytes 36872 | tf_op jit(solution)/shard_map/ppermute | solution.py:17
  487.0 12.3 %collective-permute-start.17 = (f32[6,8,16,4]{3,2,1,0:T(8,128)S(1)}, f32[6,8,16,4]{3,2,1,0:T(8,128)S(1)}, u32[]{:S(2)}, u32[]{:S(2)}) collective-permute-start(f32[6,8,16,4]{3,2,1,0:T(8,128)S(1)} %get-tuple-element.83), channel_id=1, source_target_pairs={{8,0},{16,8},{24,16},{9,1},{17,9},{25,17},{10,2},{18,10},{26,18},{... | collective-permute-start | bytes 36872 | tf_op jit(solution)/shard_map/ppermute | solution.py:18
  500.5 22.4 %collective-permute-start.18 = (f32[6,8,4,136]{3,2,1,0:T(4,128)}, f32[6,8,4,136]{3,2,1,0:T(4,128)}, u32[]{:S(2)}, u32[]{:S(2)}) collective-permute-start(f32[6,8,4,136]{3,2,1,0:T(4,128)} %get-tuple-element.69), channel_id=1, source_target_pairs={{0,1},{1,2},{2,3},{3,4},{4,5},{5,6},{6,7},{8,9},{9,10},{10,11},{11... | collective-permute-start | bytes 313352 | tf_op jit(solution)/shard_map/ppermute | solution.py:17
  505.8 17.1 %collective-permute-start.19 = (f32[6,8,4,136]{3,2,1,0:T(4,128)}, f32[6,8,4,136]{3,2,1,0:T(4,128)}, u32[]{:S(2)}, u32[]{:S(2)}) collective-permute-start(f32[6,8,4,136]{3,2,1,0:T(4,128)} %get-tuple-element.70), channel_id=1, source_target_pairs={{1,0},{2,1},{3,2},{4,3},{5,4},{6,5},{7,6},{9,8},{10,9},{11,10},{12... | collective-permute-start | bytes 313352 | tf_op jit(solution)/shard_map/ppermute | solution.py:18
  517.1 11.6 %all-to-all-start.8 = ((f32[4,1,18432]{2,1,0:T(1,128)}), f32[4,1,18432]{2,1,0:T(1,128)}, u32[]{:S(2)}, u32[]{:S(2)}) async-start(f32[4,1,18432]{2,1,0:T(1,128)} %reshape.115), calls=%async_computation.8 | async-start | bytes 589824 | tf_op jit(solution)/shard_map/all_to_all | solution.py:121
  544.7 5.4 collective-permute-start.20
  546.5 7.7 %collective-permute-start.21 = (f32[3,8,16,4]{3,2,1,0:T(8,128)S(1)}, f32[3,8,16,4]{3,2,1,0:T(8,128)S(1)}, u32[]{:S(2)}, u32[]{:S(2)}) collective-permute-start(f32[3,8,16,4]{3,2,1,0:T(8,128)S(1)} %get-tuple-element.87), channel_id=1, source_target_pairs={{8,0},{16,8},{24,16},{9,1},{17,9},{25,17},{10,2},{18,10},{26,18},{... | collective-permute-start | bytes 18440 | tf_op jit(solution)/shard_map/ppermute | solution.py:18
  554.5 10.9 %collective-permute-start.22 = (f32[3,8,4,136]{3,2,1,0:T(4,128)S(1)}, f32[3,8,4,136]{3,2,1,0:T(4,128)S(1)}, u32[]{:S(2)}, u32[]{:S(2)}) collective-permute-start(f32[3,8,4,136]{3,2,1,0:T(4,128)S(1)} %get-tuple-element.80), channel_id=1, source_target_pairs={{0,1},{1,2},{2,3},{3,4},{4,5},{5,6},{6,7},{8,9},{9,10},{10,11},{11... | collective-permute-start | bytes 156680 | tf_op jit(solution)/shard_map/ppermute | solution.py:17
  559.7 5.9 %collective-permute-start.23 = (f32[3,8,4,136]{3,2,1,0:T(4,128)S(1)}, f32[3,8,4,136]{3,2,1,0:T(4,128)S(1)}, u32[]{:S(2)}, u32[]{:S(2)}) collective-permute-start(f32[3,8,4,136]{3,2,1,0:T(4,128)S(1)} %get-tuple-element.81), channel_id=1, source_target_pairs={{1,0},{2,1},{3,2},{4,3},{5,4},{6,5},{7,6},{9,8},{10,9},{11,10},{12... | collective-permute-start | bytes 156680 | tf_op jit(solution)/shard_map/ppermute | solution.py:18
  (42 other events, 323.2 us)
where the time goes:
time: 581 us; the launch traced here: 570 us
  other arithmetic  213 us (37%)
  local copies, waits for them, and re-layouts  174 us (30%)
  starting transfers between devices  113 us (19%)
  waiting for transfers between devices  57.4 us (10%)
  blocking collectives  9.89 us (2%)
    another operation x9, other arithmetic, velocity_step(): jnp.stack([first_rate, second_rate, third_rate])  63.7 us
    ppermute x12, starting transfers between devices, extended_2(): before = lax.ppermute(last, axis, up)  46.1 us
    concatenate x9, other arithmetic, extended_2(): x = jnp.concatenate([before, x, after], axis=dim)  45.2 us
    slice x10, local copies, waits for them, and re-layouts, extended_2(): last = lax.slice_in_dim(x, length - width, length, axis=dim)  38.9 us
    unnamed x106, local copies, waits for them, and re-layouts  38.5 us
    ppermute x12, starting transfers between devices, extended_2(): after = lax.ppermute(leading, axis, down)  30.5 us
    ppermute x12, waiting for transfers between devices, extended_2(): after = lax.ppermute(leading, axis, down)  28.8 us
    reduce_sum x1, other arithmetic, body(): blended.reshape(9, 4, 2, rows_half, 2, cols_half, 2).mean(axis=(2, 4, 6))  24.3 us
  transfers between devices with their start and end apart: 32, of which 20 were waited for; matrix products, arithmetic and copies ran while one was open for 14% of the time, Pallas kernels for 0%

commit v1 on v0

v1 whole, which is shorter than its diff:
```python
import functools

import jax
import jax.numpy as jnp
import ml_dtypes
import numpy as np
from jax import lax
from jax.experimental import pallas as pl
from jax.experimental.pallas import tpu as pltpu
from jax.sharding import PartitionSpec as P

COEFFS = (1225.0 / 1024.0, -245.0 / 3072.0, 49.0 / 5120.0, -5.0 / 7168.0)
STEP = 0.1
LANES = 128
F32 = jnp.float32
BF16 = jnp.bfloat16

VX, VY, VZ, SXX, SYY, SZZ, SXY, SXZ, SYZ = range(9)
CROSSING = (VX, VY, VZ, SXZ, SYZ, SZZ)
VEL_X = ((SXX, True), (SXY, False), (SXZ, False))
VEL_Y = ((SXY, False), (SYY, True), (SYZ, False))
VEL_Z = ((SXZ, False), (SYZ, False), (SZZ, True))
STR_X = ((VX, False), (VY, True), (VZ, True))
STR_Y = ((VX, True), (VY, False), (VZ, True))
STR_Z = ((VX, True), (VY, True), (VZ, False))


def band(width, forward):
    matrix = np.zeros((width + 8, width), np.float64)
    for out in range(width):
        for tap, coeff in enumerate(COEFFS, 1):
            upper = out + tap if forward else out + tap - 1
            lower = out + 1 - tap if forward else out - tap
            matrix[4 + upper, out] += coeff
            matrix[4 + lower, out] -= coeff
    return matrix


def two_part(matrix):
    high = matrix.astype(ml_dtypes.bfloat16)
    low = (matrix - high.astype(np.float64)).astype(ml_dtypes.bfloat16)
    return np.block([[high, low], [high, np.zeros_like(low)]]).astype(ml_dtypes.bfloat16)


def lane_constants():
    tile = np.stack([two_part(band(LANES, f)[4:-4]) for f in (False, True)])
    halo = []
    for parity in range(2):
        for forward in (False, True):
            matrix = band(LANES, forward)
            after = np.zeros((8, LANES))
            before = np.zeros((8, LANES))
            after[:4] = matrix[-4:]
            before[4:] = matrix[:4]
            pair = (after, before) if parity == 0 else (before, after)
            halo.append(two_part(np.concatenate(pair)))
    halo = np.stack(halo).reshape(2, 2, 32, 2 * LANES)
    edges = np.zeros((8, LANES), np.float32)
    for k in range(4):
        edges[k, k] = 1.0
        edges[4 + k, LANES - 4 + k] = 1.0
    edges = np.concatenate([edges, edges], axis=1).astype(ml_dtypes.bfloat16)
    return tile, halo, edges


def mean_constants():
    half = LANES // 2
    place = np.zeros((2, LANES, LANES), np.float32)
    for lane in range(LANES):
        for part in range(2):
            place[part, lane, part * half + lane // 2] = 1.0 / 16.0
    return np.concatenate([place, place], axis=1).astype(ml_dtypes.bfloat16)


def split(x):
    high = x.astype(BF16)
    return high, (x - high.astype(F32)).astype(BF16)


def fold(x):
    half = x.shape[1] // 2
    return x[:, :half] + x[:, half:]


def dot(a, b, dims=((1,), (0,))):
    return lax.dot_general(a, b, (dims, ((), ())), preferred_element_type=F32)


def dot_lanes(x, matrix):
    return fold(dot(jnp.concatenate(split(x), axis=1), matrix))


def dot_rows(x, matrix):
    return fold(dot(jnp.concatenate(split(x), axis=0), matrix, ((0,), (0,))))


def flat(x):
    return x.reshape(x.shape[0] * x.shape[1], x.shape[2])


def put_rows(out_a, out_b, base, fields, parity):
    even = parity == 0
    for k, (ref, f) in enumerate(fields):
        depth, rows = ref.shape[1], ref.shape[2]
        for z in range(depth):
            first = ref[f, z, 0:4, :]
            last = ref[f, z, rows - 4 : rows, :]
            at = pl.ds(base + 4 * (k * depth + z), 4)
            out_a[at, :] = jnp.where(even, last, first)
            out_b[at, :] = jnp.where(even, first, last)


def put_columns(outs, base, fields, edges):
    for k, (ref, f) in enumerate(fields):
        x = jnp.concatenate(split(flat(ref[f])), axis=1)
        turned = dot(edges, x, ((1,), (1,)))
        blocks = turned.shape[1] // LANES
        for m in range(blocks):
            for out in outs:
                out[pl.ds(base + 8 * (k * blocks + m), 8), :] = turned[:, m * LANES : (m + 1) * LANES]


def fill_x(ext, fields, msg_a, msg_b, base, parity):
    even = parity == 0
    for k, (ref, f) in enumerate(fields):
        depth, rows = ref.shape[1], ref.shape[2]
        ext[k, :, 8 : 8 + rows, :] = ref[f]
        for z in range(depth):
            at = pl.ds(base + 4 * (k * depth + z), 4)
            a, b = msg_a[at, :], msg_b[at, :]
            ext[k, z, 8 + rows : 12 + rows, :] = jnp.where(even, a, b)
            ext[k, z, 4:8, :] = jnp.where(even, b, a)


def fill_y(out, fields, directions, msg_a, msg_b, base, parity, tile, halo):
    for k, (ref, f) in enumerate(fields):
        count = ref.shape[1] * ref.shape[2]
        forward = int(directions[k])
        inner = dot_lanes(flat(ref[f]), tile[forward])
        factor = halo[parity, forward]
        for m in range(count // LANES):
            at = pl.ds(base + 8 * (k * (count // LANES) + m), 8)
            outer = dot_rows(jnp.concatenate([msg_a[at, :], msg_b[at, :]], axis=0), factor)
            out[k, m * LANES : (m + 1) * LANES, :] = inner[m * LANES : (m + 1) * LANES] + outer


def fill_z(ext, fields, top, bottom):
    for k, (ref, f) in enumerate(fields):
        depth = ref.shape[1]
        ext[k, 4 : 4 + depth] = ref[f]
        for g in range(4):
            ext[k, g] = top(k, g)
            ext[k, 4 + depth + g] = bottom(k, g)


def taps(read, forward):
    total = None
    for tap, coeff in enumerate(COEFFS, 1):
        upper = tap if forward else tap - 1
        lower = 1 - tap if forward else -tap
        term = coeff * (read(upper) - read(lower))
        total = term if total is None else total + term
    return total


def along_x(ext, k, z, rows, forward):
    return taps(lambda d: ext[k, z, 8 + d : 8 + d + rows, :], forward)


def along_z(ext, k, z, forward):
    return taps(lambda d: ext[k, z + 4 + d], forward)


def along_y(values, k, z, rows):
    return values[k, pl.ds(pl.multiple_of(z * rows, rows), rows), :]


def velocity_half(old, buoyancy, out, ex, ey, ez):
    depth, rows = old.shape[1], old.shape[2]

    def layer(z, _):
        scale = STEP * buoyancy[0, z]
        zx = along_z(ez, 0, z, False)
        zy = along_z(ez, 1, z, False)
        zz = along_z(ez, 2, z, True)
        x = along_x(ex, 0, z, rows, True)
        out[0, z] = old[0, z] + scale * (x + along_y(ey, 0, z, rows) + zx)
        x = along_x(ex, 1, z, rows, False)
        out[1, z] = old[1, z] + scale * (x + along_y(ey, 1, z, rows) + zy)
        x = along_x(ex, 2, z, rows, False)
        out[2, z] = old[2, z] + scale * (x + along_y(ey, 2, z, rows) + zz)
        return 0

    lax.fori_loop(0, depth, layer, 0)


def stress_half(old, lame, shear, out, base, ex, ey, ez):
    depth, rows = lame.shape[1], lame.shape[2]

    def layer(z, _):
        exx = along_x(ex, 0, z, rows, False)
        eyy = along_y(ey, 1, z, rows)
        ezz = along_z(ez, 2, z, False)
        mu = STEP * shear[0, z]
        common = (STEP * lame[0, z]) * (exx + eyy + ezz)
        double = mu + mu
        out[base, z] = old(0, z) + (common + double * exx)
        out[base + 1, z] = old(1, z) + (common + double * eyy)
        out[base + 2, z] = old(2, z) + (common + double * ezz)
        x = along_x(ex, 1, z, rows, True)
        out[base + 3, z] = old(3, z) + mu * (along_y(ey, 0, z, rows) + x)
        x = along_x(ex, 2, z, rows, True)
        out[base + 4, z] = old(4, z) + mu * (along_z(ez, 0, z, True) + x)
        y = along_y(ey, 2, z, rows)
        out[base + 5, z] = old(5, z) + mu * (along_z(ez, 1, z, True) + y)
        return 0

    lax.fori_loop(0, depth, layer, 0)


def zeros_like_plane(ref):
    return jnp.zeros(ref.shape[-2:], F32)


def planes_kernel(state, past, out):
    rows = state.shape[2]
    for n, f in enumerate(CROSSING):
        for layer in range(2):
            now = state[f, layer]
            out[pl.ds((2 * n + layer) * rows, rows), :] = now
            later = 1.5 * now - 0.5 * past[f, layer]
            out[pl.ds((12 + 2 * n + layer) * rows, rows), :] = later


def pack_kernel(par, fine, coarse, edges, out_a, out_b, out_1, out_2):
    pi, pj = par[0], par[1]
    depth, rows = fine.shape[1], fine.shape[2]
    fine_x = [(fine, f) for f, _ in VEL_X]
    fine_y = [(fine, f) for f, _ in VEL_Y]
    coarse_x = [(coarse, f) for f, _ in VEL_X]
    coarse_y = [(coarse, f) for f, _ in VEL_Y]
    put_rows(out_a, out_b, 0, fine_x, pi)
    put_columns((out_a, out_b), 12 * depth, coarse_y, edges[...])
    put_columns((out_1, out_2), 0, fine_y, edges[...])
    put_rows(out_1, out_2, 24 * (depth * rows // LANES), coarse_x, pj)


def ghost_kernel(par, own, other, prow, pcol, in_a, in_b, ghost, virtual, out_a, out_b):
    pi, pj = par[0], par[1]
    row_base, col_base = par[2], par[3]
    part = own.shape[0] // 24
    fine_rows = prow.shape[1]
    even_col = pj == 0
    source = lax.broadcasted_iota(jnp.int32, (LANES, LANES), 0)
    mine = (source == pcol[...] - col_base).astype(F32)
    beyond = (source == jnp.where(even_col, 0, LANES - 1)).astype(F32)
    pick_cols = jnp.concatenate([mine, beyond], axis=1).astype(BF16)
    pick_cols = jnp.concatenate([pick_cols, pick_cols], axis=0)
    source = lax.broadcasted_iota(jnp.int32, (2 * part, LANES), 0)
    lane = lax.broadcasted_iota(jnp.int32, (2 * part, LANES), 1)
    wanted = jnp.concatenate(
        [prow[...] - row_base, jnp.full((1, LANES - fine_rows), -1, jnp.int32)], axis=1
    )
    wanted = jnp.where(lane == fine_rows, 2 * part - 1, jnp.where(lane == fine_rows + 1, 0, wanted))
    pick_rows = (source == wanted).astype(BF16)
    pick_rows = jnp.concatenate([pick_rows, pick_rows], axis=0)

    def spread(ref):
        return dot(jnp.concatenate(split(ref[...]), axis=1), pick_cols)

    from_own, from_other = spread(own), spread(other)
    first = jnp.where(even_col, from_own, from_other)
    second = jnp.where(even_col, from_other, from_own)
    lanes = lax.broadcasted_iota(jnp.int32, (LANES, LANES), 1)
    aside = jnp.zeros((LANES, LANES), F32)
    even_row = pi == 0
    base = in_a.shape[0]
    out_a[0:base, :] = in_a[...]
    out_b[0:base, :] = in_b[...]
    for p in range(24):
        at = slice(p * part, (p + 1) * part)
        plane = jnp.concatenate([first[at], second[at]], axis=0)
        full = dot(pick_rows, jnp.concatenate(split(plane), axis=0), ((0,), (0,)))
        tile = full[:, :LANES]
        aside = jnp.where(lanes == p, full[:, LANES:], aside)
        ghost[p] = tile[:fine_rows]
        below, above = tile[fine_rows : fine_rows + 1], tile[fine_rows + 1 : fine_rows + 2]
        out_a[base + p : base + p + 1, :] = jnp.where(even_row, below, above)
        out_b[base + p : base + p + 1, :] = jnp.where(even_row, above, below)
    below, above = aside[fine_rows : fine_rows + 1], aside[fine_rows + 1 : fine_rows + 2]
    pad = jnp.zeros((7, LANES), F32)
    out_a[base + 24 : base + 32, :] = jnp.concatenate([jnp.where(even_row, below, above), pad], axis=0)
    out_b[base + 24 : base + 32, :] = jnp.concatenate([jnp.where(even_row, above, below), pad], axis=0)
    virtual[...] = aside[:fine_rows]


def after_before(msg_a, msg_b, at, parity):
    even = parity == 0
    a, b = msg_a[at, :], msg_b[at, :]
    return jnp.where(even, a, b), jnp.where(even, b, a)


def corner_kernel(par, msg_a, msg_b, virtual, in_1, in_2, out_1, out_2):
    base = in_1.shape[0]
    rows = virtual.shape[0]
    corner = msg_a.shape[0] - 8
    after, before = after_before(msg_a, msg_b, slice(corner, corner + 1), par[0])
    out_1[0:base, :] = in_1[...]
    out_2[0:base, :] = in_2[...]
    row = lax.broadcasted_iota(jnp.int32, (rows, LANES), 0)
    column = virtual[...]
    column = column + jnp.where(row == 0, before, 0.0) + jnp.where(row == rows - 1, after, 0.0)
    out_1[base : base + rows, :] = column
    out_2[base : base + rows, :] = column


def first_velocity_kernel(
    par, old, normal, shearing, buoyancy, ghost, msg_a, msg_b, msg_1, msg_2, tile, halo, edges,
    out, ghost_out, out_a, out_b, out_c, ex, ey, ez,
):
    pi, pj = par[0], par[1]
    rows = old.shape[2]
    strip = msg_a.shape[0] - 32
    after, before = after_before(msg_a, msg_b, slice(strip, strip + 24), pi)
    column = msg_2[msg_2.shape[0] - rows :, :]
    row = lax.broadcasted_iota(jnp.int32, (rows, LANES), 0)
    lane = lax.broadcasted_iota(jnp.int32, (rows, LANES), 1)
    edge = lane == jnp.where(pj == 0, 0, LANES - 1)
    for p in range(24):
        plane = ghost[p]
        plane = plane + jnp.where(row == 0, before[p : p + 1], 0.0)
        plane = plane + jnp.where(row == rows - 1, after[p : p + 1], 0.0)
        ghost_out[p] = plane + jnp.where(edge, column[:, p : p + 1], 0.0)
    velocity_body(
        par, old, normal, shearing, buoyancy, ghost_out, 0, msg_a, msg_b, msg_1, msg_2,
        tile, halo, edges, out, out_a, out_b, out_c, ex, ey, ez,
    )


def stress_ref(normal, shearing, f):
    return (normal, f - SXX) if f < SXY else (shearing, f - SXY)


def velocity_body(
    par, old, normal, shearing, buoyancy, ghost, level, msg_a, msg_b, msg_1, msg_2,
    tile, halo, edges, out, out_a, out_b, out_c, ex, ey, ez,
):
    pi, pj = par[0], par[1]
    pick = functools.partial(stress_ref, normal, shearing)
    none = zeros_like_plane(old)
    order = [CROSSING.index(f) for f, _ in VEL_Z]
    fill_z(
        ez, [pick(f) for f, _ in VEL_Z],
        lambda k, g: none, lambda k, g: ghost[12 * level + 2 * order[k] + g // 2],
    )
    fill_x(ex, [pick(f) for f, _ in VEL_X], msg_a, msg_b, 0, pi)
    fill_y(
        ey, [pick(f) for f, _ in VEL_Y], [d for _, d in VEL_Y], msg_1, msg_2, 0, pj, tile, halo
    )
    velocity_half(old, buoyancy, out, ex, ey, ez)
    moved = [(out, c) for c in range(3)]
    put_rows(out_a, out_b, 0, moved, pi)
    put_columns((out_c,), 0, moved, edges[...])


def velocity_kernel(
    par, old, normal, shearing, buoyancy, ghost, msg_a, msg_b, msg_1, msg_2, tile, halo, edges,
    out, out_a, out_b, out_c, ex, ey, ez,
):
    velocity_body(
        par, old, normal, shearing, buoyancy, ghost, 1, msg_a, msg_b, msg_1, msg_2,
        tile, halo, edges, out, out_a, out_b, out_c, ex, ey, ez,
    )


def stress_fill(par, velocity, ghost, level, msg_a, msg_b, msg_1, msg_2, tile, halo, ex, ey, ez):
    pi, pj = par[0], par[1]
    none = zeros_like_plane(velocity)
    fields = [(velocity, c) for c in range(3)]
    fill_z(
        ez, fields, lambda k, g: none, lambda k, g: ghost[12 * level + 2 * k + g // 2]
    )
    fill_x(ex, fields, msg_a, msg_b, 0, pi)
    fill_y(ey, fields, [d for _, d in STR_Y], msg_1, msg_2, 0, pj, tile, halo)


def stress_kernel(
    par, velocity, normal, shearing, lame, shear, ghost, msg_a, msg_b, msg_1, msg_2, tile, halo,
    edges, out, out_a, out_b, out_c, ex, ey, ez,
):
    pi, pj = par[0], par[1]
    stress_fill(par, velocity, ghost, 0, msg_a, msg_b, msg_1, msg_2, tile, halo, ex, ey, ez)
    old = lambda c, z: normal[c, z] if c < 3 else shearing[c - 3, z]
    stress_half(old, lame, shear, out, 0, ex, ey, ez)
    put_rows(out_a, out_b, 0, [(out, f - SXX) for f, _ in VEL_X], pi)
    put_columns((out_c,), 0, [(out, f - SXX) for f, _ in VEL_Y], edges[...])


def last_stress_kernel(
    par, velocity, normal, shearing, lame, shear, ghost, start, msg_a, msg_b, msg_1, msg_2,
    tile, halo, means, out, coarse, ex, ey, ez, summed, halves,
):
    stress_fill(par, velocity, ghost, 1, msg_a, msg_b, msg_1, msg_2, tile, halo, ex, ey, ez)
    old = lambda c, z: normal[c, z] if c < 3 else shearing[c - 3, z]
    out[0:3] = velocity[...]
    stress_half(old, lame, shear, out, 3, ex, ey, ez)
    depth, rows = velocity.shape[1], velocity.shape[2]
    part = rows // 4
    for n, f in enumerate(CROSSING):
        for m in range(4):
            z = depth - 8 + 2 * m
            total = (start[f, 2 * m] + start[f, 2 * m + 1]) + (out[f, z] + out[f, z + 1])
            summed[...] = total
            pairs = summed[pl.ds(0, 2 * part, stride=2), :] + summed[pl.ds(1, 2 * part, stride=2), :]
            at = pl.ds((4 * n + m) * part, part)
            halves[0, at, :] = pairs[:part]
            halves[1, at, :] = pairs[part:]
    upper = dot(jnp.concatenate(split(halves[0]), axis=1), means[0])
    lower = dot(jnp.concatenate(split(halves[1]), axis=1), means[1])
    coarse[...] = upper + lower


def coarse_velocity_kernel(
    par, state, medium, own, other, msg_a, msg_b, msg_1, msg_2, tile, halo, edges,
    out, ghost, out_1, out_2, out_c, ex, ey, ez, *, base_c, base_r,
):
    pi, pj = par[0], par[1]
    rows = state.shape[2]
    half = LANES // 2
    even = pj == 0
    left = jnp.where(even, own[...], other[...])
    right = jnp.where(even, other[...], own[...])
    low = lax.broadcasted_iota(jnp.int32, left.shape, 1) < half
    ghost[...] = jnp.where(
        even,
        jnp.where(low, left, pltpu.roll(right, half, 1)),
        jnp.where(low, pltpu.roll(left, half, 1), right),
    )
    none = zeros_like_plane(state)
    order = [CROSSING.index(f) for f, _ in VEL_Z]
    fill_z(
        ez, [(state, f) for f, _ in VEL_Z],
        lambda k, g: ghost[pl.ds((4 * order[k] + g) * rows, rows), :], lambda k, g: none,
    )
    fill_x(ex, [(state, f) for f, _ in VEL_X], msg_1, msg_2, base_r, pj)
    fill_y(
        ey, [(state, f) for f, _ in VEL_Y], [d for _, d in VEL_Y], msg_a, msg_b, base_c, pi,
        tile, halo,
    )
    velocity_half(state, medium, out, ex, ey, ez)
    moved = [(out, c) for c in range(3)]
    put_rows(out_1, out_2, 0, moved, pj)
    put_columns((out_c,), 0, moved, edges[...])


def coarse_stress_kernel(
    par, state, medium, velocity, ghost, msg_a, msg_b, msg_1, msg_2, tile, halo,
    out, ex, ey, ez,
):
    pi, pj = par[0], par[1]
    rows = state.shape[2]
    none = zeros_like_plane(state)
    fields = [(velocity, c) for c in range(3)]
    fill_z(
        ez, fields, lambda k, g: ghost[pl.ds((4 * k + g) * rows, rows), :], lambda k, g: none
    )
    fill_x(ex, fields, msg_1, msg_2, 0, pj)
    fill_y(ey, fields, [d for _, d in STR_Y], msg_a, msg_b, 0, pi, tile, halo)
    out[0:3] = velocity[...]
    stress_half(
        lambda c, z: state[3 + c, z], medium.at[1:2], medium.at[2:3], out, 3, ex, ey, ez
    )


def call(kernel, args, outs, scratch=()):
    specs, values = [], []
    for n, arg in enumerate(args):
        if n == 0:
            specs.append(pl.BlockSpec(memory_space=pltpu.SMEM))
            values.append(arg)
        elif isinstance(arg, tuple):
            array, block, index = arg
            specs.append(pl.BlockSpec(block, functools.partial(lambda where, _: where, index)))
            values.append(array)
        else:
            specs.append(pl.BlockSpec(arg.shape, functools.partial(lambda rank, _: (0,) * rank, arg.ndim)))
            values.append(arg)
    return pl.pallas_call(
        kernel,
        grid=(1,),
        in_specs=specs,
        out_specs=[
            pl.BlockSpec(o, functools.partial(lambda rank, _: (0,) * rank, len(o))) for o in outs
        ],
        out_shape=[jax.ShapeDtypeStruct(o, F32) for o in outs],
        scratch_shapes=[pltpu.VMEM(s, F32) for s in scratch],
        compiler_params=pltpu.CompilerParams(vmem_limit_bytes=48 * 1024 * 1024),
    )(*values)


def matchings(axis):
    size = lax.axis_size(axis)
    result = []
    for start in range(2):
        pairs = []
        for low in range(start, size - 1, 2):
            pairs += [(low, low + 1), (low + 1, low)]
        result.append(pairs)
    return result


def exchange(axis, first, second):
    one, two = matchings(axis)
    return lax.ppermute(first, axis, one), lax.ppermute(second, axis, two)


def body(
    fine_state, fine_medium, coarse_state, coarse_medium, coarse_past, parent_rows, parent_cols
):
    size_x, size_y = lax.axis_size("gx"), lax.axis_size("gy")
    i, j = lax.axis_index("gx"), lax.axis_index("gy")
    depth, rows, cols = fine_state.shape[1:]
    thick, part = coarse_state.shape[1:3]
    blocks = depth * rows // LANES
    par = jnp.stack([i % 2, j % 2, i * (rows // 2), (j // 2) * LANES]).astype(jnp.int32)
    tile, halo, edges = (jnp.asarray(c) for c in lane_constants())
    means = jnp.asarray(mean_constants())
    across = [
        (p * size_y + q, (q // 2) * size_y + 2 * p + q % 2)
        for p in range(size_x)
        for q in range(size_y)
    ]
    partner = matchings("gy")[0]

    def of_state(count, start):
        return (fine_state, (count, depth, rows, cols), (start // count, 0, 0, 0))

    def of_medium(index):
        return (fine_medium, (1, depth, rows, cols), (index, 0, 0, 0))

    planes = pl.pallas_call(
        planes_kernel,
        grid=(1,),
        in_specs=[
            pl.BlockSpec((9, 2, part, LANES), lambda _: (0, 0, 0, 0)),
            pl.BlockSpec((9, 2, part, LANES), lambda _: (0, 0, 0, 0)),
        ],
        out_specs=pl.BlockSpec((24 * part, LANES), lambda _: (0, 0)),
        out_shape=jax.ShapeDtypeStruct((24 * part, LANES), F32),
    )(coarse_state, coarse_past)
    own = lax.ppermute(planes, ("gx", "gy"), across)
    other = lax.ppermute(own, "gy", partner)

    rows_msg, cols_msg = 12 * depth, 24 * blocks
    coarse_cols, coarse_rows = 24, 12 * thick
    base_x = rows_msg + coarse_cols
    base_y = cols_msg + coarse_rows
    part_a, part_b, part_1, part_2 = call(
        pack_kernel,
        [par, fine_state, coarse_state, edges],
        [(base_x, LANES)] * 2 + [(base_y, LANES)] * 2,
    )
    ghost, virtual, out_a, out_b = call(
        ghost_kernel,
        [par, own, other, parent_rows.reshape(1, rows), parent_cols.reshape(1, cols), part_a, part_b],
        [(24, rows, cols), (rows, LANES), (base_x + 32, LANES), (base_x + 32, LANES)],
    )
    msg_a, msg_b = exchange("gx", out_a, out_b)
    out_1, out_2 = call(
        corner_kernel,
        [par, msg_a, msg_b, virtual, part_1, part_2],
        [(base_y + rows, LANES)] * 2,
    )
    msg_1, msg_2 = exchange("gy", out_1, out_2)
    begin_a, begin_b, begin_1, begin_2 = msg_a, msg_b, msg_1, msg_2

    shape = (depth, rows, cols)
    scratch = [
        (3, depth, rows + 16, cols), (3, depth * rows, cols), (3, depth + 8, rows, cols),
    ]
    halves = [(rows_msg, LANES)] * 2 + [(cols_msg, LANES)]
    velocity, ghost, out_a, out_b, out_c = call(
        first_velocity_kernel,
        [par, of_state(3, 0), of_state(3, 3), of_state(3, 6), of_medium(0), ghost,
         msg_a, msg_b, msg_1, msg_2, tile, halo, edges],
        [(3,) + shape, (24, rows, cols)] + halves,
        scratch,
    )
    msg_a, msg_b = exchange("gx", out_a, out_b)
    msg_1, msg_2 = exchange("gy", out_c, out_c)
    stress, out_a, out_b, out_c = call(
        stress_kernel,
        [par, velocity, of_state(3, 3), of_state(3, 6), of_medium(1), of_medium(2), ghost,
         msg_a, msg_b, msg_1, msg_2, tile, halo, edges],
        [(6,) + shape] + halves,
        scratch,
    )
    msg_a, msg_b = exchange("gx", out_a, out_b)
    msg_1, msg_2 = exchange("gy", out_c, out_c)
    normal = (stress, (3,) + shape, (0, 0, 0, 0))
    shearing = (stress, (3,) + shape, (1, 0, 0, 0))
    velocity, out_a, out_b, out_c = call(
        velocity_kernel,
        [par, velocity, normal, shearing, of_medium(0), ghost,
         msg_a, msg_b, msg_1, msg_2, tile, halo, edges],
        [(3,) + shape] + halves,
        scratch,
    )
    msg_a, msg_b = exchange("gx", out_a, out_b)
    msg_1, msg_2 = exchange("gy", out_c, out_c)
    start = (fine_state, (9, 8, rows, cols), (0, depth // 8 - 1, 0, 0))
    fine_out, lifted = call(
        last_stress_kernel,
        [par, velocity, normal, shearing, of_medium(1), of_medium(2), ghost, start,
         msg_a, msg_b, msg_1, msg_2, tile, halo, means],
        [(9,) + shape, (24 * part, LANES)],
        scratch + [(rows, cols), (2, 24 * part, LANES)],
    )
    own = lax.ppermute(lifted, ("gx", "gy"), across)
    other = lax.ppermute(own, "gy", partner)

    shape = (thick, part, LANES)
    scratch = [
        (3, thick, part + 16, LANES), (3, thick * part, LANES), (3, thick + 8, part, LANES),
    ]
    velocity, ghost, out_1, out_2, out_c = call(
        functools.partial(coarse_velocity_kernel, base_c=rows_msg, base_r=cols_msg),
        [par, coarse_state, (coarse_medium, (1,) + shape, (0, 0, 0, 0)), own, other,
         begin_a, begin_b, begin_1, begin_2, tile, halo, edges],
        [(3,) + shape, (24 * part, LANES), (coarse_rows, LANES), (coarse_rows, LANES),
         (coarse_cols, LANES)],
        scratch,
    )
    msg_a, msg_b = exchange("gx", out_c, out_c)
    msg_1, msg_2 = exchange("gy", out_1, out_2)
    (coarse_out,) = call(
        coarse_stress_kernel,
        [par, coarse_state, coarse_medium, velocity, ghost, msg_a, msg_b, msg_1, msg_2, tile, halo],
        [(9,) + shape],
        scratch,
    )
    return (fine_out, coarse_out)


def solution(mesh):
    placed = (
        P(None, None, "gx", "gy"),
        P(None, None, "gx", "gy"),
        P(None, None, "gy", "gx"),
        P(None, None, "gy", "gx"),
        P(None, None, "gy", "gx"),
        P("gx"),
        P("gy"),
    )
    return jax.shard_map(
        body,
        mesh=mesh,
        in_specs=placed,
        out_specs=(P(None, None, "gx", "gy"), P(None, None, "gy", "gx")),
        check_vma=False,
    )
```

time: 581 us -> 130 us (0.22); the launches traced: 570 us -> 129 us
  other arithmetic: 213 us -> 0.08 us
  local copies, waits for them, and re-layouts: 174 us -> 4.14 us
  starting transfers between devices: 113 us -> 69.9 us
  waiting for transfers between devices: 57.4 us -> 18.5 us
  Pallas kernels: 0 us -> 35.6 us
  blocking collectives: 9.89 us -> 0 us
    another operation x12 -> x1, other arithmetic: 70.1 us -> 0.08 us  [body(): jnp.stack([i % 2, j % 2, i * (rows // 2), j // 2 * LANES]).astype(jnp.int32)]
    slice x29 -> x0, local copies, waits for them, and re-layouts: 58 us -> none  [the longest x10 38.9 us: extended_2(): last = lax.slice_in_dim(x, length - width, length, axis=dim)]
    concatenate x15 -> x0, other arithmetic: 52.1 us -> none  [the longest x9 45.2 us: extended_2(): x = jnp.concatenate([before, x, after], axis=dim)]
    all_to_all x8 -> x0, starting transfers between devices: 36.6 us -> none  [the longest x3 16.3 us: regrid(): lax.all_to_all(lax.all_to_all(sectioned, 'gx', split_axis=4, concat_axis=...]
    pallas_call x0 -> x10, Pallas kernels: none -> 35.6 us  [the longest x9 33.9 us: call(): pl.pallas_call(kernel, grid=(1,), in_specs=specs, out_specs=[pl.BlockSpec...]
    unnamed x106 -> x26, local copies, waits for them, and re-layouts: 38.5 us -> 4.14 us
    ppermute x24, waiting for transfers between devices: 50 us -> 18.5 us  [the longest x20 17.1 us: exchange(): return (lax.ppermute(first, axis, one), lax.ppermute(second, axis, two))]
    reduce_sum x1 -> x0, other arithmetic: 24.3 us -> none  [body(): blended.reshape(9, 4, 2, rows_half, 2, cols_half, 2).mean(axis=(2, 4, 6))]
  transfers between devices with their start and end apart: 32 -> 24, of which waited for: 20 -> 7; matrix products, arithmetic and copies ran while one was open for 14% -> 0% of each run, Pallas kernels for 0% -> 1%
where the time goes in v1:
time: 130 us; the launch traced here: 129 us
  starting transfers between devices  69.9 us (54%)
  Pallas kernels  35.6 us (27%)
  waiting for transfers between devices  18.5 us (14%)
  local copies, waits for them, and re-layouts  4.14 us (3%)
    ppermute x20, starting transfers between devices, exchange(): return (lax.ppermute(first, axis, one), lax.ppermute(second, axis, two))  67.6 us
    pallas_call x9, Pallas kernels, call(): pl.pallas_call(kernel, grid=(1,), in_specs=specs, out_specs=[pl.BlockSpec...  33.9 us
    ppermute x20, waiting for transfers between devices, exchange(): return (lax.ppermute(first, axis, one), lax.ppermute(second, axis, two))  17.1 us
    unnamed x26, local copies, waits for them, and re-layouts  4.14 us
  transfers between devices with their start and end apart: 24, of which 7 were waited for; matrix products, arithmetic and copies ran while one was open for 0% of the time, Pallas kernels for 1%

profile of v1, /device:TPU:1, one launch (start us, length us, event | category | flops | bytes accessed | tf_op | source)
XLA Modules:
  0.0 129.2 jit_solution(11222140973993330583)
XLA Ops:
  0.7 1.7 %shard_map.122 = f32[384,128]{1,0:T(8,128)} custom-call(f32[9,8,16,128]{3,2,1,0:T(8,128)} %state.5, f32[9,2,16,128]{3,2,1,0:T(8,128)} %past.1), custom_call_target="tpu_custom_call" | custom-call | tf_op jit(solution)/shard_map/pallas_call | solution.py:541
  2.3 1.6 %collective-permute-start = (f32[384,128]{1,0:T(8,128)}, f32[384,128]{1,0:T(8,128)S(1)}, u32[]{:S(2)}, u32[]{:S(2)}) collective-permute-start(f32[384,128]{1,0:T(8,128)} %shard_map.122), channel_id=1, source_target_pairs={{0,0},{1,1},{2,8},{3,9},{4,16},{5,17},{6,24},{7,25},{8,2},{9,3},{1... | collective-permute-start | bytes 589832 | tf_op jit(solution)/shard_map/ppermute | solution.py:551
  4.1 2.3 %copy-done = f32[9,16,64,128]{3,2,1,0:T(8,128)S(1)} copy-done((f32[9,16,64,128]{3,2,1,0:T(8,128)S(1)}, f32[9,16,64,128]{3,2,1,0:T(8,128)}, u32[]{:S(2)}) %copy-start) | copy-done | bytes 4718616
  6.4 1.1 copy-done.4
  7.5 0.7 copy-done.9
  8.1 1.2 shard_map.123
  9.3 1.3 shard_map.124
  10.6 17.4 %collective-permute-start.2 = (f32[248,128]{1,0:T(8,128)S(1)}, f32[248,128]{1,0:T(8,128)S(1)}, u32[]{:S(2)}, u32[]{:S(2)}) collective-permute-start(f32[248,128]{1,0:T(8,128)S(1)} %get-tuple-element.35), channel_id=1, source_target_pairs={{0,8},{8,0},{16,24},{24,16},{1,9},{9,1},{17,25},{25,17},{2,10},{10... | collective-permute-start | bytes 380936 | tf_op jit(solution)/shard_map/ppermute | solution.py:514
  28.0 0.7 collective-permute-start.3
  28.7 3.1 %collective-permute-done.2.msg_a = f32[248,128]{1,0:T(8,128)S(1)} collective-permute-done((f32[248,128]{1,0:T(8,128)S(1)}, f32[248,128]{1,0:T(8,128)S(1)}, u32[]{:S(2)}, u32[]{:S(2)}) %collective-permute-start.2) | collective-permute-done | bytes 127008 | tf_op jit(solution)/shard_map/ppermute | solution.py:514
  33.0 5.1 %collective-permute-start.5 = (f32[352,128]{1,0:T(8,128)S(1)}, f32[352,128]{1,0:T(8,128)S(1)}, u32[]{:S(2)}, u32[]{:S(2)}) collective-permute-start(f32[352,128]{1,0:T(8,128)S(1)} %get-tuple-element.41), channel_id=1, source_target_pairs={{1,2},{2,1},{3,4},{4,3},{5,6},{6,5},{9,10},{10,9},{11,12},{12,11},... | collective-permute-start | bytes 540680 | tf_op jit(solution)/shard_map/ppermute | solution.py:514
  38.1 4.9 %collective-permute-done.5.msg_2 = f32[352,128]{1,0:T(8,128)S(1)} collective-permute-done((f32[352,128]{1,0:T(8,128)S(1)}, f32[352,128]{1,0:T(8,128)S(1)}, u32[]{:S(2)}, u32[]{:S(2)}) %collective-permute-start.5) | collective-permute-done | bytes 180256 | tf_op jit(solution)/shard_map/ppermute | solution.py:514
  43.0 6.2 %shard_map.126 = (f32[3,16,64,128]{3,2,1,0:T(8,128)S(1)}, f32[24,64,128]{2,1,0:T(8,128)S(1)}, f32[192,128]{1,0:T(8,128)S(1)}, f32[192,128]{1,0:T(8,128)S(1)}, f32[192,128]{1,0:T(8,128)S(1)}) custom-call(s32[4]{0:T(128)S(1)} %pad_add_fusion.par, f32[9,16,64,128]{3,2,1,0:T(8,128)} %start.1, f32[9,16,64,128]{3,2,1,0:T(8,128)} %start.1, ...), custom_call_target="tpu_custom_call" | custom-call | tf_op jit(solution)/shard_map/pallas_call | solution.py:488
  49.2 1.6 %collective-permute-start.6 = (f32[192,128]{1,0:T(8,128)S(1)}, f32[192,128]{1,0:T(8,128)S(1)}, u32[]{:S(2)}, u32[]{:S(2)}) collective-permute-start(f32[192,128]{1,0:T(8,128)S(1)} %get-tuple-element.44), channel_id=1, source_target_pairs={{0,8},{8,0},{16,24},{24,16},{1,9},{9,1},{17,25},{25,17},{2,10},{10... | collective-permute-start | bytes 294920 | tf_op jit(solution)/shard_map/ppermute | solution.py:514
  51.5 3.9 %collective-permute-start.9 = (f32[192,128]{1,0:T(8,128)S(1)}, f32[192,128]{1,0:T(8,128)S(1)}, u32[]{:S(2)}, u32[]{:S(2)}) collective-permute-start(f32[192,128]{1,0:T(8,128)S(1)} %get-tuple-element.46), channel_id=1, source_target_pairs={{1,2},{2,1},{3,4},{4,3},{5,6},{6,5},{9,10},{10,9},{11,12},{12,11},... | collective-permute-start | bytes 294920 | tf_op jit(solution)/shard_map/ppermute | solution.py:514
  55.5 2.2 %collective-permute-done.9.msg_2 = f32[192,128]{1,0:T(8,128)S(1)} collective-permute-done((f32[192,128]{1,0:T(8,128)S(1)}, f32[192,128]{1,0:T(8,128)S(1)}, u32[]{:S(2)}, u32[]{:S(2)}) %collective-permute-start.9) | collective-permute-done | bytes 98336 | tf_op jit(solution)/shard_map/ppermute | solution.py:514
  57.7 7.0 %shard_map.127 = (f32[6,16,64,128]{3,2,1,0:T(8,128)}, f32[192,128]{1,0:T(8,128)S(1)}, f32[192,128]{1,0:T(8,128)S(1)}, f32[192,128]{1,0:T(8,128)S(1)}) custom-call(s32[4]{0:T(128)S(1)} %pad_add_fusion.par, f32[3,16,64,128]{3,2,1,0:T(8,128)S(1)} %get-tuple-element.42.velocity.old, f32[9,16,64,128]{3,2,1,0:T(8,128)} %start.1, f32[9,16,64,128]{3,2,1,0:T(8,128)} %start.1, ...), custom_call_target="tpu_custom_call" | custom-call | tf_op jit(solution)/shard_map/pallas_call | solution.py:488
  64.7 1.3 collective-permute-start.10
  66.6 5.8 %collective-permute-start.13 = (f32[192,128]{1,0:T(8,128)S(1)}, f32[192,128]{1,0:T(8,128)S(1)}, u32[]{:S(2)}, u32[]{:S(2)}) collective-permute-start(f32[192,128]{1,0:T(8,128)S(1)} %get-tuple-element.50), channel_id=1, source_target_pairs={{1,2},{2,1},{3,4},{4,3},{5,6},{6,5},{9,10},{10,9},{11,12},{12,11},... | collective-permute-start | bytes 294920 | tf_op jit(solution)/shard_map/ppermute | solution.py:514
  72.6 2.2 %collective-permute-done.13.msg_2 = f32[192,128]{1,0:T(8,128)S(1)} collective-permute-done((f32[192,128]{1,0:T(8,128)S(1)}, f32[192,128]{1,0:T(8,128)S(1)}, u32[]{:S(2)}, u32[]{:S(2)}) %collective-permute-start.13) | collective-permute-done | bytes 98336 | tf_op jit(solution)/shard_map/ppermute | solution.py:514
  74.8 5.9 %shard_map.128 = (f32[3,16,64,128]{3,2,1,0:T(8,128)S(1)}, f32[192,128]{1,0:T(8,128)S(1)}, f32[192,128]{1,0:T(8,128)S(1)}, f32[192,128]{1,0:T(8,128)S(1)}) custom-call(s32[4]{0:T(128)S(1)} %pad_add_fusion.par, f32[3,16,64,128]{3,2,1,0:T(8,128)S(1)} %get-tuple-element.42.velocity.old, f32[6,16,64,128]{3,2,1,0:T(8,128)} %get-tuple-element.47.normal.shearing, ...), custom_call_target="tpu_custom_call" | custom-call | tf_op jit(solution)/shard_map/pallas_call | solution.py:488
  80.7 1.8 %collective-permute-start.14 = (f32[192,128]{1,0:T(8,128)S(1)}, f32[192,128]{1,0:T(8,128)S(1)}, u32[]{:S(2)}, u32[]{:S(2)}) collective-permute-start(f32[192,128]{1,0:T(8,128)S(1)} %get-tuple-element.52), channel_id=1, source_target_pairs={{0,8},{8,0},{16,24},{24,16},{1,9},{9,1},{17,25},{25,17},{2,10},{10... | collective-permute-start | bytes 294920 | tf_op jit(solution)/shard_map/ppermute | solution.py:514
  83.1 4.8 %collective-permute-start.17 = (f32[192,128]{1,0:T(8,128)S(1)}, f32[192,128]{1,0:T(8,128)S(1)}, u32[]{:S(2)}, u32[]{:S(2)}) collective-permute-start(f32[192,128]{1,0:T(8,128)S(1)} %get-tuple-element.54), channel_id=1, source_target_pairs={{1,2},{2,1},{3,4},{4,3},{5,6},{6,5},{9,10},{10,9},{11,12},{12,11},... | collective-permute-start | bytes 294920 | tf_op jit(solution)/shard_map/ppermute | solution.py:514
  88.0 2.2 %collective-permute-done.17.msg_2 = f32[192,128]{1,0:T(8,128)S(1)} collective-permute-done((f32[192,128]{1,0:T(8,128)S(1)}, f32[192,128]{1,0:T(8,128)S(1)}, u32[]{:S(2)}, u32[]{:S(2)}) %collective-permute-start.17) | collective-permute-done | bytes 98336 | tf_op jit(solution)/shard_map/ppermute | solution.py:514
  90.3 8.4 %shard_map.129 = (f32[9,16,64,128]{3,2,1,0:T(8,128)}, f32[384,128]{1,0:T(8,128)S(1)}) custom-call(s32[4]{0:T(128)S(1)} %pad_add_fusion.par, f32[3,16,64,128]{3,2,1,0:T(8,128)S(1)} %get-tuple-element.51.velocity, f32[6,16,64,128]{3,2,1,0:T(8,128)} %get-tuple-element.47.normal.shearing, f32[6,16,64,128]{3,2,1,0:T(8,128)} %get-tuple-element.47.normal.shearing, ...), custom_call_target="tpu_custom_call" | custom-call | tf_op jit(solution)/shard_map/pallas_call | solution.py:488
  98.7 0.7 collective-permute-start.18
  99.4 1.4 %collective-permute-done.19.other = f32[384,128]{1,0:T(8,128)S(1)} collective-permute-done((f32[384,128]{1,0:T(8,128)S(1)}, f32[384,128]{1,0:T(8,128)S(1)}, u32[]{:S(2)}, u32[]{:S(2)}) %collective-permute-start.19) | collective-permute-done | bytes 196640 | tf_op jit(solution)/shard_map/ppermute | solution.py:620
  100.9 1.3 %shard_map.130 = (f32[3,8,16,128]{3,2,1,0:T(8,128)S(1)}, f32[384,128]{1,0:T(8,128)S(1)}, f32[96,128]{1,0:T(8,128)S(1)}, f32[96,128]{1,0:T(8,128)S(1)}, f32[24,128]{1,0:T(8,128)S(1)}) custom-call(s32[4]{0:T(128)S(1)} %pad_add_fusion.par, f32[9,8,16,128]{3,2,1,0:T(8,128)S(1)} %copy-done.5, f32[3,8,16,128]{3,2,1,0:T(8,128)S(1)} %copy-done.7, ...), custom_call_target="tpu_custom_call" | custom-call | tf_op jit(solution)/shard_map/pallas_call | solution.py:488
  102.4 21.5 %collective-permute-start.23 = (f32[96,128]{1,0:T(8,128)S(1)}, f32[96,128]{1,0:T(8,128)S(1)}, u32[]{:S(2)}, u32[]{:S(2)}) collective-permute-start(f32[96,128]{1,0:T(8,128)S(1)} %get-tuple-element.61), channel_id=1, source_target_pairs={{1,2},{2,1},{3,4},{4,3},{5,6},{6,5},{9,10},{10,9},{11,12},{12,11},... | collective-permute-start | bytes 147464 | tf_op jit(solution)/shard_map/ppermute | solution.py:514
  123.9 0.7 collective-permute-start.21
  124.7 2.5 %collective-permute-done.20.msg_a = f32[24,128]{1,0:T(8,128)S(1)} collective-permute-done((f32[24,128]{1,0:T(8,128)S(1)}, f32[24,128]{1,0:T(8,128)S(1)}, u32[]{:S(2)}, u32[]{:S(2)}) %collective-permute-start.20) | collective-permute-done | bytes 12320 | tf_op jit(solution)/shard_map/ppermute | solution.py:514
  127.2 2.0 %shard_map.131 = f32[9,8,16,128]{3,2,1,0:T(8,128)} custom-call(s32[4]{0:T(128)S(1)} %pad_add_fusion.par, f32[9,8,16,128]{3,2,1,0:T(8,128)S(1)} %copy-done.5, f32[3,8,16,128]{3,2,1,0:T(8,128)S(1)} %copy-done.7, f32[3,8,16,128]{3,2,1,0:T(8,128)S(1)} %get-tuple-element.57.velocity, f32[384,128]{1,0:T(8,128)S(1)} %get-tuple-element.58.ghost, ...), custom_call_target="tpu_custom_call" | custom-call | tf_op jit(solution)/shard_map/pallas_call | solution.py:488
  (53 shorter events, 3.9 us)
Async XLA Ops:
  2.3 1.6 %collective-permute-start = (f32[384,128]{1,0:T(8,128)}, f32[384,128]{1,0:T(8,128)S(1)}, u32[]{:S(2)}, u32[]{:S(2)}) collective-permute-start(f32[384,128]{1,0:T(8,128)} %shard_map.122), channel_id=1, source_target_pairs={{0,0},{1,1},{2,8},{3,9},{4,16},{5,17},{6,24},{7,25},{8,2},{9,3},{1... | collective-permute-start | bytes 589832 | tf_op jit(solution)/shard_map/ppermute | solution.py:551
  3.9 5.4 %collective-permute-start.1 = (f32[384,128]{1,0:T(8,128)S(1)}, f32[384,128]{1,0:T(8,128)S(1)}, u32[]{:S(2)}, u32[]{:S(2)}) collective-permute-start(f32[384,128]{1,0:T(8,128)S(1)} %collective-permute-done.own), channel_id=1, source_target_pairs={{0,1},{1,0},{2,3},{3,2},{4,5},{5,4},{6,7},{7,6},{8,9},{9,8},{10,11... | collective-permute-start | bytes 589832 | tf_op jit(solution)/shard_map/ppermute | solution.py:552
  8.1 34.8 %copy-start.1 = (f32[3,16,64,128]{3,2,1,0:T(8,128)S(1)}, f32[3,16,64,128]{3,2,1,0:T(8,128)}, u32[]{:S(2)}) copy-start(f32[3,16,64,128]{3,2,1,0:T(8,128)} %shear.3) | copy-start | bytes 4718596
  8.1 34.8 %copy-start.3 = (bf16[2,256,256]{2,1,0:T(8,128)(2,1)S(1)}, bf16[2,256,256]{2,1,0:T(8,128)(2,1)}, u32[]{:S(2)}) copy-start(bf16[2,256,256]{2,1,0:T(8,128)(2,1)} %constant.48.clone.tile) | copy-start | bytes 786436
  8.1 34.8 %copy-start.6 = (bf16[2,2,32,256]{3,2,1,0:T(8,128)(2,1)S(1)}, bf16[2,2,32,256]{3,2,1,0:T(8,128)(2,1)}, u32[]{:S(2)}) copy-start(bf16[2,2,32,256]{3,2,1,0:T(8,128)(2,1)} %constant.49.clone.halo) | copy-start | bytes 196612
  10.6 21.2 %collective-permute-start.2 = (f32[248,128]{1,0:T(8,128)S(1)}, f32[248,128]{1,0:T(8,128)S(1)}, u32[]{:S(2)}, u32[]{:S(2)}) collective-permute-start(f32[248,128]{1,0:T(8,128)S(1)} %get-tuple-element.35), channel_id=1, source_target_pairs={{0,8},{8,0},{16,24},{24,16},{1,9},{9,1},{17,25},{25,17},{2,10},{10... | collective-permute-start | bytes 380936 | tf_op jit(solution)/shard_map/ppermute | solution.py:514
  28.0 3.8 %collective-permute-start.3 = (f32[248,128]{1,0:T(8,128)S(1)}, f32[248,128]{1,0:T(8,128)S(1)}, u32[]{:S(2)}, u32[]{:S(2)}) collective-permute-start(f32[248,128]{1,0:T(8,128)S(1)} %get-tuple-element.36), channel_id=1, source_target_pairs={{8,16},{16,8},{9,17},{17,9},{10,18},{18,10},{11,19},{19,11},{12,20... | collective-permute-start | bytes 380936 | tf_op jit(solution)/shard_map/ppermute | solution.py:514
  32.4 5.7 %collective-permute-start.4 = (f32[352,128]{1,0:T(8,128)S(1)}, f32[352,128]{1,0:T(8,128)S(1)}, u32[]{:S(2)}, u32[]{:S(2)}) collective-permute-start(f32[352,128]{1,0:T(8,128)S(1)} %get-tuple-element.40), channel_id=1, source_target_pairs={{0,1},{1,0},{2,3},{3,2},{4,5},{5,4},{6,7},{7,6},{8,9},{9,8},{10,11... | collective-permute-start | bytes 540680 | tf_op jit(solution)/shard_map/ppermute | solution.py:514
  33.0 10.0 %collective-permute-start.5 = (f32[352,128]{1,0:T(8,128)S(1)}, f32[352,128]{1,0:T(8,128)S(1)}, u32[]{:S(2)}, u32[]{:S(2)}) collective-permute-start(f32[352,128]{1,0:T(8,128)S(1)} %get-tuple-element.41), channel_id=1, source_target_pairs={{1,2},{2,1},{3,4},{4,3},{5,6},{6,5},{9,10},{10,9},{11,12},{12,11},... | collective-permute-start | bytes 540680 | tf_op jit(solution)/shard_map/ppermute | solution.py:514
  49.2 6.3 %collective-permute-start.6 = (f32[192,128]{1,0:T(8,128)S(1)}, f32[192,128]{1,0:T(8,128)S(1)}, u32[]{:S(2)}, u32[]{:S(2)}) collective-permute-start(f32[192,128]{1,0:T(8,128)S(1)} %get-tuple-element.44), channel_id=1, source_target_pairs={{0,8},{8,0},{16,24},{24,16},{1,9},{9,1},{17,25},{25,17},{2,10},{10... | collective-permute-start | bytes 294920 | tf_op jit(solution)/shard_map/ppermute | solution.py:514
  50.8 4.7 %collective-permute-start.7 = (f32[192,128]{1,0:T(8,128)S(1)}, f32[192,128]{1,0:T(8,128)S(1)}, u32[]{:S(2)}, u32[]{:S(2)}) collective-permute-start(f32[192,128]{1,0:T(8,128)S(1)} %get-tuple-element.45), channel_id=1, source_target_pairs={{8,16},{16,8},{9,17},{17,9},{10,18},{18,10},{11,19},{19,11},{12,20... | collective-permute-start | bytes 294920 | tf_op jit(solution)/shard_map/ppermute | solution.py:514
  51.5 6.2 %collective-permute-start.9 = (f32[192,128]{1,0:T(8,128)S(1)}, f32[192,128]{1,0:T(8,128)S(1)}, u32[]{:S(2)}, u32[]{:S(2)}) collective-permute-start(f32[192,128]{1,0:T(8,128)S(1)} %get-tuple-element.46), channel_id=1, source_target_pairs={{1,2},{2,1},{3,4},{4,3},{5,6},{6,5},{9,10},{10,9},{11,12},{12,11},... | collective-permute-start | bytes 294920 | tf_op jit(solution)/shard_map/ppermute | solution.py:514
  55.4 2.3 %collective-permute-start.8 = (f32[192,128]{1,0:T(8,128)S(1)}, f32[192,128]{1,0:T(8,128)S(1)}, u32[]{:S(2)}, u32[]{:S(2)}) collective-permute-start(f32[192,128]{1,0:T(8,128)S(1)} %get-tuple-element.46), channel_id=1, source_target_pairs={{0,1},{1,0},{2,3},{3,2},{4,5},{5,4},{6,7},{7,6},{8,9},{9,8},{10,11... | collective-permute-start | bytes 294920 | tf_op jit(solution)/shard_map/ppermute | solution.py:514
  57.7 17.0 %copy-start.10 = (bf16[8,256]{1,0:T(8,128)(2,1)S(1)}, bf16[8,256]{1,0:T(8,128)(2,1)}, u32[]{:S(2)}) copy-start(bf16[8,256]{1,0:T(8,128)(2,1)} %constant.50.clone.edges) | copy-start | bytes 12292
  64.7 7.8 %collective-permute-start.10 = (f32[192,128]{1,0:T(8,128)S(1)}, f32[192,128]{1,0:T(8,128)S(1)}, u32[]{:S(2)}, u32[]{:S(2)}) collective-permute-start(f32[192,128]{1,0:T(8,128)S(1)} %get-tuple-element.48), channel_id=1, source_target_pairs={{0,8},{8,0},{16,24},{24,16},{1,9},{9,1},{17,25},{25,17},{2,10},{10... | collective-permute-start | bytes 294920 | tf_op jit(solution)/shard_map/ppermute | solution.py:514
  66.0 6.6 %collective-permute-start.11 = (f32[192,128]{1,0:T(8,128)S(1)}, f32[192,128]{1,0:T(8,128)S(1)}, u32[]{:S(2)}, u32[]{:S(2)}) collective-permute-start(f32[192,128]{1,0:T(8,128)S(1)} %get-tuple-element.49), channel_id=1, source_target_pairs={{8,16},{16,8},{9,17},{17,9},{10,18},{18,10},{11,19},{19,11},{12,20... | collective-permute-start | bytes 294920 | tf_op jit(solution)/shard_map/ppermute | solution.py:514
  66.6 8.1 %collective-permute-start.13 = (f32[192,128]{1,0:T(8,128)S(1)}, f32[192,128]{1,0:T(8,128)S(1)}, u32[]{:S(2)}, u32[]{:S(2)}) collective-permute-start(f32[192,128]{1,0:T(8,128)S(1)} %get-tuple-element.50), channel_id=1, source_target_pairs={{1,2},{2,1},{3,4},{4,3},{5,6},{6,5},{9,10},{10,9},{11,12},{12,11},... | collective-permute-start | bytes 294920 | tf_op jit(solution)/shard_map/ppermute | solution.py:514
  72.5 2.3 %collective-permute-start.12 = (f32[192,128]{1,0:T(8,128)S(1)}, f32[192,128]{1,0:T(8,128)S(1)}, u32[]{:S(2)}, u32[]{:S(2)}) collective-permute-start(f32[192,128]{1,0:T(8,128)S(1)} %get-tuple-element.50), channel_id=1, source_target_pairs={{0,1},{1,0},{2,3},{3,2},{4,5},{5,4},{6,7},{7,6},{8,9},{9,8},{10,11... | collective-permute-start | bytes 294920 | tf_op jit(solution)/shard_map/ppermute | solution.py:514
  74.8 15.5 %copy-start.2 = (f32[3,16,64,128]{3,2,1,0:T(8,128)S(1)}, f32[3,16,64,128]{3,2,1,0:T(8,128)}, u32[]{:S(2)}) copy-start(f32[3,16,64,128]{3,2,1,0:T(8,128)} %shear.3) | copy-start | bytes 4718596
  74.8 15.5 %copy-start.8 = (bf16[2,256,128]{2,1,0:T(8,128)(2,1)S(1)}, bf16[2,256,128]{2,1,0:T(8,128)(2,1)}, u32[]{:S(2)}) copy-start(bf16[2,256,128]{2,1,0:T(8,128)(2,1)} %constant.51.clone.means) | copy-start | bytes 393220
  80.7 7.3 %collective-permute-start.14 = (f32[192,128]{1,0:T(8,128)S(1)}, f32[192,128]{1,0:T(8,128)S(1)}, u32[]{:S(2)}, u32[]{:S(2)}) collective-permute-start(f32[192,128]{1,0:T(8,128)S(1)} %get-tuple-element.52), channel_id=1, source_target_pairs={{0,8},{8,0},{16,24},{24,16},{1,9},{9,1},{17,25},{25,17},{2,10},{10... | collective-permute-start | bytes 294920 | tf_op jit(solution)/shard_map/ppermute | solution.py:514
  82.5 5.6 %collective-permute-start.15 = (f32[192,128]{1,0:T(8,128)S(1)}, f32[192,128]{1,0:T(8,128)S(1)}, u32[]{:S(2)}, u32[]{:S(2)}) collective-permute-start(f32[192,128]{1,0:T(8,128)S(1)} %get-tuple-element.53), channel_id=1, source_target_pairs={{8,16},{16,8},{9,17},{17,9},{10,18},{18,10},{11,19},{19,11},{12,20... | collective-permute-start | bytes 294920 | tf_op jit(solution)/shard_map/ppermute | solution.py:514
  83.1 7.1 %collective-permute-start.17 = (f32[192,128]{1,0:T(8,128)S(1)}, f32[192,128]{1,0:T(8,128)S(1)}, u32[]{:S(2)}, u32[]{:S(2)}) collective-permute-start(f32[192,128]{1,0:T(8,128)S(1)} %get-tuple-element.54), channel_id=1, source_target_pairs={{1,2},{2,1},{3,4},{4,3},{5,6},{6,5},{9,10},{10,9},{11,12},{12,11},... | collective-permute-start | bytes 294920 | tf_op jit(solution)/shard_map/ppermute | solution.py:514
  87.9 2.3 %collective-permute-start.16 = (f32[192,128]{1,0:T(8,128)S(1)}, f32[192,128]{1,0:T(8,128)S(1)}, u32[]{:S(2)}, u32[]{:S(2)}) collective-permute-start(f32[192,128]{1,0:T(8,128)S(1)} %get-tuple-element.54), channel_id=1, source_target_pairs={{0,1},{1,0},{2,3},{3,2},{4,5},{5,4},{6,7},{7,6},{8,9},{9,8},{10,11... | collective-permute-start | bytes 294920 | tf_op jit(solution)/shard_map/ppermute | solution.py:514
  90.2 10.6 %copy-start.5 = (f32[9,8,16,128]{3,2,1,0:T(8,128)S(1)}, f32[9,8,16,128]{3,2,1,0:T(8,128)}, u32[]{:S(2)}) copy-start(f32[9,8,16,128]{3,2,1,0:T(8,128)} %state.5) | copy-start | bytes 1769476
  90.2 10.6 %copy-start.7 = (f32[3,8,16,128]{3,2,1,0:T(8,128)S(1)}, f32[3,8,16,128]{3,2,1,0:T(8,128)}, u32[]{:S(2)}) copy-start(f32[3,8,16,128]{3,2,1,0:T(8,128)} %medium.3) | copy-start | bytes 589828
  98.7 0.7 collective-permute-start.18
  99.3 1.5 %collective-permute-start.19 = (f32[384,128]{1,0:T(8,128)S(1)}, f32[384,128]{1,0:T(8,128)S(1)}, u32[]{:S(2)}, u32[]{:S(2)}) collective-permute-start(f32[384,128]{1,0:T(8,128)S(1)} %collective-permute-done.18.own), channel_id=1, source_target_pairs={{0,1},{1,0},{2,3},{3,2},{4,5},{5,4},{6,7},{7,6},{8,9},{9,8},{10,11... | collective-permute-start | bytes 589832 | tf_op jit(solution)/shard_map/ppermute | solution.py:620
  102.2 25.0 %collective-permute-start.22 = (f32[96,128]{1,0:T(8,128)S(1)}, f32[96,128]{1,0:T(8,128)S(1)}, u32[]{:S(2)}, u32[]{:S(2)}) collective-permute-start(f32[96,128]{1,0:T(8,128)S(1)} %get-tuple-element.60), channel_id=1, source_target_pairs={{0,1},{1,0},{2,3},{3,2},{4,5},{5,4},{6,7},{7,6},{8,9},{9,8},{10,11... | collective-permute-start | bytes 147464 | tf_op jit(solution)/shard_map/ppermute | solution.py:514
  102.4 24.8 %collective-permute-start.23 = (f32[96,128]{1,0:T(8,128)S(1)}, f32[96,128]{1,0:T(8,128)S(1)}, u32[]{:S(2)}, u32[]{:S(2)}) collective-permute-start(f32[96,128]{1,0:T(8,128)S(1)} %get-tuple-element.61), channel_id=1, source_target_pairs={{1,2},{2,1},{3,4},{4,3},{5,6},{6,5},{9,10},{10,9},{11,12},{12,11},... | collective-permute-start | bytes 147464 | tf_op jit(solution)/shard_map/ppermute | solution.py:514
  123.9 0.8 collective-permute-start.21
  124.6 2.6 %collective-permute-start.20 = (f32[24,128]{1,0:T(8,128)S(1)}, f32[24,128]{1,0:T(8,128)S(1)}, u32[]{:S(2)}, u32[]{:S(2)}) collective-permute-start(f32[24,128]{1,0:T(8,128)S(1)} %get-tuple-element.59), channel_id=1, source_target_pairs={{0,8},{8,0},{16,24},{24,16},{1,9},{9,1},{17,25},{25,17},{2,10},{10... | collective-permute-start | bytes 36872 | tf_op jit(solution)/shard_map/ppermute | solution.py:514
  (5 other events, 21.4 us)

commit v2 on v1

v2 whole, which is shorter than its diff:
```python
import functools

import jax
import jax.numpy as jnp
import ml_dtypes
import numpy as np
from jax import lax
from jax.experimental import pallas as pl
from jax.experimental.pallas import tpu as pltpu
from jax.sharding import PartitionSpec as P

COEFFS = (1225.0 / 1024.0, -245.0 / 3072.0, 49.0 / 5120.0, -5.0 / 7168.0)
STEP = 0.1
LANES = 128
F32 = jnp.float32
BF16 = jnp.bfloat16

VX, VY, VZ, SXX, SYY, SZZ, SXY, SXZ, SYZ = range(9)
CROSSING = (VX, VY, VZ, SXZ, SYZ, SZZ)
VEL_X = ((SXX, True), (SXY, False), (SXZ, False))
VEL_Y = ((SXY, False), (SYY, True), (SYZ, False))
VEL_Z = ((SXZ, False), (SYZ, False), (SZZ, True))
STR_X = ((VX, False), (VY, True), (VZ, True))
STR_Y = ((VX, True), (VY, False), (VZ, True))
STR_Z = ((VX, True), (VY, True), (VZ, False))


def band(width, forward):
    matrix = np.zeros((width + 8, width), np.float64)
    for out in range(width):
        for tap, coeff in enumerate(COEFFS, 1):
            upper = out + tap if forward else out + tap - 1
            lower = out + 1 - tap if forward else out - tap
            matrix[4 + upper, out] += coeff
            matrix[4 + lower, out] -= coeff
    return matrix


def two_part(matrix):
    high = matrix.astype(ml_dtypes.bfloat16)
    low = (matrix - high.astype(np.float64)).astype(ml_dtypes.bfloat16)
    return np.block([[high, low], [high, np.zeros_like(low)]]).astype(ml_dtypes.bfloat16)


def lane_constants():
    tile = np.stack([two_part(band(LANES, f)[4:-4]) for f in (False, True)])
    halo = []
    for parity in range(2):
        for forward in (False, True):
            matrix = band(LANES, forward)
            after = np.zeros((8, LANES))
            before = np.zeros((8, LANES))
            after[:4] = matrix[-4:]
            before[4:] = matrix[:4]
            pair = (after, before) if parity == 0 else (before, after)
            halo.append(two_part(np.concatenate(pair)))
    halo = np.stack(halo).reshape(2, 2, 32, 2 * LANES)
    return tile, halo


def mean_constants():
    half = LANES // 2
    place = np.zeros((2, LANES, LANES), np.float32)
    for lane in range(LANES):
        for part in range(2):
            place[part, lane, part * half + lane // 2] = 1.0 / 16.0
    return np.concatenate([place, place], axis=1).astype(ml_dtypes.bfloat16)


def split(x):
    high = x.astype(BF16)
    return high, (x - high.astype(F32)).astype(BF16)


def fold(x):
    half = x.shape[1] // 2
    return x[:, :half] + x[:, half:]


def dot(a, b, dims=((1,), (0,))):
    return lax.dot_general(a, b, (dims, ((), ())), preferred_element_type=F32)


def dot_lanes(x, matrix):
    return fold(dot(jnp.concatenate(split(x), axis=1), matrix))


def dot_rows(x, matrix):
    return fold(dot(jnp.concatenate(split(x), axis=0), matrix, ((0,), (0,))))


def flat(x):
    return x.reshape(x.shape[0] * x.shape[1], x.shape[2])


def upper_half(shape):
    return lax.broadcasted_iota(jnp.int32, shape, 0) < 4


def put_rows(out_a, out_b, base, fields, parity):
    parts = []
    for ref, f in fields:
        rows = ref.shape[2]
        parts.append((ref.at[:, :, 0:8, :], ref.at[:, :, rows - 8 : rows, :], f))
    put_edge_rows(out_a, out_b, base, parts, parity)


def put_edge_rows(out_a, out_b, base, fields, parity):
    even = parity == 0
    top = upper_half((8, LANES))
    for k, (head, tail, f) in enumerate(fields):
        depth = head.shape[1]
        for z in range(0, depth, 2):
            first = jnp.where(top, head[f, z], pltpu.roll(head[f, z + 1], 4, 0))
            last = jnp.where(top, pltpu.roll(tail[f, z], 4, 0), tail[f, z + 1])
            at = pl.ds(base + 4 * (k * depth + z), 8)
            out_a[at, :] = jnp.where(even, last, first)
            out_b[at, :] = jnp.where(even, first, last)


def put_columns(outs, base, fields):
    row = lax.broadcasted_iota(jnp.int32, (8, 2 * LANES), 0)
    lane = lax.broadcasted_iota(jnp.int32, (8, 2 * LANES), 1) % LANES
    edges = (lane == jnp.where(row < 4, row, LANES - 8 + row)).astype(BF16)
    for k, (ref, f) in enumerate(fields):
        x = ref[...] if f is None else flat(ref[f])
        x = jnp.concatenate(split(x), axis=1)
        turned = dot(edges, x, ((1,), (1,)))
        blocks = turned.shape[1] // LANES
        for m in range(blocks):
            for out in outs:
                out[pl.ds(base + 8 * (k * blocks + m), 8), :] = turned[:, m * LANES : (m + 1) * LANES]


def fill_x(ext, fields, msg_a, msg_b, base, parity, low=0, count=None):
    even = parity == 0
    for k, (ref, f) in enumerate(fields):
        depth, rows = ref.shape[1], ref.shape[2]
        layers = depth if count is None else count
        ext[k, :, 8 : 8 + rows, :] = ref[f, low : low + layers]
        for z in range(0, layers, 2):
            at = pl.ds(base + 4 * (k * depth + low + z), 8)
            a, b = msg_a[at, :], msg_b[at, :]
            after, before = jnp.where(even, a, b), jnp.where(even, b, a)
            ext[k, z, 8 + rows : 16 + rows, :] = after
            ext[k, z + 1, 8 + rows : 16 + rows, :] = pltpu.roll(after, 4, 0)
            ext[k, z, 0:8, :] = pltpu.roll(before, 4, 0)
            ext[k, z + 1, 0:8, :] = before


def fill_y(out, fields, directions, msg_a, msg_b, base, parity, tile, halo, low=0, count=None):
    for k, (ref, f) in enumerate(fields):
        depth, rows = ref.shape[1], ref.shape[2]
        layers = depth if count is None else count
        forward = int(directions[k])
        inner = dot_lanes(flat(ref[f, low : low + layers]), tile[forward])
        factor = halo[parity, forward]
        start, blocks = low * rows // LANES, depth * rows // LANES
        for m in range(layers * rows // LANES):
            at = pl.ds(base + 8 * (k * blocks + start + m), 8)
            outer = dot_rows(jnp.concatenate([msg_a[at, :], msg_b[at, :]], axis=0), factor)
            out[k, m * LANES : (m + 1) * LANES, :] = inner[m * LANES : (m + 1) * LANES] + outer


def fill_z(ext, fields, top, bottom, low=0, count=None):
    for k, (ref, f) in enumerate(fields):
        depth = ref.shape[1]
        layers = depth if count is None else count
        first, last = max(low - 4, 0), min(low + layers + 4, depth)
        ext[k, first - low + 4 : last - low + 4] = ref[f, first:last]
        for g in range(first - (low - 4)):
            ext[k, g] = top(k, 4 - first + low - 4 + g)
        for g in range(low + layers + 4 - last):
            ext[k, last - low + 4 + g] = bottom(k, g)


def taps(read, forward):
    total = None
    for tap, coeff in enumerate(COEFFS, 1):
        upper = tap if forward else tap - 1
        lower = 1 - tap if forward else -tap
        term = coeff * (read(upper) - read(lower))
        total = term if total is None else total + term
    return total


def along_x(ext, k, z, rows, forward):
    return taps(lambda d: ext[k, z, 8 + d : 8 + d + rows, :], forward)


def along_z(ext, k, z, forward):
    return taps(lambda d: ext[k, z + 4 + d], forward)


def along_y(values, k, z, rows):
    return values[k, pl.ds(pl.multiple_of(z * rows, rows), rows), :]


def velocity_half(old, buoyancy, out, ex, ey, ez):
    depth, rows = out.shape[1], out.shape[2]

    def layer(z, _):
        scale = STEP * buoyancy[0, z]
        zx = along_z(ez, 0, z, False)
        zy = along_z(ez, 1, z, False)
        zz = along_z(ez, 2, z, True)
        x = along_x(ex, 0, z, rows, True)
        out[0, z] = old[0, z] + scale * (x + along_y(ey, 0, z, rows) + zx)
        x = along_x(ex, 1, z, rows, False)
        out[1, z] = old[1, z] + scale * (x + along_y(ey, 1, z, rows) + zy)
        x = along_x(ex, 2, z, rows, False)
        out[2, z] = old[2, z] + scale * (x + along_y(ey, 2, z, rows) + zz)
        return 0

    lax.fori_loop(0, depth, layer, 0, unroll=2)


def stress_half(old, lame, shear, put, low, count, ex, ey, ez):
    rows = ex.shape[2] - 16

    def layer(n, _):
        z = n + low
        exx = along_x(ex, 0, n, rows, False)
        eyy = along_y(ey, 1, n, rows)
        ezz = along_z(ez, 2, n, False)
        mu = STEP * shear(z)
        common = (STEP * lame(z)) * (exx + eyy + ezz)
        double = mu + mu
        put(0, z, n, old(0, z) + (common + double * exx))
        put(1, z, n, old(1, z) + (common + double * eyy))
        put(2, z, n, old(2, z) + (common + double * ezz))
        x = along_x(ex, 1, n, rows, True)
        put(3, z, n, old(3, z) + mu * (along_y(ey, 0, n, rows) + x))
        x = along_x(ex, 2, n, rows, True)
        put(4, z, n, old(4, z) + mu * (along_z(ez, 0, n, True) + x))
        y = along_y(ey, 2, n, rows)
        put(5, z, n, old(5, z) + mu * (along_z(ez, 1, n, True) + y))
        return 0

    lax.fori_loop(0, count, layer, 0, unroll=2)


def zeros_like_plane(ref):
    return jnp.zeros(ref.shape[-2:], F32)


def pack_kernel(
    par, fine, coarse, past, out_a, out_b, out_1, out_2, planes, outer,
    turned, first, last, state, before, sems,
):
    pi, pj = par[0], par[1]
    depth, rows = fine.shape[1], fine.shape[2]
    part = coarse.shape[2]
    copies = [
        pltpu.make_async_copy(coarse, state, sems.at[0]),
        pltpu.make_async_copy(past, before, sems.at[1]),
    ]
    for k, (f, _) in enumerate(VEL_X):
        head, tail = fine.at[f, :, 0:8, :], fine.at[f, :, rows - 8 : rows, :]
        copies.append(pltpu.make_async_copy(head, first.at[k], sems.at[2 + 2 * k]))
        copies.append(pltpu.make_async_copy(tail, last.at[k], sems.at[3 + 2 * k]))
    for k, (f, _) in enumerate(VEL_Y):
        copies.append(pltpu.make_async_copy(fine.at[f], turned.at[k], sems.at[8 + k]))
    for copy in copies:
        copy.start()
    copies[0].wait()
    copies[1].wait()
    upper = pj == 0
    for n, f in enumerate(CROSSING):
        for layer in range(2):
            now = state[f, layer]
            later = 1.5 * now - 0.5 * before[f, layer]
            for p, plane in ((2 * n + layer, now), (12 + 2 * n + layer, later)):
                planes[pl.ds(p * part, part), :] = plane
                outer[p : p + 1, :] = jnp.where(upper, plane[:1], plane[part - 1 :])
    base = 12 * depth
    put_columns((out_a, out_b), base, [(state, f) for f, _ in VEL_Y])
    put_columns((out_a, out_b), base + 24, [(planes, None)])
    base = 24 * (depth * rows // LANES)
    put_rows(out_1, out_2, base, [(state, f) for f, _ in VEL_X], pj)
    base += 12 * coarse.shape[1]
    out_1[base : base + 24, :] = outer[...]
    out_2[base : base + 24, :] = outer[...]
    for copy in copies[2:8]:
        copy.wait()
    put_edge_rows(out_a, out_b, 0, [(first, last, k) for k in range(3)], pi)
    for k in range(3):
        copies[8 + k].wait()
        base = 8 * k * (depth * rows // LANES)
        put_columns((out_1, out_2), base, [(turned, k)])


def crossing_kernel(par, planes, msg_a, msg_b, msg_2, out):
    count = planes.shape[0]
    blocks = count // LANES
    out[0:count, :] = planes[...]
    out[count : count + 24, :] = msg_2[msg_2.shape[0] - 24 :, :]
    even = par[0] == 0
    base = msg_a.shape[0] - 8 * blocks
    left, right = [], []
    for m in range(blocks):
        a = msg_a[pl.ds(base + 8 * m, 8), :]
        b = msg_b[pl.ds(base + 8 * m, 8), :]
        left.append(jnp.where(even, b, a)[7:8])
        right.append(jnp.where(even, a, b)[0:1])
    fill = [jnp.zeros((8 - blocks, LANES), F32)]
    out[count + 24 : count + 32, :] = jnp.concatenate(left + fill, axis=0)
    out[count + 32 : count + 40, :] = jnp.concatenate(right + fill, axis=0)


def expand_ghosts(par, own, other, corner_1, corner_2, prow, pcol, ghost):
    core = par[1]
    row_base, col_base = par[2], par[3]
    part = (own.shape[0] - 40) // 24
    rows = prow.shape[1]
    low = core == 0
    count = 24 * part
    source = lax.broadcasted_iota(jnp.int32, (LANES, LANES), 0)
    pick_cols = (source == pcol[...] - col_base).astype(BF16)
    pick_cols = jnp.concatenate([pick_cols, pick_cols], axis=0)
    source = lax.broadcasted_iota(jnp.int32, (2 * part, rows), 0)
    pick_rows = (source == prow[...] - row_base).astype(BF16)
    pick_rows = jnp.concatenate([pick_rows, pick_rows], axis=0)

    def spread(x):
        return dot(jnp.concatenate(split(x), axis=1), pick_cols)

    mine, theirs = spread(own[0 : count + 24, :]), spread(other[0 : count + 24, :])
    first, second = jnp.where(low, mine, theirs), jnp.where(low, theirs, mine)
    above, below = first[count:], second[count:]
    beside = []
    for ref in (own, other):
        side = jnp.where(low, ref[count + 24 : count + 32, :], ref[count + 32 : count + 40, :])
        side = jnp.concatenate([side, jnp.zeros((LANES - 8, LANES), F32)], axis=0)
        beside.append(side.T)
    side_1 = jnp.where(low, beside[0], beside[1])
    side_2 = jnp.where(low, beside[1], beside[0])
    turn = jnp.where(low, 1, LANES - 1)
    top = pltpu.roll(jnp.where(low, corner_1[...], corner_2[...]), turn, 1)
    bottom = pltpu.roll(jnp.where(low, corner_2[...], corner_1[...]), turn, 1)

    lane = lax.broadcasted_iota(jnp.int32, (rows, LANES), 1)
    row = lax.broadcasted_iota(jnp.int32, (rows, LANES), 0)
    edge = lane == jnp.where(low, 0, LANES - 1)
    edge_row = edge[:1]
    above = above + jnp.where(edge_row, top, 0.0)
    below = below + jnp.where(edge_row, bottom, 0.0)
    group = LANES // part
    columns = []
    for q in range(group):
        at = slice(q * part, (q + 1) * part)
        column = jnp.concatenate([side_1[at], side_2[at]], axis=0)
        columns.append(dot(pick_rows, jnp.concatenate(split(column), axis=0), ((0,), (0,))))
    for p in range(24):
        at = slice(p * part, (p + 1) * part)
        plane = jnp.concatenate([first[at], second[at]], axis=0)
        full = dot(pick_rows, jnp.concatenate(split(plane), axis=0), ((0,), (0,)))
        column = columns[p % group][:, p // group : p // group + 1]
        full = full + jnp.where(edge, column, 0.0)
        full = full + jnp.where(row == 0, above[p : p + 1], 0.0)
        ghost[p] = full + jnp.where(row == rows - 1, below[p : p + 1], 0.0)


def ghost_kernel(
    par, half, buoyancy, own, other, corner_1, corner_2, prow, pcol,
    out, ghost, out_a, out_b, out_c,
):
    expand_ghosts(par, own, other, corner_1, corner_2, prow, pcol, ghost)
    depth = half.shape[1]
    for c, (f, forward) in enumerate(VEL_Z):
        out[c, 0 : depth - 4] = half[c, 0 : depth - 4]
        n = CROSSING.index(f)
        planes = [ghost[2 * n], ghost[2 * n + 1]]
        for z in range(depth - 4, depth):
            total = None
            for tap, coeff in enumerate(COEFFS, 1):
                g = z + (tap if forward else tap - 1) - depth
                if g >= 0:
                    term = coeff * planes[g // 2]
                    total = term if total is None else total + term
            value = half[c, z]
            if total is not None:
                value = value + (STEP * buoyancy[0, z]) * total
            out[c, z] = value
    moved = [(out, c) for c in range(3)]
    put_rows(out_a, out_b, 0, moved, par[0])
    put_columns((out_c,), 0, moved)


def stress_fields(ref, table):
    offset = 9 - ref.shape[0]
    return [(ref, f - offset) for f, _ in table]


def velocity_fill(par, stress, msg_a, msg_b, msg_1, msg_2, tile, halo, bottom, ex, ey, ez):
    pi, pj = par[0], par[1]
    none = zeros_like_plane(stress)
    fill_z(ez, stress_fields(stress, VEL_Z), lambda k, g: none, bottom)
    fill_x(ex, stress_fields(stress, VEL_X), msg_a, msg_b, 0, pi)
    fill_y(
        ey, stress_fields(stress, VEL_Y), [d for _, d in VEL_Y], msg_1, msg_2, 0, pj, tile, halo
    )


def first_velocity_kernel(
    par, state, buoyancy, msg_a, msg_b, msg_1, msg_2, tile, halo, out, ex, ey, ez
):
    none = zeros_like_plane(state)
    velocity_fill(
        par, state, msg_a, msg_b, msg_1, msg_2, tile, halo, lambda k, g: none, ex, ey, ez
    )
    velocity_half(state, buoyancy, out, ex, ey, ez)


def velocity_kernel(
    par, old, stress, buoyancy, ghost, msg_a, msg_b, msg_1, msg_2, tile, halo,
    out, out_a, out_b, out_c, ex, ey, ez,
):
    order = [CROSSING.index(f) for f, _ in VEL_Z]
    velocity_fill(
        par, stress, msg_a, msg_b, msg_1, msg_2, tile, halo,
        lambda k, g: ghost[12 + 2 * order[k] + g // 2], ex, ey, ez,
    )
    velocity_half(old, buoyancy, out, ex, ey, ez)
    moved = [(out, c) for c in range(3)]
    put_rows(out_a, out_b, 0, moved, par[0])
    put_columns((out_c,), 0, moved)


def stress_fill(
    par, velocity, bottom, msg_a, msg_b, msg_1, msg_2, tile, halo, ex, ey, ez, low, count
):
    pi, pj = par[0], par[1]
    none = zeros_like_plane(velocity)
    fields = [(velocity, c) for c in range(3)]
    fill_z(ez, fields, lambda k, g: none, bottom, low, count)
    fill_x(ex, fields, msg_a, msg_b, 0, pi, low, count)
    fill_y(
        ey, fields, [d for _, d in STR_Y], msg_1, msg_2, 0, pj, tile, halo, low, count
    )


def stress_kernel(
    par, velocity, state, medium, ghost, msg_a, msg_b, msg_1, msg_2, tile, halo,
    out, out_a, out_b, out_c, ex, ey, ez,
):
    depth = velocity.shape[1]
    stress_fill(
        par, velocity, lambda k, g: ghost[2 * k + g // 2], msg_a, msg_b, msg_1, msg_2,
        tile, halo, ex, ey, ez, 0, depth,
    )

    def put(c, z, n, value):
        out[c, z] = value

    stress_half(
        lambda c, z: state[SXX + c, z], lambda z: medium[1, z], lambda z: medium[2, z],
        put, 0, depth, ex, ey, ez,
    )
    put_rows(out_a, out_b, 0, stress_fields(out, VEL_X), par[0])
    put_columns((out_c,), 0, stress_fields(out, VEL_Y))


def lower_stress_kernel(
    par, velocity, stress, medium, ghost, start, msg_a, msg_b, msg_1, msg_2, tile, halo, means,
    out, coarse, ex, ey, ez, summed, halves,
):
    depth, rows = velocity.shape[1], velocity.shape[2]
    low = depth - 8
    stress_fill(
        par, velocity, lambda k, g: ghost[12 + 2 * k + g // 2], msg_a, msg_b, msg_1, msg_2,
        tile, halo, ex, ey, ez, low, 8,
    )
    out[0:3] = velocity[:, low:]

    def put(c, z, n, value):
        out[SXX + c, n] = value

    stress_half(
        lambda c, z: stress[c, z], lambda z: medium[1, z], lambda z: medium[2, z],
        put, low, 8, ex, ey, ez,
    )
    part = rows // 4
    for n, f in enumerate(CROSSING):
        for m in range(4):
            z = 2 * m
            total = (start[f, low + z] + start[f, low + z + 1]) + (out[f, z] + out[f, z + 1])
            summed[...] = total
            pairs = summed[pl.ds(0, 2 * part, stride=2), :] + summed[pl.ds(1, 2 * part, stride=2), :]
            at = pl.ds((4 * n + m) * part, part)
            halves[0, at, :] = pairs[:part]
            halves[1, at, :] = pairs[part:]
    upper = dot(jnp.concatenate(split(halves[0]), axis=1), means[0])
    lower = dot(jnp.concatenate(split(halves[1]), axis=1), means[1])
    coarse[...] = upper + lower


def upper_stress_kernel(
    par, below, velocity, stress, medium, msg_a, msg_b, msg_1, msg_2, tile, halo,
    out, done, ex, ey, ez,
):
    stress_fill(
        par, velocity, None, msg_a, msg_b, msg_1, msg_2, tile, halo, ex, ey, ez, 0, 8
    )
    out[0:3] = velocity[:, 0:8]

    def put(c, z, n, value):
        out[SXX + c, n] = value

    stress_half(
        lambda c, z: stress[c, z], lambda z: medium[1, z], lambda z: medium[2, z],
        put, 0, 8, ex, ey, ez,
    )
    done[...] = jnp.zeros_like(done)


def coarse_velocity_kernel(
    par, state, medium, own, other, msg_a, msg_b, msg_1, msg_2, tile, halo, done,
    out, ghost, out_1, out_2, out_c, ex, ey, ez, *, base_c, base_r,
):
    pi, pj = par[0], par[1]
    rows = state.shape[2]
    half = LANES // 2
    even = pj == 0
    left = jnp.where(even, own[...], other[...])
    right = jnp.where(even, other[...], own[...])
    low = lax.broadcasted_iota(jnp.int32, left.shape, 1) < half
    ghost[...] = jnp.where(
        even,
        jnp.where(low, left, pltpu.roll(right, half, 1)),
        jnp.where(low, pltpu.roll(left, half, 1), right),
    )
    none = zeros_like_plane(state)
    order = [CROSSING.index(f) for f, _ in VEL_Z]
    fill_z(
        ez, stress_fields(state, VEL_Z),
        lambda k, g: ghost[pl.ds((4 * order[k] + g) * rows, rows), :], lambda k, g: none,
    )
    fill_x(ex, stress_fields(state, VEL_X), msg_1, msg_2, base_r, pj)
    fill_y(
        ey, stress_fields(state, VEL_Y), [d for _, d in VEL_Y], msg_a, msg_b, base_c, pi,
        tile, halo,
    )
    velocity_half(state, medium, out, ex, ey, ez)
    moved = [(out, c) for c in range(3)]
    put_rows(out_1, out_2, 0, moved, pj)
    put_columns((out_c,), 0, moved)


def coarse_stress_kernel(
    par, state, medium, velocity, ghost, msg_a, msg_b, msg_1, msg_2, tile, halo,
    out, ex, ey, ez,
):
    pi, pj = par[0], par[1]
    depth, rows = state.shape[1], state.shape[2]
    none = zeros_like_plane(state)
    fields = [(velocity, c) for c in range(3)]
    fill_z(
        ez, fields, lambda k, g: ghost[pl.ds((4 * k + g) * rows, rows), :], lambda k, g: none
    )
    fill_x(ex, fields, msg_1, msg_2, 0, pj)
    fill_y(ey, fields, [d for _, d in STR_Y], msg_a, msg_b, 0, pi, tile, halo)
    out[0:3] = velocity[...]

    def put(c, z, n, value):
        out[SXX + c, z] = value

    stress_half(
        lambda c, z: state[SXX + c, z], lambda z: medium[1, z], lambda z: medium[2, z],
        put, 0, depth, ex, ey, ez,
    )


def whole(shape):
    return pl.BlockSpec(shape, functools.partial(lambda rank, _: (0,) * rank, len(shape)))


def call(kernel, args, outs, scratch=(), parts=(), flops=0, copied=0, **options):
    specs = [pl.BlockSpec(memory_space=pltpu.SMEM)]
    for n, a in enumerate(args[1:]):
        specs.append(pl.BlockSpec(memory_space=pltpu.HBM) if n < copied else whole(a.shape))
    if "above" in options:
        array = options.pop("above")
        specs.insert(1, pl.BlockSpec(memory_space=pl.ANY))
        args = [args[0], array] + list(args[1:])
        options["input_output_aliases"] = {1: 0}
    out_specs, out_shapes = [], []
    for n, shape in enumerate(outs):
        if n < len(parts):
            full, place = parts[n]
            out_specs.append(pl.BlockSpec(shape, functools.partial(lambda p, _: p, place)))
            out_shapes.append(jax.ShapeDtypeStruct(full, F32))
        else:
            out_specs.append(whole(shape))
            out_shapes.append(jax.ShapeDtypeStruct(shape, F32))
    size = sum(4 * int(np.prod(a.shape)) for a in args) + sum(4 * int(np.prod(o)) for o in outs)
    return pl.pallas_call(
        kernel,
        grid=(1,),
        in_specs=specs,
        out_specs=out_specs,
        out_shape=out_shapes,
        scratch_shapes=[pltpu.VMEM(s, F32) for s in scratch]
        + ([pltpu.SemaphoreType.DMA((11,))] if copied else []),
        compiler_params=pltpu.CompilerParams(vmem_limit_bytes=(60 if copied else 20) * 1024 * 1024),
        cost_estimate=pl.CostEstimate(flops=flops, bytes_accessed=size, transcendentals=0),
        **options,
    )(*args)


def matchings(axis):
    size = lax.axis_size(axis)
    result = []
    for start in range(2):
        pairs = []
        for low in range(start, size - 1, 2):
            pairs += [(low, low + 1), (low + 1, low)]
        result.append(pairs)
    return result


def exchange(axis, first, second):
    one, two = matchings(axis)
    return lax.ppermute(first, axis, one), lax.ppermute(second, axis, two)


def body(
    fine_state, fine_medium, coarse_state, coarse_medium, coarse_past, parent_rows, parent_cols
):
    size_x, size_y = lax.axis_size("gx"), lax.axis_size("gy")
    i, j = lax.axis_index("gx"), lax.axis_index("gy")
    depth, rows, cols = fine_state.shape[1:]
    thick, part = coarse_state.shape[1:3]
    blocks = depth * rows // LANES
    par = jnp.stack([i % 2, j % 2, i * (rows // 2), (j // 2) * LANES]).astype(jnp.int32)
    tile, halo = (jnp.asarray(c) for c in lane_constants())
    means = jnp.asarray(mean_constants())
    across = [
        (p * size_y + q, (q // 2) * size_y + 2 * p + q % 2)
        for p in range(size_x)
        for q in range(size_y)
    ]
    partner = matchings("gy")[0]

    corners = ([], [])
    for a in range(size_x):
        for b in range(size_y):
            above = b % 2 == 1
            chip = b // 2 + 1 if above else b // 2 - 1
            for n in range(2):
                left = above if n == 0 else not above
                near = a + 1 if left else a - 1
                if 0 <= chip < size_x and 0 <= near < size_x:
                    corners[n].append((a * size_y + b, chip * size_y + 2 * near + (0 if left else 1)))
    both = ("gx", "gy")

    rows_msg, cols_msg = 12 * depth, 24 * blocks
    coarse_cols, coarse_rows = 24, 12 * thick
    count = 24 * part
    out_a, out_b, out_1, out_2, planes, outer = call(
        pack_kernel,
        [par, fine_state, coarse_state, coarse_past],
        [(rows_msg + coarse_cols + count * 8 // LANES, LANES)] * 2
        + [(cols_msg + coarse_rows + 24, LANES)] * 2
        + [(count, LANES), (24, LANES)],
        [(3,) + fine_state.shape[1:], (3, depth, 8, cols), (3, depth, 8, cols),
         coarse_state.shape, coarse_past.shape],
        copied=3,
    )
    msg_a, msg_b = exchange("gx", out_a, out_b)
    msg_1, msg_2 = exchange("gy", out_1, out_2)
    begin = msg_a, msg_b, msg_1, msg_2
    (crossing,) = call(
        crossing_kernel, [par, planes, msg_a, msg_b, msg_2], [(count + 40, LANES)]
    )
    crossing, outer = lax.optimization_barrier((crossing, outer))
    own = lax.ppermute(crossing, both, across)
    corner_1 = lax.ppermute(outer, both, corners[0])
    corner_2 = lax.ppermute(outer, both, corners[1])

    shape = (depth, rows, cols)

    def scratch_of(depth, rows):
        return [
            (3, depth, rows + 16, LANES), (3, depth * rows, LANES), (3, depth + 8, rows, LANES),
        ]

    cells = depth * rows * cols
    halves = [(rows_msg, LANES)] * 2 + [(cols_msg, LANES)]
    (half,) = call(
        first_velocity_kernel,
        [par, fine_state, fine_medium, msg_a, msg_b, msg_1, msg_2, tile, halo],
        [(3,) + shape],
        scratch_of(depth, rows),
        flops=400 * cells,
    )
    own, half, corner_1, corner_2 = lax.optimization_barrier((own, half, corner_1, corner_2))
    other = lax.ppermute(own, "gy", partner)
    velocity, ghost, out_a, out_b, out_c = call(
        ghost_kernel,
        [par, half, fine_medium, own, other, corner_1, corner_2,
         parent_rows.reshape(1, rows), parent_cols.reshape(1, cols)],
        [(3,) + shape, (24, rows, cols)] + halves,
    )
    msgs = exchange("gx", out_a, out_b) + exchange("gy", out_c, out_c)
    stress, out_a, out_b, out_c = call(
        stress_kernel,
        [par, velocity, fine_state, fine_medium, ghost, *msgs, tile, halo],
        [(6,) + shape] + halves,
        scratch_of(depth, rows),
        flops=400 * cells,
    )
    msgs = exchange("gx", out_a, out_b) + exchange("gy", out_c, out_c)
    velocity, out_a, out_b, out_c = call(
        velocity_kernel,
        [par, velocity, stress, fine_medium, ghost, *msgs, tile, halo],
        [(3,) + shape] + halves,
        scratch_of(depth, rows),
        flops=400 * cells,
    )
    msgs = exchange("gx", out_a, out_b) + exchange("gy", out_c, out_c)
    half_shape = (9, 8, rows, cols)
    lower, lifted = call(
        lower_stress_kernel,
        [par, velocity, stress, fine_medium, ghost, fine_state, *msgs, tile, halo, means],
        [half_shape, (count, LANES)],
        scratch_of(8, rows) + [(rows, cols), (2, count, LANES)],
        parts=[((9,) + shape, (0, depth // 8 - 1, 0, 0))],
        flops=200 * cells,
    )
    own = lax.ppermute(lifted, both, across)
    fine_out, done = call(
        upper_stress_kernel,
        [par, velocity, stress, fine_medium, *msgs, tile, halo],
        [half_shape, (8, LANES)],
        scratch_of(8, rows),
        parts=[((9,) + shape, (0, 0, 0, 0))],
        flops=200 * cells,
        above=lower,
    )
    own, done = lax.optimization_barrier((own, done))
    other = lax.ppermute(own, "gy", partner)

    shape = (thick, part, LANES)
    velocity, ghost, out_1, out_2, out_c = call(
        functools.partial(coarse_velocity_kernel, base_c=rows_msg, base_r=cols_msg),
        [par, coarse_state, coarse_medium, own, other, *begin, tile, halo, done],
        [(3,) + shape, (count, LANES), (coarse_rows, LANES), (coarse_rows, LANES),
         (coarse_cols, LANES)],
        scratch_of(thick, part),
    )
    msgs = exchange("gx", out_c, out_c) + exchange("gy", out_1, out_2)
    (coarse_out,) = call(
        coarse_stress_kernel,
        [par, coarse_state, coarse_medium, velocity, ghost, *msgs, tile, halo],
        [(9,) + shape],
        scratch_of(thick, part),
    )
    return (fine_out, coarse_out)


def solution(mesh):
    placed = (
        P(None, None, "gx", "gy"),
        P(None, None, "gx", "gy"),
        P(None, None, "gy", "gx"),
        P(None, None, "gy", "gx"),
        P(None, None, "gy", "gx"),
        P("gx"),
        P("gy"),
    )
    return jax.shard_map(
        body,
        mesh=mesh,
        in_specs=placed,
        out_specs=(P(None, None, "gx", "gy"), P(None, None, "gy", "gx")),
        check_vma=False,
    )
```

time: 130 us -> 108 us (0.83)
  starting transfers between devices: 69.9 us -> 59.8 us
  Pallas kernels: 35.6 us -> 28.4 us
  waiting for transfers between devices: 18.5 us -> 14.3 us
    ppermute x20, starting transfers between devices: 67.6 us -> 44 us  [exchange(): return (lax.ppermute(first, axis, one), lax.ppermute(second, axis, two))]
    ppermute x2 -> x4, starting transfers between devices: 2.24 us -> 15.8 us  [the longest x1 13.8 us: body(): corner_1 = lax.ppermute(outer, both, corners[0])]
    pallas_call x10, Pallas kernels: 35.6 us -> 28.4 us  [call(): pl.pallas_call(kernel, grid=(1,), in_specs=specs, out_specs=out_specs, ou...]
    ppermute x20, waiting for transfers between devices: 17.1 us -> 11.3 us  [exchange(): return (lax.ppermute(first, axis, one), lax.ppermute(second, axis, two))]
    ppermute x2, waiting for transfers between devices: 1.43 us -> 2.9 us  [body(): other = lax.ppermute(own, 'gy', partner)]
    unnamed x26 -> x24, local copies, waits for them, and re-layouts: 4.14 us -> 3.31 us
  transfers between devices with their start and end apart: 24 -> 26, of which waited for: 7 -> 8; matrix products, arithmetic and copies ran while one was open for 0% -> 0% of each run, Pallas kernels for 1% -> 7%
where the time goes in v2:
time: 108 us; the launch traced here: 107 us
  starting transfers between devices  59.8 us (55%)
  Pallas kernels  28.4 us (26%)
  waiting for transfers between devices  14.3 us (13%)
  local copies, waits for them, and re-layouts  3.31 us (3%)
    ppermute x20, starting transfers between devices, exchange(): return (lax.ppermute(first, axis, one), lax.ppermute(second, axis, two))  44 us
    pallas_call x10, Pallas kernels, call(): pl.pallas_call(kernel, grid=(1,), in_specs=specs, out_specs=out_specs, ou...  28.4 us
    ppermute x1, starting transfers between devices, body(): corner_1 = lax.ppermute(outer, both, corners[0])  13.8 us
    ppermute x20, waiting for transfers between devices, exchange(): return (lax.ppermute(first, axis, one), lax.ppermute(second, axis, two))  11.3 us
    unnamed x24, local copies, waits for them, and re-layouts  3.31 us
    ppermute x2, waiting for transfers between devices, body(): other = lax.ppermute(own, 'gy', partner)  2.9 us
  transfers between devices with their start and end apart: 26, of which 8 were waited for; matrix products, arithmetic and copies ran while one was open for 0% of the time, Pallas kernels for 7%

profile of v2, /device:TPU:1, one launch (start us, length us, event | category | flops | bytes accessed | tf_op | source)
XLA Modules:
  0.0 107.5 jit_solution(17308385211921958883)
XLA Ops:
  1.3 3.8 %shard_map.113 = (f32[240,128]{1,0:T(8,128)}, f32[240,128]{1,0:T(8,128)}, f32[312,128]{1,0:T(8,128)}, f32[312,128]{1,0:T(8,128)}, f32[384,128]{1,0:T(8,128)}, /*index=5*/f32[24,128]{1,0:T(8,128)}) custom-call(s32[4]{0:T(128)} %pad_add_fusion.par, f32[9,16,64,128]{3,2,1,0:T(8,128)} %start.1, f32[9,8,16,128]{3,2,1,0:T(8,128)} %state.7, f32[9,2,16,128]{3,2,1,0:T(8,128)} %past.1), custom_call_target="tpu_custom_call" | custom-call | bytes 6230032 | tf_op jit(solution)/shard_map/pallas_call | solution.py:597
  5.1 4.5 %collective-permute-start.2 = (f32[312,128]{1,0:T(8,128)}, f32[312,128]{1,0:T(8,128)S(1)}, u32[]{:S(2)}, u32[]{:S(2)}) collective-permute-start(f32[312,128]{1,0:T(8,128)} %get-tuple-element.41), channel_id=1, source_target_pairs={{1,2},{2,1},{3,4},{4,3},{5,6},{6,5},{9,10},{10,9},{11,12},{12,11},... | collective-permute-start | bytes 479240 | tf_op jit(solution)/shard_map/ppermute | solution.py:624
  9.6 1.4 %collective-permute-start = (f32[240,128]{1,0:T(8,128)}, f32[240,128]{1,0:T(8,128)S(1)}, u32[]{:S(2)}, u32[]{:S(2)}) collective-permute-start(f32[240,128]{1,0:T(8,128)} %get-tuple-element.39), channel_id=1, source_target_pairs={{0,8},{8,0},{16,24},{24,16},{1,9},{9,1},{17,25},{25,17},{2,10},{10... | collective-permute-start | bytes 368648 | tf_op jit(solution)/shard_map/ppermute | solution.py:624
  11.7 2.0 %collective-permute-done.msg_a = f32[240,128]{1,0:T(8,128)S(1)} collective-permute-done((f32[240,128]{1,0:T(8,128)}, f32[240,128]{1,0:T(8,128)S(1)}, u32[]{:S(2)}, u32[]{:S(2)}) %collective-permute-start) | collective-permute-done | bytes 122912 | tf_op jit(solution)/shard_map/ppermute | solution.py:624
  13.7 0.9 copy-done.7
  15.2 0.7 collective-permute-start.3
  15.9 0.7 collective-permute-start.6
  16.6 13.8 %collective-permute-start.5 = (f32[24,128]{1,0:T(8,128)}, f32[24,128]{1,0:T(8,128)S(1)}, u32[]{:S(2)}, u32[]{:S(2)}) collective-permute-start(f32[24,128]{1,0:T(8,128)} %get-tuple-element.45), channel_id=1, source_target_pairs={{1,10},{3,18},{5,26},{9,12},{10,1},{11,20},{12,9},{13,28},{14,17},... | collective-permute-start | bytes 36872 | tf_op jit(solution)/shard_map/ppermute | solution.py:678
  30.4 2.3 %copy-done = f32[9,16,64,128]{3,2,1,0:T(8,128)S(1)} copy-done((f32[9,16,64,128]{3,2,1,0:T(8,128)S(1)}, f32[9,16,64,128]{3,2,1,0:T(8,128)}, u32[]{:S(2)}) %copy-start) | copy-done | bytes 4718616
  32.8 3.5 %shard_map.115.half = f32[3,16,64,128]{3,2,1,0:T(8,128)S(1)} custom-call(s32[4]{0:T(128)S(1)} %copy-done.9, f32[9,16,64,128]{3,2,1,0:T(8,128)S(1)} %copy-done, f32[3,16,64,128]{3,2,1,0:T(8,128)S(1)} %copy-done.2, f32[240,128]{1,0:T(8,128)S(1)} %collective-permute-done.msg_a, f32[240,128]{1,0:T(8,128)S(1)} %collective-permute-done.1.msg_b, ...), custom_call_target="tpu_custom_call" | custom-call | flops 52428800 | bytes 9084944 | tf_op jit(solution)/shard_map/pallas_call | solution.py:597
  36.4 1.5 %collective-permute-done.7.other = f32[424,128]{1,0:T(8,128)S(1)} collective-permute-done((f32[424,128]{1,0:T(8,128)S(1)}, f32[424,128]{1,0:T(8,128)S(1)}, u32[]{:S(2)}, u32[]{:S(2)}) %collective-permute-start.7) | collective-permute-done | bytes 217120 | tf_op jit(solution)/shard_map/ppermute | solution.py:698
  37.8 1.5 %shard_map.116 = (f32[3,16,64,128]{3,2,1,0:T(8,128)S(1)}, f32[24,64,128]{2,1,0:T(8,128)S(1)}, f32[192,128]{1,0:T(8,128)S(1)}, f32[192,128]{1,0:T(8,128)S(1)}, f32[192,128]{1,0:T(8,128)S(1)}) custom-call(s32[4]{0:T(128)S(1)} %copy-done.9, f32[3,16,64,128]{3,2,1,0:T(8,128)S(1)} %shard_map.115.half, f32[3,16,64,128]{3,2,1,0:T(8,128)S(1)} %copy-done.2, ...), custom_call_target="tpu_custom_call" | custom-call | bytes 6259472 | tf_op jit(solution)/shard_map/pallas_call | solution.py:597
  39.3 0.7 collective-permute-start.9
  40.0 3.2 %collective-permute-start.11 = (f32[192,128]{1,0:T(8,128)S(1)}, f32[192,128]{1,0:T(8,128)S(1)}, u32[]{:S(2)}, u32[]{:S(2)}) collective-permute-start(f32[192,128]{1,0:T(8,128)S(1)} %get-tuple-element.54), channel_id=1, source_target_pairs={{1,2},{2,1},{3,4},{4,3},{5,6},{6,5},{9,10},{10,9},{11,12},{12,11},... | collective-permute-start | bytes 294920 | tf_op jit(solution)/shard_map/ppermute | solution.py:624
  43.6 2.9 %collective-permute-done.11.msg_2 = f32[192,128]{1,0:T(8,128)S(1)} collective-permute-done((f32[192,128]{1,0:T(8,128)S(1)}, f32[192,128]{1,0:T(8,128)S(1)}, u32[]{:S(2)}, u32[]{:S(2)}) %collective-permute-start.11) | collective-permute-done | bytes 98336 | tf_op jit(solution)/shard_map/ppermute | solution.py:624
  46.5 4.2 %shard_map.117 = (f32[6,16,64,128]{3,2,1,0:T(8,128)S(1)}, f32[192,128]{1,0:T(8,128)S(1)}, f32[192,128]{1,0:T(8,128)S(1)}, f32[192,128]{1,0:T(8,128)S(1)}) custom-call(s32[4]{0:T(128)S(1)} %copy-done.9, f32[3,16,64,128]{3,2,1,0:T(8,128)S(1)} %get-tuple-element.50.velocity.old, f32[9,16,64,128]{3,2,1,0:T(8,128)S(1)} %copy-done.1, ...), custom_call_target="tpu_custom_call" | custom-call | flops 52428800 | bytes 13139984 | tf_op jit(solution)/shard_map/pallas_call | solution.py:597
  50.8 2.1 %collective-permute-start.12 = (f32[192,128]{1,0:T(8,128)S(1)}, f32[192,128]{1,0:T(8,128)S(1)}, u32[]{:S(2)}, u32[]{:S(2)}) collective-permute-start(f32[192,128]{1,0:T(8,128)S(1)} %get-tuple-element.56), channel_id=1, source_target_pairs={{0,8},{8,0},{16,24},{24,16},{1,9},{9,1},{17,25},{25,17},{2,10},{10... | collective-permute-start | bytes 294920 | tf_op jit(solution)/shard_map/ppermute | solution.py:624
  53.6 4.5 %collective-permute-start.15 = (f32[192,128]{1,0:T(8,128)S(1)}, f32[192,128]{1,0:T(8,128)S(1)}, u32[]{:S(2)}, u32[]{:S(2)}) collective-permute-start(f32[192,128]{1,0:T(8,128)S(1)} %get-tuple-element.58), channel_id=1, source_target_pairs={{1,2},{2,1},{3,4},{4,3},{5,6},{6,5},{9,10},{10,9},{11,12},{12,11},... | collective-permute-start | bytes 294920 | tf_op jit(solution)/shard_map/ppermute | solution.py:624
  58.2 2.2 %collective-permute-done.15.msg_2 = f32[192,128]{1,0:T(8,128)S(1)} collective-permute-done((f32[192,128]{1,0:T(8,128)S(1)}, f32[192,128]{1,0:T(8,128)S(1)}, u32[]{:S(2)}, u32[]{:S(2)}) %collective-permute-start.15) | collective-permute-done | bytes 98336 | tf_op jit(solution)/shard_map/ppermute | solution.py:624
  60.4 3.9 %shard_map.118 = (f32[3,16,64,128]{3,2,1,0:T(8,128)S(1)}, f32[192,128]{1,0:T(8,128)S(1)}, f32[192,128]{1,0:T(8,128)S(1)}, f32[192,128]{1,0:T(8,128)S(1)}) custom-call(s32[4]{0:T(128)S(1)} %copy-done.9, f32[3,16,64,128]{3,2,1,0:T(8,128)S(1)} %get-tuple-element.50.velocity.old, f32[6,16,64,128]{3,2,1,0:T(8,128)S(1)} %get-tuple-element.55.stress, ...), custom_call_target="tpu_custom_call" | custom-call | flops 52428800 | bytes 9994256 | tf_op jit(solution)/shard_map/pallas_call | solution.py:597
  64.3 1.8 %collective-permute-start.16 = (f32[192,128]{1,0:T(8,128)S(1)}, f32[192,128]{1,0:T(8,128)S(1)}, u32[]{:S(2)}, u32[]{:S(2)}) collective-permute-start(f32[192,128]{1,0:T(8,128)S(1)} %get-tuple-element.60), channel_id=1, source_target_pairs={{0,8},{8,0},{16,24},{24,16},{1,9},{9,1},{17,25},{25,17},{2,10},{10... | collective-permute-start | bytes 294920 | tf_op jit(solution)/shard_map/ppermute | solution.py:624
  66.8 4.0 %collective-permute-start.19 = (f32[192,128]{1,0:T(8,128)S(1)}, f32[192,128]{1,0:T(8,128)S(1)}, u32[]{:S(2)}, u32[]{:S(2)}) collective-permute-start(f32[192,128]{1,0:T(8,128)S(1)} %get-tuple-element.62), channel_id=1, source_target_pairs={{1,2},{2,1},{3,4},{4,3},{5,6},{6,5},{9,10},{10,9},{11,12},{12,11},... | collective-permute-start | bytes 294920 | tf_op jit(solution)/shard_map/ppermute | solution.py:624
  70.9 2.2 %collective-permute-done.19.msg_2 = f32[192,128]{1,0:T(8,128)S(1)} collective-permute-done((f32[192,128]{1,0:T(8,128)S(1)}, f32[192,128]{1,0:T(8,128)S(1)}, u32[]{:S(2)}, u32[]{:S(2)}) %collective-permute-start.19) | collective-permute-done | bytes 98336 | tf_op jit(solution)/shard_map/ppermute | solution.py:624
  73.1 4.2 %shard_map.119 = (f32[9,16,64,128]{3,2,1,0:T(8,128)}, f32[384,128]{1,0:T(8,128)S(1)}) custom-call(s32[4]{0:T(128)S(1)} %copy-done.9, f32[3,16,64,128]{3,2,1,0:T(8,128)S(1)} %get-tuple-element.59.velocity, f32[6,16,64,128]{3,2,1,0:T(8,128)S(1)} %get-tuple-element.55.stress, f32[3,16,64,128]{3,2,1,0:T(8,128)S(1)} %copy-done.2, ...), custom_call_target="tpu_custom_call" | custom-call | flops 26214400 | bytes 15663120 | tf_op jit(solution)/shard_map/pallas_call | solution.py:597
  78.0 3.6 %shard_map.120 = (f32[9,16,64,128]{3,2,1,0:T(8,128)}, f32[8,128]{1,0:T(8,128)S(1)}) custom-call(s32[4]{0:T(128)S(1)} %copy-done.9, f32[9,16,64,128]{3,2,1,0:T(8,128)} %get-tuple-element.63.below, f32[3,16,64,128]{3,2,1,0:T(8,128)S(1)} %get-tuple-element.59.velocity, ...), custom_call_target="tpu_custom_call", output_to_operand_aliasing={{0}: (1, {})} | custom-call | flops 26214400 | bytes 14422032 | tf_op jit(solution)/shard_map/pallas_call | solution.py:597
  81.6 1.4 %collective-permute-done.21.other = f32[384,128]{1,0:T(8,128)S(1)} collective-permute-done((f32[384,128]{1,0:T(8,128)S(1)}, f32[384,128]{1,0:T(8,128)S(1)}, u32[]{:S(2)}, u32[]{:S(2)}) %collective-permute-start.21) | collective-permute-done | bytes 196640 | tf_op jit(solution)/shard_map/ppermute | solution.py:742
  83.1 1.2 %shard_map.121 = (f32[3,8,16,128]{3,2,1,0:T(8,128)S(1)}, f32[384,128]{1,0:T(8,128)S(1)}, f32[96,128]{1,0:T(8,128)S(1)}, f32[96,128]{1,0:T(8,128)S(1)}, f32[24,128]{1,0:T(8,128)S(1)}) custom-call(s32[4]{0:T(128)S(1)} %copy-done.9, f32[9,8,16,128]{3,2,1,0:T(8,128)S(1)} %copy-done.4, f32[3,8,16,128]{3,2,1,0:T(8,128)S(1)} %copy-done.6, ...), custom_call_target="tpu_custom_call" | custom-call | bytes 2908176 | tf_op jit(solution)/shard_map/pallas_call | solution.py:597
  84.5 17.8 %collective-permute-start.25 = (f32[96,128]{1,0:T(8,128)S(1)}, f32[96,128]{1,0:T(8,128)S(1)}, u32[]{:S(2)}, u32[]{:S(2)}) collective-permute-start(f32[96,128]{1,0:T(8,128)S(1)} %get-tuple-element.73), channel_id=1, source_target_pairs={{1,2},{2,1},{3,4},{4,3},{5,6},{6,5},{9,10},{10,9},{11,12},{12,11},... | collective-permute-start | bytes 147464 | tf_op jit(solution)/shard_map/ppermute | solution.py:624
  102.3 0.7 collective-permute-start.23
  102.9 0.9 collective-permute-start.22
  103.8 1.8 %collective-permute-done.22.msg_a = f32[24,128]{1,0:T(8,128)S(1)} collective-permute-done((f32[24,128]{1,0:T(8,128)S(1)}, f32[24,128]{1,0:T(8,128)S(1)}, u32[]{:S(2)}, u32[]{:S(2)}) %collective-permute-start.22) | collective-permute-done | bytes 12320 | tf_op jit(solution)/shard_map/ppermute | solution.py:624
  105.5 1.9 %shard_map.122 = f32[9,8,16,128]{3,2,1,0:T(8,128)} custom-call(s32[4]{0:T(128)S(1)} %copy-done.9, f32[9,8,16,128]{3,2,1,0:T(8,128)S(1)} %copy-done.4, f32[3,8,16,128]{3,2,1,0:T(8,128)S(1)} %copy-done.6, f32[3,8,16,128]{3,2,1,0:T(8,128)S(1)} %get-tuple-element.69.velocity, f32[384,128]{1,0:T(8,128)S(1)} %get-tuple-element.70.ghost, ...), custom_call_target="tpu_custom_call" | custom-call | bytes 2547728 | tf_op jit(solution)/shard_map/pallas_call | solution.py:597
  (55 shorter events, 4.8 us)
Async XLA Ops:
  0.7 29.8 %copy-start.2 = (f32[3,16,64,128]{3,2,1,0:T(8,128)S(1)}, f32[3,16,64,128]{3,2,1,0:T(8,128)}, u32[]{:S(2)}) copy-start(f32[3,16,64,128]{3,2,1,0:T(8,128)} %medium.7) | copy-start | bytes 4718596
  0.7 29.8 %copy-start.3 = (bf16[2,256,256]{2,1,0:T(8,128)(2,1)S(1)}, bf16[2,256,256]{2,1,0:T(8,128)(2,1)}, u32[]{:S(2)}) copy-start(bf16[2,256,256]{2,1,0:T(8,128)(2,1)} %constant.46.clone.tile) | copy-start | bytes 786436
  0.7 29.8 %copy-start.5 = (bf16[2,2,32,256]{3,2,1,0:T(8,128)(2,1)S(1)}, bf16[2,2,32,256]{3,2,1,0:T(8,128)(2,1)}, u32[]{:S(2)}) copy-start(bf16[2,2,32,256]{3,2,1,0:T(8,128)(2,1)} %constant.47.clone.halo) | copy-start | bytes 196612
  5.1 8.5 %collective-permute-start.2 = (f32[312,128]{1,0:T(8,128)}, f32[312,128]{1,0:T(8,128)S(1)}, u32[]{:S(2)}, u32[]{:S(2)}) collective-permute-start(f32[312,128]{1,0:T(8,128)} %get-tuple-element.41), channel_id=1, source_target_pairs={{1,2},{2,1},{3,4},{4,3},{5,6},{6,5},{9,10},{10,9},{11,12},{12,11},... | collective-permute-start | bytes 479240 | tf_op jit(solution)/shard_map/ppermute | solution.py:624
  9.6 4.0 %collective-permute-start = (f32[240,128]{1,0:T(8,128)}, f32[240,128]{1,0:T(8,128)S(1)}, u32[]{:S(2)}, u32[]{:S(2)}) collective-permute-start(f32[240,128]{1,0:T(8,128)} %get-tuple-element.39), channel_id=1, source_target_pairs={{0,8},{8,0},{16,24},{24,16},{1,9},{9,1},{17,25},{25,17},{2,10},{10... | collective-permute-start | bytes 368648 | tf_op jit(solution)/shard_map/ppermute | solution.py:624
  11.0 2.6 %collective-permute-start.1 = (f32[240,128]{1,0:T(8,128)}, f32[240,128]{1,0:T(8,128)S(1)}, u32[]{:S(2)}, u32[]{:S(2)}) collective-permute-start(f32[240,128]{1,0:T(8,128)} %get-tuple-element.40), channel_id=1, source_target_pairs={{8,16},{16,8},{9,17},{17,9},{10,18},{18,10},{11,19},{19,11},{12,20... | collective-permute-start | bytes 368648 | tf_op jit(solution)/shard_map/ppermute | solution.py:624
  15.2 21.1 %collective-permute-start.3 = (f32[424,128]{1,0:T(8,128)S(1)}, f32[424,128]{1,0:T(8,128)S(1)}, u32[]{:S(2)}, u32[]{:S(2)}) collective-permute-start(f32[424,128]{1,0:T(8,128)S(1)} %shard_map.114), channel_id=1, source_target_pairs={{0,0},{1,1},{2,8},{3,9},{4,16},{5,17},{6,24},{7,25},{8,2},{9,3},{1... | collective-permute-start | bytes 651272 | tf_op jit(solution)/shard_map/ppermute | solution.py:677
  15.8 22.0 %copy-start.10 = (s32[64]{0:T(128)S(1)}, s32[64]{0:T(128)}, u32[]{:S(2)}) copy-start(s32[64]{0:T(128)} %param.15) | copy-start | bytes 772
  15.8 22.0 %copy-start.11 = (s32[128]{0:T(128)S(1)}, s32[128]{0:T(128)}, u32[]{:S(2)}) copy-start(s32[128]{0:T(128)} %param.16) | copy-start | bytes 1540
  15.9 14.5 %collective-permute-start.4 = (f32[312,128]{1,0:T(8,128)}, f32[312,128]{1,0:T(8,128)S(1)}, u32[]{:S(2)}, u32[]{:S(2)}) collective-permute-start(f32[312,128]{1,0:T(8,128)} %get-tuple-element.44), channel_id=1, source_target_pairs={{0,1},{1,0},{2,3},{3,2},{4,5},{5,4},{6,7},{7,6},{8,9},{9,8},{10,11... | collective-permute-start | bytes 479240 | tf_op jit(solution)/shard_map/ppermute | solution.py:624
  15.9 20.3 %collective-permute-start.6 = (f32[24,128]{1,0:T(8,128)}, f32[24,128]{1,0:T(8,128)S(1)}, u32[]{:S(2)}, u32[]{:S(2)}) collective-permute-start(f32[24,128]{1,0:T(8,128)} %get-tuple-element.45), channel_id=1, source_target_pairs={{2,2},{4,10},{6,18},{9,9},{10,4},{11,17},{12,12},{13,25},{14,20},{... | collective-permute-start | bytes 36872 | tf_op jit(solution)/shard_map/ppermute | solution.py:679
  16.6 19.7 %collective-permute-start.5 = (f32[24,128]{1,0:T(8,128)}, f32[24,128]{1,0:T(8,128)S(1)}, u32[]{:S(2)}, u32[]{:S(2)}) collective-permute-start(f32[24,128]{1,0:T(8,128)} %get-tuple-element.45), channel_id=1, source_target_pairs={{1,10},{3,18},{5,26},{9,12},{10,1},{11,20},{12,9},{13,28},{14,17},... | collective-permute-start | bytes 36872 | tf_op jit(solution)/shard_map/ppermute | solution.py:678
  32.8 13.8 %copy-start.1 = (f32[9,16,64,128]{3,2,1,0:T(8,128)S(1)}, f32[9,16,64,128]{3,2,1,0:T(8,128)}, u32[]{:S(2)}) copy-start(f32[9,16,64,128]{3,2,1,0:T(8,128)} %start.1) | copy-start | bytes 14155780
  36.3 1.5 %collective-permute-start.7 = (f32[424,128]{1,0:T(8,128)S(1)}, f32[424,128]{1,0:T(8,128)S(1)}, u32[]{:S(2)}, u32[]{:S(2)}) collective-permute-start(f32[424,128]{1,0:T(8,128)S(1)} %collective-permute-done.3.own), channel_id=1, source_target_pairs={{0,1},{1,0},{2,3},{3,2},{4,5},{5,4},{6,7},{7,6},{8,9},{9,8},{10,11... | collective-permute-start | bytes 651272 | tf_op jit(solution)/shard_map/ppermute | solution.py:698
  39.3 4.3 %collective-permute-start.8 = (f32[192,128]{1,0:T(8,128)S(1)}, f32[192,128]{1,0:T(8,128)S(1)}, u32[]{:S(2)}, u32[]{:S(2)}) collective-permute-start(f32[192,128]{1,0:T(8,128)S(1)} %get-tuple-element.52), channel_id=1, source_target_pairs={{0,8},{8,0},{16,24},{24,16},{1,9},{9,1},{17,25},{25,17},{2,10},{10... | collective-permute-start | bytes 294920 | tf_op jit(solution)/shard_map/ppermute | solution.py:624
  39.3 4.3 %collective-permute-start.9 = (f32[192,128]{1,0:T(8,128)S(1)}, f32[192,128]{1,0:T(8,128)S(1)}, u32[]{:S(2)}, u32[]{:S(2)}) collective-permute-start(f32[192,128]{1,0:T(8,128)S(1)} %get-tuple-element.53), channel_id=1, source_target_pairs={{8,16},{16,8},{9,17},{17,9},{10,18},{18,10},{11,19},{19,11},{12,20... | collective-permute-start | bytes 294920 | tf_op jit(solution)/shard_map/ppermute | solution.py:624
  40.0 6.5 %collective-permute-start.11 = (f32[192,128]{1,0:T(8,128)S(1)}, f32[192,128]{1,0:T(8,128)S(1)}, u32[]{:S(2)}, u32[]{:S(2)}) collective-permute-start(f32[192,128]{1,0:T(8,128)S(1)} %get-tuple-element.54), channel_id=1, source_target_pairs={{1,2},{2,1},{3,4},{4,3},{5,6},{6,5},{9,10},{10,9},{11,12},{12,11},... | collective-permute-start | bytes 294920 | tf_op jit(solution)/shard_map/ppermute | solution.py:624
  43.2 3.3 %collective-permute-start.10 = (f32[192,128]{1,0:T(8,128)S(1)}, f32[192,128]{1,0:T(8,128)S(1)}, u32[]{:S(2)}, u32[]{:S(2)}) collective-permute-start(f32[192,128]{1,0:T(8,128)S(1)} %get-tuple-element.54), channel_id=1, source_target_pairs={{0,1},{1,0},{2,3},{3,2},{4,5},{5,4},{6,7},{7,6},{8,9},{9,8},{10,11... | collective-permute-start | bytes 294920 | tf_op jit(solution)/shard_map/ppermute | solution.py:624
  50.8 7.4 %collective-permute-start.12 = (f32[192,128]{1,0:T(8,128)S(1)}, f32[192,128]{1,0:T(8,128)S(1)}, u32[]{:S(2)}, u32[]{:S(2)}) collective-permute-start(f32[192,128]{1,0:T(8,128)S(1)} %get-tuple-element.56), channel_id=1, source_target_pairs={{0,8},{8,0},{16,24},{24,16},{1,9},{9,1},{17,25},{25,17},{2,10},{10... | collective-permute-start | bytes 294920 | tf_op jit(solution)/shard_map/ppermute | solution.py:624
  52.9 5.3 %collective-permute-start.13 = (f32[192,128]{1,0:T(8,128)S(1)}, f32[192,128]{1,0:T(8,128)S(1)}, u32[]{:S(2)}, u32[]{:S(2)}) collective-permute-start(f32[192,128]{1,0:T(8,128)S(1)} %get-tuple-element.57), channel_id=1, source_target_pairs={{8,16},{16,8},{9,17},{17,9},{10,18},{18,10},{11,19},{19,11},{12,20... | collective-permute-start | bytes 294920 | tf_op jit(solution)/shard_map/ppermute | solution.py:624
  53.6 6.8 %collective-permute-start.15 = (f32[192,128]{1,0:T(8,128)S(1)}, f32[192,128]{1,0:T(8,128)S(1)}, u32[]{:S(2)}, u32[]{:S(2)}) collective-permute-start(f32[192,128]{1,0:T(8,128)S(1)} %get-tuple-element.58), channel_id=1, source_target_pairs={{1,2},{2,1},{3,4},{4,3},{5,6},{6,5},{9,10},{10,9},{11,12},{12,11},... | collective-permute-start | bytes 294920 | tf_op jit(solution)/shard_map/ppermute | solution.py:624
  58.1 2.3 %collective-permute-start.14 = (f32[192,128]{1,0:T(8,128)S(1)}, f32[192,128]{1,0:T(8,128)S(1)}, u32[]{:S(2)}, u32[]{:S(2)}) collective-permute-start(f32[192,128]{1,0:T(8,128)S(1)} %get-tuple-element.58), channel_id=1, source_target_pairs={{0,1},{1,0},{2,3},{3,2},{4,5},{5,4},{6,7},{7,6},{8,9},{9,8},{10,11... | collective-permute-start | bytes 294920 | tf_op jit(solution)/shard_map/ppermute | solution.py:624
  64.3 6.6 %collective-permute-start.16 = (f32[192,128]{1,0:T(8,128)S(1)}, f32[192,128]{1,0:T(8,128)S(1)}, u32[]{:S(2)}, u32[]{:S(2)}) collective-permute-start(f32[192,128]{1,0:T(8,128)S(1)} %get-tuple-element.60), channel_id=1, source_target_pairs={{0,8},{8,0},{16,24},{24,16},{1,9},{9,1},{17,25},{25,17},{2,10},{10... | collective-permute-start | bytes 294920 | tf_op jit(solution)/shard_map/ppermute | solution.py:624
  66.2 4.7 %collective-permute-start.17 = (f32[192,128]{1,0:T(8,128)S(1)}, f32[192,128]{1,0:T(8,128)S(1)}, u32[]{:S(2)}, u32[]{:S(2)}) collective-permute-start(f32[192,128]{1,0:T(8,128)S(1)} %get-tuple-element.61), channel_id=1, source_target_pairs={{8,16},{16,8},{9,17},{17,9},{10,18},{18,10},{11,19},{19,11},{12,20... | collective-permute-start | bytes 294920 | tf_op jit(solution)/shard_map/ppermute | solution.py:624
  66.8 6.3 %collective-permute-start.19 = (f32[192,128]{1,0:T(8,128)S(1)}, f32[192,128]{1,0:T(8,128)S(1)}, u32[]{:S(2)}, u32[]{:S(2)}) collective-permute-start(f32[192,128]{1,0:T(8,128)S(1)} %get-tuple-element.62), channel_id=1, source_target_pairs={{1,2},{2,1},{3,4},{4,3},{5,6},{6,5},{9,10},{10,9},{11,12},{12,11},... | collective-permute-start | bytes 294920 | tf_op jit(solution)/shard_map/ppermute | solution.py:624
  70.8 2.3 %collective-permute-start.18 = (f32[192,128]{1,0:T(8,128)S(1)}, f32[192,128]{1,0:T(8,128)S(1)}, u32[]{:S(2)}, u32[]{:S(2)}) collective-permute-start(f32[192,128]{1,0:T(8,128)S(1)} %get-tuple-element.62), channel_id=1, source_target_pairs={{0,1},{1,0},{2,3},{3,2},{4,5},{5,4},{6,7},{7,6},{8,9},{9,8},{10,11... | collective-permute-start | bytes 294920 | tf_op jit(solution)/shard_map/ppermute | solution.py:624
  77.3 4.3 %collective-permute-start.20 = (f32[384,128]{1,0:T(8,128)S(1)}, f32[384,128]{1,0:T(8,128)S(1)}, u32[]{:S(2)}, u32[]{:S(2)}) collective-permute-start(f32[384,128]{1,0:T(8,128)S(1)} %get-tuple-element.65), channel_id=1, source_target_pairs={{0,0},{1,1},{2,8},{3,9},{4,16},{5,17},{6,24},{7,25},{8,2},{9,3},{1... | collective-permute-start | bytes 589832 | tf_op jit(solution)/shard_map/ppermute | solution.py:731
  81.6 1.4 %collective-permute-start.21 = (f32[384,128]{1,0:T(8,128)S(1)}, f32[384,128]{1,0:T(8,128)S(1)}, u32[]{:S(2)}, u32[]{:S(2)}) collective-permute-start(f32[384,128]{1,0:T(8,128)S(1)} %collective-permute-done.20.own), channel_id=1, source_target_pairs={{0,1},{1,0},{2,3},{3,2},{4,5},{5,4},{6,7},{7,6},{8,9},{9,8},{10,11... | collective-permute-start | bytes 589832 | tf_op jit(solution)/shard_map/ppermute | solution.py:742
  84.3 21.2 %collective-permute-start.24 = (f32[96,128]{1,0:T(8,128)S(1)}, f32[96,128]{1,0:T(8,128)S(1)}, u32[]{:S(2)}, u32[]{:S(2)}) collective-permute-start(f32[96,128]{1,0:T(8,128)S(1)} %get-tuple-element.72), channel_id=1, source_target_pairs={{0,1},{1,0},{2,3},{3,2},{4,5},{5,4},{6,7},{7,6},{8,9},{9,8},{10,11... | collective-permute-start | bytes 147464 | tf_op jit(solution)/shard_map/ppermute | solution.py:624
  84.5 21.1 %collective-permute-start.25 = (f32[96,128]{1,0:T(8,128)S(1)}, f32[96,128]{1,0:T(8,128)S(1)}, u32[]{:S(2)}, u32[]{:S(2)}) collective-permute-start(f32[96,128]{1,0:T(8,128)S(1)} %get-tuple-element.73), channel_id=1, source_target_pairs={{1,2},{2,1},{3,4},{4,3},{5,6},{6,5},{9,10},{10,9},{11,12},{12,11},... | collective-permute-start | bytes 147464 | tf_op jit(solution)/shard_map/ppermute | solution.py:624
  102.3 1.5 %collective-permute-start.23 = (f32[24,128]{1,0:T(8,128)S(1)}, f32[24,128]{1,0:T(8,128)S(1)}, u32[]{:S(2)}, u32[]{:S(2)}) collective-permute-start(f32[24,128]{1,0:T(8,128)S(1)} %get-tuple-element.71), channel_id=1, source_target_pairs={{8,16},{16,8},{9,17},{17,9},{10,18},{18,10},{11,19},{19,11},{12,20... | collective-permute-start | bytes 36872 | tf_op jit(solution)/shard_map/ppermute | solution.py:624
  102.9 2.6 %collective-permute-start.22 = (f32[24,128]{1,0:T(8,128)S(1)}, f32[24,128]{1,0:T(8,128)S(1)}, u32[]{:S(2)}, u32[]{:S(2)}) collective-permute-start(f32[24,128]{1,0:T(8,128)S(1)} %get-tuple-element.71), channel_id=1, source_target_pairs={{0,8},{8,0},{16,24},{24,16},{1,9},{9,1},{17,25},{25,17},{2,10},{10... | collective-permute-start | bytes 36872 | tf_op jit(solution)/shard_map/ppermute | solution.py:624
  (6 other events, 38.5 us)

commit v3 on v2

--- a/solution.py
+++ b/solution.py
@@ -23,6 +23,11 @@
 STR_X = ((VX, False), (VY, True), (VZ, True))
 STR_Y = ((VX, True), (VY, False), (VZ, True))
 STR_Z = ((VX, True), (VY, True), (VZ, False))
+
+
+def above_planes(table):
+    skip = table is VEL_Z
+    return [(k, m) for k, (_, forward) in enumerate(table) for m in range(int(skip and forward), 4)]
 
 
 def band(width, forward):
@@ -212,7 +217,7 @@
         out[2, z] = old[2, z] + scale * (x + along_y(ey, 2, z, rows) + zz)
         return 0
 
-    lax.fori_loop(0, depth, layer, 0, unroll=2)
+    lax.fori_loop(0, depth, layer, 0, unroll=2 if rows > 16 else depth)
 
 
 def stress_half(old, lame, shear, put, low, count, ex, ey, ez):
@@ -237,7 +242,7 @@
         put(5, z, n, old(5, z) + mu * (along_z(ez, 1, n, True) + y))
         return 0
 
-    lax.fori_loop(0, count, layer, 0, unroll=2)
+    lax.fori_loop(0, count, layer, 0, unroll=2 if rows > 16 else count)
 
 
 def zeros_like_plane(ref):
@@ -363,7 +368,7 @@
 
 def ghost_kernel(
     par, half, buoyancy, own, other, corner_1, corner_2, prow, pcol,
-    out, ghost, out_a, out_b, out_c,
+    out, ghost, out_a, out_b, out_1, out_2,
 ):
     expand_ghosts(par, own, other, corner_1, corner_2, prow, pcol, ghost)
     depth = half.shape[1]
@@ -384,7 +389,7 @@
             out[c, z] = value
     moved = [(out, c) for c in range(3)]
     put_rows(out_a, out_b, 0, moved, par[0])
-    put_columns((out_c,), 0, moved)
+    put_columns((out_1, out_2), 0, moved)
 
 
 def stress_fields(ref, table):
@@ -413,8 +418,8 @@
 
 
 def velocity_kernel(
-    par, old, stress, buoyancy, ghost, msg_a, msg_b, msg_1, msg_2, tile, halo,
-    out, out_a, out_b, out_c, ex, ey, ez,
+    par, old, stress, buoyancy, ghost, start, msg_a, msg_b, msg_1, msg_2, tile, halo, means,
+    out, out_a, out_b, out_1, out_2, coarse, ex, ey, ez, summed, halves,
 ):
     order = [CROSSING.index(f) for f, _ in VEL_Z]
     velocity_fill(
@@ -424,7 +429,9 @@
     velocity_half(old, buoyancy, out, ex, ey, ez)
     moved = [(out, c) for c in range(3)]
     put_rows(out_a, out_b, 0, moved, par[0])
-    put_columns((out_c,), 0, moved)
+    put_columns((out_1, out_2), 0, moved)
+    low = out.shape[1] - 8
+    lift(start, STR_Z, [out.at[c, low:] for c in range(3)], means, coarse, summed, halves)
 
 
 def stress_fill(
@@ -442,7 +449,7 @@
 
 def stress_kernel(
     par, velocity, state, medium, ghost, msg_a, msg_b, msg_1, msg_2, tile, halo,
-    out, out_a, out_b, out_c, ex, ey, ez,
+    out, out_a, out_b, out_1, out_2, ex, ey, ez,
 ):
     depth = velocity.shape[1]
     stress_fill(
@@ -458,7 +465,26 @@
         put, 0, depth, ex, ey, ez,
     )
     put_rows(out_a, out_b, 0, stress_fields(out, VEL_X), par[0])
-    put_columns((out_c,), 0, stress_fields(out, VEL_Y))
+    put_columns((out_1, out_2), 0, stress_fields(out, VEL_Y))
+
+
+def lift(start, table, fields, means, coarse, summed, halves):
+    rows = summed.shape[0]
+    part = rows // 4
+    low = start.shape[1] - 8
+    for n, (k, m) in enumerate(above_planes(table)):
+        f, new = table[k][0], fields[k]
+        z = 2 * m
+        total = (start[f, low + z] + start[f, low + z + 1]) + (new[z] + new[z + 1])
+        summed[...] = total
+        pairs = summed[pl.ds(0, 2 * part, stride=2), :] + summed[pl.ds(1, 2 * part, stride=2), :]
+        at = pl.ds(n * part, part)
+        halves[0, at, :] = pairs[:part]
+        halves[1, at, :] = pairs[part:]
+    count = coarse.shape[0]
+    upper = dot(jnp.concatenate(split(halves[0, 0:count]), axis=1), means[0])
+    lower = dot(jnp.concatenate(split(halves[1, 0:count]), axis=1), means[1])
+    coarse[...] = upper + lower
 
 
 def lower_stress_kernel(
@@ -471,28 +497,16 @@
         par, velocity, lambda k, g: ghost[12 + 2 * k + g // 2], msg_a, msg_b, msg_1, msg_2,
         tile, halo, ex, ey, ez, low, 8,
     )
-    out[0:3] = velocity[:, low:]
 
     def put(c, z, n, value):
-        out[SXX + c, n] = value
+        out[c, n] = value
 
     stress_half(
         lambda c, z: stress[c, z], lambda z: medium[1, z], lambda z: medium[2, z],
         put, low, 8, ex, ey, ez,
     )
-    part = rows // 4
-    for n, f in enumerate(CROSSING):
-        for m in range(4):
-            z = 2 * m
-            total = (start[f, low + z] + start[f, low + z + 1]) + (out[f, z] + out[f, z + 1])
-            summed[...] = total
-            pairs = summed[pl.ds(0, 2 * part, stride=2), :] + summed[pl.ds(1, 2 * part, stride=2), :]
-            at = pl.ds((4 * n + m) * part, part)
-            halves[0, at, :] = pairs[:part]
-            halves[1, at, :] = pairs[part:]
-    upper = dot(jnp.concatenate(split(halves[0]), axis=1), means[0])
-    lower = dot(jnp.concatenate(split(halves[1]), axis=1), means[1])
-    coarse[...] = upper + lower
+    fields = [out.at[f - SXX] for f, _ in VEL_Z]
+    lift(start, VEL_Z, fields, means, coarse, summed, halves)
 
 
 def upper_stress_kernel(
@@ -502,7 +516,8 @@
     stress_fill(
         par, velocity, None, msg_a, msg_b, msg_1, msg_2, tile, halo, ex, ey, ez, 0, 8
     )
-    out[0:3] = velocity[:, 0:8]
+    out[0:3] = velocity[...]
+    out[SXX:, velocity.shape[1] - 8 :] = below[...]
 
     def put(c, z, n, value):
         out[SXX + c, n] = value
@@ -514,14 +529,9 @@
     done[...] = jnp.zeros_like(done)
 
 
-def coarse_velocity_kernel(
-    par, state, medium, own, other, msg_a, msg_b, msg_1, msg_2, tile, halo, done,
-    out, ghost, out_1, out_2, out_c, ex, ey, ez, *, base_c, base_r,
-):
-    pi, pj = par[0], par[1]
-    rows = state.shape[2]
+def join(par, own, other, ghost, table, rows):
     half = LANES // 2
-    even = pj == 0
+    even = par[1] == 0
     left = jnp.where(even, own[...], other[...])
     right = jnp.where(even, other[...], own[...])
     low = lax.broadcasted_iota(jnp.int32, left.shape, 1) < half
@@ -530,11 +540,28 @@
         jnp.where(low, left, pltpu.roll(right, half, 1)),
         jnp.where(low, pltpu.roll(left, half, 1), right),
     )
+    planes = above_planes(table)
+    none = jnp.zeros((rows, LANES), F32)
+
+    def layer(k, m):
+        if (k, m) not in planes:
+            return none
+        return ghost[pl.ds(planes.index((k, m)) * rows, rows), :]
+
+    return layer
+
+
+def coarse_velocity_kernel(
+    par, state, medium, own, other, msg_a, msg_b, msg_1, msg_2, tile, halo, done,
+    out, out_1, out_2, out_c, ex, ey, ez, ghost, *, base_c, base_r,
+):
+    pi, pj = par[0], par[1]
+    rows = state.shape[2]
+    above = join(par, own, other, ghost, VEL_Z, state.shape[2])
     none = zeros_like_plane(state)
-    order = [CROSSING.index(f) for f, _ in VEL_Z]
     fill_z(
         ez, stress_fields(state, VEL_Z),
-        lambda k, g: ghost[pl.ds((4 * order[k] + g) * rows, rows), :], lambda k, g: none,
+        above, lambda k, g: none,
     )
     fill_x(ex, stress_fields(state, VEL_X), msg_1, msg_2, base_r, pj)
     fill_y(
@@ -548,15 +575,16 @@
 
 
 def coarse_stress_kernel(
-    par, state, medium, velocity, ghost, msg_a, msg_b, msg_1, msg_2, tile, halo,
-    out, ex, ey, ez,
+    par, state, medium, velocity, own, other, msg_a, msg_b, msg_1, msg_2, tile, halo,
+    out, ex, ey, ez, ghost,
 ):
     pi, pj = par[0], par[1]
+    above = join(par, own, other, ghost, STR_Z, state.shape[2])
     depth, rows = state.shape[1], state.shape[2]
     none = zeros_like_plane(state)
     fields = [(velocity, c) for c in range(3)]
     fill_z(
-        ez, fields, lambda k, g: ghost[pl.ds((4 * k + g) * rows, rows), :], lambda k, g: none
+        ez, fields, above, lambda k, g: none
     )
     fill_x(ex, fields, msg_1, msg_2, 0, pj)
     fill_y(ey, fields, [d for _, d in STR_Y], msg_a, msg_b, 0, pi, tile, halo)
@@ -575,36 +603,21 @@
     return pl.BlockSpec(shape, functools.partial(lambda rank, _: (0,) * rank, len(shape)))
 
 
-def call(kernel, args, outs, scratch=(), parts=(), flops=0, copied=0, **options):
+def call(kernel, args, outs, scratch=(), flops=0, copied=0, light=False):
     specs = [pl.BlockSpec(memory_space=pltpu.SMEM)]
     for n, a in enumerate(args[1:]):
         specs.append(pl.BlockSpec(memory_space=pltpu.HBM) if n < copied else whole(a.shape))
-    if "above" in options:
-        array = options.pop("above")
-        specs.insert(1, pl.BlockSpec(memory_space=pl.ANY))
-        args = [args[0], array] + list(args[1:])
-        options["input_output_aliases"] = {1: 0}
-    out_specs, out_shapes = [], []
-    for n, shape in enumerate(outs):
-        if n < len(parts):
-            full, place = parts[n]
-            out_specs.append(pl.BlockSpec(shape, functools.partial(lambda p, _: p, place)))
-            out_shapes.append(jax.ShapeDtypeStruct(full, F32))
-        else:
-            out_specs.append(whole(shape))
-            out_shapes.append(jax.ShapeDtypeStruct(shape, F32))
-    size = sum(4 * int(np.prod(a.shape)) for a in args) + sum(4 * int(np.prod(o)) for o in outs)
+    size = 1024 if light else sum(4 * int(np.prod(a.shape)) for a in args) + sum(4 * int(np.prod(o)) for o in outs)
     return pl.pallas_call(
         kernel,
         grid=(1,),
         in_specs=specs,
-        out_specs=out_specs,
-        out_shape=out_shapes,
+        out_specs=[whole(o) for o in outs],
+        out_shape=[jax.ShapeDtypeStruct(o, F32) for o in outs],
         scratch_shapes=[pltpu.VMEM(s, F32) for s in scratch]
         + ([pltpu.SemaphoreType.DMA((11,))] if copied else []),
-        compiler_params=pltpu.CompilerParams(vmem_limit_bytes=(60 if copied else 20) * 1024 * 1024),
+        compiler_params=pltpu.CompilerParams(vmem_limit_bytes=(52 if copied else 24) * 1024 * 1024),
         cost_estimate=pl.CostEstimate(flops=flops, bytes_accessed=size, transcendentals=0),
-        **options,
     )(*args)
 
 
@@ -686,7 +699,7 @@
         ]
 
     cells = depth * rows * cols
-    halves = [(rows_msg, LANES)] * 2 + [(cols_msg, LANES)]
+    halves = [(rows_msg, LANES)] * 2 + [(cols_msg + 16, LANES), (cols_msg + 8, LANES)]
     (half,) = call(
         first_velocity_kernel,
         [par, fine_state, fine_medium, msg_a, msg_b, msg_1, msg_2, tile, halo],
@@ -696,65 +709,64 @@
     )
     own, half, corner_1, corner_2 = lax.optimization_barrier((own, half, corner_1, corner_2))
     other = lax.ppermute(own, "gy", partner)
-    velocity, ghost, out_a, out_b, out_c = call(
+    velocity, ghost, out_a, out_b, out_1, out_2 = call(
         ghost_kernel,
         [par, half, fine_medium, own, other, corner_1, corner_2,
          parent_rows.reshape(1, rows), parent_cols.reshape(1, cols)],
         [(3,) + shape, (24, rows, cols)] + halves,
     )
-    msgs = exchange("gx", out_a, out_b) + exchange("gy", out_c, out_c)
-    stress, out_a, out_b, out_c = call(
+    msgs = exchange("gx", out_a, out_b) + exchange("gy", out_1, out_2)
+    stress, out_a, out_b, out_1, out_2 = call(
         stress_kernel,
         [par, velocity, fine_state, fine_medium, ghost, *msgs, tile, halo],
         [(6,) + shape] + halves,
         scratch_of(depth, rows),
         flops=400 * cells,
     )
-    msgs = exchange("gx", out_a, out_b) + exchange("gy", out_c, out_c)
-    velocity, out_a, out_b, out_c = call(
+    msgs = exchange("gx", out_a, out_b) + exchange("gy", out_1, out_2)
+    moved_v, moved_s = (len(above_planes(t)) * part for t in (STR_Z, VEL_Z))
+    lift_scratch = [(rows, cols), (2, count // 2, LANES)]
+    velocity, out_a, out_b, out_1, out_2, lifted = call(
         velocity_kernel,
-        [par, velocity, stress, fine_medium, ghost, *msgs, tile, halo],
-        [(3,) + shape] + halves,
-        scratch_of(depth, rows),
+        [par, velocity, stress, fine_medium, ghost, fine_state, *msgs, tile, halo, means],
+        [(3,) + shape] + halves + [(moved_v, LANES)],
+        scratch_of(depth, rows) + lift_scratch,
         flops=400 * cells,
     )
-    msgs = exchange("gx", out_a, out_b) + exchange("gy", out_c, out_c)
-    half_shape = (9, 8, rows, cols)
-    lower, lifted = call(
+    msgs = exchange("gx", out_a, out_b) + exchange("gy", out_1, out_2)
+    moving = lax.ppermute(lifted, both, across)
+    below, lifted = call(
         lower_stress_kernel,
         [par, velocity, stress, fine_medium, ghost, fine_state, *msgs, tile, halo, means],
-        [half_shape, (count, LANES)],
-        scratch_of(8, rows) + [(rows, cols), (2, count, LANES)],
-        parts=[((9,) + shape, (0, depth // 8 - 1, 0, 0))],
-        flops=200 * cells,
+        [(6, 8, rows, cols), (moved_s, LANES)],
+        scratch_of(8, rows) + lift_scratch,
+        light=True,
     )
     own = lax.ppermute(lifted, both, across)
     fine_out, done = call(
         upper_stress_kernel,
-        [par, velocity, stress, fine_medium, *msgs, tile, halo],
-        [half_shape, (8, LANES)],
+        [par, below, velocity, stress, fine_medium, *msgs, tile, halo],
+        [(9,) + shape, (8, LANES)],
         scratch_of(8, rows),
-        parts=[((9,) + shape, (0, 0, 0, 0))],
         flops=200 * cells,
-        above=lower,
-    )
-    own, done = lax.optimization_barrier((own, done))
+    )
+    own, done, moving = lax.optimization_barrier((own, done, moving))
     other = lax.ppermute(own, "gy", partner)
+    moving_other = lax.ppermute(moving, "gy", partner)
 
     shape = (thick, part, LANES)
-    velocity, ghost, out_1, out_2, out_c = call(
+    velocity, out_1, out_2, out_c = call(
         functools.partial(coarse_velocity_kernel, base_c=rows_msg, base_r=cols_msg),
         [par, coarse_state, coarse_medium, own, other, *begin, tile, halo, done],
-        [(3,) + shape, (count, LANES), (coarse_rows, LANES), (coarse_rows, LANES),
-         (coarse_cols, LANES)],
-        scratch_of(thick, part),
+        [(3,) + shape, (coarse_rows, LANES), (coarse_rows, LANES), (coarse_cols, LANES)],
+        scratch_of(thick, part) + [(moved_s, LANES)],
     )
     msgs = exchange("gx", out_c, out_c) + exchange("gy", out_1, out_2)
     (coarse_out,) = call(
         coarse_stress_kernel,
-        [par, coarse_state, coarse_medium, velocity, ghost, *msgs, tile, halo],
+        [par, coarse_state, coarse_medium, velocity, moving, moving_other, *msgs, tile, halo],
         [(9,) + shape],
-        scratch_of(thick, part),
+        scratch_of(thick, part) + [(moved_v, LANES)],
     )
     return (fine_out, coarse_out)
 

time: 108 us -> 103 us (0.954)
  waiting for transfers between devices: 14.3 us -> 9.86 us
  Pallas kernels: 28.4 us -> 27.3 us
    ppermute x20, waiting for transfers between devices: 11.3 us -> 7.61 us  [exchange(): return (lax.ppermute(first, axis, one), lax.ppermute(second, axis, two))]
    ppermute x0 -> x2, starting transfers between devices: none -> 1.17 us  [the longest x1 0.67 us: body(): moving = lax.ppermute(lifted, both, across)]
  transfers between devices with their start and end apart: 26 -> 28, of which waited for: 8 -> 7; matrix products, arithmetic and copies ran while one was open for 0% -> 0% of each run, Pallas kernels for 7% -> 11%
where the time goes in v3:
time: 103 us; the launch traced here: 102 us
  starting transfers between devices  60 us (58%)
  Pallas kernels  27.3 us (27%)
  waiting for transfers between devices  9.86 us (10%)
  local copies, waits for them, and re-layouts  3.9 us (4%)
    ppermute x20, starting transfers between devices, exchange(): return (lax.ppermute(first, axis, one), lax.ppermute(second, axis, two))  43 us
    pallas_call x10, Pallas kernels, call(): pl.pallas_call(kernel, grid=(1,), in_specs=specs, out_specs=[whole(o) for...  27.3 us
    ppermute x1, starting transfers between devices, body(): corner_1 = lax.ppermute(outer, both, corners[0])  13.8 us
    ppermute x20, waiting for transfers between devices, exchange(): return (lax.ppermute(first, axis, one), lax.ppermute(second, axis, two))  7.61 us
    unnamed x24, local copies, waits for them, and re-layouts  3.9 us
    ppermute x2, waiting for transfers between devices, body(): other = lax.ppermute(own, 'gy', partner)  2.24 us
  transfers between devices with their start and end apart: 28, of which 7 were waited for; matrix products, arithmetic and copies ran while one was open for 0% of the time, Pallas kernels for 11%

profile of v3, /device:TPU:1, one launch (start us, length us, event | category | flops | bytes accessed | tf_op | source)
XLA Modules:
  0.0 102.2 jit_solution(11086770797634185235)
XLA Ops:
  0.7 1.2 %copy-done.4 = f32[9,8,16,128]{3,2,1,0:T(8,128)S(1)} copy-done((f32[9,8,16,128]{3,2,1,0:T(8,128)S(1)}, f32[9,8,16,128]{3,2,1,0:T(8,128)}, u32[]{:S(2)}) %copy-start.4) | copy-done | bytes 589848
  1.9 0.9 copy-done.9
  2.8 3.4 %shard_map.113 = (f32[240,128]{1,0:T(8,128)S(1)}, f32[240,128]{1,0:T(8,128)S(1)}, f32[312,128]{1,0:T(8,128)S(1)}, f32[312,128]{1,0:T(8,128)S(1)}, f32[384,128]{1,0:T(8,128)S(1)}, /*index=5*/f32[24,128]{1,0:T(8,128)S(1)}) custom-call(s32[4]{0:T(128)S(1)} %pad_add_fusion.par, f32[9,16,64,128]{3,2,1,0:T(8,128)} %start.3, f32[9,8,16,128]{3,2,1,0:T(8,128)S(1)} %copy-done.4, ...), custom_call_target="tpu_custom_call" | custom-call | bytes 6230032 | tf_op jit(solution)/shard_map/pallas_call | solution.py:611
  6.2 4.5 %collective-permute-start.2 = (f32[312,128]{1,0:T(8,128)S(1)}, f32[312,128]{1,0:T(8,128)S(1)}, u32[]{:S(2)}, u32[]{:S(2)}) collective-permute-start(f32[312,128]{1,0:T(8,128)S(1)} %get-tuple-element.45), channel_id=1, source_target_pairs={{1,2},{2,1},{3,4},{4,3},{5,6},{6,5},{9,10},{10,9},{11,12},{12,11},... | collective-permute-start | bytes 479240 | tf_op jit(solution)/shard_map/ppermute | solution.py:637
  10.7 1.4 %collective-permute-start = (f32[240,128]{1,0:T(8,128)S(1)}, f32[240,128]{1,0:T(8,128)S(1)}, u32[]{:S(2)}, u32[]{:S(2)}) collective-permute-start(f32[240,128]{1,0:T(8,128)S(1)} %get-tuple-element.43), channel_id=1, source_target_pairs={{0,8},{8,0},{16,24},{24,16},{1,9},{9,1},{17,25},{25,17},{2,10},{10... | collective-permute-start | bytes 368648 | tf_op jit(solution)/shard_map/ppermute | solution.py:637
  12.7 1.8 %collective-permute-done.msg_a = f32[240,128]{1,0:T(8,128)S(1)} collective-permute-done((f32[240,128]{1,0:T(8,128)S(1)}, f32[240,128]{1,0:T(8,128)S(1)}, u32[]{:S(2)}, u32[]{:S(2)}) %collective-permute-start) | collective-permute-done | bytes 122912 | tf_op jit(solution)/shard_map/ppermute | solution.py:637
  15.1 0.7 collective-permute-start.3
  16.5 13.8 %collective-permute-start.5 = (f32[24,128]{1,0:T(8,128)S(1)}, f32[24,128]{1,0:T(8,128)S(1)}, u32[]{:S(2)}, u32[]{:S(2)}) collective-permute-start(f32[24,128]{1,0:T(8,128)S(1)} %get-tuple-element.49), channel_id=1, source_target_pairs={{1,10},{3,18},{5,26},{9,12},{10,1},{11,20},{12,9},{13,28},{14,17},... | collective-permute-start | bytes 36872 | tf_op jit(solution)/shard_map/ppermute | solution.py:691
  30.4 0.9 copy-done.2
  31.3 0.8 copy-done.5
  32.2 3.5 %shard_map.115.half = f32[3,16,64,128]{3,2,1,0:T(8,128)S(1)} custom-call(s32[4]{0:T(128)S(1)} %pad_add_fusion.par, f32[9,16,64,128]{3,2,1,0:T(8,128)S(1)} %copy-done, f32[3,16,64,128]{3,2,1,0:T(8,128)S(1)} %copy-done.1, f32[240,128]{1,0:T(8,128)S(1)} %collective-permute-done.msg_a, f32[240,128]{1,0:T(8,128)S(1)} %collective-permute-done.1.msg_b, ...), custom_call_target="tpu_custom_call" | custom-call | flops 52428800 | bytes 9084944 | tf_op jit(solution)/shard_map/pallas_call | solution.py:611
  35.8 1.5 %collective-permute-done.7.other = f32[424,128]{1,0:T(8,128)S(1)} collective-permute-done((f32[424,128]{1,0:T(8,128)S(1)}, f32[424,128]{1,0:T(8,128)S(1)}, u32[]{:S(2)}, u32[]{:S(2)}) %collective-permute-start.7) | collective-permute-done | bytes 217120 | tf_op jit(solution)/shard_map/ppermute | solution.py:711
  37.2 1.5 %shard_map.116 = (f32[3,16,64,128]{3,2,1,0:T(8,128)S(1)}, f32[24,64,128]{2,1,0:T(8,128)S(1)}, f32[192,128]{1,0:T(8,128)S(1)}, f32[192,128]{1,0:T(8,128)S(1)}, f3...) custom-call(s32[4]{0:T(128)S(1)} %pad_add_fusion.par, f32[3,16,64,128]{3,2,1,0:T(8,128)S(1)} %shard_map.115.half, ...), custom_call_target="tpu_custom_call" | custom-call | bytes 6370064 | tf_op jit(solution)/shard_map/pallas_call | solution.py:611
  38.9 3.1 %collective-permute-start.11 = (f32[200,128]{1,0:T(8,128)S(1)}, f32[200,128]{1,0:T(8,128)S(1)}, u32[]{:S(2)}, u32[]{:S(2)}) collective-permute-start(f32[200,128]{1,0:T(8,128)S(1)} %get-tuple-element.59), channel_id=1, source_target_pairs={{1,2},{2,1},{3,4},{4,3},{5,6},{6,5},{9,10},{10,9},{11,12},{12,11},... | collective-permute-start | bytes 307208 | tf_op jit(solution)/shard_map/ppermute | solution.py:637
  42.8 2.7 %collective-permute-done.8.msg_a = f32[192,128]{1,0:T(8,128)S(1)} collective-permute-done((f32[192,128]{1,0:T(8,128)S(1)}, f32[192,128]{1,0:T(8,128)S(1)}, u32[]{:S(2)}, u32[]{:S(2)}) %collective-permute-start.8) | collective-permute-done | bytes 98336 | tf_op jit(solution)/shard_map/ppermute | solution.py:637
  45.5 4.3 %shard_map.117 = (f32[6,16,64,128]{3,2,1,0:T(8,128)S(1)}, f32[192,128]{1,0:T(8,128)S(1)}, f32[192,128]{1,0:T(8,128)S(1)}, f32[208,128]{1,0:T(8,128)S(1)}, f32[200,128]{1,0:T(8,128)S(1)}) custom-call(s32[4]{0:T(128)S(1)} %pad_add_fusion.par, f32[3,16,64,128]{3,2,1,0:T(8,128)S(1)} %get-tuple-element.54.velocity.old, f32[9,16,64,128]{3,2,1,0:T(8,128)S(1)} %copy-done, ...), custom_call_target="tpu_custom_call" | custom-call | flops 52428800 | bytes 13262864 | tf_op jit(solution)/shard_map/pallas_call | solution.py:611
  49.8 3.7 %collective-permute-start.15 = (f32[200,128]{1,0:T(8,128)S(1)}, f32[200,128]{1,0:T(8,128)S(1)}, u32[]{:S(2)}, u32[]{:S(2)}) collective-permute-start(f32[200,128]{1,0:T(8,128)S(1)} %get-tuple-element.64), channel_id=1, source_target_pairs={{1,2},{2,1},{3,4},{4,3},{5,6},{6,5},{9,10},{10,9},{11,12},{12,11},... | collective-permute-start | bytes 307208 | tf_op jit(solution)/shard_map/ppermute | solution.py:637
  53.5 4.5 %collective-permute-start.12 = (f32[192,128]{1,0:T(8,128)S(1)}, f32[192,128]{1,0:T(8,128)S(1)}, u32[]{:S(2)}, u32[]{:S(2)}) collective-permute-start(f32[192,128]{1,0:T(8,128)S(1)} %get-tuple-element.61), channel_id=1, source_target_pairs={{0,8},{8,0},{16,24},{24,16},{1,9},{9,1},{17,25},{25,17},{2,10},{10... | collective-permute-start | bytes 294920 | tf_op jit(solution)/shard_map/ppermute | solution.py:637
  58.7 1.3 %collective-permute-done.12.msg_a = f32[192,128]{1,0:T(8,128)S(1)} collective-permute-done((f32[192,128]{1,0:T(8,128)S(1)}, f32[192,128]{1,0:T(8,128)S(1)}, u32[]{:S(2)}, u32[]{:S(2)}) %collective-permute-start.12) | collective-permute-done | bytes 98336 | tf_op jit(solution)/shard_map/ppermute | solution.py:637
  60.1 4.2 %shard_map.118 = (f32[3,16,64,128]{3,2,1,0:T(8,128)S(1)}, f32[192,128]{1,0:T(8,128)S(1)}, f32[192,128]{1,0:T(8,128)S(1)}, f32[208,128]{1,0:T(8,128)S(1)}, f32[20...) custom-call(s32[4]{0:T(128)S(1)} %pad_add_fusion.par, f32[3,16,64,128]{3,2,1,0:T(8,128)S(1)} %get-tuple-element.54.velocity.old, ...), custom_call_target="tpu_custom_call" | custom-call | flops 52428800 | bytes 15196176 | tf_op jit(solution)/shard_map/pallas_call | solution.py:611
  64.3 3.6 %collective-permute-start.19 = (f32[200,128]{1,0:T(8,128)S(1)}, f32[200,128]{1,0:T(8,128)S(1)}, u32[]{:S(2)}, u32[]{:S(2)}) collective-permute-start(f32[200,128]{1,0:T(8,128)S(1)} %get-tuple-element.69), channel_id=1, source_target_pairs={{1,2},{2,1},{3,4},{4,3},{5,6},{6,5},{9,10},{10,9},{11,12},{12,11},... | collective-permute-start | bytes 307208 | tf_op jit(solution)/shard_map/ppermute | solution.py:637
  68.0 3.7 %collective-permute-start.16 = (f32[192,128]{1,0:T(8,128)S(1)}, f32[192,128]{1,0:T(8,128)S(1)}, u32[]{:S(2)}, u32[]{:S(2)}) collective-permute-start(f32[192,128]{1,0:T(8,128)S(1)} %get-tuple-element.66), channel_id=1, source_target_pairs={{0,8},{8,0},{16,24},{24,16},{1,9},{9,1},{17,25},{25,17},{2,10},{10... | collective-permute-start | bytes 294920 | tf_op jit(solution)/shard_map/ppermute | solution.py:637
  72.3 0.7 collective-permute-start.21
  73.0 0.7 collective-permute-done.16.msg_a
  73.7 2.5 %shard_map.119 = (f32[6,8,64,128]{3,2,1,0:T(8,128)S(1)}, f32[176,128]{1,0:T(8,128)S(1)}) custom-call(s32[4]{0:T(128)S(1)} %pad_add_fusion.par, f32[3,16,64,128]{3,2,1,0:T(8,128)S(1)} %get-tuple-element.65.velocity, f32[6,16,64,128]{3,2,1,0:T(8,128)S(1)} %get-tuple-element.60.stress, f32[3,16,64,128]{3,2,1,0:T(8,128)S(1)} %copy-done.1, ...), custom_call_target="tpu_custom_call" | custom-call | bytes 1024 | tf_op jit(solution)/shard_map/pallas_call | solution.py:611
  76.9 4.6 %shard_map.120 = (f32[9,16,64,128]{3,2,1,0:T(8,128)}, f32[8,128]{1,0:T(8,128)S(1)}) custom-call(s32[4]{0:T(128)S(1)} %pad_add_fusion.par, f32[6,8,64,128]{3,2,1,0:T(8,128)S(1)} %get-tuple-element.70.below, f32[3,16,64,128]{3,2,1,0:T(8,128)S(1)} %get-tuple-element.65.velocity, f32[6,16,64,128]{3,2,1,0:T(8,128)S(1)} %get-tuple-element.60.stress, ...), custom_call_target="tpu_custom_call" | custom-call | flops 26214400 | bytes 13647888 | tf_op jit(solution)/shard_map/pallas_call | solution.py:611
  82.0 0.8 collective-permute-done.22.other
  82.8 1.1 %shard_map.121 = (f32[3,8,16,128]{3,2,1,0:T(8,128)S(1)}, f32[96,128]{1,0:T(8,128)S(1)}, f32[96,128]{1,0:T(8,128)S(1)}, f32[24,128]{1,0:T(8,128)S(1)}) custom-call(s32[4]{0:T(128)S(1)} %pad_add_fusion.par, f32[9,8,16,128]{3,2,1,0:T(8,128)S(1)} %copy-done.4, f32[3,8,16,128]{3,2,1,0:T(8,128)S(1)} %copy-done.7, f32[176,128]{1,0:T(8,128)S(1)} %collective-permute-done.20.own, ...), custom_call_target="tpu_custom_call" | custom-call | bytes 2498576 | tf_op jit(solution)/shard_map/pallas_call | solution.py:611
  84.0 11.2 %collective-permute-start.27 = (f32[96,128]{1,0:T(8,128)S(1)}, f32[96,128]{1,0:T(8,128)S(1)}, u32[]{:S(2)}, u32[]{:S(2)}) collective-permute-start(f32[96,128]{1,0:T(8,128)S(1)} %get-tuple-element.81), channel_id=1, source_target_pairs={{1,2},{2,1},{3,4},{4,3},{5,6},{6,5},{9,10},{10,9},{11,12},{12,11},... | collective-permute-start | bytes 147464 | tf_op jit(solution)/shard_map/ppermute | solution.py:637
  95.9 3.4 %collective-permute-start.24 = (f32[24,128]{1,0:T(8,128)S(1)}, f32[24,128]{1,0:T(8,128)S(1)}, u32[]{:S(2)}, u32[]{:S(2)}) collective-permute-start(f32[24,128]{1,0:T(8,128)S(1)} %get-tuple-element.79), channel_id=1, source_target_pairs={{0,8},{8,0},{16,24},{24,16},{1,9},{9,1},{17,25},{25,17},{2,10},{10... | collective-permute-start | bytes 36872 | tf_op jit(solution)/shard_map/ppermute | solution.py:637
  99.3 1.1 %collective-permute-done.24.msg_a = f32[24,128]{1,0:T(8,128)S(1)} collective-permute-done((f32[24,128]{1,0:T(8,128)S(1)}, f32[24,128]{1,0:T(8,128)S(1)}, u32[]{:S(2)}, u32[]{:S(2)}) %collective-permute-start.24) | collective-permute-done | bytes 12320 | tf_op jit(solution)/shard_map/ppermute | solution.py:637
  100.4 1.8 %shard_map.122 = f32[9,8,16,128]{3,2,1,0:T(8,128)} custom-call(s32[4]{0:T(128)S(1)} %pad_add_fusion.par, f32[9,8,16,128]{3,2,1,0:T(8,128)S(1)} %copy-done.4, f32[3,8,16,128]{3,2,1,0:T(8,128)S(1)} %copy-done.7, f32[3,8,16,128]{3,2,1,0:T(8,128)S(1)} %get-tuple-element.77.velocity, f32[192,128]{1,0:T(8,128)S(1)} %collective-permute-done.21.own, ...), custom_call_target="tpu_custom_call" | custom-call | bytes 2547728 | tf_op jit(solution)/shard_map/pallas_call | solution.py:611
  (59 shorter events, 6.6 us)
Async XLA Ops:
  0.7 29.7 %copy-start.1 = (f32[3,16,64,128]{3,2,1,0:T(8,128)S(1)}, f32[3,16,64,128]{3,2,1,0:T(8,128)}, u32[]{:S(2)}) copy-start(f32[3,16,64,128]{3,2,1,0:T(8,128)} %medium.7) | copy-start | bytes 4718596
  2.8 27.5 %copy-start = (f32[9,16,64,128]{3,2,1,0:T(8,128)S(1)}, f32[9,16,64,128]{3,2,1,0:T(8,128)}, u32[]{:S(2)}) copy-start(f32[9,16,64,128]{3,2,1,0:T(8,128)} %start.3) | copy-start | bytes 14155780
  6.2 8.3 %collective-permute-start.2 = (f32[312,128]{1,0:T(8,128)S(1)}, f32[312,128]{1,0:T(8,128)S(1)}, u32[]{:S(2)}, u32[]{:S(2)}) collective-permute-start(f32[312,128]{1,0:T(8,128)S(1)} %get-tuple-element.45), channel_id=1, source_target_pairs={{1,2},{2,1},{3,4},{4,3},{5,6},{6,5},{9,10},{10,9},{11,12},{12,11},... | collective-permute-start | bytes 479240 | tf_op jit(solution)/shard_map/ppermute | solution.py:637
  10.7 3.8 %collective-permute-start = (f32[240,128]{1,0:T(8,128)S(1)}, f32[240,128]{1,0:T(8,128)S(1)}, u32[]{:S(2)}, u32[]{:S(2)}) collective-permute-start(f32[240,128]{1,0:T(8,128)S(1)} %get-tuple-element.43), channel_id=1, source_target_pairs={{0,8},{8,0},{16,24},{24,16},{1,9},{9,1},{17,25},{25,17},{2,10},{10... | collective-permute-start | bytes 368648 | tf_op jit(solution)/shard_map/ppermute | solution.py:637
  12.1 2.4 %collective-permute-start.1 = (f32[240,128]{1,0:T(8,128)S(1)}, f32[240,128]{1,0:T(8,128)S(1)}, u32[]{:S(2)}, u32[]{:S(2)}) collective-permute-start(f32[240,128]{1,0:T(8,128)S(1)} %get-tuple-element.44), channel_id=1, source_target_pairs={{8,16},{16,8},{9,17},{17,9},{10,18},{18,10},{11,19},{19,11},{12,20... | collective-permute-start | bytes 368648 | tf_op jit(solution)/shard_map/ppermute | solution.py:637
  15.1 20.6 %collective-permute-start.3 = (f32[424,128]{1,0:T(8,128)S(1)}, f32[424,128]{1,0:T(8,128)S(1)}, u32[]{:S(2)}, u32[]{:S(2)}) collective-permute-start(f32[424,128]{1,0:T(8,128)S(1)} %shard_map.114), channel_id=1, source_target_pairs={{0,0},{1,1},{2,8},{3,9},{4,16},{5,17},{6,24},{7,25},{8,2},{9,3},{1... | collective-permute-start | bytes 651272 | tf_op jit(solution)/shard_map/ppermute | solution.py:690
  15.8 21.5 %copy-start.10 = (s32[64]{0:T(128)S(1)}, s32[64]{0:T(128)}, u32[]{:S(2)}) copy-start(s32[64]{0:T(128)} %param.15) | copy-start | bytes 772
  15.8 14.5 %collective-permute-start.4 = (f32[312,128]{1,0:T(8,128)S(1)}, f32[312,128]{1,0:T(8,128)S(1)}, u32[]{:S(2)}, u32[]{:S(2)}) collective-permute-start(f32[312,128]{1,0:T(8,128)S(1)} %get-tuple-element.48), channel_id=1, source_target_pairs={{0,1},{1,0},{2,3},{3,2},{4,5},{5,4},{6,7},{7,6},{8,9},{9,8},{10,11... | collective-permute-start | bytes 479240 | tf_op jit(solution)/shard_map/ppermute | solution.py:637
  15.9 19.8 %collective-permute-start.6 = (f32[24,128]{1,0:T(8,128)S(1)}, f32[24,128]{1,0:T(8,128)S(1)}, u32[]{:S(2)}, u32[]{:S(2)}) collective-permute-start(f32[24,128]{1,0:T(8,128)S(1)} %get-tuple-element.49), channel_id=1, source_target_pairs={{2,2},{4,10},{6,18},{9,9},{10,4},{11,17},{12,12},{13,25},{14,20},{... | collective-permute-start | bytes 36872 | tf_op jit(solution)/shard_map/ppermute | solution.py:692
  16.5 19.1 %collective-permute-start.5 = (f32[24,128]{1,0:T(8,128)S(1)}, f32[24,128]{1,0:T(8,128)S(1)}, u32[]{:S(2)}, u32[]{:S(2)}) collective-permute-start(f32[24,128]{1,0:T(8,128)S(1)} %get-tuple-element.49), channel_id=1, source_target_pairs={{1,10},{3,18},{5,26},{9,12},{10,1},{11,20},{12,9},{13,28},{14,17},... | collective-permute-start | bytes 36872 | tf_op jit(solution)/shard_map/ppermute | solution.py:691
  35.7 1.5 %collective-permute-start.7 = (f32[424,128]{1,0:T(8,128)S(1)}, f32[424,128]{1,0:T(8,128)S(1)}, u32[]{:S(2)}, u32[]{:S(2)}) collective-permute-start(f32[424,128]{1,0:T(8,128)S(1)} %collective-permute-done.3.own), channel_id=1, source_target_pairs={{0,1},{1,0},{2,3},{3,2},{4,5},{5,4},{6,7},{7,6},{8,9},{9,8},{10,11... | collective-permute-start | bytes 651272 | tf_op jit(solution)/shard_map/ppermute | solution.py:711
  38.7 6.8 %collective-permute-start.10 = (f32[208,128]{1,0:T(8,128)S(1)}, f32[208,128]{1,0:T(8,128)S(1)}, u32[]{:S(2)}, u32[]{:S(2)}) collective-permute-start(f32[208,128]{1,0:T(8,128)S(1)} %get-tuple-element.58), channel_id=1, source_target_pairs={{0,1},{1,0},{2,3},{3,2},{4,5},{5,4},{6,7},{7,6},{8,9},{9,8},{10,11... | collective-permute-start | bytes 319496 | tf_op jit(solution)/shard_map/ppermute | solution.py:637
  38.9 6.6 %collective-permute-start.11 = (f32[200,128]{1,0:T(8,128)S(1)}, f32[200,128]{1,0:T(8,128)S(1)}, u32[]{:S(2)}, u32[]{:S(2)}) collective-permute-start(f32[200,128]{1,0:T(8,128)S(1)} %get-tuple-element.59), channel_id=1, source_target_pairs={{1,2},{2,1},{3,4},{4,3},{5,6},{6,5},{9,10},{10,9},{11,12},{12,11},... | collective-permute-start | bytes 307208 | tf_op jit(solution)/shard_map/ppermute | solution.py:637
  42.0 3.5 %collective-permute-start.8 = (f32[192,128]{1,0:T(8,128)S(1)}, f32[192,128]{1,0:T(8,128)S(1)}, u32[]{:S(2)}, u32[]{:S(2)}) collective-permute-start(f32[192,128]{1,0:T(8,128)S(1)} %get-tuple-element.56), channel_id=1, source_target_pairs={{0,8},{8,0},{16,24},{24,16},{1,9},{9,1},{17,25},{25,17},{2,10},{10... | collective-permute-start | bytes 294920 | tf_op jit(solution)/shard_map/ppermute | solution.py:637
  42.1 3.4 %collective-permute-start.9 = (f32[192,128]{1,0:T(8,128)S(1)}, f32[192,128]{1,0:T(8,128)S(1)}, u32[]{:S(2)}, u32[]{:S(2)}) collective-permute-start(f32[192,128]{1,0:T(8,128)S(1)} %get-tuple-element.57), channel_id=1, source_target_pairs={{8,16},{16,8},{9,17},{17,9},{10,18},{18,10},{11,19},{19,11},{12,20... | collective-permute-start | bytes 294920 | tf_op jit(solution)/shard_map/ppermute | solution.py:637
  45.5 14.5 %copy-start.8 = (bf16[2,256,128]{2,1,0:T(8,128)(2,1)S(1)}, bf16[2,256,128]{2,1,0:T(8,128)(2,1)}, u32[]{:S(2)}) copy-start(bf16[2,256,128]{2,1,0:T(8,128)(2,1)} %constant.48.clone.means) | copy-start | bytes 393220
  49.8 10.2 %collective-permute-start.14 = (f32[208,128]{1,0:T(8,128)S(1)}, f32[208,128]{1,0:T(8,128)S(1)}, u32[]{:S(2)}, u32[]{:S(2)}) collective-permute-start(f32[208,128]{1,0:T(8,128)S(1)} %get-tuple-element.63), channel_id=1, source_target_pairs={{0,1},{1,0},{2,3},{3,2},{4,5},{5,4},{6,7},{7,6},{8,9},{9,8},{10,11... | collective-permute-start | bytes 319496 | tf_op jit(solution)/shard_map/ppermute | solution.py:637
  49.8 10.2 %collective-permute-start.15 = (f32[200,128]{1,0:T(8,128)S(1)}, f32[200,128]{1,0:T(8,128)S(1)}, u32[]{:S(2)}, u32[]{:S(2)}) collective-permute-start(f32[200,128]{1,0:T(8,128)S(1)} %get-tuple-element.64), channel_id=1, source_target_pairs={{1,2},{2,1},{3,4},{4,3},{5,6},{6,5},{9,10},{10,9},{11,12},{12,11},... | collective-permute-start | bytes 307208 | tf_op jit(solution)/shard_map/ppermute | solution.py:637
  53.5 6.5 %collective-permute-start.12 = (f32[192,128]{1,0:T(8,128)S(1)}, f32[192,128]{1,0:T(8,128)S(1)}, u32[]{:S(2)}, u32[]{:S(2)}) collective-permute-start(f32[192,128]{1,0:T(8,128)S(1)} %get-tuple-element.61), channel_id=1, source_target_pairs={{0,8},{8,0},{16,24},{24,16},{1,9},{9,1},{17,25},{25,17},{2,10},{10... | collective-permute-start | bytes 294920 | tf_op jit(solution)/shard_map/ppermute | solution.py:637
  58.0 2.0 %collective-permute-start.13 = (f32[192,128]{1,0:T(8,128)S(1)}, f32[192,128]{1,0:T(8,128)S(1)}, u32[]{:S(2)}, u32[]{:S(2)}) collective-permute-start(f32[192,128]{1,0:T(8,128)S(1)} %get-tuple-element.62), channel_id=1, source_target_pairs={{8,16},{16,8},{9,17},{17,9},{10,18},{18,10},{11,19},{19,11},{12,20... | collective-permute-start | bytes 294920 | tf_op jit(solution)/shard_map/ppermute | solution.py:637
  64.2 9.4 %collective-permute-start.18 = (f32[208,128]{1,0:T(8,128)S(1)}, f32[208,128]{1,0:T(8,128)S(1)}, u32[]{:S(2)}, u32[]{:S(2)}) collective-permute-start(f32[208,128]{1,0:T(8,128)S(1)} %get-tuple-element.68), channel_id=1, source_target_pairs={{0,1},{1,0},{2,3},{3,2},{4,5},{5,4},{6,7},{7,6},{8,9},{9,8},{10,11... | collective-permute-start | bytes 319496 | tf_op jit(solution)/shard_map/ppermute | solution.py:637
  64.3 9.4 %collective-permute-start.19 = (f32[200,128]{1,0:T(8,128)S(1)}, f32[200,128]{1,0:T(8,128)S(1)}, u32[]{:S(2)}, u32[]{:S(2)}) collective-permute-start(f32[200,128]{1,0:T(8,128)S(1)} %get-tuple-element.69), channel_id=1, source_target_pairs={{1,2},{2,1},{3,4},{4,3},{5,6},{6,5},{9,10},{10,9},{11,12},{12,11},... | collective-permute-start | bytes 307208 | tf_op jit(solution)/shard_map/ppermute | solution.py:637
  68.0 5.7 %collective-permute-start.16 = (f32[192,128]{1,0:T(8,128)S(1)}, f32[192,128]{1,0:T(8,128)S(1)}, u32[]{:S(2)}, u32[]{:S(2)}) collective-permute-start(f32[192,128]{1,0:T(8,128)S(1)} %get-tuple-element.66), channel_id=1, source_target_pairs={{0,8},{8,0},{16,24},{24,16},{1,9},{9,1},{17,25},{25,17},{2,10},{10... | collective-permute-start | bytes 294920 | tf_op jit(solution)/shard_map/ppermute | solution.py:637
  71.7 2.0 %collective-permute-start.17 = (f32[192,128]{1,0:T(8,128)S(1)}, f32[192,128]{1,0:T(8,128)S(1)}, u32[]{:S(2)}, u32[]{:S(2)}) collective-permute-start(f32[192,128]{1,0:T(8,128)S(1)} %get-tuple-element.67), channel_id=1, source_target_pairs={{8,16},{16,8},{9,17},{17,9},{10,18},{18,10},{11,19},{19,11},{12,20... | collective-permute-start | bytes 294920 | tf_op jit(solution)/shard_map/ppermute | solution.py:637
  72.3 9.2 %collective-permute-start.21 = (f32[192,128]{1,0:T(8,128)S(1)}, f32[192,128]{1,0:T(8,128)S(1)}, u32[]{:S(2)}, u32[]{:S(2)}) collective-permute-start(f32[192,128]{1,0:T(8,128)S(1)} %get-tuple-element.74), channel_id=1, source_target_pairs={{0,0},{1,1},{2,8},{3,9},{4,16},{5,17},{6,24},{7,25},{8,2},{9,3},{1... | collective-permute-start | bytes 294920 | tf_op jit(solution)/shard_map/ppermute | solution.py:737
  76.2 5.3 %collective-permute-start.20 = (f32[176,128]{1,0:T(8,128)S(1)}, f32[176,128]{1,0:T(8,128)S(1)}, u32[]{:S(2)}, u32[]{:S(2)}) collective-permute-start(f32[176,128]{1,0:T(8,128)S(1)} %get-tuple-element.72), channel_id=1, source_target_pairs={{0,0},{1,1},{2,8},{3,9},{4,16},{5,17},{6,24},{7,25},{8,2},{9,3},{1... | collective-permute-start | bytes 270344 | tf_op jit(solution)/shard_map/ppermute | solution.py:745
  81.5 1.3 %collective-permute-start.22 = (f32[176,128]{1,0:T(8,128)S(1)}, f32[176,128]{1,0:T(8,128)S(1)}, u32[]{:S(2)}, u32[]{:S(2)}) collective-permute-start(f32[176,128]{1,0:T(8,128)S(1)} %collective-permute-done.20.own), channel_id=1, source_target_pairs={{0,1},{1,0},{2,3},{3,2},{4,5},{5,4},{6,7},{7,6},{8,9},{9,8},{10,11... | collective-permute-start | bytes 270344 | tf_op jit(solution)/shard_map/ppermute | solution.py:754
  81.5 17.8 %collective-permute-start.23 = (f32[192,128]{1,0:T(8,128)S(1)}, f32[192,128]{1,0:T(8,128)S(1)}, u32[]{:S(2)}, u32[]{:S(2)}) collective-permute-start(f32[192,128]{1,0:T(8,128)S(1)} %collective-permute-done.21.own), channel_id=1, source_target_pairs={{0,1},{1,0},{2,3},{3,2},{4,5},{5,4},{6,7},{7,6},{8,9},{9,8},{10,11... | collective-permute-start | bytes 294920 | tf_op jit(solution)/shard_map/ppermute | solution.py:755
  83.9 16.5 %collective-permute-start.26 = (f32[96,128]{1,0:T(8,128)S(1)}, f32[96,128]{1,0:T(8,128)S(1)}, u32[]{:S(2)}, u32[]{:S(2)}) collective-permute-start(f32[96,128]{1,0:T(8,128)S(1)} %get-tuple-element.80), channel_id=1, source_target_pairs={{0,1},{1,0},{2,3},{3,2},{4,5},{5,4},{6,7},{7,6},{8,9},{9,8},{10,11... | collective-permute-start | bytes 147464 | tf_op jit(solution)/shard_map/ppermute | solution.py:637
  84.0 16.4 %collective-permute-start.27 = (f32[96,128]{1,0:T(8,128)S(1)}, f32[96,128]{1,0:T(8,128)S(1)}, u32[]{:S(2)}, u32[]{:S(2)}) collective-permute-start(f32[96,128]{1,0:T(8,128)S(1)} %get-tuple-element.81), channel_id=1, source_target_pairs={{1,2},{2,1},{3,4},{4,3},{5,6},{6,5},{9,10},{10,9},{11,12},{12,11},... | collective-permute-start | bytes 147464 | tf_op jit(solution)/shard_map/ppermute | solution.py:637
  95.2 4.1 %collective-permute-start.25 = (f32[24,128]{1,0:T(8,128)S(1)}, f32[24,128]{1,0:T(8,128)S(1)}, u32[]{:S(2)}, u32[]{:S(2)}) collective-permute-start(f32[24,128]{1,0:T(8,128)S(1)} %get-tuple-element.79), channel_id=1, source_target_pairs={{8,16},{16,8},{9,17},{17,9},{10,18},{18,10},{11,19},{19,11},{12,20... | collective-permute-start | bytes 36872 | tf_op jit(solution)/shard_map/ppermute | solution.py:637
  95.9 4.5 %collective-permute-start.24 = (f32[24,128]{1,0:T(8,128)S(1)}, f32[24,128]{1,0:T(8,128)S(1)}, u32[]{:S(2)}, u32[]{:S(2)}) collective-permute-start(f32[24,128]{1,0:T(8,128)S(1)} %get-tuple-element.79), channel_id=1, source_target_pairs={{0,8},{8,0},{16,24},{24,16},{1,9},{9,1},{17,25},{25,17},{2,10},{10... | collective-permute-start | bytes 36872 | tf_op jit(solution)/shard_map/ppermute | solution.py:637
  (8 other events, 26.3 us)

commit v4 on v3

--- a/solution.py
+++ b/solution.py
@@ -217,7 +217,7 @@
         out[2, z] = old[2, z] + scale * (x + along_y(ey, 2, z, rows) + zz)
         return 0
 
-    lax.fori_loop(0, depth, layer, 0, unroll=2 if rows > 16 else depth)
+    lax.fori_loop(0, depth, layer, 0, unroll=4 if rows > 16 else depth)
 
 
 def stress_half(old, lame, shear, put, low, count, ex, ey, ez):
@@ -242,7 +242,7 @@
         put(5, z, n, old(5, z) + mu * (along_z(ez, 1, n, True) + y))
         return 0
 
-    lax.fori_loop(0, count, layer, 0, unroll=2 if rows > 16 else count)
+    lax.fori_loop(0, count, layer, 0, unroll=4 if rows > 16 else count)
 
 
 def zeros_like_plane(ref):
@@ -295,11 +295,9 @@
         put_columns((out_1, out_2), base, [(turned, k)])
 
 
-def crossing_kernel(par, planes, msg_a, msg_b, msg_2, out):
+def crossing_kernel(par, planes, msg_a, msg_b, msg_2, first, second):
     count = planes.shape[0]
     blocks = count // LANES
-    out[0:count, :] = planes[...]
-    out[count : count + 24, :] = msg_2[msg_2.shape[0] - 24 :, :]
     even = par[0] == 0
     base = msg_a.shape[0] - 8 * blocks
     left, right = [], []
@@ -309,17 +307,22 @@
         left.append(jnp.where(even, b, a)[7:8])
         right.append(jnp.where(even, a, b)[0:1])
     fill = [jnp.zeros((8 - blocks, LANES), F32)]
-    out[count + 24 : count + 32, :] = jnp.concatenate(left + fill, axis=0)
-    out[count + 32 : count + 40, :] = jnp.concatenate(right + fill, axis=0)
-
-
-def expand_ghosts(par, own, other, corner_1, corner_2, prow, pcol, ghost):
+    left, right = (jnp.concatenate(side + fill, axis=0) for side in (left, right))
+    half = count // 2
+    first[0:half, :] = planes[:half, :]
+    first[half : half + 24, :] = msg_2[msg_2.shape[0] - 24 :, :]
+    first[half + 24 : half + 32, :] = left
+    first[half + 32 : half + 40, :] = right
+    second[...] = planes[half:, :]
+
+
+def expand_ghosts(par, own, other, corner_1, corner_2, prow, pcol, ghost, level, planes):
     core = par[1]
     row_base, col_base = par[2], par[3]
-    part = (own.shape[0] - 40) // 24
+    part = (own.shape[0] - 40) // 12
     rows = prow.shape[1]
     low = core == 0
-    count = 24 * part
+    count = 12 * part
     source = lax.broadcasted_iota(jnp.int32, (LANES, LANES), 0)
     pick_cols = (source == pcol[...] - col_base).astype(BF16)
     pick_cols = jnp.concatenate([pick_cols, pick_cols], axis=0)
@@ -330,7 +333,10 @@
     def spread(x):
         return dot(jnp.concatenate(split(x), axis=1), pick_cols)
 
-    mine, theirs = spread(own[0 : count + 24, :]), spread(other[0 : count + 24, :])
+    mine, theirs = (
+        spread(jnp.concatenate([main[0:count, :], ref[count : count + 24, :]], axis=0))
+        for main, ref in zip(planes, (own, other))
+    )
     first, second = jnp.where(low, mine, theirs), jnp.where(low, theirs, mine)
     above, below = first[count:], second[count:]
     beside = []
@@ -356,21 +362,30 @@
         at = slice(q * part, (q + 1) * part)
         column = jnp.concatenate([side_1[at], side_2[at]], axis=0)
         columns.append(dot(pick_rows, jnp.concatenate(split(column), axis=0), ((0,), (0,))))
-    for p in range(24):
-        at = slice(p * part, (p + 1) * part)
+    for n in range(12):
+        p = 12 * level + n
+        at = slice(n * part, (n + 1) * part)
         plane = jnp.concatenate([first[at], second[at]], axis=0)
         full = dot(pick_rows, jnp.concatenate(split(plane), axis=0), ((0,), (0,)))
         column = columns[p % group][:, p // group : p // group + 1]
         full = full + jnp.where(edge, column, 0.0)
         full = full + jnp.where(row == 0, above[p : p + 1], 0.0)
-        ghost[p] = full + jnp.where(row == rows - 1, below[p : p + 1], 0.0)
+        ghost[n] = full + jnp.where(row == rows - 1, below[p : p + 1], 0.0)
+
+
+def later_ghost_kernel(
+    par, own, other, corner_1, corner_2, prow, pcol, later_own, later_other, ghost
+):
+    planes = later_own, later_other
+    expand_ghosts(par, own, other, corner_1, corner_2, prow, pcol, ghost, 1, planes)
 
 
 def ghost_kernel(
     par, half, buoyancy, own, other, corner_1, corner_2, prow, pcol,
     out, ghost, out_a, out_b, out_1, out_2,
 ):
-    expand_ghosts(par, own, other, corner_1, corner_2, prow, pcol, ghost)
+    planes = own, other
+    expand_ghosts(par, own, other, corner_1, corner_2, prow, pcol, ghost, 0, planes)
     depth = half.shape[1]
     for c, (f, forward) in enumerate(VEL_Z):
         out[c, 0 : depth - 4] = half[c, 0 : depth - 4]
@@ -424,7 +439,7 @@
     order = [CROSSING.index(f) for f, _ in VEL_Z]
     velocity_fill(
         par, stress, msg_a, msg_b, msg_1, msg_2, tile, halo,
-        lambda k, g: ghost[12 + 2 * order[k] + g // 2], ex, ey, ez,
+        lambda k, g: ghost[2 * order[k] + g // 2], ex, ey, ez,
     )
     velocity_half(old, buoyancy, out, ex, ey, ez)
     moved = [(out, c) for c in range(3)]
@@ -494,7 +509,7 @@
     depth, rows = velocity.shape[1], velocity.shape[2]
     low = depth - 8
     stress_fill(
-        par, velocity, lambda k, g: ghost[12 + 2 * k + g // 2], msg_a, msg_b, msg_1, msg_2,
+        par, velocity, lambda k, g: ghost[2 * k + g // 2], msg_a, msg_b, msg_1, msg_2,
         tile, halo, ex, ey, ez, low, 8,
     )
 
@@ -616,7 +631,7 @@
         out_shape=[jax.ShapeDtypeStruct(o, F32) for o in outs],
         scratch_shapes=[pltpu.VMEM(s, F32) for s in scratch]
         + ([pltpu.SemaphoreType.DMA((11,))] if copied else []),
-        compiler_params=pltpu.CompilerParams(vmem_limit_bytes=(52 if copied else 24) * 1024 * 1024),
+        compiler_params=pltpu.CompilerParams(vmem_limit_bytes=(46 if copied else 24) * 1024 * 1024),
         cost_estimate=pl.CostEstimate(flops=flops, bytes_accessed=size, transcendentals=0),
     )(*args)
 
@@ -683,8 +698,10 @@
     msg_a, msg_b = exchange("gx", out_a, out_b)
     msg_1, msg_2 = exchange("gy", out_1, out_2)
     begin = msg_a, msg_b, msg_1, msg_2
-    (crossing,) = call(
-        crossing_kernel, [par, planes, msg_a, msg_b, msg_2], [(count + 40, LANES)]
+    crossing, later = call(
+        crossing_kernel,
+        [par, planes, msg_a, msg_b, msg_2],
+        [(count // 2 + 40, LANES), (count // 2, LANES)],
     )
     crossing, outer = lax.optimization_barrier((crossing, outer))
     own = lax.ppermute(crossing, both, across)
@@ -699,7 +716,7 @@
         ]
 
     cells = depth * rows * cols
-    halves = [(rows_msg, LANES)] * 2 + [(cols_msg + 16, LANES), (cols_msg + 8, LANES)]
+    halves = [(rows_msg + 8, LANES)] * 2 + [(cols_msg + 24, LANES), (cols_msg + 16, LANES)]
     (half,) = call(
         first_velocity_kernel,
         [par, fine_state, fine_medium, msg_a, msg_b, msg_1, msg_2, tile, halo],
@@ -709,13 +726,16 @@
     )
     own, half, corner_1, corner_2 = lax.optimization_barrier((own, half, corner_1, corner_2))
     other = lax.ppermute(own, "gy", partner)
+    parents = parent_rows.reshape(1, rows), parent_cols.reshape(1, cols)
     velocity, ghost, out_a, out_b, out_1, out_2 = call(
         ghost_kernel,
         [par, half, fine_medium, own, other, corner_1, corner_2,
-         parent_rows.reshape(1, rows), parent_cols.reshape(1, cols)],
-        [(3,) + shape, (24, rows, cols)] + halves,
+         *parents],
+        [(3,) + shape, (12, rows, cols)] + halves,
     )
     msgs = exchange("gx", out_a, out_b) + exchange("gy", out_1, out_2)
+    later, velocity = lax.optimization_barrier((later, velocity))
+    later = lax.ppermute(later, both, across)
     stress, out_a, out_b, out_1, out_2 = call(
         stress_kernel,
         [par, velocity, fine_state, fine_medium, ghost, *msgs, tile, halo],
@@ -724,6 +744,13 @@
         flops=400 * cells,
     )
     msgs = exchange("gx", out_a, out_b) + exchange("gy", out_1, out_2)
+    later, stress = lax.optimization_barrier((later, stress))
+    later_other = lax.ppermute(later, "gy", partner)
+    (ghost,) = call(
+        later_ghost_kernel,
+        [par, own, other, corner_1, corner_2, *parents, later, later_other],
+        [(12, rows, cols)],
+    )
     moved_v, moved_s = (len(above_planes(t)) * part for t in (STR_Z, VEL_Z))
     lift_scratch = [(rows, cols), (2, count // 2, LANES)]
     velocity, out_a, out_b, out_1, out_2, lifted = call(

time: 103 us -> 102 us (level)
    ppermute x20, waiting for transfers between devices: 7.61 us -> 5.67 us  [exchange(): return (lax.ppermute(first, axis, one), lax.ppermute(second, axis, two))]
    ppermute x0 -> x2, waiting for transfers between devices: none -> 1.29 us  [the longest x1 1.29 us: body(): later_other = lax.ppermute(later, 'gy', partner)]
    ppermute x1, starting transfers between devices: 13.8 us -> 12.7 us  [body(): corner_1 = lax.ppermute(outer, both, corners[0])]
    unnamed x24 -> x20, local copies, waits for them, and re-layouts: 3.9 us -> 4.35 us
    pallas_call x10 -> x11, Pallas kernels: 27.3 us -> 27 us  [call(): pl.pallas_call(kernel, grid=(1,), in_specs=specs, out_specs=[whole(o) for...]
  transfers between devices with their start and end apart: 28 -> 30, of which waited for: 7 -> 7; matrix products, arithmetic and copies ran while one was open for 0% -> 0% of each run, Pallas kernels for 11% -> 17%
where the time goes in v4:
time: 102 us; the launch traced here: 101 us
  starting transfers between devices  59.5 us (58%)
  Pallas kernels  27 us (26%)
  waiting for transfers between devices  9.07 us (9%)
  local copies, waits for them, and re-layouts  4.35 us (4%)
  between operations  1.03 us (1%)
    ppermute x20, starting transfers between devices, exchange(): return (lax.ppermute(first, axis, one), lax.ppermute(second, axis, two))  42.6 us
    pallas_call x11, Pallas kernels, call(): pl.pallas_call(kernel, grid=(1,), in_specs=specs, out_specs=[whole(o) for...  27 us
    ppermute x1, starting transfers between devices, body(): corner_1 = lax.ppermute(outer, both, corners[0])  12.7 us
    ppermute x20, waiting for transfers between devices, exchange(): return (lax.ppermute(first, axis, one), lax.ppermute(second, axis, two))  5.67 us
    unnamed x20, local copies, waits for them, and re-layouts  4.35 us
    ppermute x2, waiting for transfers between devices, body(): other = lax.ppermute(own, 'gy', partner)  2.1 us
  transfers between devices with their start and end apart: 30, of which 7 were waited for; matrix products, arithmetic and copies ran while one was open for 0% of the time, Pallas kernels for 17%

profile of v4, /device:TPU:1, one launch (start us, length us, event | category | flops | bytes accessed | tf_op | source)
XLA Modules:
  0.0 101.0 jit_solution(7397981118896394538)
XLA Ops:
  0.7 2.3 %copy-done = f32[9,16,64,128]{3,2,1,0:T(8,128)S(1)} copy-done((f32[9,16,64,128]{3,2,1,0:T(8,128)S(1)}, f32[9,16,64,128]{3,2,1,0:T(8,128)}, u32[]{:S(2)}) %copy-start) | copy-done | bytes 4718616
  3.1 1.1 %copy-done.3 = f32[9,8,16,128]{3,2,1,0:T(8,128)S(1)} copy-done((f32[9,8,16,128]{3,2,1,0:T(8,128)S(1)}, f32[9,8,16,128]{3,2,1,0:T(8,128)}, u32[]{:S(2)}) %copy-start.3) | copy-done | bytes 589848
  4.1 0.9 copy-done.7
  5.1 2.1 %shard_map.113 = (f32[240,128]{1,0:T(8,128)S(1)}, f32[240,128]{1,0:T(8,128)S(1)}, f32[312,128]{1,0:T(8,128)S(1)}, f32[312,128]{1,0:T(8,128)S(1)}, f32[384,128]{1,0:T(8,128)S(1)}, /*index=5*/f32[24,128]{1,0:T(8,128)S(1)}) custom-call(s32[4]{0:T(128)S(1)} %pad_add_fusion.par, f32[9,16,64,128]{3,2,1,0:T(8,128)S(1)} %copy-done, f32[9,8,16,128]{3,2,1,0:T(8,128)S(1)} %copy-done.3, ...), custom_call_target="tpu_custom_call" | custom-call | bytes 6230032 | tf_op jit(solution)/shard_map/pallas_call | solution.py:626
  7.2 4.5 %collective-permute-start.2 = (f32[312,128]{1,0:T(8,128)S(1)}, f32[312,128]{1,0:T(8,128)S(1)}, u32[]{:S(2)}, u32[]{:S(2)}) collective-permute-start(f32[312,128]{1,0:T(8,128)S(1)} %get-tuple-element.51), channel_id=1, source_target_pairs={{1,2},{2,1},{3,4},{4,3},{5,6},{6,5},{9,10},{10,9},{11,12},{12,11},... | collective-permute-start | bytes 479240 | tf_op jit(solution)/shard_map/ppermute | solution.py:652
  11.7 1.4 %collective-permute-start = (f32[240,128]{1,0:T(8,128)S(1)}, f32[240,128]{1,0:T(8,128)S(1)}, u32[]{:S(2)}, u32[]{:S(2)}) collective-permute-start(f32[240,128]{1,0:T(8,128)S(1)} %get-tuple-element.49), channel_id=1, source_target_pairs={{0,8},{8,0},{16,24},{24,16},{1,9},{9,1},{17,25},{25,17},{2,10},{10... | collective-permute-start | bytes 368648 | tf_op jit(solution)/shard_map/ppermute | solution.py:652
  13.8 1.7 %collective-permute-done.msg_a = f32[240,128]{1,0:T(8,128)S(1)} collective-permute-done((f32[240,128]{1,0:T(8,128)S(1)}, f32[240,128]{1,0:T(8,128)S(1)}, u32[]{:S(2)}, u32[]{:S(2)}) %collective-permute-start) | collective-permute-done | bytes 122912 | tf_op jit(solution)/shard_map/ppermute | solution.py:652
  16.1 0.7 collective-permute-start.3
  17.5 12.7 %collective-permute-start.5 = (f32[24,128]{1,0:T(8,128)S(1)}, f32[24,128]{1,0:T(8,128)S(1)}, u32[]{:S(2)}, u32[]{:S(2)}) collective-permute-start(f32[24,128]{1,0:T(8,128)S(1)} %get-tuple-element.57), channel_id=1, source_target_pairs={{1,10},{3,18},{5,26},{9,12},{10,1},{11,20},{12,9},{13,28},{14,17},... | collective-permute-start | bytes 36872 | tf_op jit(solution)/shard_map/ppermute | solution.py:708
  30.2 3.5 %shard_map.115.half = f32[3,16,64,128]{3,2,1,0:T(8,128)S(1)} custom-call(s32[4]{0:T(128)S(1)} %pad_add_fusion.par, f32[9,16,64,128]{3,2,1,0:T(8,128)S(1)} %copy-done, f32[3,16,64,128]{3,2,1,0:T(8,128)S(1)} %copy-done.1, f32[240,128]{1,0:T(8,128)S(1)} %collective-permute-done.msg_a, f32[240,128]{1,0:T(8,128)S(1)} %collective-permute-done.1.msg_b, ...), custom_call_target="tpu_custom_call" | custom-call | flops 52428800 | bytes 9084944 | tf_op jit(solution)/shard_map/pallas_call | solution.py:626
  33.8 1.3 %collective-permute-done.7.other = f32[232,128]{1,0:T(8,128)S(1)} collective-permute-done((f32[232,128]{1,0:T(8,128)S(1)}, f32[232,128]{1,0:T(8,128)S(1)}, u32[]{:S(2)}, u32[]{:S(2)}) %collective-permute-start.7) | collective-permute-done | bytes 118816 | tf_op jit(solution)/shard_map/ppermute | solution.py:728
  35.1 1.4 %shard_map.116 = (f32[3,16,64,128]{3,2,1,0:T(8,128)S(1)}, f32[12,64,128]{2,1,0:T(8,128)S(1)}, f32[200,128]{1,0:T(8,128)S(1)}, f32[200,128]{1,0:T(8,128)S(1)}, f3...) custom-call(s32[4]{0:T(128)S(1)} %pad_add_fusion.par, f32[3,16,64,128]{3,2,1,0:T(8,128)S(1)} %shard_map.115.half, ...), custom_call_target="tpu_custom_call" | custom-call | bytes 5796624 | tf_op jit(solution)/shard_map/pallas_call | solution.py:626
  36.7 3.7 %collective-permute-start.12 = (f32[208,128]{1,0:T(8,128)S(1)}, f32[208,128]{1,0:T(8,128)S(1)}, u32[]{:S(2)}, u32[]{:S(2)}) collective-permute-start(f32[208,128]{1,0:T(8,128)S(1)} %get-tuple-element.69), channel_id=1, source_target_pairs={{1,2},{2,1},{3,4},{4,3},{5,6},{6,5},{9,10},{10,9},{11,12},{12,11},... | collective-permute-start | bytes 319496 | tf_op jit(solution)/shard_map/ppermute | solution.py:652
  41.8 2.1 %collective-permute-done.9.msg_a = f32[200,128]{1,0:T(8,128)S(1)} collective-permute-done((f32[200,128]{1,0:T(8,128)S(1)}, f32[200,128]{1,0:T(8,128)S(1)}, u32[]{:S(2)}, u32[]{:S(2)}) %collective-permute-start.9) | collective-permute-done | bytes 102432 | tf_op jit(solution)/shard_map/ppermute | solution.py:652
  44.0 4.3 %shard_map.117 = (f32[6,16,64,128]{3,2,1,0:T(8,128)S(1)}, f32[200,128]{1,0:T(8,128)S(1)}, f32[200,128]{1,0:T(8,128)S(1)}, f32[216,128]{1,0:T(8,128)S(1)}, f32[208,128]{1,0:T(8,128)S(1)}) custom-call(s32[4]{0:T(128)S(1)} %pad_add_fusion.par, f32[3,16,64,128]{3,2,1,0:T(8,128)S(1)} %get-tuple-element.63.velocity.old, f32[9,16,64,128]{3,2,1,0:T(8,128)S(1)} %copy-done, ...), custom_call_target="tpu_custom_call" | custom-call | flops 52428800 | bytes 12902416 | tf_op jit(solution)/shard_map/pallas_call | solution.py:626
  48.2 5.3 %collective-permute-start.17 = (f32[208,128]{1,0:T(8,128)S(1)}, f32[208,128]{1,0:T(8,128)S(1)}, u32[]{:S(2)}, u32[]{:S(2)}) collective-permute-start(f32[208,128]{1,0:T(8,128)S(1)} %get-tuple-element.76), channel_id=1, source_target_pairs={{1,2},{2,1},{3,4},{4,3},{5,6},{6,5},{9,10},{10,9},{11,12},{12,11},... | collective-permute-start | bytes 319496 | tf_op jit(solution)/shard_map/ppermute | solution.py:652
  53.6 2.8 %collective-permute-start.14 = (f32[200,128]{1,0:T(8,128)S(1)}, f32[200,128]{1,0:T(8,128)S(1)}, u32[]{:S(2)}, u32[]{:S(2)}) collective-permute-start(f32[200,128]{1,0:T(8,128)S(1)} %get-tuple-element.73), channel_id=1, source_target_pairs={{0,8},{8,0},{16,24},{24,16},{1,9},{9,1},{17,25},{25,17},{2,10},{10... | collective-permute-start | bytes 307208 | tf_op jit(solution)/shard_map/ppermute | solution.py:652
  57.1 1.3 %collective-permute-done.13.later_other = f32[192,128]{1,0:T(8,128)S(1)} collective-permute-done((f32[192,128]{1,0:T(8,128)S(1)}, f32[192,128]{1,0:T(8,128)S(1)}, u32[]{:S(2)}, u32[]{:S(2)}) %collective-permute-start.13) | collective-permute-done | bytes 98336 | tf_op jit(solution)/shard_map/ppermute | solution.py:748
  58.4 1.0 %shard_map.118.ghost = f32[12,64,128]{2,1,0:T(8,128)S(1)} custom-call(s32[4]{0:T(128)S(1)} %pad_add_fusion.par, f32[232,128]{1,0:T(8,128)S(1)} %collective-permute-done.3.own, f32[232,128]{1,0:T(8,128)S(1)} %collective-permute-done.7.other, f32[24,128]{1,0:T(8,128)S(1)} %collective-permute-done.5.corner_1, f32[24,128]{1,0:T(8,128)S(1)} %collective-permute-done.6.corner_2, ...), custom_call_target="tpu_custom_call" | custom-call | bytes 852752 | tf_op jit(solution)/shard_map/pallas_call | solution.py:626
  59.5 4.1 %shard_map.119 = (f32[3,16,64,128]{3,2,1,0:T(8,128)S(1)}, f32[200,128]{1,0:T(8,128)S(1)}, f32[200,128]{1,0:T(8,128)S(1)}, f32[216,128]{1,0:T(8,128)S(1)}, f32[20...) custom-call(s32[4]{0:T(128)S(1)} %pad_add_fusion.par, f32[3,16,64,128]{3,2,1,0:T(8,128)S(1)} %get-tuple-element.63.velocity.old, ...), custom_call_target="tpu_custom_call" | custom-call | flops 52428800 | bytes 14835728 | tf_op jit(solution)/shard_map/pallas_call | solution.py:626
  63.9 3.1 %collective-permute-start.21 = (f32[208,128]{1,0:T(8,128)S(1)}, f32[208,128]{1,0:T(8,128)S(1)}, u32[]{:S(2)}, u32[]{:S(2)}) collective-permute-start(f32[208,128]{1,0:T(8,128)S(1)} %get-tuple-element.81), channel_id=1, source_target_pairs={{1,2},{2,1},{3,4},{4,3},{5,6},{6,5},{9,10},{10,9},{11,12},{12,11},... | collective-permute-start | bytes 319496 | tf_op jit(solution)/shard_map/ppermute | solution.py:652
  67.0 3.1 %collective-permute-start.18 = (f32[200,128]{1,0:T(8,128)S(1)}, f32[200,128]{1,0:T(8,128)S(1)}, u32[]{:S(2)}, u32[]{:S(2)}) collective-permute-start(f32[200,128]{1,0:T(8,128)S(1)} %get-tuple-element.78), channel_id=1, source_target_pairs={{0,8},{8,0},{16,24},{24,16},{1,9},{9,1},{17,25},{25,17},{2,10},{10... | collective-permute-start | bytes 307208 | tf_op jit(solution)/shard_map/ppermute | solution.py:652
  71.5 0.7 collective-permute-done.18.msg_a
  72.2 2.5 %shard_map.120 = (f32[6,8,64,128]{3,2,1,0:T(8,128)S(1)}, f32[176,128]{1,0:T(8,128)S(1)}) custom-call(s32[4]{0:T(128)S(1)} %pad_add_fusion.par, f32[3,16,64,128]{3,2,1,0:T(8,128)S(1)} %get-tuple-element.77.velocity, f32[6,16,64,128]{3,2,1,0:T(8,128)S(1)} %get-tuple-element.71.stress, f32[3,16,64,128]{3,2,1,0:T(8,128)S(1)} %copy-done.1, ...), custom_call_target="tpu_custom_call" | custom-call | bytes 1024 | tf_op jit(solution)/shard_map/pallas_call | solution.py:626
  74.7 0.8 collective-permute-start.22
  75.6 4.6 %shard_map.121 = (f32[9,16,64,128]{3,2,1,0:T(8,128)}, f32[8,128]{1,0:T(8,128)S(1)}) custom-call(s32[4]{0:T(128)S(1)} %pad_add_fusion.par, f32[6,8,64,128]{3,2,1,0:T(8,128)S(1)} %get-tuple-element.82.below, f32[3,16,64,128]{3,2,1,0:T(8,128)S(1)} %get-tuple-element.77.velocity, f32[6,16,64,128]{3,2,1,0:T(8,128)S(1)} %get-tuple-element.71.stress, ...), custom_call_target="tpu_custom_call" | custom-call | flops 26214400 | bytes 13664272 | tf_op jit(solution)/shard_map/pallas_call | solution.py:626
  80.7 0.8 collective-permute-done.24.other
  81.5 1.1 %shard_map.122 = (f32[3,8,16,128]{3,2,1,0:T(8,128)S(1)}, f32[96,128]{1,0:T(8,128)S(1)}, f32[96,128]{1,0:T(8,128)S(1)}, f32[24,128]{1,0:T(8,128)S(1)}) custom-call(s32[4]{0:T(128)S(1)} %pad_add_fusion.par, f32[9,8,16,128]{3,2,1,0:T(8,128)S(1)} %copy-done.3, f32[3,8,16,128]{3,2,1,0:T(8,128)S(1)} %copy-done.5, f32[176,128]{1,0:T(8,128)S(1)} %collective-permute-done.22.own, ...), custom_call_target="tpu_custom_call" | custom-call | bytes 2498576 | tf_op jit(solution)/shard_map/pallas_call | solution.py:626
  82.7 11.0 %collective-permute-start.29 = (f32[96,128]{1,0:T(8,128)S(1)}, f32[96,128]{1,0:T(8,128)S(1)}, u32[]{:S(2)}, u32[]{:S(2)}) collective-permute-start(f32[96,128]{1,0:T(8,128)S(1)} %get-tuple-element.93), channel_id=1, source_target_pairs={{1,2},{2,1},{3,4},{4,3},{5,6},{6,5},{9,10},{10,9},{11,12},{12,11},... | collective-permute-start | bytes 147464 | tf_op jit(solution)/shard_map/ppermute | solution.py:652
  94.4 3.7 %collective-permute-start.26 = (f32[24,128]{1,0:T(8,128)S(1)}, f32[24,128]{1,0:T(8,128)S(1)}, u32[]{:S(2)}, u32[]{:S(2)}) collective-permute-start(f32[24,128]{1,0:T(8,128)S(1)} %get-tuple-element.91), channel_id=1, source_target_pairs={{0,8},{8,0},{16,24},{24,16},{1,9},{9,1},{17,25},{25,17},{2,10},{10... | collective-permute-start | bytes 36872 | tf_op jit(solution)/shard_map/ppermute | solution.py:652
  98.1 1.1 %collective-permute-done.26.msg_a = f32[24,128]{1,0:T(8,128)S(1)} collective-permute-done((f32[24,128]{1,0:T(8,128)S(1)}, f32[24,128]{1,0:T(8,128)S(1)}, u32[]{:S(2)}, u32[]{:S(2)}) %collective-permute-start.26) | collective-permute-done | bytes 12320 | tf_op jit(solution)/shard_map/ppermute | solution.py:652
  99.2 1.8 %shard_map.123 = f32[9,8,16,128]{3,2,1,0:T(8,128)} custom-call(s32[4]{0:T(128)S(1)} %pad_add_fusion.par, f32[9,8,16,128]{3,2,1,0:T(8,128)S(1)} %copy-done.3, f32[3,8,16,128]{3,2,1,0:T(8,128)S(1)} %copy-done.5, f32[3,8,16,128]{3,2,1,0:T(8,128)S(1)} %get-tuple-element.89.velocity, f32[192,128]{1,0:T(8,128)S(1)} %collective-permute-done.23.own, ...), custom_call_target="tpu_custom_call" | custom-call | bytes 2547728 | tf_op jit(solution)/shard_map/pallas_call | solution.py:626
  (60 shorter events, 7.4 us)
Async XLA Ops:
  5.1 25.1 %copy-start.2 = (bf16[2,256,256]{2,1,0:T(8,128)(2,1)S(1)}, bf16[2,256,256]{2,1,0:T(8,128)(2,1)}, u32[]{:S(2)}) copy-start(bf16[2,256,256]{2,1,0:T(8,128)(2,1)} %constant.46.clone.tile) | copy-start | bytes 786436
  5.1 25.1 %copy-start.4 = (bf16[2,2,32,256]{3,2,1,0:T(8,128)(2,1)S(1)}, bf16[2,2,32,256]{3,2,1,0:T(8,128)(2,1)}, u32[]{:S(2)}) copy-start(bf16[2,2,32,256]{3,2,1,0:T(8,128)(2,1)} %constant.47.clone.halo) | copy-start | bytes 196612
  7.2 8.3 %collective-permute-start.2 = (f32[312,128]{1,0:T(8,128)S(1)}, f32[312,128]{1,0:T(8,128)S(1)}, u32[]{:S(2)}, u32[]{:S(2)}) collective-permute-start(f32[312,128]{1,0:T(8,128)S(1)} %get-tuple-element.51), channel_id=1, source_target_pairs={{1,2},{2,1},{3,4},{4,3},{5,6},{6,5},{9,10},{10,9},{11,12},{12,11},... | collective-permute-start | bytes 479240 | tf_op jit(solution)/shard_map/ppermute | solution.py:652
  11.7 3.8 %collective-permute-start = (f32[240,128]{1,0:T(8,128)S(1)}, f32[240,128]{1,0:T(8,128)S(1)}, u32[]{:S(2)}, u32[]{:S(2)}) collective-permute-start(f32[240,128]{1,0:T(8,128)S(1)} %get-tuple-element.49), channel_id=1, source_target_pairs={{0,8},{8,0},{16,24},{24,16},{1,9},{9,1},{17,25},{25,17},{2,10},{10... | collective-permute-start | bytes 368648 | tf_op jit(solution)/shard_map/ppermute | solution.py:652
  13.1 2.4 %collective-permute-start.1 = (f32[240,128]{1,0:T(8,128)S(1)}, f32[240,128]{1,0:T(8,128)S(1)}, u32[]{:S(2)}, u32[]{:S(2)}) collective-permute-start(f32[240,128]{1,0:T(8,128)S(1)} %get-tuple-element.50), channel_id=1, source_target_pairs={{8,16},{16,8},{9,17},{17,9},{10,18},{18,10},{11,19},{19,11},{12,20... | collective-permute-start | bytes 368648 | tf_op jit(solution)/shard_map/ppermute | solution.py:652
  13.7 16.4 %collective-permute-start.4 = (f32[312,128]{1,0:T(8,128)S(1)}, f32[312,128]{1,0:T(8,128)S(1)}, u32[]{:S(2)}, u32[]{:S(2)}) collective-permute-start(f32[312,128]{1,0:T(8,128)S(1)} %get-tuple-element.56), channel_id=1, source_target_pairs={{0,1},{1,0},{2,3},{3,2},{4,5},{5,4},{6,7},{7,6},{8,9},{9,8},{10,11... | collective-permute-start | bytes 479240 | tf_op jit(solution)/shard_map/ppermute | solution.py:652
  16.1 17.6 %collective-permute-start.3 = (f32[232,128]{1,0:T(8,128)S(1)}, f32[232,128]{1,0:T(8,128)S(1)}, u32[]{:S(2)}, u32[]{:S(2)}) collective-permute-start(f32[232,128]{1,0:T(8,128)S(1)} %get-tuple-element.55), channel_id=1, source_target_pairs={{0,0},{1,1},{2,8},{3,9},{4,16},{5,17},{6,24},{7,25},{8,2},{9,3},{1... | collective-permute-start | bytes 356360 | tf_op jit(solution)/shard_map/ppermute | solution.py:707
  16.8 16.9 %collective-permute-start.6 = (f32[24,128]{1,0:T(8,128)S(1)}, f32[24,128]{1,0:T(8,128)S(1)}, u32[]{:S(2)}, u32[]{:S(2)}) collective-permute-start(f32[24,128]{1,0:T(8,128)S(1)} %get-tuple-element.57), channel_id=1, source_target_pairs={{2,2},{4,10},{6,18},{9,9},{10,4},{11,17},{12,12},{13,25},{14,20},{... | collective-permute-start | bytes 36872 | tf_op jit(solution)/shard_map/ppermute | solution.py:709
  17.5 16.2 %collective-permute-start.5 = (f32[24,128]{1,0:T(8,128)S(1)}, f32[24,128]{1,0:T(8,128)S(1)}, u32[]{:S(2)}, u32[]{:S(2)}) collective-permute-start(f32[24,128]{1,0:T(8,128)S(1)} %get-tuple-element.57), channel_id=1, source_target_pairs={{1,10},{3,18},{5,26},{9,12},{10,1},{11,20},{12,9},{13,28},{14,17},... | collective-permute-start | bytes 36872 | tf_op jit(solution)/shard_map/ppermute | solution.py:708
  33.7 1.4 %collective-permute-start.7 = (f32[232,128]{1,0:T(8,128)S(1)}, f32[232,128]{1,0:T(8,128)S(1)}, u32[]{:S(2)}, u32[]{:S(2)}) collective-permute-start(f32[232,128]{1,0:T(8,128)S(1)} %collective-permute-done.3.own), channel_id=1, source_target_pairs={{0,1},{1,0},{2,3},{3,2},{4,5},{5,4},{6,7},{7,6},{8,9},{9,8},{10,11... | collective-permute-start | bytes 356360 | tf_op jit(solution)/shard_map/ppermute | solution.py:728
  36.5 7.4 %collective-permute-start.11 = (f32[216,128]{1,0:T(8,128)S(1)}, f32[216,128]{1,0:T(8,128)S(1)}, u32[]{:S(2)}, u32[]{:S(2)}) collective-permute-start(f32[216,128]{1,0:T(8,128)S(1)} %get-tuple-element.68), channel_id=1, source_target_pairs={{0,1},{1,0},{2,3},{3,2},{4,5},{5,4},{6,7},{7,6},{8,9},{9,8},{10,11... | collective-permute-start | bytes 331784 | tf_op jit(solution)/shard_map/ppermute | solution.py:652
  36.7 7.3 %collective-permute-start.12 = (f32[208,128]{1,0:T(8,128)S(1)}, f32[208,128]{1,0:T(8,128)S(1)}, u32[]{:S(2)}, u32[]{:S(2)}) collective-permute-start(f32[208,128]{1,0:T(8,128)S(1)} %get-tuple-element.69), channel_id=1, source_target_pairs={{1,2},{2,1},{3,4},{4,3},{5,6},{6,5},{9,10},{10,9},{11,12},{12,11},... | collective-permute-start | bytes 319496 | tf_op jit(solution)/shard_map/ppermute | solution.py:652
  40.4 3.6 %collective-permute-start.9 = (f32[200,128]{1,0:T(8,128)S(1)}, f32[200,128]{1,0:T(8,128)S(1)}, u32[]{:S(2)}, u32[]{:S(2)}) collective-permute-start(f32[200,128]{1,0:T(8,128)S(1)} %get-tuple-element.66), channel_id=1, source_target_pairs={{0,8},{8,0},{16,24},{24,16},{1,9},{9,1},{17,25},{25,17},{2,10},{10... | collective-permute-start | bytes 307208 | tf_op jit(solution)/shard_map/ppermute | solution.py:652
  40.5 3.5 %collective-permute-start.10 = (f32[200,128]{1,0:T(8,128)S(1)}, f32[200,128]{1,0:T(8,128)S(1)}, u32[]{:S(2)}, u32[]{:S(2)}) collective-permute-start(f32[200,128]{1,0:T(8,128)S(1)} %get-tuple-element.67), channel_id=1, source_target_pairs={{8,16},{16,8},{9,17},{17,9},{10,18},{18,10},{11,19},{19,11},{12,20... | collective-permute-start | bytes 307208 | tf_op jit(solution)/shard_map/ppermute | solution.py:652
  41.1 15.9 %collective-permute-start.8 = (f32[192,128]{1,0:T(8,128)S(1)}, f32[192,128]{1,0:T(8,128)S(1)}, u32[]{:S(2)}, u32[]{:S(2)}) collective-permute-start(f32[192,128]{1,0:T(8,128)S(1)} %get-tuple-element.64), channel_id=1, source_target_pairs={{0,0},{1,1},{2,8},{3,9},{4,16},{5,17},{6,24},{7,25},{8,2},{9,3},{1... | collective-permute-start | bytes 294920 | tf_op jit(solution)/shard_map/ppermute | solution.py:738
  48.2 11.3 %collective-permute-start.16 = (f32[216,128]{1,0:T(8,128)S(1)}, f32[216,128]{1,0:T(8,128)S(1)}, u32[]{:S(2)}, u32[]{:S(2)}) collective-permute-start(f32[216,128]{1,0:T(8,128)S(1)} %get-tuple-element.75), channel_id=1, source_target_pairs={{0,1},{1,0},{2,3},{3,2},{4,5},{5,4},{6,7},{7,6},{8,9},{9,8},{10,11... | collective-permute-start | bytes 331784 | tf_op jit(solution)/shard_map/ppermute | solution.py:652
  48.2 11.2 %collective-permute-start.17 = (f32[208,128]{1,0:T(8,128)S(1)}, f32[208,128]{1,0:T(8,128)S(1)}, u32[]{:S(2)}, u32[]{:S(2)}) collective-permute-start(f32[208,128]{1,0:T(8,128)S(1)} %get-tuple-element.76), channel_id=1, source_target_pairs={{1,2},{2,1},{3,4},{4,3},{5,6},{6,5},{9,10},{10,9},{11,12},{12,11},... | collective-permute-start | bytes 319496 | tf_op jit(solution)/shard_map/ppermute | solution.py:652
  53.6 5.9 %collective-permute-start.14 = (f32[200,128]{1,0:T(8,128)S(1)}, f32[200,128]{1,0:T(8,128)S(1)}, u32[]{:S(2)}, u32[]{:S(2)}) collective-permute-start(f32[200,128]{1,0:T(8,128)S(1)} %get-tuple-element.73), channel_id=1, source_target_pairs={{0,8},{8,0},{16,24},{24,16},{1,9},{9,1},{17,25},{25,17},{2,10},{10... | collective-permute-start | bytes 307208 | tf_op jit(solution)/shard_map/ppermute | solution.py:652
  56.4 3.1 %collective-permute-start.15 = (f32[200,128]{1,0:T(8,128)S(1)}, f32[200,128]{1,0:T(8,128)S(1)}, u32[]{:S(2)}, u32[]{:S(2)}) collective-permute-start(f32[200,128]{1,0:T(8,128)S(1)} %get-tuple-element.74), channel_id=1, source_target_pairs={{8,16},{16,8},{9,17},{17,9},{10,18},{18,10},{11,19},{19,11},{12,20... | collective-permute-start | bytes 307208 | tf_op jit(solution)/shard_map/ppermute | solution.py:652
  57.1 1.4 %collective-permute-start.13 = (f32[192,128]{1,0:T(8,128)S(1)}, f32[192,128]{1,0:T(8,128)S(1)}, u32[]{:S(2)}, u32[]{:S(2)}) collective-permute-start(f32[192,128]{1,0:T(8,128)S(1)} %collective-permute-done.8.later_own), channel_id=1, source_target_pairs={{0,1},{1,0},{2,3},{3,2},{4,5},{5,4},{6,7},{7,6},{8,9},{9,8},{10,11... | collective-permute-start | bytes 294920 | tf_op jit(solution)/shard_map/ppermute | solution.py:748
  63.7 8.5 %collective-permute-start.20 = (f32[216,128]{1,0:T(8,128)S(1)}, f32[216,128]{1,0:T(8,128)S(1)}, u32[]{:S(2)}, u32[]{:S(2)}) collective-permute-start(f32[216,128]{1,0:T(8,128)S(1)} %get-tuple-element.80), channel_id=1, source_target_pairs={{0,1},{1,0},{2,3},{3,2},{4,5},{5,4},{6,7},{7,6},{8,9},{9,8},{10,11... | collective-permute-start | bytes 331784 | tf_op jit(solution)/shard_map/ppermute | solution.py:652
  63.9 8.3 %collective-permute-start.21 = (f32[208,128]{1,0:T(8,128)S(1)}, f32[208,128]{1,0:T(8,128)S(1)}, u32[]{:S(2)}, u32[]{:S(2)}) collective-permute-start(f32[208,128]{1,0:T(8,128)S(1)} %get-tuple-element.81), channel_id=1, source_target_pairs={{1,2},{2,1},{3,4},{4,3},{5,6},{6,5},{9,10},{10,9},{11,12},{12,11},... | collective-permute-start | bytes 319496 | tf_op jit(solution)/shard_map/ppermute | solution.py:652
  67.0 5.2 %collective-permute-start.18 = (f32[200,128]{1,0:T(8,128)S(1)}, f32[200,128]{1,0:T(8,128)S(1)}, u32[]{:S(2)}, u32[]{:S(2)}) collective-permute-start(f32[200,128]{1,0:T(8,128)S(1)} %get-tuple-element.78), channel_id=1, source_target_pairs={{0,8},{8,0},{16,24},{24,16},{1,9},{9,1},{17,25},{25,17},{2,10},{10... | collective-permute-start | bytes 307208 | tf_op jit(solution)/shard_map/ppermute | solution.py:652
  70.2 2.1 %collective-permute-start.19 = (f32[200,128]{1,0:T(8,128)S(1)}, f32[200,128]{1,0:T(8,128)S(1)}, u32[]{:S(2)}, u32[]{:S(2)}) collective-permute-start(f32[200,128]{1,0:T(8,128)S(1)} %get-tuple-element.79), channel_id=1, source_target_pairs={{8,16},{16,8},{9,17},{17,9},{10,18},{18,10},{11,19},{19,11},{12,20... | collective-permute-start | bytes 307208 | tf_op jit(solution)/shard_map/ppermute | solution.py:652
  70.8 9.3 %collective-permute-start.23 = (f32[192,128]{1,0:T(8,128)S(1)}, f32[192,128]{1,0:T(8,128)S(1)}, u32[]{:S(2)}, u32[]{:S(2)}) collective-permute-start(f32[192,128]{1,0:T(8,128)S(1)} %get-tuple-element.86), channel_id=1, source_target_pairs={{0,0},{1,1},{2,8},{3,9},{4,16},{5,17},{6,24},{7,25},{8,2},{9,3},{1... | collective-permute-start | bytes 294920 | tf_op jit(solution)/shard_map/ppermute | solution.py:764
  74.7 5.4 %collective-permute-start.22 = (f32[176,128]{1,0:T(8,128)S(1)}, f32[176,128]{1,0:T(8,128)S(1)}, u32[]{:S(2)}, u32[]{:S(2)}) collective-permute-start(f32[176,128]{1,0:T(8,128)S(1)} %get-tuple-element.84), channel_id=1, source_target_pairs={{0,0},{1,1},{2,8},{3,9},{4,16},{5,17},{6,24},{7,25},{8,2},{9,3},{1... | collective-permute-start | bytes 270344 | tf_op jit(solution)/shard_map/ppermute | solution.py:772
  80.2 1.3 %collective-permute-start.24 = (f32[176,128]{1,0:T(8,128)S(1)}, f32[176,128]{1,0:T(8,128)S(1)}, u32[]{:S(2)}, u32[]{:S(2)}) collective-permute-start(f32[176,128]{1,0:T(8,128)S(1)} %collective-permute-done.22.own), channel_id=1, source_target_pairs={{0,1},{1,0},{2,3},{3,2},{4,5},{5,4},{6,7},{7,6},{8,9},{9,8},{10,11... | collective-permute-start | bytes 270344 | tf_op jit(solution)/shard_map/ppermute | solution.py:781
  80.2 17.9 %collective-permute-start.25 = (f32[192,128]{1,0:T(8,128)S(1)}, f32[192,128]{1,0:T(8,128)S(1)}, u32[]{:S(2)}, u32[]{:S(2)}) collective-permute-start(f32[192,128]{1,0:T(8,128)S(1)} %collective-permute-done.23.own), channel_id=1, source_target_pairs={{0,1},{1,0},{2,3},{3,2},{4,5},{5,4},{6,7},{7,6},{8,9},{9,8},{10,11... | collective-permute-start | bytes 294920 | tf_op jit(solution)/shard_map/ppermute | solution.py:782
  82.5 16.6 %collective-permute-start.28 = (f32[96,128]{1,0:T(8,128)S(1)}, f32[96,128]{1,0:T(8,128)S(1)}, u32[]{:S(2)}, u32[]{:S(2)}) collective-permute-start(f32[96,128]{1,0:T(8,128)S(1)} %get-tuple-element.92), channel_id=1, source_target_pairs={{0,1},{1,0},{2,3},{3,2},{4,5},{5,4},{6,7},{7,6},{8,9},{9,8},{10,11... | collective-permute-start | bytes 147464 | tf_op jit(solution)/shard_map/ppermute | solution.py:652
  82.7 16.5 %collective-permute-start.29 = (f32[96,128]{1,0:T(8,128)S(1)}, f32[96,128]{1,0:T(8,128)S(1)}, u32[]{:S(2)}, u32[]{:S(2)}) collective-permute-start(f32[96,128]{1,0:T(8,128)S(1)} %get-tuple-element.93), channel_id=1, source_target_pairs={{1,2},{2,1},{3,4},{4,3},{5,6},{6,5},{9,10},{10,9},{11,12},{12,11},... | collective-permute-start | bytes 147464 | tf_op jit(solution)/shard_map/ppermute | solution.py:652
  93.7 4.4 %collective-permute-start.27 = (f32[24,128]{1,0:T(8,128)S(1)}, f32[24,128]{1,0:T(8,128)S(1)}, u32[]{:S(2)}, u32[]{:S(2)}) collective-permute-start(f32[24,128]{1,0:T(8,128)S(1)} %get-tuple-element.91), channel_id=1, source_target_pairs={{8,16},{16,8},{9,17},{17,9},{10,18},{18,10},{11,19},{19,11},{12,20... | collective-permute-start | bytes 36872 | tf_op jit(solution)/shard_map/ppermute | solution.py:652
  94.4 4.8 %collective-permute-start.26 = (f32[24,128]{1,0:T(8,128)S(1)}, f32[24,128]{1,0:T(8,128)S(1)}, u32[]{:S(2)}, u32[]{:S(2)}) collective-permute-start(f32[24,128]{1,0:T(8,128)S(1)} %get-tuple-element.91), channel_id=1, source_target_pairs={{0,8},{8,0},{16,24},{24,16},{1,9},{9,1},{17,25},{25,17},{2,10},{10... | collective-permute-start | bytes 36872 | tf_op jit(solution)/shard_map/ppermute | solution.py:652
  (8 other events, 88.8 us)

commit v5 on v4

--- a/solution.py
+++ b/solution.py
@@ -249,9 +249,15 @@
     return jnp.zeros(ref.shape[-2:], F32)
 
 
+def after_before(msg_a, msg_b, at, parity):
+    even = parity == 0
+    a, b = msg_a[at, :], msg_b[at, :]
+    return jnp.where(even, a, b), jnp.where(even, b, a)
+
+
 def pack_kernel(
-    par, fine, coarse, past, out_a, out_b, out_1, out_2, planes, outer,
-    turned, first, last, state, before, sems,
+    par, fine, coarse, past, medium, out_a, out_b, out_1, out_2, planes, outer,
+    turned, first, last, state, before, light, sems,
 ):
     pi, pj = par[0], par[1]
     depth, rows = fine.shape[1], fine.shape[2]
@@ -259,17 +265,18 @@
     copies = [
         pltpu.make_async_copy(coarse, state, sems.at[0]),
         pltpu.make_async_copy(past, before, sems.at[1]),
+        pltpu.make_async_copy(medium.at[0:1, depth - 4 :], light, sems.at[2]),
     ]
     for k, (f, _) in enumerate(VEL_X):
         head, tail = fine.at[f, :, 0:8, :], fine.at[f, :, rows - 8 : rows, :]
-        copies.append(pltpu.make_async_copy(head, first.at[k], sems.at[2 + 2 * k]))
-        copies.append(pltpu.make_async_copy(tail, last.at[k], sems.at[3 + 2 * k]))
+        copies.append(pltpu.make_async_copy(head, first.at[k], sems.at[3 + 2 * k]))
+        copies.append(pltpu.make_async_copy(tail, last.at[k], sems.at[4 + 2 * k]))
     for k, (f, _) in enumerate(VEL_Y):
-        copies.append(pltpu.make_async_copy(fine.at[f], turned.at[k], sems.at[8 + k]))
+        copies.append(pltpu.make_async_copy(fine.at[f], turned.at[k], sems.at[9 + k]))
     for copy in copies:
         copy.start()
-    copies[0].wait()
-    copies[1].wait()
+    for copy in copies[:3]:
+        copy.wait()
     upper = pj == 0
     for n, f in enumerate(CROSSING):
         for layer in range(2):
@@ -280,17 +287,19 @@
                 outer[p : p + 1, :] = jnp.where(upper, plane[:1], plane[part - 1 :])
     base = 12 * depth
     put_columns((out_a, out_b), base, [(state, f) for f, _ in VEL_Y])
-    put_columns((out_a, out_b), base + 24, [(planes, None)])
+    put_rows(out_a, out_b, base + 24, [(light, 0)], pi)
+    put_columns((out_a, out_b), base + 40, [(planes, None)])
     base = 24 * (depth * rows // LANES)
     put_rows(out_1, out_2, base, [(state, f) for f, _ in VEL_X], pj)
     base += 12 * coarse.shape[1]
-    out_1[base : base + 24, :] = outer[...]
-    out_2[base : base + 24, :] = outer[...]
-    for copy in copies[2:8]:
+    put_columns((out_1, out_2), base, [(light, 0)])
+    out_1[base + 16 : base + 40, :] = outer[...]
+    out_2[base + 16 : base + 40, :] = outer[...]
+    for copy in copies[3:9]:
         copy.wait()
     put_edge_rows(out_a, out_b, 0, [(first, last, k) for k in range(3)], pi)
     for k in range(3):
-        copies[8 + k].wait()
+        copies[9 + k].wait()
         base = 8 * k * (depth * rows // LANES)
         put_columns((out_1, out_2), base, [(turned, k)])
 
@@ -316,7 +325,9 @@
     second[...] = planes[half:, :]
 
 
-def expand_ghosts(par, own, other, corner_1, corner_2, prow, pcol, ghost, level, planes):
+def expand_ghosts(
+    par, own, other, prow, pcol, ghost, level, planes, ends=None, known=None
+):
     core = par[1]
     row_base, col_base = par[2], par[3]
     part = (own.shape[0] - 40) // 12
@@ -346,17 +357,27 @@
         beside.append(side.T)
     side_1 = jnp.where(low, beside[0], beside[1])
     side_2 = jnp.where(low, beside[1], beside[0])
-    turn = jnp.where(low, 1, LANES - 1)
-    top = pltpu.roll(jnp.where(low, corner_1[...], corner_2[...]), turn, 1)
-    bottom = pltpu.roll(jnp.where(low, corner_2[...], corner_1[...]), turn, 1)
-
     lane = lax.broadcasted_iota(jnp.int32, (rows, LANES), 1)
     row = lax.broadcasted_iota(jnp.int32, (rows, LANES), 0)
     edge = lane == jnp.where(low, 0, LANES - 1)
     edge_row = edge[:1]
-    above = above + jnp.where(edge_row, top, 0.0)
-    below = below + jnp.where(edge_row, bottom, 0.0)
+    if ends is not None:
+        above = above + jnp.where(edge_row, ends[0], 0.0)
+        below = below + jnp.where(edge_row, ends[1], 0.0)
     group = LANES // part
+    if known is not None:
+        own_row, other_row = own[count : count + 24, :], other[count : count + 24, :]
+        for base, x in (
+            (48, jnp.where(low, own_row, other_row)), (72, jnp.where(low, other_row, own_row))
+        ):
+            x = jnp.where(low, x[:, :1], x[:, LANES - 1 :])
+            known[base : base + 24, :] = jnp.broadcast_to(x, (24, LANES))
+        for p in range(24):
+            q, t = p % group, p // group
+            last = side_2[(q + 1) * part - 1 : (q + 1) * part, t : t + 1]
+            first_row = side_1[q * part : q * part + 1, t : t + 1]
+            known[p : p + 1, :] = jnp.broadcast_to(last, (1, LANES))
+            known[24 + p : 25 + p, :] = jnp.broadcast_to(first_row, (1, LANES))
     columns = []
     for q in range(group):
         at = slice(q * part, (q + 1) * part)
@@ -373,38 +394,119 @@
         ghost[n] = full + jnp.where(row == rows - 1, below[p : p + 1], 0.0)
 
 
+def ends_of(par, msg_a, msg_b):
+    base = msg_a.shape[0] - 24
+    below, above = after_before(msg_a, msg_b, slice(base, base + 24), par[0])
+    return above, below
+
+
 def later_ghost_kernel(
-    par, own, other, corner_1, corner_2, prow, pcol, later_own, later_other, ghost
+    par, own, other, prow, pcol, later_own, later_other, msg_a, msg_b, ghost
 ):
     planes = later_own, later_other
-    expand_ghosts(par, own, other, corner_1, corner_2, prow, pcol, ghost, 1, planes)
+    ends = ends_of(par, msg_a, msg_b)
+    expand_ghosts(par, own, other, prow, pcol, ghost, 1, planes, ends=ends)
+
+
+def ghost_rate(planes, z, depth, forward):
+    total = None
+    for tap, coeff in enumerate(COEFFS, 1):
+        g = z + (tap if forward else tap - 1) - depth
+        if g >= 0:
+            term = coeff * planes[g // 2]
+            total = term if total is None else total + term
+    return total
 
 
 def ghost_kernel(
-    par, half, buoyancy, own, other, corner_1, corner_2, prow, pcol,
-    out, ghost, out_a, out_b, out_1, out_2,
+    par, half, buoyancy, own, other, prow, pcol,
+    out, ghost, known, out_a, out_b, out_1, out_2,
 ):
     planes = own, other
-    expand_ghosts(par, own, other, corner_1, corner_2, prow, pcol, ghost, 0, planes)
+    expand_ghosts(par, own, other, prow, pcol, ghost, 0, planes, known=known)
     depth = half.shape[1]
     for c, (f, forward) in enumerate(VEL_Z):
         out[c, 0 : depth - 4] = half[c, 0 : depth - 4]
         n = CROSSING.index(f)
         planes = [ghost[2 * n], ghost[2 * n + 1]]
         for z in range(depth - 4, depth):
-            total = None
-            for tap, coeff in enumerate(COEFFS, 1):
-                g = z + (tap if forward else tap - 1) - depth
-                if g >= 0:
-                    term = coeff * planes[g // 2]
-                    total = term if total is None else total + term
             value = half[c, z]
-            if total is not None:
-                value = value + (STEP * buoyancy[0, z]) * total
+            rate = ghost_rate(planes, z, depth, forward)
+            if rate is not None:
+                value = value + (STEP * buoyancy[0, z]) * rate
             out[c, z] = value
     moved = [(out, c) for c in range(3)]
     put_rows(out_a, out_b, 0, moved, par[0])
     put_columns((out_1, out_2), 0, moved)
+    even = par[0] == 0
+    up, down = known[0:24, :], known[24:48, :]
+    base = 12 * depth
+    out_a[base:, :] = jnp.where(even, up, down)
+    out_b[base:, :] = jnp.where(even, down, up)
+
+
+def add_corners(
+    par, half, buoyancy, half_ghost, known, begin_a, begin_b, begin_2, msg_a, msg_b, msg_2,
+    velocity, ghost, rows_a, rows_b, cols_2, base_x, base_y,
+):
+    pi, low = par[0], par[1] == 0
+    depth, rows = half.shape[1], half.shape[2]
+    lane = lax.broadcasted_iota(jnp.int32, (rows, LANES), 1)
+    row = lax.broadcasted_iota(jnp.int32, (rows, LANES), 0)
+    edge = lane == jnp.where(low, 0, LANES - 1)
+    first, last = edge & (row == 0), edge & (row == rows - 1)
+    above, below = ends_of(par, msg_a, msg_b)
+    for n in range(12):
+        plane = half_ghost[n] + jnp.where(first, above[n : n + 1], 0.0)
+        ghost[n] = plane + jnp.where(last, below[n : n + 1], 0.0)
+    for source, target in ((msg_a, rows_a), (msg_b, rows_b), (msg_2, cols_2)):
+        target[...] = source[...]
+    even = pi == 0
+    near = lax.broadcasted_iota(jnp.int32, (8, LANES), 0)
+    lane = lax.broadcasted_iota(jnp.int32, (8, LANES), 1)
+    edge = lane == jnp.where(low, 0, LANES - 1)
+    beside = near == jnp.where(low, 7, 0)
+    blocks = depth * rows // LANES
+    none = jnp.zeros((1, LANES), F32)
+
+    def rates(x, n, z, forward):
+        found = []
+        for odd in range(2):
+            rate = ghost_rate([x[2 * n : 2 * n + 1], x[2 * n + 1 : 2 * n + 2]], z + odd, depth, forward)
+            found.append(none if rate is None else rate)
+        return found
+
+    up, down = known[0:12, :], known[24:36, :]
+    row_above, row_below = known[48:60, :], known[72:84, :]
+    for c, (f, forward) in enumerate(VEL_Z):
+        n = CROSSING.index(f)
+        velocity[c, 0 : depth - 4] = half[c, 0 : depth - 4]
+        for pair in range(2):
+            z = depth - 4 + 2 * pair
+            tops, bottoms = rates(above, n, z, forward), rates(below, n, z, forward)
+            for odd in range(2):
+                change = jnp.where(first, tops[odd], 0.0) + jnp.where(last, bottoms[odd], 0.0)
+                scale = STEP * buoyancy[0, z + odd]
+                velocity[c, z + odd] = half[c, z + odd] + scale * change
+            after, before = after_before(
+                begin_a, begin_b, slice(base_x + 8 * pair, base_x + 8 * pair + 8), pi
+            )
+            rate = rates(up, n, z, forward)
+            change = jnp.where(near == 0, rate[0], jnp.where(near == 4, rate[1], 0.0))
+            after = jnp.where(edge, (STEP * after) * change, 0.0)
+            rate = rates(down, n, z, forward)
+            change = jnp.where(near == 3, rate[0], jnp.where(near == 7, rate[1], 0.0))
+            before = jnp.where(edge, (STEP * before) * change, 0.0)
+            at = pl.ds(4 * (c * depth + z), 8)
+            rows_a[at, :] = rows_a[at, :] + jnp.where(even, after, before)
+            rows_b[at, :] = rows_b[at, :] + jnp.where(even, before, after)
+            tops, bottoms = rates(row_above, n, z, forward), rates(row_below, n, z, forward)
+            change = jnp.where(lane == 0, tops[0], jnp.where(lane == rows - 1, bottoms[0], 0.0))
+            change = jnp.where(lane == rows, tops[1], change)
+            change = jnp.where(lane == 2 * rows - 1, bottoms[1], change)
+            light = begin_2[base_y + 8 * pair : base_y + 8 * pair + 8, :]
+            at = pl.ds(8 * (c * blocks + blocks - 2 + pair), 8)
+            cols_2[at, :] = cols_2[at, :] + jnp.where(beside, (STEP * light) * change, 0.0)
 
 
 def stress_fields(ref, table):
@@ -463,12 +565,17 @@
 
 
 def stress_kernel(
-    par, velocity, state, medium, ghost, msg_a, msg_b, msg_1, msg_2, tile, halo,
-    out, out_a, out_b, out_1, out_2, ex, ey, ez,
-):
-    depth = velocity.shape[1]
+    par, half, state, medium, half_ghost, known, begin_a, begin_b, begin_2, msg_a, msg_b, msg_1,
+    msg_2, tile, halo, out, velocity, out_a, out_b, out_1, out_2, ex, ey, ez, ghost, rows_a, rows_b,
+    cols_2, *, base_x, base_y,
+):
+    depth = half.shape[1]
+    add_corners(
+        par, half, medium, half_ghost, known, begin_a, begin_b, begin_2, msg_a, msg_b, msg_2,
+        velocity, ghost, rows_a, rows_b, cols_2, base_x, base_y,
+    )
     stress_fill(
-        par, velocity, lambda k, g: ghost[2 * k + g // 2], msg_a, msg_b, msg_1, msg_2,
+        par, velocity, lambda k, g: ghost[2 * k + g // 2], rows_a, rows_b, msg_1, cols_2,
         tile, halo, ex, ey, ez, 0, depth,
     )
 
@@ -630,8 +737,8 @@
         out_specs=[whole(o) for o in outs],
         out_shape=[jax.ShapeDtypeStruct(o, F32) for o in outs],
         scratch_shapes=[pltpu.VMEM(s, F32) for s in scratch]
-        + ([pltpu.SemaphoreType.DMA((11,))] if copied else []),
-        compiler_params=pltpu.CompilerParams(vmem_limit_bytes=(46 if copied else 24) * 1024 * 1024),
+        + ([pltpu.SemaphoreType.DMA((12,))] if copied else []),
+        compiler_params=pltpu.CompilerParams(vmem_limit_bytes=(54 if copied else 24) * 1024 * 1024),
         cost_estimate=pl.CostEstimate(flops=flops, bytes_accessed=size, transcendentals=0),
     )(*args)
 
@@ -670,16 +777,6 @@
     ]
     partner = matchings("gy")[0]
 
-    corners = ([], [])
-    for a in range(size_x):
-        for b in range(size_y):
-            above = b % 2 == 1
-            chip = b // 2 + 1 if above else b // 2 - 1
-            for n in range(2):
-                left = above if n == 0 else not above
-                near = a + 1 if left else a - 1
-                if 0 <= chip < size_x and 0 <= near < size_x:
-                    corners[n].append((a * size_y + b, chip * size_y + 2 * near + (0 if left else 1)))
     both = ("gx", "gy")
 
     rows_msg, cols_msg = 12 * depth, 24 * blocks
@@ -687,13 +784,13 @@
     count = 24 * part
     out_a, out_b, out_1, out_2, planes, outer = call(
         pack_kernel,
-        [par, fine_state, coarse_state, coarse_past],
-        [(rows_msg + coarse_cols + count * 8 // LANES, LANES)] * 2
-        + [(cols_msg + coarse_rows + 24, LANES)] * 2
+        [par, fine_state, coarse_state, coarse_past, fine_medium],
+        [(rows_msg + coarse_cols + 16 + count * 8 // LANES, LANES)] * 2
+        + [(cols_msg + coarse_rows + 40, LANES)] * 2
         + [(count, LANES), (24, LANES)],
         [(3,) + fine_state.shape[1:], (3, depth, 8, cols), (3, depth, 8, cols),
-         coarse_state.shape, coarse_past.shape],
-        copied=3,
+         coarse_state.shape, coarse_past.shape, (1, 4, rows, cols)],
+        copied=4,
     )
     msg_a, msg_b = exchange("gx", out_a, out_b)
     msg_1, msg_2 = exchange("gy", out_1, out_2)
@@ -703,10 +800,7 @@
         [par, planes, msg_a, msg_b, msg_2],
         [(count // 2 + 40, LANES), (count // 2, LANES)],
     )
-    crossing, outer = lax.optimization_barrier((crossing, outer))
     own = lax.ppermute(crossing, both, across)
-    corner_1 = lax.ppermute(outer, both, corners[0])
-    corner_2 = lax.ppermute(outer, both, corners[1])
 
     shape = (depth, rows, cols)
 
@@ -724,23 +818,28 @@
         scratch_of(depth, rows),
         flops=400 * cells,
     )
-    own, half, corner_1, corner_2 = lax.optimization_barrier((own, half, corner_1, corner_2))
+    own, half = lax.optimization_barrier((own, half))
     other = lax.ppermute(own, "gy", partner)
     parents = parent_rows.reshape(1, rows), parent_cols.reshape(1, cols)
-    velocity, ghost, out_a, out_b, out_1, out_2 = call(
+    half, half_ghost, known, out_a, out_b, out_1, out_2 = call(
         ghost_kernel,
-        [par, half, fine_medium, own, other, corner_1, corner_2,
-         *parents],
-        [(3,) + shape, (12, rows, cols)] + halves,
+        [par, half, fine_medium, own, other, *parents],
+        [(3,) + shape, (12, rows, cols), (96, LANES)] + [(rows_msg + 24, LANES)] * 2
+        + [(cols_msg + 40, LANES), (cols_msg + 32, LANES)],
     )
     msgs = exchange("gx", out_a, out_b) + exchange("gy", out_1, out_2)
-    later, velocity = lax.optimization_barrier((later, velocity))
+    later, half = lax.optimization_barrier((later, half))
     later = lax.ppermute(later, both, across)
-    stress, out_a, out_b, out_1, out_2 = call(
-        stress_kernel,
-        [par, velocity, fine_state, fine_medium, ghost, *msgs, tile, halo],
-        [(6,) + shape] + halves,
-        scratch_of(depth, rows),
+    ends = msgs[:2]
+    stress, velocity, out_a, out_b, out_1, out_2 = call(
+        functools.partial(
+            stress_kernel, base_x=rows_msg + coarse_cols, base_y=cols_msg + coarse_rows
+        ),
+        [par, half, fine_state, fine_medium, half_ghost, known, begin[0], begin[1], begin[3],
+         *msgs, tile, halo],
+        [(6,) + shape, (3,) + shape] + halves,
+        scratch_of(depth, rows)
+        + [(12, rows, cols)] + [(rows_msg + 24, LANES)] * 2 + [(cols_msg + 32, LANES)],
         flops=400 * cells,
     )
     msgs = exchange("gx", out_a, out_b) + exchange("gy", out_1, out_2)
@@ -748,7 +847,7 @@
     later_other = lax.ppermute(later, "gy", partner)
     (ghost,) = call(
         later_ghost_kernel,
-        [par, own, other, corner_1, corner_2, *parents, later, later_other],
+        [par, own, other, *parents, later, later_other, *ends],
         [(12, rows, cols)],
     )
     moved_v, moved_s = (len(above_planes(t)) * part for t in (STR_Z, VEL_Z))

time: 102 us -> 99.5 us (0.975)
  local copies, waits for them, and re-layouts: 4.35 us -> 0.98 us
  starting transfers between devices: 59.5 us -> 58.2 us
    ppermute x2 -> x0, starting transfers between devices: 13.3 us -> none  [the longest x1 12.7 us: body(): corner_1 = lax.ppermute(outer, both, corners[0])]
    ppermute x20, starting transfers between devices: 42.6 us -> 54.7 us  [exchange(): return (lax.ppermute(first, axis, one), lax.ppermute(second, axis, two))]
    unnamed x20 -> x22, local copies, waits for them, and re-layouts: 4.35 us -> 0.98 us
  transfers between devices with their start and end apart: 30 -> 28, of which waited for: 7 -> 8; matrix products, arithmetic and copies ran while one was open for 0% -> 0% of each run, Pallas kernels for 17% -> 17%
where the time goes in v5:
time: 99.5 us; the launch traced here: 98.3 us
  starting transfers between devices  58.2 us (58%)
  Pallas kernels  28 us (28%)
  waiting for transfers between devices  9.51 us (10%)
  between operations  1.02 us (1%)
    ppermute x20, starting transfers between devices, exchange(): return (lax.ppermute(first, axis, one), lax.ppermute(second, axis, two))  54.7 us
    pallas_call x11, Pallas kernels, call(): pl.pallas_call(kernel, grid=(1,), in_specs=specs, out_specs=[whole(o) for...  28 us
    ppermute x20, waiting for transfers between devices, exchange(): return (lax.ppermute(first, axis, one), lax.ppermute(second, axis, two))  6.11 us
    ppermute x2, waiting for transfers between devices, body(): other = lax.ppermute(own, 'gy', partner)  2.1 us
  transfers between devices with their start and end apart: 28, of which 8 were waited for; matrix products, arithmetic and copies ran while one was open for 0% of the time, Pallas kernels for 17%

profile of v5, /device:TPU:1, one launch (start us, length us, event | category | flops | bytes accessed | tf_op | source)
XLA Modules:
  0.0 98.3 jit_solution(14846806323040740814)
XLA Ops:
  1.3 4.3 %shard_map.113 = (f32[256,128]{1,0:T(8,128)}, f32[256,128]{1,0:T(8,128)}, f32[328,128]{1,0:T(8,128)}, f32[328,128]{1,0:T(8,128)}, f32[384,128]{1,0:T(8,128)}, /*index=5*/f32[24,128]{1,0:T(8,128)}) custom-call(s32[4]{0:T(128)} %pad_add_fusion.par, f32[9,16,64,128]{3,2,1,0:T(8,128)} %start.3, f32[9,8,16,128]{3,2,1,0:T(8,128)} %state.7, ...), custom_call_target="tpu_custom_call" | custom-call | bytes 7835664 | tf_op jit(solution)/shard_map/pallas_call | solution.py:733
  5.6 4.5 %collective-permute-start.2 = (f32[328,128]{1,0:T(8,128)}, f32[328,128]{1,0:T(8,128)S(1)}, u32[]{:S(2)}, u32[]{:S(2)}) collective-permute-start(f32[328,128]{1,0:T(8,128)} %get-tuple-element.48), channel_id=1, source_target_pairs={{1,2},{2,1},{3,4},{4,3},{5,6},{6,5},{9,10},{10,9},{11,12},{12,11},... | collective-permute-start | bytes 503816 | tf_op jit(solution)/shard_map/ppermute | solution.py:759
  10.1 1.4 %collective-permute-start = (f32[256,128]{1,0:T(8,128)}, f32[256,128]{1,0:T(8,128)S(1)}, u32[]{:S(2)}, u32[]{:S(2)}) collective-permute-start(f32[256,128]{1,0:T(8,128)} %get-tuple-element.46), channel_id=1, source_target_pairs={{0,8},{8,0},{16,24},{24,16},{1,9},{9,1},{17,25},{25,17},{2,10},{10... | collective-permute-start | bytes 393224 | tf_op jit(solution)/shard_map/ppermute | solution.py:759
  12.2 2.0 %collective-permute-done.msg_a.begin_a = f32[256,128]{1,0:T(8,128)S(1)} collective-permute-done((f32[256,128]{1,0:T(8,128)}, f32[256,128]{1,0:T(8,128)S(1)}, u32[]{:S(2)}, u32[]{:S(2)}) %collective-permute-start) | collective-permute-done | bytes 131104 | tf_op jit(solution)/shard_map/ppermute | solution.py:759
  14.3 0.9 copy-done.7
  15.8 0.7 collective-permute-start.3
  16.5 3.2 %shard_map.115.half = f32[3,16,64,128]{3,2,1,0:T(8,128)S(1)} custom-call(s32[4]{0:T(128)S(1)} %copy-done.8, f32[9,16,64,128]{3,2,1,0:T(8,128)S(1)} %copy-done, f32[3,16,64,128]{3,2,1,0:T(8,128)S(1)} %copy-done.1, f32[256,128]{1,0:T(8,128)S(1)} %collective-permute-done.msg_a.begin_a, f32[256,128]{1,0:T(8,128)S(1)} %collective-permute-done.1.msg_b.begin_b, ...), custom_call_target="tpu_custom_call" | custom-call | flops 52428800 | bytes 9117712 | tf_op jit(solution)/shard_map/pallas_call | solution.py:733
  19.8 1.3 %collective-permute-done.5.other = f32[232,128]{1,0:T(8,128)S(1)} collective-permute-done((f32[232,128]{1,0:T(8,128)S(1)}, f32[232,128]{1,0:T(8,128)S(1)}, u32[]{:S(2)}, u32[]{:S(2)}) %collective-permute-start.5) | collective-permute-done | bytes 118816 | tf_op jit(solution)/shard_map/ppermute | solution.py:822
  21.2 1.4 %shard_map.116 = (f32[3,16,64,128]{3,2,1,0:T(8,128)S(1)}, f32[12,64,128]{2,1,0:T(8,128)S(1)}, f32[96,128]{1,0:T(8,128)S(1)}, f32[216,128]{1,0:T(8,128)S(1)}, f32...) custom-call(s32[4]{0:T(128)S(1)} %copy-done.8, f32[3,16,64,128]{3,2,1,0:T(8,128)S(1)} %shard_map.115.half, ...), custom_call_target="tpu_custom_call" | custom-call | bytes 5853968 | tf_op jit(solution)/shard_map/pallas_call | solution.py:733
  22.7 13.4 %collective-permute-start.9 = (f32[224,128]{1,0:T(8,128)S(1)}, f32[224,128]{1,0:T(8,128)S(1)}, u32[]{:S(2)}, u32[]{:S(2)}) collective-permute-start(f32[224,128]{1,0:T(8,128)S(1)} %get-tuple-element.61), channel_id=1, source_target_pairs={{1,2},{2,1},{3,4},{4,3},{5,6},{6,5},{9,10},{10,9},{11,12},{12,11},... | collective-permute-start | bytes 344072 | tf_op jit(solution)/shard_map/ppermute | solution.py:759
  36.2 0.7 collective-permute-start.7
  36.9 0.7 collective-permute-start.10
  37.5 2.2 %collective-permute-done.6.msg_a = f32[216,128]{1,0:T(8,128)S(1)} collective-permute-done((f32[216,128]{1,0:T(8,128)S(1)}, f32[216,128]{1,0:T(8,128)S(1)}, u32[]{:S(2)}, u32[]{:S(2)}) %collective-permute-start.6) | collective-permute-done | bytes 110624 | tf_op jit(solution)/shard_map/ppermute | solution.py:759
  39.8 3.8 %shard_map.117 = (f32[6,16,64,128]{3,2,1,0:T(8,128)S(1)}, f32[3,16,64,128]{3,2,1,0:T(8,128)S(1)}, f32[200,128]{1,0:T(8,128)S(1)}, f32[200,128]{1,0:T(8,128)S(1)}...) custom-call(s32[4]{0:T(128)S(1)} %copy-done.8, f32[3,16,64,128]{3,2,1,0:T(8,128)S(1)} %get-tuple-element.55.half, ...), custom_call_target="tpu_custom_call" | custom-call | flops 52428800 | bytes 14987280 | tf_op jit(solution)/shard_map/pallas_call | solution.py:733
  43.6 6.5 %collective-permute-start.15 = (f32[208,128]{1,0:T(8,128)S(1)}, f32[208,128]{1,0:T(8,128)S(1)}, u32[]{:S(2)}, u32[]{:S(2)}) collective-permute-start(f32[208,128]{1,0:T(8,128)S(1)} %get-tuple-element.70), channel_id=1, source_target_pairs={{1,2},{2,1},{3,4},{4,3},{5,6},{6,5},{9,10},{10,9},{11,12},{12,11},... | collective-permute-start | bytes 319496 | tf_op jit(solution)/shard_map/ppermute | solution.py:759
  50.2 2.5 %collective-permute-start.12 = (f32[200,128]{1,0:T(8,128)S(1)}, f32[200,128]{1,0:T(8,128)S(1)}, u32[]{:S(2)}, u32[]{:S(2)}) collective-permute-start(f32[200,128]{1,0:T(8,128)S(1)} %get-tuple-element.67), channel_id=1, source_target_pairs={{0,8},{8,0},{16,24},{24,16},{1,9},{9,1},{17,25},{25,17},{2,10},{10... | collective-permute-start | bytes 307208 | tf_op jit(solution)/shard_map/ppermute | solution.py:759
  53.4 1.3 %collective-permute-done.11.later_other = f32[192,128]{1,0:T(8,128)S(1)} collective-permute-done((f32[192,128]{1,0:T(8,128)S(1)}, f32[192,128]{1,0:T(8,128)S(1)}, u32[]{:S(2)}, u32[]{:S(2)}) %collective-permute-start.11) | collective-permute-done | bytes 98336 | tf_op jit(solution)/shard_map/ppermute | solution.py:847
  54.7 1.0 %shard_map.118.ghost = f32[12,64,128]{2,1,0:T(8,128)S(1)} custom-call(s32[4]{0:T(128)S(1)} %copy-done.8, f32[232,128]{1,0:T(8,128)S(1)} %collective-permute-done.3.own, f32[232,128]{1,0:T(8,128)S(1)} %collective-permute-done.5.other, s32[1,64]{1,0:T(1,128)S(1)} %bitcast.7, s32[1,128]{1,0:T(1,128)S(1)} %bitcast.9, ...), custom_call_target="tpu_custom_call" | custom-call | bytes 1049360 | tf_op jit(solution)/shard_map/pallas_call | solution.py:733
  55.8 4.0 %shard_map.119 = (f32[3,16,64,128]{3,2,1,0:T(8,128)S(1)}, f32[200,128]{1,0:T(8,128)S(1)}, f32[200,128]{1,0:T(8,128)S(1)}, f32[216,128]{1,0:T(8,128)S(1)}, f32[20...) custom-call(s32[4]{0:T(128)S(1)} %copy-done.8, f32[3,16,64,128]{3,2,1,0:T(8,128)S(1)} %get-tuple-element.62.old, ...), custom_call_target="tpu_custom_call" | custom-call | flops 52428800 | bytes 14835728 | tf_op jit(solution)/shard_map/pallas_call | solution.py:733
  60.0 3.9 %collective-permute-start.19 = (f32[208,128]{1,0:T(8,128)S(1)}, f32[208,128]{1,0:T(8,128)S(1)}, u32[]{:S(2)}, u32[]{:S(2)}) collective-permute-start(f32[208,128]{1,0:T(8,128)S(1)} %get-tuple-element.75), channel_id=1, source_target_pairs={{1,2},{2,1},{3,4},{4,3},{5,6},{6,5},{9,10},{10,9},{11,12},{12,11},... | collective-permute-start | bytes 319496 | tf_op jit(solution)/shard_map/ppermute | solution.py:759
  63.9 3.7 %collective-permute-start.16 = (f32[200,128]{1,0:T(8,128)S(1)}, f32[200,128]{1,0:T(8,128)S(1)}, u32[]{:S(2)}, u32[]{:S(2)}) collective-permute-start(f32[200,128]{1,0:T(8,128)S(1)} %get-tuple-element.72), channel_id=1, source_target_pairs={{0,8},{8,0},{16,24},{24,16},{1,9},{9,1},{17,25},{25,17},{2,10},{10... | collective-permute-start | bytes 307208 | tf_op jit(solution)/shard_map/ppermute | solution.py:759
  68.3 0.7 collective-permute-start.21
  69.0 0.7 collective-permute-done.16.msg_a
  69.7 2.3 %shard_map.120 = (f32[6,8,64,128]{3,2,1,0:T(8,128)S(1)}, f32[176,128]{1,0:T(8,128)S(1)}) custom-call(s32[4]{0:T(128)S(1)} %copy-done.8, f32[3,16,64,128]{3,2,1,0:T(8,128)S(1)} %get-tuple-element.71.velocity, f32[6,16,64,128]{3,2,1,0:T(8,128)S(1)} %get-tuple-element.65.stress, f32[3,16,64,128]{3,2,1,0:T(8,128)S(1)} %copy-done.1, ...), custom_call_target="tpu_custom_call" | custom-call | bytes 1024 | tf_op jit(solution)/shard_map/pallas_call | solution.py:733
  72.0 0.8 collective-permute-start.20
  72.9 4.4 %shard_map.121 = (f32[9,16,64,128]{3,2,1,0:T(8,128)}, f32[8,128]{1,0:T(8,128)S(1)}) custom-call(s32[4]{0:T(128)S(1)} %copy-done.8, f32[6,8,64,128]{3,2,1,0:T(8,128)S(1)} %get-tuple-element.76.below, f32[3,16,64,128]{3,2,1,0:T(8,128)S(1)} %get-tuple-element.71.velocity, f32[6,16,64,128]{3,2,1,0:T(8,128)S(1)} %get-tuple-element.65.stress, ...), custom_call_target="tpu_custom_call" | custom-call | flops 26214400 | bytes 13664272 | tf_op jit(solution)/shard_map/pallas_call | solution.py:733
  77.8 0.8 collective-permute-done.22.other
  78.6 1.1 %shard_map.122 = (f32[3,8,16,128]{3,2,1,0:T(8,128)S(1)}, f32[96,128]{1,0:T(8,128)S(1)}, f32[96,128]{1,0:T(8,128)S(1)}, f32[24,128]{1,0:T(8,128)S(1)}) custom-call(s32[4]{0:T(128)S(1)} %copy-done.8, f32[9,8,16,128]{3,2,1,0:T(8,128)S(1)} %copy-done.3, f32[3,8,16,128]{3,2,1,0:T(8,128)S(1)} %copy-done.5, f32[176,128]{1,0:T(8,128)S(1)} %collective-permute-done.20.own, ...), custom_call_target="tpu_custom_call" | custom-call | bytes 2531344 | tf_op jit(solution)/shard_map/pallas_call | solution.py:733
  79.9 11.3 %collective-permute-start.27 = (f32[96,128]{1,0:T(8,128)S(1)}, f32[96,128]{1,0:T(8,128)S(1)}, u32[]{:S(2)}, u32[]{:S(2)}) collective-permute-start(f32[96,128]{1,0:T(8,128)S(1)} %get-tuple-element.87), channel_id=1, source_target_pairs={{1,2},{2,1},{3,4},{4,3},{5,6},{6,5},{9,10},{10,9},{11,12},{12,11},... | collective-permute-start | bytes 147464 | tf_op jit(solution)/shard_map/ppermute | solution.py:759
  91.8 3.5 %collective-permute-start.24 = (f32[24,128]{1,0:T(8,128)S(1)}, f32[24,128]{1,0:T(8,128)S(1)}, u32[]{:S(2)}, u32[]{:S(2)}) collective-permute-start(f32[24,128]{1,0:T(8,128)S(1)} %get-tuple-element.85), channel_id=1, source_target_pairs={{0,8},{8,0},{16,24},{24,16},{1,9},{9,1},{17,25},{25,17},{2,10},{10... | collective-permute-start | bytes 36872 | tf_op jit(solution)/shard_map/ppermute | solution.py:759
  95.4 1.1 %collective-permute-done.24.msg_a = f32[24,128]{1,0:T(8,128)S(1)} collective-permute-done((f32[24,128]{1,0:T(8,128)S(1)}, f32[24,128]{1,0:T(8,128)S(1)}, u32[]{:S(2)}, u32[]{:S(2)}) %collective-permute-start.24) | collective-permute-done | bytes 12320 | tf_op jit(solution)/shard_map/ppermute | solution.py:759
  96.5 1.8 %shard_map.123 = f32[9,8,16,128]{3,2,1,0:T(8,128)} custom-call(s32[4]{0:T(128)S(1)} %copy-done.8, f32[9,8,16,128]{3,2,1,0:T(8,128)S(1)} %copy-done.3, f32[3,8,16,128]{3,2,1,0:T(8,128)S(1)} %copy-done.5, f32[3,8,16,128]{3,2,1,0:T(8,128)S(1)} %get-tuple-element.83.velocity, f32[192,128]{1,0:T(8,128)S(1)} %collective-permute-done.21.own, ...), custom_call_target="tpu_custom_call" | custom-call | bytes 2547728 | tf_op jit(solution)/shard_map/pallas_call | solution.py:733
  (58 shorter events, 5.3 us)
Async XLA Ops:
  1.3 15.2 %copy-start.1 = (f32[3,16,64,128]{3,2,1,0:T(8,128)S(1)}, f32[3,16,64,128]{3,2,1,0:T(8,128)}, u32[]{:S(2)}) copy-start(f32[3,16,64,128]{3,2,1,0:T(8,128)} %medium.9) | copy-start | bytes 4718596
  1.3 15.2 %copy-start.2 = (bf16[2,256,256]{2,1,0:T(8,128)(2,1)S(1)}, bf16[2,256,256]{2,1,0:T(8,128)(2,1)}, u32[]{:S(2)}) copy-start(bf16[2,256,256]{2,1,0:T(8,128)(2,1)} %constant.46.clone.tile) | copy-start | bytes 786436
  1.3 15.2 %copy-start.4 = (bf16[2,2,32,256]{3,2,1,0:T(8,128)(2,1)S(1)}, bf16[2,2,32,256]{3,2,1,0:T(8,128)(2,1)}, u32[]{:S(2)}) copy-start(bf16[2,2,32,256]{3,2,1,0:T(8,128)(2,1)} %constant.47.clone.halo) | copy-start | bytes 196612
  5.6 8.7 %collective-permute-start.2 = (f32[328,128]{1,0:T(8,128)}, f32[328,128]{1,0:T(8,128)S(1)}, u32[]{:S(2)}, u32[]{:S(2)}) collective-permute-start(f32[328,128]{1,0:T(8,128)} %get-tuple-element.48), channel_id=1, source_target_pairs={{1,2},{2,1},{3,4},{4,3},{5,6},{6,5},{9,10},{10,9},{11,12},{12,11},... | collective-permute-start | bytes 503816 | tf_op jit(solution)/shard_map/ppermute | solution.py:759
  10.1 4.1 %collective-permute-start = (f32[256,128]{1,0:T(8,128)}, f32[256,128]{1,0:T(8,128)S(1)}, u32[]{:S(2)}, u32[]{:S(2)}) collective-permute-start(f32[256,128]{1,0:T(8,128)} %get-tuple-element.46), channel_id=1, source_target_pairs={{0,8},{8,0},{16,24},{24,16},{1,9},{9,1},{17,25},{25,17},{2,10},{10... | collective-permute-start | bytes 393224 | tf_op jit(solution)/shard_map/ppermute | solution.py:759
  11.5 2.7 %collective-permute-start.1 = (f32[256,128]{1,0:T(8,128)}, f32[256,128]{1,0:T(8,128)S(1)}, u32[]{:S(2)}, u32[]{:S(2)}) collective-permute-start(f32[256,128]{1,0:T(8,128)} %get-tuple-element.47), channel_id=1, source_target_pairs={{8,16},{16,8},{9,17},{17,9},{10,18},{18,10},{11,19},{19,11},{12,20... | collective-permute-start | bytes 393224 | tf_op jit(solution)/shard_map/ppermute | solution.py:759
  12.1 4.3 %collective-permute-start.4 = (f32[328,128]{1,0:T(8,128)}, f32[328,128]{1,0:T(8,128)S(1)}, u32[]{:S(2)}, u32[]{:S(2)}) collective-permute-start(f32[328,128]{1,0:T(8,128)} %get-tuple-element.51), channel_id=1, source_target_pairs={{0,1},{1,0},{2,3},{3,2},{4,5},{5,4},{6,7},{7,6},{8,9},{9,8},{10,11... | collective-permute-start | bytes 503816 | tf_op jit(solution)/shard_map/ppermute | solution.py:759
  15.8 4.0 %collective-permute-start.3 = (f32[232,128]{1,0:T(8,128)S(1)}, f32[232,128]{1,0:T(8,128)S(1)}, u32[]{:S(2)}, u32[]{:S(2)}) collective-permute-start(f32[232,128]{1,0:T(8,128)S(1)} %get-tuple-element.50), channel_id=1, source_target_pairs={{0,0},{1,1},{2,8},{3,9},{4,16},{5,17},{6,24},{7,25},{8,2},{9,3},{1... | collective-permute-start | bytes 356360 | tf_op jit(solution)/shard_map/ppermute | solution.py:803
  19.8 1.4 %collective-permute-start.5 = (f32[232,128]{1,0:T(8,128)S(1)}, f32[232,128]{1,0:T(8,128)S(1)}, u32[]{:S(2)}, u32[]{:S(2)}) collective-permute-start(f32[232,128]{1,0:T(8,128)S(1)} %collective-permute-done.3.own), channel_id=1, source_target_pairs={{0,1},{1,0},{2,3},{3,2},{4,5},{5,4},{6,7},{7,6},{8,9},{9,8},{10,11... | collective-permute-start | bytes 356360 | tf_op jit(solution)/shard_map/ppermute | solution.py:822
  22.6 17.2 %collective-permute-start.8 = (f32[232,128]{1,0:T(8,128)S(1)}, f32[232,128]{1,0:T(8,128)S(1)}, u32[]{:S(2)}, u32[]{:S(2)}) collective-permute-start(f32[232,128]{1,0:T(8,128)S(1)} %get-tuple-element.60), channel_id=1, source_target_pairs={{0,1},{1,0},{2,3},{3,2},{4,5},{5,4},{6,7},{7,6},{8,9},{9,8},{10,11... | collective-permute-start | bytes 356360 | tf_op jit(solution)/shard_map/ppermute | solution.py:759
  22.7 17.0 %collective-permute-start.9 = (f32[224,128]{1,0:T(8,128)S(1)}, f32[224,128]{1,0:T(8,128)S(1)}, u32[]{:S(2)}, u32[]{:S(2)}) collective-permute-start(f32[224,128]{1,0:T(8,128)S(1)} %get-tuple-element.61), channel_id=1, source_target_pairs={{1,2},{2,1},{3,4},{4,3},{5,6},{6,5},{9,10},{10,9},{11,12},{12,11},... | collective-permute-start | bytes 344072 | tf_op jit(solution)/shard_map/ppermute | solution.py:759
  36.1 3.7 %collective-permute-start.6 = (f32[216,128]{1,0:T(8,128)S(1)}, f32[216,128]{1,0:T(8,128)S(1)}, u32[]{:S(2)}, u32[]{:S(2)}) collective-permute-start(f32[216,128]{1,0:T(8,128)S(1)} %get-tuple-element.58), channel_id=1, source_target_pairs={{0,8},{8,0},{16,24},{24,16},{1,9},{9,1},{17,25},{25,17},{2,10},{10... | collective-permute-start | bytes 331784 | tf_op jit(solution)/shard_map/ppermute | solution.py:759
  36.2 3.6 %collective-permute-start.7 = (f32[216,128]{1,0:T(8,128)S(1)}, f32[216,128]{1,0:T(8,128)S(1)}, u32[]{:S(2)}, u32[]{:S(2)}) collective-permute-start(f32[216,128]{1,0:T(8,128)S(1)} %get-tuple-element.59), channel_id=1, source_target_pairs={{8,16},{16,8},{9,17},{17,9},{10,18},{18,10},{11,19},{19,11},{12,20... | collective-permute-start | bytes 331784 | tf_op jit(solution)/shard_map/ppermute | solution.py:759
  36.9 16.4 %collective-permute-start.10 = (f32[192,128]{1,0:T(8,128)S(1)}, f32[192,128]{1,0:T(8,128)S(1)}, u32[]{:S(2)}, u32[]{:S(2)}) collective-permute-start(f32[192,128]{1,0:T(8,128)S(1)} %get-tuple-element.63), channel_id=1, source_target_pairs={{0,0},{1,1},{2,8},{3,9},{4,16},{5,17},{6,24},{7,25},{8,2},{9,3},{1... | collective-permute-start | bytes 294920 | tf_op jit(solution)/shard_map/ppermute | solution.py:832
  39.8 16.0 %copy-start.6 = (bf16[2,256,128]{2,1,0:T(8,128)(2,1)S(1)}, bf16[2,256,128]{2,1,0:T(8,128)(2,1)}, u32[]{:S(2)}) copy-start(bf16[2,256,128]{2,1,0:T(8,128)(2,1)} %constant.48.clone.means) | copy-start | bytes 393220
  43.6 12.1 %collective-permute-start.14 = (f32[216,128]{1,0:T(8,128)S(1)}, f32[216,128]{1,0:T(8,128)S(1)}, u32[]{:S(2)}, u32[]{:S(2)}) collective-permute-start(f32[216,128]{1,0:T(8,128)S(1)} %get-tuple-element.69), channel_id=1, source_target_pairs={{0,1},{1,0},{2,3},{3,2},{4,5},{5,4},{6,7},{7,6},{8,9},{9,8},{10,11... | collective-permute-start | bytes 331784 | tf_op jit(solution)/shard_map/ppermute | solution.py:759
  43.6 12.1 %collective-permute-start.15 = (f32[208,128]{1,0:T(8,128)S(1)}, f32[208,128]{1,0:T(8,128)S(1)}, u32[]{:S(2)}, u32[]{:S(2)}) collective-permute-start(f32[208,128]{1,0:T(8,128)S(1)} %get-tuple-element.70), channel_id=1, source_target_pairs={{1,2},{2,1},{3,4},{4,3},{5,6},{6,5},{9,10},{10,9},{11,12},{12,11},... | collective-permute-start | bytes 319496 | tf_op jit(solution)/shard_map/ppermute | solution.py:759
  50.2 5.6 %collective-permute-start.12 = (f32[200,128]{1,0:T(8,128)S(1)}, f32[200,128]{1,0:T(8,128)S(1)}, u32[]{:S(2)}, u32[]{:S(2)}) collective-permute-start(f32[200,128]{1,0:T(8,128)S(1)} %get-tuple-element.67), channel_id=1, source_target_pairs={{0,8},{8,0},{16,24},{24,16},{1,9},{9,1},{17,25},{25,17},{2,10},{10... | collective-permute-start | bytes 307208 | tf_op jit(solution)/shard_map/ppermute | solution.py:759
  52.7 3.1 %collective-permute-start.13 = (f32[200,128]{1,0:T(8,128)S(1)}, f32[200,128]{1,0:T(8,128)S(1)}, u32[]{:S(2)}, u32[]{:S(2)}) collective-permute-start(f32[200,128]{1,0:T(8,128)S(1)} %get-tuple-element.68), channel_id=1, source_target_pairs={{8,16},{16,8},{9,17},{17,9},{10,18},{18,10},{11,19},{19,11},{12,20... | collective-permute-start | bytes 307208 | tf_op jit(solution)/shard_map/ppermute | solution.py:759
  53.3 1.4 %collective-permute-start.11 = (f32[192,128]{1,0:T(8,128)S(1)}, f32[192,128]{1,0:T(8,128)S(1)}, u32[]{:S(2)}, u32[]{:S(2)}) collective-permute-start(f32[192,128]{1,0:T(8,128)S(1)} %collective-permute-done.10.later_own), channel_id=1, source_target_pairs={{0,1},{1,0},{2,3},{3,2},{4,5},{5,4},{6,7},{7,6},{8,9},{9,8},{10,11... | collective-permute-start | bytes 294920 | tf_op jit(solution)/shard_map/ppermute | solution.py:847
  59.8 9.9 %collective-permute-start.18 = (f32[216,128]{1,0:T(8,128)S(1)}, f32[216,128]{1,0:T(8,128)S(1)}, u32[]{:S(2)}, u32[]{:S(2)}) collective-permute-start(f32[216,128]{1,0:T(8,128)S(1)} %get-tuple-element.74), channel_id=1, source_target_pairs={{0,1},{1,0},{2,3},{3,2},{4,5},{5,4},{6,7},{7,6},{8,9},{9,8},{10,11... | collective-permute-start | bytes 331784 | tf_op jit(solution)/shard_map/ppermute | solution.py:759
  60.0 9.7 %collective-permute-start.19 = (f32[208,128]{1,0:T(8,128)S(1)}, f32[208,128]{1,0:T(8,128)S(1)}, u32[]{:S(2)}, u32[]{:S(2)}) collective-permute-start(f32[208,128]{1,0:T(8,128)S(1)} %get-tuple-element.75), channel_id=1, source_target_pairs={{1,2},{2,1},{3,4},{4,3},{5,6},{6,5},{9,10},{10,9},{11,12},{12,11},... | collective-permute-start | bytes 319496 | tf_op jit(solution)/shard_map/ppermute | solution.py:759
  63.9 5.7 %collective-permute-start.16 = (f32[200,128]{1,0:T(8,128)S(1)}, f32[200,128]{1,0:T(8,128)S(1)}, u32[]{:S(2)}, u32[]{:S(2)}) collective-permute-start(f32[200,128]{1,0:T(8,128)S(1)} %get-tuple-element.72), channel_id=1, source_target_pairs={{0,8},{8,0},{16,24},{24,16},{1,9},{9,1},{17,25},{25,17},{2,10},{10... | collective-permute-start | bytes 307208 | tf_op jit(solution)/shard_map/ppermute | solution.py:759
  67.6 2.1 %collective-permute-start.17 = (f32[200,128]{1,0:T(8,128)S(1)}, f32[200,128]{1,0:T(8,128)S(1)}, u32[]{:S(2)}, u32[]{:S(2)}) collective-permute-start(f32[200,128]{1,0:T(8,128)S(1)} %get-tuple-element.73), channel_id=1, source_target_pairs={{8,16},{16,8},{9,17},{17,9},{10,18},{18,10},{11,19},{19,11},{12,20... | collective-permute-start | bytes 307208 | tf_op jit(solution)/shard_map/ppermute | solution.py:759
  68.3 9.0 %collective-permute-start.21 = (f32[192,128]{1,0:T(8,128)S(1)}, f32[192,128]{1,0:T(8,128)S(1)}, u32[]{:S(2)}, u32[]{:S(2)}) collective-permute-start(f32[192,128]{1,0:T(8,128)S(1)} %get-tuple-element.80), channel_id=1, source_target_pairs={{0,0},{1,1},{2,8},{3,9},{4,16},{5,17},{6,24},{7,25},{8,2},{9,3},{1... | collective-permute-start | bytes 294920 | tf_op jit(solution)/shard_map/ppermute | solution.py:863
  72.0 5.3 %collective-permute-start.20 = (f32[176,128]{1,0:T(8,128)S(1)}, f32[176,128]{1,0:T(8,128)S(1)}, u32[]{:S(2)}, u32[]{:S(2)}) collective-permute-start(f32[176,128]{1,0:T(8,128)S(1)} %get-tuple-element.78), channel_id=1, source_target_pairs={{0,0},{1,1},{2,8},{3,9},{4,16},{5,17},{6,24},{7,25},{8,2},{9,3},{1... | collective-permute-start | bytes 270344 | tf_op jit(solution)/shard_map/ppermute | solution.py:871
  77.3 1.3 %collective-permute-start.22 = (f32[176,128]{1,0:T(8,128)S(1)}, f32[176,128]{1,0:T(8,128)S(1)}, u32[]{:S(2)}, u32[]{:S(2)}) collective-permute-start(f32[176,128]{1,0:T(8,128)S(1)} %collective-permute-done.20.own), channel_id=1, source_target_pairs={{0,1},{1,0},{2,3},{3,2},{4,5},{5,4},{6,7},{7,6},{8,9},{9,8},{10,11... | collective-permute-start | bytes 270344 | tf_op jit(solution)/shard_map/ppermute | solution.py:880
  77.3 18.0 %collective-permute-start.23 = (f32[192,128]{1,0:T(8,128)S(1)}, f32[192,128]{1,0:T(8,128)S(1)}, u32[]{:S(2)}, u32[]{:S(2)}) collective-permute-start(f32[192,128]{1,0:T(8,128)S(1)} %collective-permute-done.21.own), channel_id=1, source_target_pairs={{0,1},{1,0},{2,3},{3,2},{4,5},{5,4},{6,7},{7,6},{8,9},{9,8},{10,11... | collective-permute-start | bytes 294920 | tf_op jit(solution)/shard_map/ppermute | solution.py:881
  79.7 16.7 %collective-permute-start.26 = (f32[96,128]{1,0:T(8,128)S(1)}, f32[96,128]{1,0:T(8,128)S(1)}, u32[]{:S(2)}, u32[]{:S(2)}) collective-permute-start(f32[96,128]{1,0:T(8,128)S(1)} %get-tuple-element.86), channel_id=1, source_target_pairs={{0,1},{1,0},{2,3},{3,2},{4,5},{5,4},{6,7},{7,6},{8,9},{9,8},{10,11... | collective-permute-start | bytes 147464 | tf_op jit(solution)/shard_map/ppermute | solution.py:759
  79.9 16.6 %collective-permute-start.27 = (f32[96,128]{1,0:T(8,128)S(1)}, f32[96,128]{1,0:T(8,128)S(1)}, u32[]{:S(2)}, u32[]{:S(2)}) collective-permute-start(f32[96,128]{1,0:T(8,128)S(1)} %get-tuple-element.87), channel_id=1, source_target_pairs={{1,2},{2,1},{3,4},{4,3},{5,6},{6,5},{9,10},{10,9},{11,12},{12,11},... | collective-permute-start | bytes 147464 | tf_op jit(solution)/shard_map/ppermute | solution.py:759
  91.2 4.2 %collective-permute-start.25 = (f32[24,128]{1,0:T(8,128)S(1)}, f32[24,128]{1,0:T(8,128)S(1)}, u32[]{:S(2)}, u32[]{:S(2)}) collective-permute-start(f32[24,128]{1,0:T(8,128)S(1)} %get-tuple-element.85), channel_id=1, source_target_pairs={{8,16},{16,8},{9,17},{17,9},{10,18},{18,10},{11,19},{19,11},{12,20... | collective-permute-start | bytes 36872 | tf_op jit(solution)/shard_map/ppermute | solution.py:759
  91.8 4.6 %collective-permute-start.24 = (f32[24,128]{1,0:T(8,128)S(1)}, f32[24,128]{1,0:T(8,128)S(1)}, u32[]{:S(2)}, u32[]{:S(2)}) collective-permute-start(f32[24,128]{1,0:T(8,128)S(1)} %get-tuple-element.85), channel_id=1, source_target_pairs={{0,8},{8,0},{16,24},{24,16},{1,9},{9,1},{17,25},{25,17},{2,10},{10... | collective-permute-start | bytes 36872 | tf_op jit(solution)/shard_map/ppermute | solution.py:759
  (7 other events, 51.4 us)

commit v6 on v5

--- a/solution.py
+++ b/solution.py
@@ -329,7 +329,7 @@
     par, own, other, prow, pcol, ghost, level, planes, ends=None, known=None
 ):
     core = par[1]
-    row_base, col_base = par[2], par[3]
+    row_base, col_base = par[2] * (prow.shape[1] // 2), par[3] * LANES
     part = (own.shape[0] - 40) // 12
     rows = prow.shape[1]
     low = core == 0
@@ -726,12 +726,17 @@
 
 
 def call(kernel, args, outs, scratch=(), flops=0, copied=0, light=False):
-    specs = [pl.BlockSpec(memory_space=pltpu.SMEM)]
-    for n, a in enumerate(args[1:]):
+    specs = []
+    for n, a in enumerate(args):
         specs.append(pl.BlockSpec(memory_space=pltpu.HBM) if n < copied else whole(a.shape))
     size = 1024 if light else sum(4 * int(np.prod(a.shape)) for a in args) + sum(4 * int(np.prod(o)) for o in outs)
+
+    def placed(*refs):
+        i, j = lax.axis_index("gx"), lax.axis_index("gy")
+        kernel((i % 2, j % 2, i, j // 2), *refs)
+
     return pl.pallas_call(
-        kernel,
+        placed,
         grid=(1,),
         in_specs=specs,
         out_specs=[whole(o) for o in outs],
@@ -767,7 +772,6 @@
     depth, rows, cols = fine_state.shape[1:]
     thick, part = coarse_state.shape[1:3]
     blocks = depth * rows // LANES
-    par = jnp.stack([i % 2, j % 2, i * (rows // 2), (j // 2) * LANES]).astype(jnp.int32)
     tile, halo = (jnp.asarray(c) for c in lane_constants())
     means = jnp.asarray(mean_constants())
     across = [
@@ -784,7 +788,7 @@
     count = 24 * part
     out_a, out_b, out_1, out_2, planes, outer = call(
         pack_kernel,
-        [par, fine_state, coarse_state, coarse_past, fine_medium],
+        [fine_state, coarse_state, coarse_past, fine_medium],
         [(rows_msg + coarse_cols + 16 + count * 8 // LANES, LANES)] * 2
         + [(cols_msg + coarse_rows + 40, LANES)] * 2
         + [(count, LANES), (24, LANES)],
@@ -797,7 +801,7 @@
     begin = msg_a, msg_b, msg_1, msg_2
     crossing, later = call(
         crossing_kernel,
-        [par, planes, msg_a, msg_b, msg_2],
+        [planes, msg_a, msg_b, msg_2],
         [(count // 2 + 40, LANES), (count // 2, LANES)],
     )
     own = lax.ppermute(crossing, both, across)
@@ -813,7 +817,7 @@
     halves = [(rows_msg + 8, LANES)] * 2 + [(cols_msg + 24, LANES), (cols_msg + 16, LANES)]
     (half,) = call(
         first_velocity_kernel,
-        [par, fine_state, fine_medium, msg_a, msg_b, msg_1, msg_2, tile, halo],
+        [fine_state, fine_medium, msg_a, msg_b, msg_1, msg_2, tile, halo],
         [(3,) + shape],
         scratch_of(depth, rows),
         flops=400 * cells,
@@ -823,7 +827,7 @@
     parents = parent_rows.reshape(1, rows), parent_cols.reshape(1, cols)
     half, half_ghost, known, out_a, out_b, out_1, out_2 = call(
         ghost_kernel,
-        [par, half, fine_medium, own, other, *parents],
+        [half, fine_medium, own, other, *parents],
         [(3,) + shape, (12, rows, cols), (96, LANES)] + [(rows_msg + 24, LANES)] * 2
         + [(cols_msg + 40, LANES), (cols_msg + 32, LANES)],
     )
@@ -835,7 +839,7 @@
         functools.partial(
             stress_kernel, base_x=rows_msg + coarse_cols, base_y=cols_msg + coarse_rows
         ),
-        [par, half, fine_state, fine_medium, half_ghost, known, begin[0], begin[1], begin[3],
+        [half, fine_state, fine_medium, half_ghost, known, begin[0], begin[1], begin[3],
          *msgs, tile, halo],
         [(6,) + shape, (3,) + shape] + halves,
         scratch_of(depth, rows)
@@ -847,14 +851,14 @@
     later_other = lax.ppermute(later, "gy", partner)
     (ghost,) = call(
         later_ghost_kernel,
-        [par, own, other, *parents, later, later_other, *ends],
+        [own, other, *parents, later, later_other, *ends],
         [(12, rows, cols)],
     )
     moved_v, moved_s = (len(above_planes(t)) * part for t in (STR_Z, VEL_Z))
     lift_scratch = [(rows, cols), (2, count // 2, LANES)]
     velocity, out_a, out_b, out_1, out_2, lifted = call(
         velocity_kernel,
-        [par, velocity, stress, fine_medium, ghost, fine_state, *msgs, tile, halo, means],
+        [velocity, stress, fine_medium, ghost, fine_state, *msgs, tile, halo, means],
         [(3,) + shape] + halves + [(moved_v, LANES)],
         scratch_of(depth, rows) + lift_scratch,
         flops=400 * cells,
@@ -863,7 +867,7 @@
     moving = lax.ppermute(lifted, both, across)
     below, lifted = call(
         lower_stress_kernel,
-        [par, velocity, stress, fine_medium, ghost, fine_state, *msgs, tile, halo, means],
+        [velocity, stress, fine_medium, ghost, fine_state, *msgs, tile, halo, means],
         [(6, 8, rows, cols), (moved_s, LANES)],
         scratch_of(8, rows) + lift_scratch,
         light=True,
@@ -871,7 +875,7 @@
     own = lax.ppermute(lifted, both, across)
     fine_out, done = call(
         upper_stress_kernel,
-        [par, below, velocity, stress, fine_medium, *msgs, tile, halo],
+        [below, velocity, stress, fine_medium, *msgs, tile, halo],
         [(9,) + shape, (8, LANES)],
         scratch_of(8, rows),
         flops=200 * cells,
@@ -883,14 +887,14 @@
     shape = (thick, part, LANES)
     velocity, out_1, out_2, out_c = call(
         functools.partial(coarse_velocity_kernel, base_c=rows_msg, base_r=cols_msg),
-        [par, coarse_state, coarse_medium, own, other, *begin, tile, halo, done],
+        [coarse_state, coarse_medium, own, other, *begin, tile, halo, done],
         [(3,) + shape, (coarse_rows, LANES), (coarse_rows, LANES), (coarse_cols, LANES)],
         scratch_of(thick, part) + [(moved_s, LANES)],
     )
     msgs = exchange("gx", out_c, out_c) + exchange("gy", out_1, out_2)
     (coarse_out,) = call(
         coarse_stress_kernel,
-        [par, coarse_state, coarse_medium, velocity, moving, moving_other, *msgs, tile, halo],
+        [coarse_state, coarse_medium, velocity, moving, moving_other, *msgs, tile, halo],
         [(9,) + shape],
         scratch_of(thick, part) + [(moved_v, LANES)],
     )

time: 99.5 us -> 93.9 us (0.944)
  Pallas kernels: 28 us -> 21.8 us
  starting transfers between devices: 58.2 us -> 59.5 us
    pallas_call x11, Pallas kernels: 28 us -> 21.8 us  [call(): pl.pallas_call(placed, grid=(1,), in_specs=specs, out_specs=[whole(o) for...]
    ppermute x20, starting transfers between devices: 54.7 us -> 56 us  [exchange(): return (lax.ppermute(first, axis, one), lax.ppermute(second, axis, two))]
  transfers between devices with their start and end apart: 28 -> 28, of which waited for: 8 -> 8; matrix products, arithmetic and copies ran while one was open for 0% -> 0% of each run, Pallas kernels for 17% -> 14%
where the time goes in v6:
time: 93.9 us; the launch traced here: 92.8 us
  starting transfers between devices  59.5 us (63%)
  Pallas kernels  21.8 us (23%)
  waiting for transfers between devices  9.51 us (10%)
  between operations  1.01 us (1%)
  local copies, waits for them, and re-layouts  0.98 us (1%)
    ppermute x20, starting transfers between devices, exchange(): return (lax.ppermute(first, axis, one), lax.ppermute(second, axis, two))  56 us
    pallas_call x11, Pallas kernels, call(): pl.pallas_call(placed, grid=(1,), in_specs=specs, out_specs=[whole(o) for...  21.8 us
    ppermute x20, waiting for transfers between devices, exchange(): return (lax.ppermute(first, axis, one), lax.ppermute(second, axis, two))  6.11 us
    ppermute x2, waiting for transfers between devices, body(): other = lax.ppermute(own, 'gy', partner)  2.1 us
  transfers between devices with their start and end apart: 28, of which 8 were waited for; matrix products, arithmetic and copies ran while one was open for 0% of the time, Pallas kernels for 14%

profile of v6, /device:TPU:1, one launch (start us, length us, event | category | flops | bytes accessed | tf_op | source)
XLA Modules:
  0.0 92.8 jit_solution(12043903883481899761)
XLA Ops:
  0.7 3.2 %shard_map.113 = (f32[256,128]{1,0:T(8,128)}, f32[256,128]{1,0:T(8,128)}, f32[328,128]{1,0:T(8,128)}, f32[328,128]{1,0:T(8,128)}, f32[384,128]{1,0:T(8,128)}, /*index=5*/f32[24,128]{1,0:T(8,128)}) custom-call(f32[9,16,64,128]{3,2,1,0:T(8,128)} %refs_4_.3, f32[9,8,16,128]{3,2,1,0:T(8,128)} %refs_0_.7, f32[9,2,16,128]{3,2,1,0:T(8,128)} %refs_2_.4, ...), custom_call_target="tpu_custom_call" | custom-call | bytes 7835648 | tf_op jit(solution)/shard_map/pallas_call | solution.py:738
  3.9 4.5 %collective-permute-start.2 = (f32[328,128]{1,0:T(8,128)}, f32[328,128]{1,0:T(8,128)S(1)}, u32[]{:S(2)}, u32[]{:S(2)}) collective-permute-start(f32[328,128]{1,0:T(8,128)} %get-tuple-element.48), channel_id=1, source_target_pairs={{1,2},{2,1},{3,4},{4,3},{5,6},{6,5},{9,10},{10,9},{11,12},{12,11},... | collective-permute-start | bytes 503816 | tf_op jit(solution)/shard_map/ppermute | solution.py:764
  8.4 1.4 %collective-permute-start = (f32[256,128]{1,0:T(8,128)}, f32[256,128]{1,0:T(8,128)S(1)}, u32[]{:S(2)}, u32[]{:S(2)}) collective-permute-start(f32[256,128]{1,0:T(8,128)} %get-tuple-element.46), channel_id=1, source_target_pairs={{0,8},{8,0},{16,24},{24,16},{1,9},{9,1},{17,25},{25,17},{2,10},{10... | collective-permute-start | bytes 393224 | tf_op jit(solution)/shard_map/ppermute | solution.py:764
  9.8 0.7 collective-permute-start.1
  10.5 2.0 %collective-permute-done.refs_1_.refs_2_.refs_5_.refs_4_ = f32[256,128]{1,0:T(8,128)S(1)} collective-permute-done((f32[256,128]{1,0:T(8,128)}, f32[256,128]{1,0:T(8,128)S(1)}, u32[]{:S(2)}, u32[]{:S(2)}) %collective-permute-start) | collective-permute-done | bytes 131104 | tf_op jit(solution)/shard_map/ppermute | solution.py:764
  12.6 0.9 copy-done.7
  13.6 0.7 collective-permute-start.3
  14.3 2.7 %shard_map.115.refs_0_ = f32[3,16,64,128]{3,2,1,0:T(8,128)S(1)} custom-call(f32[9,16,64,128]{3,2,1,0:T(8,128)S(1)} %copy-done, f32[3,16,64,128]{3,2,1,0:T(8,128)S(1)} %copy-done.1, f32[256,128]{1,0:T(8,128)S(1)} %collective-permute-done.refs_1_.refs_2_.refs_5_.refs_4_, f32[256,128]{1,0:T(8,128)S(1)} %collective-permute-done.1.refs_2_.refs_3_.refs_6_.refs_5_, ...), custom_call_target="tpu_custom_call" | custom-call | flops 52428800 | bytes 9117696 | tf_op jit(solution)/shard_map/pallas_call | solution.py:738
  17.1 1.3 %collective-permute-done.5.refs_3_.refs_1_ = f32[232,128]{1,0:T(8,128)S(1)} collective-permute-done((f32[232,128]{1,0:T(8,128)S(1)}, f32[232,128]{1,0:T(8,128)S(1)}, u32[]{:S(2)}, u32[]{:S(2)}) %collective-permute-start.5) | collective-permute-done | bytes 118816 | tf_op jit(solution)/shard_map/ppermute | solution.py:826
  18.4 0.9 shard_map.116
  19.4 13.9 %collective-permute-start.9 = (f32[224,128]{1,0:T(8,128)S(1)}, f32[224,128]{1,0:T(8,128)S(1)}, u32[]{:S(2)}, u32[]{:S(2)}) collective-permute-start(f32[224,128]{1,0:T(8,128)S(1)} %get-tuple-element.61), channel_id=1, source_target_pairs={{1,2},{2,1},{3,4},{4,3},{5,6},{6,5},{9,10},{10,9},{11,12},{12,11},... | collective-permute-start | bytes 344072 | tf_op jit(solution)/shard_map/ppermute | solution.py:764
  33.4 0.7 collective-permute-start.7
  34.1 0.7 collective-permute-start.10
  34.8 2.2 %collective-permute-done.6.refs_8_.refs_6_ = f32[216,128]{1,0:T(8,128)S(1)} collective-permute-done((f32[216,128]{1,0:T(8,128)S(1)}, f32[216,128]{1,0:T(8,128)S(1)}, u32[]{:S(2)}, u32[]{:S(2)}) %collective-permute-start.6) | collective-permute-done | bytes 110624 | tf_op jit(solution)/shard_map/ppermute | solution.py:764
  37.0 3.3 %shard_map.117 = (f32[6,16,64,128]{3,2,1,0:T(8,128)S(1)}, f32[3,16,64,128]{3,2,1,0:T(8,128)S(1)}, f32[200,128]{1,0:T(8,128)S(1)}, f32[200,128]{1,0:T(8,128)S(1)}...) custom-call(f32[3,16,64,128]{3,2,1,0:T(8,128)S(1)} %get-tuple-element.55.refs_0_, f32[9,16,64,128]{3,2,1,0:T(8,128)S(1)} %copy-done, ...), custom_call_target="tpu_custom_call" | custom-call | flops 52428800 | bytes 14987264 | tf_op jit(solution)/shard_map/pallas_call | solution.py:738
  40.3 6.5 %collective-permute-start.15 = (f32[208,128]{1,0:T(8,128)S(1)}, f32[208,128]{1,0:T(8,128)S(1)}, u32[]{:S(2)}, u32[]{:S(2)}) collective-permute-start(f32[208,128]{1,0:T(8,128)S(1)} %get-tuple-element.70), channel_id=1, source_target_pairs={{1,2},{2,1},{3,4},{4,3},{5,6},{6,5},{9,10},{10,9},{11,12},{12,11},... | collective-permute-start | bytes 319496 | tf_op jit(solution)/shard_map/ppermute | solution.py:764
  46.9 2.5 %collective-permute-start.12 = (f32[200,128]{1,0:T(8,128)S(1)}, f32[200,128]{1,0:T(8,128)S(1)}, u32[]{:S(2)}, u32[]{:S(2)}) collective-permute-start(f32[200,128]{1,0:T(8,128)S(1)} %get-tuple-element.67), channel_id=1, source_target_pairs={{0,8},{8,0},{16,24},{24,16},{1,9},{9,1},{17,25},{25,17},{2,10},{10... | collective-permute-start | bytes 307208 | tf_op jit(solution)/shard_map/ppermute | solution.py:764
  50.1 1.3 %collective-permute-done.11.refs_5_ = f32[192,128]{1,0:T(8,128)S(1)} collective-permute-done((f32[192,128]{1,0:T(8,128)S(1)}, f32[192,128]{1,0:T(8,128)S(1)}, u32[]{:S(2)}, u32[]{:S(2)}) %collective-permute-start.11) | collective-permute-done | bytes 98336 | tf_op jit(solution)/shard_map/ppermute | solution.py:851
  51.9 3.5 %shard_map.119 = (f32[3,16,64,128]{3,2,1,0:T(8,128)S(1)}, f32[200,128]{1,0:T(8,128)S(1)}, f32[200,128]{1,0:T(8,128)S(1)}, f32[216,128]{1,0:T(8,128)S(1)}, f32[20...) custom-call(f32[3,16,64,128]{3,2,1,0:T(8,128)S(1)} %get-tuple-element.62.refs_0_, ...), custom_call_target="tpu_custom_call" | custom-call | flops 52428800 | bytes 14835712 | tf_op jit(solution)/shard_map/pallas_call | solution.py:738
  55.7 3.9 %collective-permute-start.19 = (f32[208,128]{1,0:T(8,128)S(1)}, f32[208,128]{1,0:T(8,128)S(1)}, u32[]{:S(2)}, u32[]{:S(2)}) collective-permute-start(f32[208,128]{1,0:T(8,128)S(1)} %get-tuple-element.75), channel_id=1, source_target_pairs={{1,2},{2,1},{3,4},{4,3},{5,6},{6,5},{9,10},{10,9},{11,12},{12,11},... | collective-permute-start | bytes 319496 | tf_op jit(solution)/shard_map/ppermute | solution.py:764
  59.7 3.8 %collective-permute-start.16 = (f32[200,128]{1,0:T(8,128)S(1)}, f32[200,128]{1,0:T(8,128)S(1)}, u32[]{:S(2)}, u32[]{:S(2)}) collective-permute-start(f32[200,128]{1,0:T(8,128)S(1)} %get-tuple-element.72), channel_id=1, source_target_pairs={{0,8},{8,0},{16,24},{24,16},{1,9},{9,1},{17,25},{25,17},{2,10},{10... | collective-permute-start | bytes 307208 | tf_op jit(solution)/shard_map/ppermute | solution.py:764
  64.1 0.7 collective-permute-start.21
  64.8 0.7 collective-permute-done.16.refs_5_.refs_4_
  65.5 1.9 %shard_map.120 = (f32[6,8,64,128]{3,2,1,0:T(8,128)S(1)}, f32[176,128]{1,0:T(8,128)S(1)}) custom-call(f32[3,16,64,128]{3,2,1,0:T(8,128)S(1)} %get-tuple-element.71.refs_0_.refs_1_, f32[6,16,64,128]{3,2,1,0:T(8,128)S(1)} %get-tuple-element.65.refs_1_.refs_2_, f32[3,16,64,128]{3,2,1,0:T(8,128)S(1)} %copy-done.1, f32[12,64,128]{2,1,0:T(8,128)S(1)} %shard_map.118.refs_3_, ...), custom_call_target="tpu_custom_call" | custom-call | bytes 1024 | tf_op jit(solution)/shard_map/pallas_call | solution.py:738
  67.4 0.8 collective-permute-start.20
  68.3 4.0 %shard_map.121 = (f32[9,16,64,128]{3,2,1,0:T(8,128)}, f32[8,128]{1,0:T(8,128)S(1)}) custom-call(f32[6,8,64,128]{3,2,1,0:T(8,128)S(1)} %get-tuple-element.76.refs_0_, f32[3,16,64,128]{3,2,1,0:T(8,128)S(1)} %get-tuple-element.71.refs_0_.refs_1_, f32[6,16,64,128]{3,2,1,0:T(8,128)S(1)} %get-tuple-element.65.refs_1_.refs_2_, f32[3,16,64,128]{3,2,1,0:T(8,128)S(1)} %copy-done.1, ...), custom_call_target="tpu_custom_call" | custom-call | flops 26214400 | bytes 13664256 | tf_op jit(solution)/shard_map/pallas_call | solution.py:738
  72.8 0.8 collective-permute-done.22.refs_3_
  74.3 12.2 %collective-permute-start.27 = (f32[96,128]{1,0:T(8,128)S(1)}, f32[96,128]{1,0:T(8,128)S(1)}, u32[]{:S(2)}, u32[]{:S(2)}) collective-permute-start(f32[96,128]{1,0:T(8,128)S(1)} %get-tuple-element.87), channel_id=1, source_target_pairs={{1,2},{2,1},{3,4},{4,3},{5,6},{6,5},{9,10},{10,9},{11,12},{12,11},... | collective-permute-start | bytes 147464 | tf_op jit(solution)/shard_map/ppermute | solution.py:764
  86.5 0.7 collective-permute-start.25
  87.1 3.3 %collective-permute-start.24 = (f32[24,128]{1,0:T(8,128)S(1)}, f32[24,128]{1,0:T(8,128)S(1)}, u32[]{:S(2)}, u32[]{:S(2)}) collective-permute-start(f32[24,128]{1,0:T(8,128)S(1)} %get-tuple-element.85), channel_id=1, source_target_pairs={{0,8},{8,0},{16,24},{24,16},{1,9},{9,1},{17,25},{25,17},{2,10},{10... | collective-permute-start | bytes 36872 | tf_op jit(solution)/shard_map/ppermute | solution.py:764
  90.4 1.1 %collective-permute-done.24.refs_5_ = f32[24,128]{1,0:T(8,128)S(1)} collective-permute-done((f32[24,128]{1,0:T(8,128)S(1)}, f32[24,128]{1,0:T(8,128)S(1)}, u32[]{:S(2)}, u32[]{:S(2)}) %collective-permute-start.24) | collective-permute-done | bytes 12320 | tf_op jit(solution)/shard_map/ppermute | solution.py:764
  91.5 1.3 %shard_map.123 = f32[9,8,16,128]{3,2,1,0:T(8,128)} custom-call(f32[9,8,16,128]{3,2,1,0:T(8,128)S(1)} %copy-done.3, f32[3,8,16,128]{3,2,1,0:T(8,128)S(1)} %copy-done.5, f32[3,8,16,128]{3,2,1,0:T(8,128)S(1)} %get-tuple-element.83.refs_2_, f32[192,128]{1,0:T(8,128)S(1)} %collective-permute-done.21.refs_3_, f32[192,128]{1,0:T(8,128)S(1)} %collective-permute-done.23.refs_4_, ...), custom_call_target="tpu_custom_call" | custom-call | bytes 2547712 | tf_op jit(solution)/shard_map/pallas_call | solution.py:738
  (55 shorter events, 3.9 us)
Async XLA Ops:
  0.6 13.6 %copy-start.2 = (bf16[2,256,256]{2,1,0:T(8,128)(2,1)S(1)}, bf16[2,256,256]{2,1,0:T(8,128)(2,1)}, u32[]{:S(2)}) copy-start(bf16[2,256,256]{2,1,0:T(8,128)(2,1)} %constant.6.clone.refs_6_.refs_12_.refs_9_.refs_8_) | copy-start | bytes 786436
  0.6 13.6 %copy-start.4 = (bf16[2,2,32,256]{3,2,1,0:T(8,128)(2,1)S(1)}, bf16[2,2,32,256]{3,2,1,0:T(8,128)(2,1)}, u32[]{:S(2)}) copy-start(bf16[2,2,32,256]{3,2,1,0:T(8,128)(2,1)} %constant.7.clone.refs_7_.refs_13_.refs_10_.refs_9_) | copy-start | bytes 196612
  0.7 13.6 %copy-start = (f32[9,16,64,128]{3,2,1,0:T(8,128)S(1)}, f32[9,16,64,128]{3,2,1,0:T(8,128)}, u32[]{:S(2)}) copy-start(f32[9,16,64,128]{3,2,1,0:T(8,128)} %refs_4_.3) | copy-start | bytes 14155780
  3.9 8.7 %collective-permute-start.2 = (f32[328,128]{1,0:T(8,128)}, f32[328,128]{1,0:T(8,128)S(1)}, u32[]{:S(2)}, u32[]{:S(2)}) collective-permute-start(f32[328,128]{1,0:T(8,128)} %get-tuple-element.48), channel_id=1, source_target_pairs={{1,2},{2,1},{3,4},{4,3},{5,6},{6,5},{9,10},{10,9},{11,12},{12,11},... | collective-permute-start | bytes 503816 | tf_op jit(solution)/shard_map/ppermute | solution.py:764
  8.4 4.1 %collective-permute-start = (f32[256,128]{1,0:T(8,128)}, f32[256,128]{1,0:T(8,128)S(1)}, u32[]{:S(2)}, u32[]{:S(2)}) collective-permute-start(f32[256,128]{1,0:T(8,128)} %get-tuple-element.46), channel_id=1, source_target_pairs={{0,8},{8,0},{16,24},{24,16},{1,9},{9,1},{17,25},{25,17},{2,10},{10... | collective-permute-start | bytes 393224 | tf_op jit(solution)/shard_map/ppermute | solution.py:764
  9.8 2.7 %collective-permute-start.1 = (f32[256,128]{1,0:T(8,128)}, f32[256,128]{1,0:T(8,128)S(1)}, u32[]{:S(2)}, u32[]{:S(2)}) collective-permute-start(f32[256,128]{1,0:T(8,128)} %get-tuple-element.47), channel_id=1, source_target_pairs={{8,16},{16,8},{9,17},{17,9},{10,18},{18,10},{11,19},{19,11},{12,20... | collective-permute-start | bytes 393224 | tf_op jit(solution)/shard_map/ppermute | solution.py:764
  10.5 3.8 %collective-permute-start.4 = (f32[328,128]{1,0:T(8,128)}, f32[328,128]{1,0:T(8,128)S(1)}, u32[]{:S(2)}, u32[]{:S(2)}) collective-permute-start(f32[328,128]{1,0:T(8,128)} %get-tuple-element.51), channel_id=1, source_target_pairs={{0,1},{1,0},{2,3},{3,2},{4,5},{5,4},{6,7},{7,6},{8,9},{9,8},{10,11... | collective-permute-start | bytes 503816 | tf_op jit(solution)/shard_map/ppermute | solution.py:764
  13.6 3.4 %collective-permute-start.3 = (f32[232,128]{1,0:T(8,128)S(1)}, f32[232,128]{1,0:T(8,128)S(1)}, u32[]{:S(2)}, u32[]{:S(2)}) collective-permute-start(f32[232,128]{1,0:T(8,128)S(1)} %get-tuple-element.50), channel_id=1, source_target_pairs={{0,0},{1,1},{2,8},{3,9},{4,16},{5,17},{6,24},{7,25},{8,2},{9,3},{1... | collective-permute-start | bytes 356360 | tf_op jit(solution)/shard_map/ppermute | solution.py:807
  17.0 1.4 %collective-permute-start.5 = (f32[232,128]{1,0:T(8,128)S(1)}, f32[232,128]{1,0:T(8,128)S(1)}, u32[]{:S(2)}, u32[]{:S(2)}) collective-permute-start(f32[232,128]{1,0:T(8,128)S(1)} %collective-permute-done.3.refs_2_.refs_0_), channel_id=1, source_target_pairs={{0,1},{1,0},{2,3},{3,2},{4,5},{5,4},{6,7},{7,6},{8,9},{9,8},{10,11... | collective-permute-start | bytes 356360 | tf_op jit(solution)/shard_map/ppermute | solution.py:826
  19.2 17.8 %collective-permute-start.8 = (f32[232,128]{1,0:T(8,128)S(1)}, f32[232,128]{1,0:T(8,128)S(1)}, u32[]{:S(2)}, u32[]{:S(2)}) collective-permute-start(f32[232,128]{1,0:T(8,128)S(1)} %get-tuple-element.60), channel_id=1, source_target_pairs={{0,1},{1,0},{2,3},{3,2},{4,5},{5,4},{6,7},{7,6},{8,9},{9,8},{10,11... | collective-permute-start | bytes 356360 | tf_op jit(solution)/shard_map/ppermute | solution.py:764
  19.4 17.6 %collective-permute-start.9 = (f32[224,128]{1,0:T(8,128)S(1)}, f32[224,128]{1,0:T(8,128)S(1)}, u32[]{:S(2)}, u32[]{:S(2)}) collective-permute-start(f32[224,128]{1,0:T(8,128)S(1)} %get-tuple-element.61), channel_id=1, source_target_pairs={{1,2},{2,1},{3,4},{4,3},{5,6},{6,5},{9,10},{10,9},{11,12},{12,11},... | collective-permute-start | bytes 344072 | tf_op jit(solution)/shard_map/ppermute | solution.py:764
  33.3 3.7 %collective-permute-start.6 = (f32[216,128]{1,0:T(8,128)S(1)}, f32[216,128]{1,0:T(8,128)S(1)}, u32[]{:S(2)}, u32[]{:S(2)}) collective-permute-start(f32[216,128]{1,0:T(8,128)S(1)} %get-tuple-element.58), channel_id=1, source_target_pairs={{0,8},{8,0},{16,24},{24,16},{1,9},{9,1},{17,25},{25,17},{2,10},{10... | collective-permute-start | bytes 331784 | tf_op jit(solution)/shard_map/ppermute | solution.py:764
  33.4 3.6 %collective-permute-start.7 = (f32[216,128]{1,0:T(8,128)S(1)}, f32[216,128]{1,0:T(8,128)S(1)}, u32[]{:S(2)}, u32[]{:S(2)}) collective-permute-start(f32[216,128]{1,0:T(8,128)S(1)} %get-tuple-element.59), channel_id=1, source_target_pairs={{8,16},{16,8},{9,17},{17,9},{10,18},{18,10},{11,19},{19,11},{12,20... | collective-permute-start | bytes 331784 | tf_op jit(solution)/shard_map/ppermute | solution.py:764
  34.1 15.9 %collective-permute-start.10 = (f32[192,128]{1,0:T(8,128)S(1)}, f32[192,128]{1,0:T(8,128)S(1)}, u32[]{:S(2)}, u32[]{:S(2)}) collective-permute-start(f32[192,128]{1,0:T(8,128)S(1)} %get-tuple-element.63), channel_id=1, source_target_pairs={{0,0},{1,1},{2,8},{3,9},{4,16},{5,17},{6,24},{7,25},{8,2},{9,3},{1... | collective-permute-start | bytes 294920 | tf_op jit(solution)/shard_map/ppermute | solution.py:836
  37.0 14.9 %copy-start.6 = (bf16[2,256,128]{2,1,0:T(8,128)(2,1)S(1)}, bf16[2,256,128]{2,1,0:T(8,128)(2,1)}, u32[]{:S(2)}) copy-start(bf16[2,256,128]{2,1,0:T(8,128)(2,1)} %constant.8.clone.refs_11_) | copy-start | bytes 393220
  40.3 11.6 %collective-permute-start.14 = (f32[216,128]{1,0:T(8,128)S(1)}, f32[216,128]{1,0:T(8,128)S(1)}, u32[]{:S(2)}, u32[]{:S(2)}) collective-permute-start(f32[216,128]{1,0:T(8,128)S(1)} %get-tuple-element.69), channel_id=1, source_target_pairs={{0,1},{1,0},{2,3},{3,2},{4,5},{5,4},{6,7},{7,6},{8,9},{9,8},{10,11... | collective-permute-start | bytes 331784 | tf_op jit(solution)/shard_map/ppermute | solution.py:764
  40.3 11.6 %collective-permute-start.15 = (f32[208,128]{1,0:T(8,128)S(1)}, f32[208,128]{1,0:T(8,128)S(1)}, u32[]{:S(2)}, u32[]{:S(2)}) collective-permute-start(f32[208,128]{1,0:T(8,128)S(1)} %get-tuple-element.70), channel_id=1, source_target_pairs={{1,2},{2,1},{3,4},{4,3},{5,6},{6,5},{9,10},{10,9},{11,12},{12,11},... | collective-permute-start | bytes 319496 | tf_op jit(solution)/shard_map/ppermute | solution.py:764
  46.9 5.0 %collective-permute-start.12 = (f32[200,128]{1,0:T(8,128)S(1)}, f32[200,128]{1,0:T(8,128)S(1)}, u32[]{:S(2)}, u32[]{:S(2)}) collective-permute-start(f32[200,128]{1,0:T(8,128)S(1)} %get-tuple-element.67), channel_id=1, source_target_pairs={{0,8},{8,0},{16,24},{24,16},{1,9},{9,1},{17,25},{25,17},{2,10},{10... | collective-permute-start | bytes 307208 | tf_op jit(solution)/shard_map/ppermute | solution.py:764
  49.3 2.6 %collective-permute-start.13 = (f32[200,128]{1,0:T(8,128)S(1)}, f32[200,128]{1,0:T(8,128)S(1)}, u32[]{:S(2)}, u32[]{:S(2)}) collective-permute-start(f32[200,128]{1,0:T(8,128)S(1)} %get-tuple-element.68), channel_id=1, source_target_pairs={{8,16},{16,8},{9,17},{17,9},{10,18},{18,10},{11,19},{19,11},{12,20... | collective-permute-start | bytes 307208 | tf_op jit(solution)/shard_map/ppermute | solution.py:764
  50.0 1.4 %collective-permute-start.11 = (f32[192,128]{1,0:T(8,128)S(1)}, f32[192,128]{1,0:T(8,128)S(1)}, u32[]{:S(2)}, u32[]{:S(2)}) collective-permute-start(f32[192,128]{1,0:T(8,128)S(1)} %collective-permute-done.10.refs_4_), channel_id=1, source_target_pairs={{0,1},{1,0},{2,3},{3,2},{4,5},{5,4},{6,7},{7,6},{8,9},{9,8},{10,11... | collective-permute-start | bytes 294920 | tf_op jit(solution)/shard_map/ppermute | solution.py:851
  55.5 10.0 %collective-permute-start.18 = (f32[216,128]{1,0:T(8,128)S(1)}, f32[216,128]{1,0:T(8,128)S(1)}, u32[]{:S(2)}, u32[]{:S(2)}) collective-permute-start(f32[216,128]{1,0:T(8,128)S(1)} %get-tuple-element.74), channel_id=1, source_target_pairs={{0,1},{1,0},{2,3},{3,2},{4,5},{5,4},{6,7},{7,6},{8,9},{9,8},{10,11... | collective-permute-start | bytes 331784 | tf_op jit(solution)/shard_map/ppermute | solution.py:764
  55.7 9.8 %collective-permute-start.19 = (f32[208,128]{1,0:T(8,128)S(1)}, f32[208,128]{1,0:T(8,128)S(1)}, u32[]{:S(2)}, u32[]{:S(2)}) collective-permute-start(f32[208,128]{1,0:T(8,128)S(1)} %get-tuple-element.75), channel_id=1, source_target_pairs={{1,2},{2,1},{3,4},{4,3},{5,6},{6,5},{9,10},{10,9},{11,12},{12,11},... | collective-permute-start | bytes 319496 | tf_op jit(solution)/shard_map/ppermute | solution.py:764
  59.7 5.8 %collective-permute-start.16 = (f32[200,128]{1,0:T(8,128)S(1)}, f32[200,128]{1,0:T(8,128)S(1)}, u32[]{:S(2)}, u32[]{:S(2)}) collective-permute-start(f32[200,128]{1,0:T(8,128)S(1)} %get-tuple-element.72), channel_id=1, source_target_pairs={{0,8},{8,0},{16,24},{24,16},{1,9},{9,1},{17,25},{25,17},{2,10},{10... | collective-permute-start | bytes 307208 | tf_op jit(solution)/shard_map/ppermute | solution.py:764
  63.4 2.1 %collective-permute-start.17 = (f32[200,128]{1,0:T(8,128)S(1)}, f32[200,128]{1,0:T(8,128)S(1)}, u32[]{:S(2)}, u32[]{:S(2)}) collective-permute-start(f32[200,128]{1,0:T(8,128)S(1)} %get-tuple-element.73), channel_id=1, source_target_pairs={{8,16},{16,8},{9,17},{17,9},{10,18},{18,10},{11,19},{19,11},{12,20... | collective-permute-start | bytes 307208 | tf_op jit(solution)/shard_map/ppermute | solution.py:764
  64.1 8.1 %collective-permute-start.21 = (f32[192,128]{1,0:T(8,128)S(1)}, f32[192,128]{1,0:T(8,128)S(1)}, u32[]{:S(2)}, u32[]{:S(2)}) collective-permute-start(f32[192,128]{1,0:T(8,128)S(1)} %get-tuple-element.80), channel_id=1, source_target_pairs={{0,0},{1,1},{2,8},{3,9},{4,16},{5,17},{6,24},{7,25},{8,2},{9,3},{1... | collective-permute-start | bytes 294920 | tf_op jit(solution)/shard_map/ppermute | solution.py:867
  67.4 4.8 %collective-permute-start.20 = (f32[176,128]{1,0:T(8,128)S(1)}, f32[176,128]{1,0:T(8,128)S(1)}, u32[]{:S(2)}, u32[]{:S(2)}) collective-permute-start(f32[176,128]{1,0:T(8,128)S(1)} %get-tuple-element.78), channel_id=1, source_target_pairs={{0,0},{1,1},{2,8},{3,9},{4,16},{5,17},{6,24},{7,25},{8,2},{9,3},{1... | collective-permute-start | bytes 270344 | tf_op jit(solution)/shard_map/ppermute | solution.py:875
  72.2 1.3 %collective-permute-start.22 = (f32[176,128]{1,0:T(8,128)S(1)}, f32[176,128]{1,0:T(8,128)S(1)}, u32[]{:S(2)}, u32[]{:S(2)}) collective-permute-start(f32[176,128]{1,0:T(8,128)S(1)} %collective-permute-done.20.refs_2_), channel_id=1, source_target_pairs={{0,1},{1,0},{2,3},{3,2},{4,5},{5,4},{6,7},{7,6},{8,9},{9,8},{10,11... | collective-permute-start | bytes 270344 | tf_op jit(solution)/shard_map/ppermute | solution.py:884
  72.3 18.1 %collective-permute-start.23 = (f32[192,128]{1,0:T(8,128)S(1)}, f32[192,128]{1,0:T(8,128)S(1)}, u32[]{:S(2)}, u32[]{:S(2)}) collective-permute-start(f32[192,128]{1,0:T(8,128)S(1)} %collective-permute-done.21.refs_3_), channel_id=1, source_target_pairs={{0,1},{1,0},{2,3},{3,2},{4,5},{5,4},{6,7},{7,6},{8,9},{9,8},{10,11... | collective-permute-start | bytes 294920 | tf_op jit(solution)/shard_map/ppermute | solution.py:885
  74.1 17.4 %collective-permute-start.26 = (f32[96,128]{1,0:T(8,128)S(1)}, f32[96,128]{1,0:T(8,128)S(1)}, u32[]{:S(2)}, u32[]{:S(2)}) collective-permute-start(f32[96,128]{1,0:T(8,128)S(1)} %get-tuple-element.86), channel_id=1, source_target_pairs={{0,1},{1,0},{2,3},{3,2},{4,5},{5,4},{6,7},{7,6},{8,9},{9,8},{10,11... | collective-permute-start | bytes 147464 | tf_op jit(solution)/shard_map/ppermute | solution.py:764
  74.3 17.2 %collective-permute-start.27 = (f32[96,128]{1,0:T(8,128)S(1)}, f32[96,128]{1,0:T(8,128)S(1)}, u32[]{:S(2)}, u32[]{:S(2)}) collective-permute-start(f32[96,128]{1,0:T(8,128)S(1)} %get-tuple-element.87), channel_id=1, source_target_pairs={{1,2},{2,1},{3,4},{4,3},{5,6},{6,5},{9,10},{10,9},{11,12},{12,11},... | collective-permute-start | bytes 147464 | tf_op jit(solution)/shard_map/ppermute | solution.py:764
  86.5 3.9 %collective-permute-start.25 = (f32[24,128]{1,0:T(8,128)S(1)}, f32[24,128]{1,0:T(8,128)S(1)}, u32[]{:S(2)}, u32[]{:S(2)}) collective-permute-start(f32[24,128]{1,0:T(8,128)S(1)} %get-tuple-element.85), channel_id=1, source_target_pairs={{8,16},{16,8},{9,17},{17,9},{10,18},{18,10},{11,19},{19,11},{12,20... | collective-permute-start | bytes 36872 | tf_op jit(solution)/shard_map/ppermute | solution.py:764
  87.1 4.3 %collective-permute-start.24 = (f32[24,128]{1,0:T(8,128)S(1)}, f32[24,128]{1,0:T(8,128)S(1)}, u32[]{:S(2)}, u32[]{:S(2)}) collective-permute-start(f32[24,128]{1,0:T(8,128)S(1)} %get-tuple-element.85), channel_id=1, source_target_pairs={{0,8},{8,0},{16,24},{24,16},{1,9},{9,1},{17,25},{25,17},{2,10},{10... | collective-permute-start | bytes 36872 | tf_op jit(solution)/shard_map/ppermute | solution.py:764
  (6 other events, 34.7 us)

commit v7 on v6

--- a/solution.py
+++ b/solution.py
@@ -128,7 +128,7 @@
     lane = lax.broadcasted_iota(jnp.int32, (8, 2 * LANES), 1) % LANES
     edges = (lane == jnp.where(row < 4, row, LANES - 8 + row)).astype(BF16)
     for k, (ref, f) in enumerate(fields):
-        x = ref[...] if f is None else flat(ref[f])
+        x = jnp.concatenate([r[...] for r in ref], axis=0) if f is None else flat(ref[f])
         x = jnp.concatenate(split(x), axis=1)
         turned = dot(edges, x, ((1,), (1,)))
         blocks = turned.shape[1] // LANES
@@ -256,7 +256,7 @@
 
 
 def pack_kernel(
-    par, fine, coarse, past, medium, out_a, out_b, out_1, out_2, planes, outer,
+    par, fine, coarse, past, medium, out_a, out_b, out_1, out_2, planes, planes_2, outer,
     turned, first, last, state, before, light, sems,
 ):
     pi, pj = par[0], par[1]
@@ -283,12 +283,13 @@
             now = state[f, layer]
             later = 1.5 * now - 0.5 * before[f, layer]
             for p, plane in ((2 * n + layer, now), (12 + 2 * n + layer, later)):
-                planes[pl.ds(p * part, part), :] = plane
+                target = planes if p < 12 else planes_2
+                target[pl.ds(p % 12 * part, part), :] = plane
                 outer[p : p + 1, :] = jnp.where(upper, plane[:1], plane[part - 1 :])
     base = 12 * depth
     put_columns((out_a, out_b), base, [(state, f) for f, _ in VEL_Y])
     put_rows(out_a, out_b, base + 24, [(light, 0)], pi)
-    put_columns((out_a, out_b), base + 40, [(planes, None)])
+    put_columns((out_a, out_b), base + 40, [((planes, planes_2), None)])
     base = 24 * (depth * rows // LANES)
     put_rows(out_1, out_2, base, [(state, f) for f, _ in VEL_X], pj)
     base += 12 * coarse.shape[1]
@@ -304,8 +305,8 @@
         put_columns((out_1, out_2), base, [(turned, k)])
 
 
-def crossing_kernel(par, planes, msg_a, msg_b, msg_2, first, second):
-    count = planes.shape[0]
+def crossing_kernel(par, planes, msg_a, msg_b, msg_2, first):
+    count = 2 * planes.shape[0]
     blocks = count // LANES
     even = par[0] == 0
     base = msg_a.shape[0] - 8 * blocks
@@ -318,11 +319,10 @@
     fill = [jnp.zeros((8 - blocks, LANES), F32)]
     left, right = (jnp.concatenate(side + fill, axis=0) for side in (left, right))
     half = count // 2
-    first[0:half, :] = planes[:half, :]
+    first[0:half, :] = planes[...]
     first[half : half + 24, :] = msg_2[msg_2.shape[0] - 24 :, :]
     first[half + 24 : half + 32, :] = left
     first[half + 32 : half + 40, :] = right
-    second[...] = planes[half:, :]
 
 
 def expand_ghosts(
@@ -786,12 +786,12 @@
     rows_msg, cols_msg = 12 * depth, 24 * blocks
     coarse_cols, coarse_rows = 24, 12 * thick
     count = 24 * part
-    out_a, out_b, out_1, out_2, planes, outer = call(
+    out_a, out_b, out_1, out_2, planes, later, _ = call(
         pack_kernel,
         [fine_state, coarse_state, coarse_past, fine_medium],
         [(rows_msg + coarse_cols + 16 + count * 8 // LANES, LANES)] * 2
-        + [(cols_msg + coarse_rows + 40, LANES)] * 2
-        + [(count, LANES), (24, LANES)],
+        + [(cols_msg + coarse_rows + 56, LANES), (cols_msg + coarse_rows + 40, LANES)]
+        + [(count // 2, LANES)] * 2 + [(24, LANES)],
         [(3,) + fine_state.shape[1:], (3, depth, 8, cols), (3, depth, 8, cols),
          coarse_state.shape, coarse_past.shape, (1, 4, rows, cols)],
         copied=4,
@@ -799,10 +799,10 @@
     msg_a, msg_b = exchange("gx", out_a, out_b)
     msg_1, msg_2 = exchange("gy", out_1, out_2)
     begin = msg_a, msg_b, msg_1, msg_2
-    crossing, later = call(
+    (crossing,) = call(
         crossing_kernel,
         [planes, msg_a, msg_b, msg_2],
-        [(count // 2 + 40, LANES), (count // 2, LANES)],
+        [(count // 2 + 40, LANES)],
     )
     own = lax.ppermute(crossing, both, across)
 

time: 93.9 us -> 93.7 us (level)
  no operation moved by 1% of the time
where the time goes in v7:
time: 93.7 us; the launch traced here: 92.6 us
  starting transfers between devices  59.4 us (63%)
  Pallas kernels  21.7 us (23%)
  waiting for transfers between devices  9.5 us (10%)
  between operations  1.03 us (1%)
  local copies, waits for them, and re-layouts  0.95 us (1%)
    ppermute x20, starting transfers between devices, exchange(): return (lax.ppermute(first, axis, one), lax.ppermute(second, axis, two))  55.9 us
    pallas_call x11, Pallas kernels, call(): pl.pallas_call(placed, grid=(1,), in_specs=specs, out_specs=[whole(o) for...  21.7 us
    ppermute x20, waiting for transfers between devices, exchange(): return (lax.ppermute(first, axis, one), lax.ppermute(second, axis, two))  6.1 us
    ppermute x2, waiting for transfers between devices, body(): other = lax.ppermute(own, 'gy', partner)  2.1 us
  transfers between devices with their start and end apart: 28, of which 8 were waited for; matrix products, arithmetic and copies ran while one was open for 0% of the time, Pallas kernels for 14%

profile of v7, /device:TPU:1, one launch (start us, length us, event | category | flops | bytes accessed | tf_op | source)
XLA Modules:
  0.0 92.6 jit_solution(8755082297407568455)
XLA Ops:
  0.7 3.2 %shard_map.113 = (f32[256,128]{1,0:T(8,128)}, f32[256,128]{1,0:T(8,128)}, f32[344,128]{1,0:T(8,128)}, f32[328,128]{1,0:T(8,128)}, f32[192,128]{1,0:T(8,128)}, /*index=5*/f32[192,128]{1,0:T(8,128)}, f32[24,128]{1,0:T(8,128)}) custom-call(f32[9,16,64,128]{3,2,1,0:T(8,128)} %refs_4_.3, f32[9,8,16,128]{3,2,1,0:T(8,128)} %refs_0_.7, f32[9,2,16,128]{3,2,1,0:T(8,128)} %refs_2_.4, ...), custom_call_target="tpu_custom_call" | custom-call | bytes 7843840 | tf_op jit(solution)/shard_map/pallas_call | solution.py:738
  3.9 4.5 %collective-permute-start.2 = (f32[328,128]{1,0:T(8,128)}, f32[328,128]{1,0:T(8,128)S(1)}, u32[]{:S(2)}, u32[]{:S(2)}) collective-permute-start(f32[328,128]{1,0:T(8,128)} %get-tuple-element.48), channel_id=1, source_target_pairs={{1,2},{2,1},{3,4},{4,3},{5,6},{6,5},{9,10},{10,9},{11,12},{12,11},... | collective-permute-start | bytes 503816 | tf_op jit(solution)/shard_map/ppermute | solution.py:764
  8.4 1.4 %collective-permute-start = (f32[256,128]{1,0:T(8,128)}, f32[256,128]{1,0:T(8,128)S(1)}, u32[]{:S(2)}, u32[]{:S(2)}) collective-permute-start(f32[256,128]{1,0:T(8,128)} %get-tuple-element.46), channel_id=1, source_target_pairs={{0,8},{8,0},{16,24},{24,16},{1,9},{9,1},{17,25},{25,17},{2,10},{10... | collective-permute-start | bytes 393224 | tf_op jit(solution)/shard_map/ppermute | solution.py:764
  9.8 0.7 collective-permute-start.1
  10.5 2.0 %collective-permute-done.refs_1_.refs_2_.refs_5_.refs_4_ = f32[256,128]{1,0:T(8,128)S(1)} collective-permute-done((f32[256,128]{1,0:T(8,128)}, f32[256,128]{1,0:T(8,128)S(1)}, u32[]{:S(2)}, u32[]{:S(2)}) %collective-permute-start) | collective-permute-done | bytes 131104 | tf_op jit(solution)/shard_map/ppermute | solution.py:764
  12.6 0.9 copy-done.7
  13.5 0.7 collective-permute-start.3
  14.2 2.7 %shard_map.115.refs_0_ = f32[3,16,64,128]{3,2,1,0:T(8,128)S(1)} custom-call(f32[9,16,64,128]{3,2,1,0:T(8,128)S(1)} %copy-done, f32[3,16,64,128]{3,2,1,0:T(8,128)S(1)} %copy-done.1, f32[256,128]{1,0:T(8,128)S(1)} %collective-permute-done.refs_1_.refs_2_.refs_5_.refs_4_, f32[256,128]{1,0:T(8,128)S(1)} %collective-permute-done.1.refs_2_.refs_3_.refs_6_.refs_5_, ...), custom_call_target="tpu_custom_call" | custom-call | flops 52428800 | bytes 9125888 | tf_op jit(solution)/shard_map/pallas_call | solution.py:738
  17.0 1.3 %collective-permute-done.5.refs_3_.refs_1_ = f32[232,128]{1,0:T(8,128)S(1)} collective-permute-done((f32[232,128]{1,0:T(8,128)S(1)}, f32[232,128]{1,0:T(8,128)S(1)}, u32[]{:S(2)}, u32[]{:S(2)}) %collective-permute-start.5) | collective-permute-done | bytes 118816 | tf_op jit(solution)/shard_map/ppermute | solution.py:826
  18.3 0.9 shard_map.116
  19.3 13.9 %collective-permute-start.9 = (f32[224,128]{1,0:T(8,128)S(1)}, f32[224,128]{1,0:T(8,128)S(1)}, u32[]{:S(2)}, u32[]{:S(2)}) collective-permute-start(f32[224,128]{1,0:T(8,128)S(1)} %get-tuple-element.59), channel_id=1, source_target_pairs={{1,2},{2,1},{3,4},{4,3},{5,6},{6,5},{9,10},{10,9},{11,12},{12,11},... | collective-permute-start | bytes 344072 | tf_op jit(solution)/shard_map/ppermute | solution.py:764
  33.4 0.7 collective-permute-start.7
  34.0 0.7 collective-permute-start.10
  34.7 2.2 %collective-permute-done.6.refs_8_.refs_6_ = f32[216,128]{1,0:T(8,128)S(1)} collective-permute-done((f32[216,128]{1,0:T(8,128)S(1)}, f32[216,128]{1,0:T(8,128)S(1)}, u32[]{:S(2)}, u32[]{:S(2)}) %collective-permute-start.6) | collective-permute-done | bytes 110624 | tf_op jit(solution)/shard_map/ppermute | solution.py:764
  37.0 3.3 %shard_map.117 = (f32[6,16,64,128]{3,2,1,0:T(8,128)S(1)}, f32[3,16,64,128]{3,2,1,0:T(8,128)S(1)}, f32[200,128]{1,0:T(8,128)S(1)}, f32[200,128]{1,0:T(8,128)S(1)}...) custom-call(f32[3,16,64,128]{3,2,1,0:T(8,128)S(1)} %get-tuple-element.53.refs_0_, f32[9,16,64,128]{3,2,1,0:T(8,128)S(1)} %copy-done, ...), custom_call_target="tpu_custom_call" | custom-call | flops 52428800 | bytes 14987264 | tf_op jit(solution)/shard_map/pallas_call | solution.py:738
  40.2 6.5 %collective-permute-start.15 = (f32[208,128]{1,0:T(8,128)S(1)}, f32[208,128]{1,0:T(8,128)S(1)}, u32[]{:S(2)}, u32[]{:S(2)}) collective-permute-start(f32[208,128]{1,0:T(8,128)S(1)} %get-tuple-element.68), channel_id=1, source_target_pairs={{1,2},{2,1},{3,4},{4,3},{5,6},{6,5},{9,10},{10,9},{11,12},{12,11},... | collective-permute-start | bytes 319496 | tf_op jit(solution)/shard_map/ppermute | solution.py:764
  46.8 2.5 %collective-permute-start.12 = (f32[200,128]{1,0:T(8,128)S(1)}, f32[200,128]{1,0:T(8,128)S(1)}, u32[]{:S(2)}, u32[]{:S(2)}) collective-permute-start(f32[200,128]{1,0:T(8,128)S(1)} %get-tuple-element.65), channel_id=1, source_target_pairs={{0,8},{8,0},{16,24},{24,16},{1,9},{9,1},{17,25},{25,17},{2,10},{10... | collective-permute-start | bytes 307208 | tf_op jit(solution)/shard_map/ppermute | solution.py:764
  50.0 1.3 %collective-permute-done.11.refs_5_ = f32[192,128]{1,0:T(8,128)S(1)} collective-permute-done((f32[192,128]{1,0:T(8,128)S(1)}, f32[192,128]{1,0:T(8,128)S(1)}, u32[]{:S(2)}, u32[]{:S(2)}) %collective-permute-start.11) | collective-permute-done | bytes 98336 | tf_op jit(solution)/shard_map/ppermute | solution.py:851
  51.9 3.5 %shard_map.119 = (f32[3,16,64,128]{3,2,1,0:T(8,128)S(1)}, f32[200,128]{1,0:T(8,128)S(1)}, f32[200,128]{1,0:T(8,128)S(1)}, f32[216,128]{1,0:T(8,128)S(1)}, f32[20...) custom-call(f32[3,16,64,128]{3,2,1,0:T(8,128)S(1)} %get-tuple-element.60.refs_0_, ...), custom_call_target="tpu_custom_call" | custom-call | flops 52428800 | bytes 14835712 | tf_op jit(solution)/shard_map/pallas_call | solution.py:738
  55.6 3.9 %collective-permute-start.19 = (f32[208,128]{1,0:T(8,128)S(1)}, f32[208,128]{1,0:T(8,128)S(1)}, u32[]{:S(2)}, u32[]{:S(2)}) collective-permute-start(f32[208,128]{1,0:T(8,128)S(1)} %get-tuple-element.73), channel_id=1, source_target_pairs={{1,2},{2,1},{3,4},{4,3},{5,6},{6,5},{9,10},{10,9},{11,12},{12,11},... | collective-permute-start | bytes 319496 | tf_op jit(solution)/shard_map/ppermute | solution.py:764
  59.6 3.8 %collective-permute-start.16 = (f32[200,128]{1,0:T(8,128)S(1)}, f32[200,128]{1,0:T(8,128)S(1)}, u32[]{:S(2)}, u32[]{:S(2)}) collective-permute-start(f32[200,128]{1,0:T(8,128)S(1)} %get-tuple-element.70), channel_id=1, source_target_pairs={{0,8},{8,0},{16,24},{24,16},{1,9},{9,1},{17,25},{25,17},{2,10},{10... | collective-permute-start | bytes 307208 | tf_op jit(solution)/shard_map/ppermute | solution.py:764
  64.0 0.7 collective-permute-start.21
  64.7 0.7 collective-permute-done.16.refs_5_.refs_4_
  65.4 1.9 %shard_map.120 = (f32[6,8,64,128]{3,2,1,0:T(8,128)S(1)}, f32[176,128]{1,0:T(8,128)S(1)}) custom-call(f32[3,16,64,128]{3,2,1,0:T(8,128)S(1)} %get-tuple-element.69.refs_0_.refs_1_, f32[6,16,64,128]{3,2,1,0:T(8,128)S(1)} %get-tuple-element.63.refs_1_.refs_2_, f32[3,16,64,128]{3,2,1,0:T(8,128)S(1)} %copy-done.1, f32[12,64,128]{2,1,0:T(8,128)S(1)} %shard_map.118.refs_3_, ...), custom_call_target="tpu_custom_call" | custom-call | bytes 1024 | tf_op jit(solution)/shard_map/pallas_call | solution.py:738
  67.3 0.8 collective-permute-start.20
  68.2 4.0 %shard_map.121 = (f32[9,16,64,128]{3,2,1,0:T(8,128)}, f32[8,128]{1,0:T(8,128)S(1)}) custom-call(f32[6,8,64,128]{3,2,1,0:T(8,128)S(1)} %get-tuple-element.74.refs_0_, f32[3,16,64,128]{3,2,1,0:T(8,128)S(1)} %get-tuple-element.69.refs_0_.refs_1_, f32[6,16,64,128]{3,2,1,0:T(8,128)S(1)} %get-tuple-element.63.refs_1_.refs_2_, f32[3,16,64,128]{3,2,1,0:T(8,128)S(1)} %copy-done.1, ...), custom_call_target="tpu_custom_call" | custom-call | flops 26214400 | bytes 13664256 | tf_op jit(solution)/shard_map/pallas_call | solution.py:738
  72.7 0.8 collective-permute-done.22.refs_3_
  74.1 12.2 %collective-permute-start.27 = (f32[96,128]{1,0:T(8,128)S(1)}, f32[96,128]{1,0:T(8,128)S(1)}, u32[]{:S(2)}, u32[]{:S(2)}) collective-permute-start(f32[96,128]{1,0:T(8,128)S(1)} %get-tuple-element.85), channel_id=1, source_target_pairs={{1,2},{2,1},{3,4},{4,3},{5,6},{6,5},{9,10},{10,9},{11,12},{12,11},... | collective-permute-start | bytes 147464 | tf_op jit(solution)/shard_map/ppermute | solution.py:764
  86.3 0.7 collective-permute-start.25
  87.0 3.2 %collective-permute-start.24 = (f32[24,128]{1,0:T(8,128)S(1)}, f32[24,128]{1,0:T(8,128)S(1)}, u32[]{:S(2)}, u32[]{:S(2)}) collective-permute-start(f32[24,128]{1,0:T(8,128)S(1)} %get-tuple-element.83), channel_id=1, source_target_pairs={{0,8},{8,0},{16,24},{24,16},{1,9},{9,1},{17,25},{25,17},{2,10},{10... | collective-permute-start | bytes 36872 | tf_op jit(solution)/shard_map/ppermute | solution.py:764
  90.2 1.1 %collective-permute-done.24.refs_5_ = f32[24,128]{1,0:T(8,128)S(1)} collective-permute-done((f32[24,128]{1,0:T(8,128)S(1)}, f32[24,128]{1,0:T(8,128)S(1)}, u32[]{:S(2)}, u32[]{:S(2)}) %collective-permute-start.24) | collective-permute-done | bytes 12320 | tf_op jit(solution)/shard_map/ppermute | solution.py:764
  91.3 1.3 %shard_map.123 = f32[9,8,16,128]{3,2,1,0:T(8,128)} custom-call(f32[9,8,16,128]{3,2,1,0:T(8,128)S(1)} %copy-done.3, f32[3,8,16,128]{3,2,1,0:T(8,128)S(1)} %copy-done.5, f32[3,8,16,128]{3,2,1,0:T(8,128)S(1)} %get-tuple-element.81.refs_2_, f32[192,128]{1,0:T(8,128)S(1)} %collective-permute-done.21.refs_3_, f32[192,128]{1,0:T(8,128)S(1)} %collective-permute-done.23.refs_4_, ...), custom_call_target="tpu_custom_call" | custom-call | bytes 2547712 | tf_op jit(solution)/shard_map/pallas_call | solution.py:738
  (57 shorter events, 3.8 us)
Async XLA Ops:
  0.6 13.6 %copy-start.2 = (bf16[2,256,256]{2,1,0:T(8,128)(2,1)S(1)}, bf16[2,256,256]{2,1,0:T(8,128)(2,1)}, u32[]{:S(2)}) copy-start(bf16[2,256,256]{2,1,0:T(8,128)(2,1)} %constant.6.clone.refs_6_.refs_12_.refs_9_.refs_8_) | copy-start | bytes 786436
  0.6 13.6 %copy-start.4 = (bf16[2,2,32,256]{3,2,1,0:T(8,128)(2,1)S(1)}, bf16[2,2,32,256]{3,2,1,0:T(8,128)(2,1)}, u32[]{:S(2)}) copy-start(bf16[2,2,32,256]{3,2,1,0:T(8,128)(2,1)} %constant.7.clone.refs_7_.refs_13_.refs_10_.refs_9_) | copy-start | bytes 196612
  3.9 8.7 %collective-permute-start.2 = (f32[328,128]{1,0:T(8,128)}, f32[328,128]{1,0:T(8,128)S(1)}, u32[]{:S(2)}, u32[]{:S(2)}) collective-permute-start(f32[328,128]{1,0:T(8,128)} %get-tuple-element.48), channel_id=1, source_target_pairs={{1,2},{2,1},{3,4},{4,3},{5,6},{6,5},{9,10},{10,9},{11,12},{12,11},... | collective-permute-start | bytes 503816 | tf_op jit(solution)/shard_map/ppermute | solution.py:764
  8.4 4.1 %collective-permute-start = (f32[256,128]{1,0:T(8,128)}, f32[256,128]{1,0:T(8,128)S(1)}, u32[]{:S(2)}, u32[]{:S(2)}) collective-permute-start(f32[256,128]{1,0:T(8,128)} %get-tuple-element.46), channel_id=1, source_target_pairs={{0,8},{8,0},{16,24},{24,16},{1,9},{9,1},{17,25},{25,17},{2,10},{10... | collective-permute-start | bytes 393224 | tf_op jit(solution)/shard_map/ppermute | solution.py:764
  9.8 2.7 %collective-permute-start.1 = (f32[256,128]{1,0:T(8,128)}, f32[256,128]{1,0:T(8,128)S(1)}, u32[]{:S(2)}, u32[]{:S(2)}) collective-permute-start(f32[256,128]{1,0:T(8,128)} %get-tuple-element.47), channel_id=1, source_target_pairs={{8,16},{16,8},{9,17},{17,9},{10,18},{18,10},{11,19},{19,11},{12,20... | collective-permute-start | bytes 393224 | tf_op jit(solution)/shard_map/ppermute | solution.py:764
  10.4 3.7 %collective-permute-start.4 = (f32[344,128]{1,0:T(8,128)}, f32[344,128]{1,0:T(8,128)S(1)}, u32[]{:S(2)}, u32[]{:S(2)}) collective-permute-start(f32[344,128]{1,0:T(8,128)} %get-tuple-element.49), channel_id=1, source_target_pairs={{0,1},{1,0},{2,3},{3,2},{4,5},{5,4},{6,7},{7,6},{8,9},{9,8},{10,11... | collective-permute-start | bytes 528392 | tf_op jit(solution)/shard_map/ppermute | solution.py:764
  13.5 3.4 %collective-permute-start.3 = (f32[232,128]{1,0:T(8,128)S(1)}, f32[232,128]{1,0:T(8,128)S(1)}, u32[]{:S(2)}, u32[]{:S(2)}) collective-permute-start(f32[232,128]{1,0:T(8,128)S(1)} %shard_map.114), channel_id=1, source_target_pairs={{0,0},{1,1},{2,8},{3,9},{4,16},{5,17},{6,24},{7,25},{8,2},{9,3},{1... | collective-permute-start | bytes 356360 | tf_op jit(solution)/shard_map/ppermute | solution.py:807
  16.9 1.4 %collective-permute-start.5 = (f32[232,128]{1,0:T(8,128)S(1)}, f32[232,128]{1,0:T(8,128)S(1)}, u32[]{:S(2)}, u32[]{:S(2)}) collective-permute-start(f32[232,128]{1,0:T(8,128)S(1)} %collective-permute-done.3.refs_2_.refs_0_), channel_id=1, source_target_pairs={{0,1},{1,0},{2,3},{3,2},{4,5},{5,4},{6,7},{7,6},{8,9},{9,8},{10,11... | collective-permute-start | bytes 356360 | tf_op jit(solution)/shard_map/ppermute | solution.py:826
  18.3 15.7 %copy-start.10 = (f32[192,128]{1,0:T(8,128)S(1)}, f32[192,128]{1,0:T(8,128)}, u32[]{:S(2)}) copy-start(f32[192,128]{1,0:T(8,128)} %get-tuple-element.61) | copy-start | bytes 294916
  19.2 17.8 %collective-permute-start.8 = (f32[232,128]{1,0:T(8,128)S(1)}, f32[232,128]{1,0:T(8,128)S(1)}, u32[]{:S(2)}, u32[]{:S(2)}) collective-permute-start(f32[232,128]{1,0:T(8,128)S(1)} %get-tuple-element.58), channel_id=1, source_target_pairs={{0,1},{1,0},{2,3},{3,2},{4,5},{5,4},{6,7},{7,6},{8,9},{9,8},{10,11... | collective-permute-start | bytes 356360 | tf_op jit(solution)/shard_map/ppermute | solution.py:764
  19.3 17.6 %collective-permute-start.9 = (f32[224,128]{1,0:T(8,128)S(1)}, f32[224,128]{1,0:T(8,128)S(1)}, u32[]{:S(2)}, u32[]{:S(2)}) collective-permute-start(f32[224,128]{1,0:T(8,128)S(1)} %get-tuple-element.59), channel_id=1, source_target_pairs={{1,2},{2,1},{3,4},{4,3},{5,6},{6,5},{9,10},{10,9},{11,12},{12,11},... | collective-permute-start | bytes 344072 | tf_op jit(solution)/shard_map/ppermute | solution.py:764
  33.3 3.7 %collective-permute-start.6 = (f32[216,128]{1,0:T(8,128)S(1)}, f32[216,128]{1,0:T(8,128)S(1)}, u32[]{:S(2)}, u32[]{:S(2)}) collective-permute-start(f32[216,128]{1,0:T(8,128)S(1)} %get-tuple-element.56), channel_id=1, source_target_pairs={{0,8},{8,0},{16,24},{24,16},{1,9},{9,1},{17,25},{25,17},{2,10},{10... | collective-permute-start | bytes 331784 | tf_op jit(solution)/shard_map/ppermute | solution.py:764
  33.4 3.6 %collective-permute-start.7 = (f32[216,128]{1,0:T(8,128)S(1)}, f32[216,128]{1,0:T(8,128)S(1)}, u32[]{:S(2)}, u32[]{:S(2)}) collective-permute-start(f32[216,128]{1,0:T(8,128)S(1)} %get-tuple-element.57), channel_id=1, source_target_pairs={{8,16},{16,8},{9,17},{17,9},{10,18},{18,10},{11,19},{19,11},{12,20... | collective-permute-start | bytes 331784 | tf_op jit(solution)/shard_map/ppermute | solution.py:764
  34.0 15.9 %collective-permute-start.10 = (f32[192,128]{1,0:T(8,128)S(1)}, f32[192,128]{1,0:T(8,128)S(1)}, u32[]{:S(2)}, u32[]{:S(2)}) collective-permute-start(f32[192,128]{1,0:T(8,128)S(1)} %copy-done.10), channel_id=1, source_target_pairs={{0,0},{1,1},{2,8},{3,9},{4,16},{5,17},{6,24},{7,25},{8,2},{9,3},{1... | collective-permute-start | bytes 294920 | tf_op jit(solution)/shard_map/ppermute | solution.py:836
  36.9 14.9 %copy-start.6 = (bf16[2,256,128]{2,1,0:T(8,128)(2,1)S(1)}, bf16[2,256,128]{2,1,0:T(8,128)(2,1)}, u32[]{:S(2)}) copy-start(bf16[2,256,128]{2,1,0:T(8,128)(2,1)} %constant.8.clone.refs_11_) | copy-start | bytes 393220
  40.2 11.6 %collective-permute-start.14 = (f32[216,128]{1,0:T(8,128)S(1)}, f32[216,128]{1,0:T(8,128)S(1)}, u32[]{:S(2)}, u32[]{:S(2)}) collective-permute-start(f32[216,128]{1,0:T(8,128)S(1)} %get-tuple-element.67), channel_id=1, source_target_pairs={{0,1},{1,0},{2,3},{3,2},{4,5},{5,4},{6,7},{7,6},{8,9},{9,8},{10,11... | collective-permute-start | bytes 331784 | tf_op jit(solution)/shard_map/ppermute | solution.py:764
  40.2 11.6 %collective-permute-start.15 = (f32[208,128]{1,0:T(8,128)S(1)}, f32[208,128]{1,0:T(8,128)S(1)}, u32[]{:S(2)}, u32[]{:S(2)}) collective-permute-start(f32[208,128]{1,0:T(8,128)S(1)} %get-tuple-element.68), channel_id=1, source_target_pairs={{1,2},{2,1},{3,4},{4,3},{5,6},{6,5},{9,10},{10,9},{11,12},{12,11},... | collective-permute-start | bytes 319496 | tf_op jit(solution)/shard_map/ppermute | solution.py:764
  46.8 5.0 %collective-permute-start.12 = (f32[200,128]{1,0:T(8,128)S(1)}, f32[200,128]{1,0:T(8,128)S(1)}, u32[]{:S(2)}, u32[]{:S(2)}) collective-permute-start(f32[200,128]{1,0:T(8,128)S(1)} %get-tuple-element.65), channel_id=1, source_target_pairs={{0,8},{8,0},{16,24},{24,16},{1,9},{9,1},{17,25},{25,17},{2,10},{10... | collective-permute-start | bytes 307208 | tf_op jit(solution)/shard_map/ppermute | solution.py:764
  49.3 2.6 %collective-permute-start.13 = (f32[200,128]{1,0:T(8,128)S(1)}, f32[200,128]{1,0:T(8,128)S(1)}, u32[]{:S(2)}, u32[]{:S(2)}) collective-permute-start(f32[200,128]{1,0:T(8,128)S(1)} %get-tuple-element.66), channel_id=1, source_target_pairs={{8,16},{16,8},{9,17},{17,9},{10,18},{18,10},{11,19},{19,11},{12,20... | collective-permute-start | bytes 307208 | tf_op jit(solution)/shard_map/ppermute | solution.py:764
  49.9 1.4 %collective-permute-start.11 = (f32[192,128]{1,0:T(8,128)S(1)}, f32[192,128]{1,0:T(8,128)S(1)}, u32[]{:S(2)}, u32[]{:S(2)}) collective-permute-start(f32[192,128]{1,0:T(8,128)S(1)} %collective-permute-done.10.refs_4_), channel_id=1, source_target_pairs={{0,1},{1,0},{2,3},{3,2},{4,5},{5,4},{6,7},{7,6},{8,9},{9,8},{10,11... | collective-permute-start | bytes 294920 | tf_op jit(solution)/shard_map/ppermute | solution.py:851
  55.4 10.0 %collective-permute-start.18 = (f32[216,128]{1,0:T(8,128)S(1)}, f32[216,128]{1,0:T(8,128)S(1)}, u32[]{:S(2)}, u32[]{:S(2)}) collective-permute-start(f32[216,128]{1,0:T(8,128)S(1)} %get-tuple-element.72), channel_id=1, source_target_pairs={{0,1},{1,0},{2,3},{3,2},{4,5},{5,4},{6,7},{7,6},{8,9},{9,8},{10,11... | collective-permute-start | bytes 331784 | tf_op jit(solution)/shard_map/ppermute | solution.py:764
  55.6 9.8 %collective-permute-start.19 = (f32[208,128]{1,0:T(8,128)S(1)}, f32[208,128]{1,0:T(8,128)S(1)}, u32[]{:S(2)}, u32[]{:S(2)}) collective-permute-start(f32[208,128]{1,0:T(8,128)S(1)} %get-tuple-element.73), channel_id=1, source_target_pairs={{1,2},{2,1},{3,4},{4,3},{5,6},{6,5},{9,10},{10,9},{11,12},{12,11},... | collective-permute-start | bytes 319496 | tf_op jit(solution)/shard_map/ppermute | solution.py:764
  59.6 5.8 %collective-permute-start.16 = (f32[200,128]{1,0:T(8,128)S(1)}, f32[200,128]{1,0:T(8,128)S(1)}, u32[]{:S(2)}, u32[]{:S(2)}) collective-permute-start(f32[200,128]{1,0:T(8,128)S(1)} %get-tuple-element.70), channel_id=1, source_target_pairs={{0,8},{8,0},{16,24},{24,16},{1,9},{9,1},{17,25},{25,17},{2,10},{10... | collective-permute-start | bytes 307208 | tf_op jit(solution)/shard_map/ppermute | solution.py:764
  63.4 2.1 %collective-permute-start.17 = (f32[200,128]{1,0:T(8,128)S(1)}, f32[200,128]{1,0:T(8,128)S(1)}, u32[]{:S(2)}, u32[]{:S(2)}) collective-permute-start(f32[200,128]{1,0:T(8,128)S(1)} %get-tuple-element.71), channel_id=1, source_target_pairs={{8,16},{16,8},{9,17},{17,9},{10,18},{18,10},{11,19},{19,11},{12,20... | collective-permute-start | bytes 307208 | tf_op jit(solution)/shard_map/ppermute | solution.py:764
  64.0 8.1 %collective-permute-start.21 = (f32[192,128]{1,0:T(8,128)S(1)}, f32[192,128]{1,0:T(8,128)S(1)}, u32[]{:S(2)}, u32[]{:S(2)}) collective-permute-start(f32[192,128]{1,0:T(8,128)S(1)} %get-tuple-element.78), channel_id=1, source_target_pairs={{0,0},{1,1},{2,8},{3,9},{4,16},{5,17},{6,24},{7,25},{8,2},{9,3},{1... | collective-permute-start | bytes 294920 | tf_op jit(solution)/shard_map/ppermute | solution.py:867
  67.3 4.8 %collective-permute-start.20 = (f32[176,128]{1,0:T(8,128)S(1)}, f32[176,128]{1,0:T(8,128)S(1)}, u32[]{:S(2)}, u32[]{:S(2)}) collective-permute-start(f32[176,128]{1,0:T(8,128)S(1)} %get-tuple-element.76), channel_id=1, source_target_pairs={{0,0},{1,1},{2,8},{3,9},{4,16},{5,17},{6,24},{7,25},{8,2},{9,3},{1... | collective-permute-start | bytes 270344 | tf_op jit(solution)/shard_map/ppermute | solution.py:875
  72.2 1.3 %collective-permute-start.22 = (f32[176,128]{1,0:T(8,128)S(1)}, f32[176,128]{1,0:T(8,128)S(1)}, u32[]{:S(2)}, u32[]{:S(2)}) collective-permute-start(f32[176,128]{1,0:T(8,128)S(1)} %collective-permute-done.20.refs_2_), channel_id=1, source_target_pairs={{0,1},{1,0},{2,3},{3,2},{4,5},{5,4},{6,7},{7,6},{8,9},{9,8},{10,11... | collective-permute-start | bytes 270344 | tf_op jit(solution)/shard_map/ppermute | solution.py:884
  72.2 18.0 %collective-permute-start.23 = (f32[192,128]{1,0:T(8,128)S(1)}, f32[192,128]{1,0:T(8,128)S(1)}, u32[]{:S(2)}, u32[]{:S(2)}) collective-permute-start(f32[192,128]{1,0:T(8,128)S(1)} %collective-permute-done.21.refs_3_), channel_id=1, source_target_pairs={{0,1},{1,0},{2,3},{3,2},{4,5},{5,4},{6,7},{7,6},{8,9},{9,8},{10,11... | collective-permute-start | bytes 294920 | tf_op jit(solution)/shard_map/ppermute | solution.py:885
  74.0 17.3 %collective-permute-start.26 = (f32[96,128]{1,0:T(8,128)S(1)}, f32[96,128]{1,0:T(8,128)S(1)}, u32[]{:S(2)}, u32[]{:S(2)}) collective-permute-start(f32[96,128]{1,0:T(8,128)S(1)} %get-tuple-element.84), channel_id=1, source_target_pairs={{0,1},{1,0},{2,3},{3,2},{4,5},{5,4},{6,7},{7,6},{8,9},{9,8},{10,11... | collective-permute-start | bytes 147464 | tf_op jit(solution)/shard_map/ppermute | solution.py:764
  74.1 17.2 %collective-permute-start.27 = (f32[96,128]{1,0:T(8,128)S(1)}, f32[96,128]{1,0:T(8,128)S(1)}, u32[]{:S(2)}, u32[]{:S(2)}) collective-permute-start(f32[96,128]{1,0:T(8,128)S(1)} %get-tuple-element.85), channel_id=1, source_target_pairs={{1,2},{2,1},{3,4},{4,3},{5,6},{6,5},{9,10},{10,9},{11,12},{12,11},... | collective-permute-start | bytes 147464 | tf_op jit(solution)/shard_map/ppermute | solution.py:764
  86.3 3.9 %collective-permute-start.25 = (f32[24,128]{1,0:T(8,128)S(1)}, f32[24,128]{1,0:T(8,128)S(1)}, u32[]{:S(2)}, u32[]{:S(2)}) collective-permute-start(f32[24,128]{1,0:T(8,128)S(1)} %get-tuple-element.83), channel_id=1, source_target_pairs={{8,16},{16,8},{9,17},{17,9},{10,18},{18,10},{11,19},{19,11},{12,20... | collective-permute-start | bytes 36872 | tf_op jit(solution)/shard_map/ppermute | solution.py:764
  87.0 4.3 %collective-permute-start.24 = (f32[24,128]{1,0:T(8,128)S(1)}, f32[24,128]{1,0:T(8,128)S(1)}, u32[]{:S(2)}, u32[]{:S(2)}) collective-permute-start(f32[24,128]{1,0:T(8,128)S(1)} %get-tuple-element.83), channel_id=1, source_target_pairs={{0,8},{8,0},{16,24},{24,16},{1,9},{9,1},{17,25},{25,17},{2,10},{10... | collective-permute-start | bytes 36872 | tf_op jit(solution)/shard_map/ppermute | solution.py:764
  (7 other events, 48.2 us)

commit v8 on v7

--- a/solution.py
+++ b/solution.py
@@ -217,7 +217,7 @@
         out[2, z] = old[2, z] + scale * (x + along_y(ey, 2, z, rows) + zz)
         return 0
 
-    lax.fori_loop(0, depth, layer, 0, unroll=4 if rows > 16 else depth)
+    lax.fori_loop(0, depth, layer, 0, unroll=8 if rows > 16 else depth)
 
 
 def stress_half(old, lame, shear, put, low, count, ex, ey, ez):
@@ -242,7 +242,7 @@
         put(5, z, n, old(5, z) + mu * (along_z(ez, 1, n, True) + y))
         return 0
 
-    lax.fori_loop(0, count, layer, 0, unroll=4 if rows > 16 else count)
+    lax.fori_loop(0, count, layer, 0, unroll=8 if rows > 16 else count)
 
 
 def zeros_like_plane(ref):

time: 93.7 us -> 93.5 us (level)
  transfers between devices with their start and end apart: 28 -> 28, of which waited for: 8 -> 8; matrix products, arithmetic and copies ran while one was open for 0% -> 0% of each run, Pallas kernels for 14% -> 13%
where the time goes in v8:
time: 93.5 us; the launch traced here: 92.1 us
  starting transfers between devices  59.5 us (64%)
  Pallas kernels  21.2 us (23%)
  waiting for transfers between devices  9.5 us (10%)
  between operations  1.02 us (1%)
  local copies, waits for them, and re-layouts  0.95 us (1%)
    ppermute x20, starting transfers between devices, exchange(): return (lax.ppermute(first, axis, one), lax.ppermute(second, axis, two))  56 us
    pallas_call x11, Pallas kernels, call(): pl.pallas_call(placed, grid=(1,), in_specs=specs, out_specs=[whole(o) for...  21.2 us
    ppermute x20, waiting for transfers between devices, exchange(): return (lax.ppermute(first, axis, one), lax.ppermute(second, axis, two))  6.1 us
    ppermute x2, waiting for transfers between devices, body(): other = lax.ppermute(own, 'gy', partner)  2.1 us
  transfers between devices with their start and end apart: 28, of which 8 were waited for; matrix products, arithmetic and copies ran while one was open for 0% of the time, Pallas kernels for 13%

profile of v8, /device:TPU:1, one launch (start us, length us, event | category | flops | bytes accessed | tf_op | source)
XLA Modules:
  0.0 92.1 jit_solution(1175725578181530956)
XLA Ops:
  0.7 3.2 %shard_map.113 = (f32[256,128]{1,0:T(8,128)}, f32[256,128]{1,0:T(8,128)}, f32[344,128]{1,0:T(8,128)}, f32[328,128]{1,0:T(8,128)}, f32[192,128]{1,0:T(8,128)}, /*index=5*/f32[192,128]{1,0:T(8,128)}, f32[24,128]{1,0:T(8,128)}) custom-call(f32[9,16,64,128]{3,2,1,0:T(8,128)} %refs_4_.3, f32[9,8,16,128]{3,2,1,0:T(8,128)} %refs_0_.7, f32[9,2,16,128]{3,2,1,0:T(8,128)} %refs_2_.4, ...), custom_call_target="tpu_custom_call" | custom-call | bytes 7843840 | tf_op jit(solution)/shard_map/pallas_call | solution.py:738
  3.9 4.5 %collective-permute-start.2 = (f32[328,128]{1,0:T(8,128)}, f32[328,128]{1,0:T(8,128)S(1)}, u32[]{:S(2)}, u32[]{:S(2)}) collective-permute-start(f32[328,128]{1,0:T(8,128)} %get-tuple-element.48), channel_id=1, source_target_pairs={{1,2},{2,1},{3,4},{4,3},{5,6},{6,5},{9,10},{10,9},{11,12},{12,11},... | collective-permute-start | bytes 503816 | tf_op jit(solution)/shard_map/ppermute | solution.py:764
  8.4 1.4 %collective-permute-start = (f32[256,128]{1,0:T(8,128)}, f32[256,128]{1,0:T(8,128)S(1)}, u32[]{:S(2)}, u32[]{:S(2)}) collective-permute-start(f32[256,128]{1,0:T(8,128)} %get-tuple-element.46), channel_id=1, source_target_pairs={{0,8},{8,0},{16,24},{24,16},{1,9},{9,1},{17,25},{25,17},{2,10},{10... | collective-permute-start | bytes 393224 | tf_op jit(solution)/shard_map/ppermute | solution.py:764
  9.8 0.7 collective-permute-start.1
  10.5 2.0 %collective-permute-done.refs_1_.refs_2_.refs_5_.refs_4_ = f32[256,128]{1,0:T(8,128)S(1)} collective-permute-done((f32[256,128]{1,0:T(8,128)}, f32[256,128]{1,0:T(8,128)S(1)}, u32[]{:S(2)}, u32[]{:S(2)}) %collective-permute-start) | collective-permute-done | bytes 131104 | tf_op jit(solution)/shard_map/ppermute | solution.py:764
  12.6 0.9 copy-done.7
  13.5 0.7 collective-permute-start.3
  14.2 2.6 %shard_map.115.refs_0_ = f32[3,16,64,128]{3,2,1,0:T(8,128)S(1)} custom-call(f32[9,16,64,128]{3,2,1,0:T(8,128)S(1)} %copy-done, f32[3,16,64,128]{3,2,1,0:T(8,128)S(1)} %copy-done.1, f32[256,128]{1,0:T(8,128)S(1)} %collective-permute-done.refs_1_.refs_2_.refs_5_.refs_4_, f32[256,128]{1,0:T(8,128)S(1)} %collective-permute-done.1.refs_2_.refs_3_.refs_6_.refs_5_, ...), custom_call_target="tpu_custom_call" | custom-call | flops 52428800 | bytes 9125888 | tf_op jit(solution)/shard_map/pallas_call | solution.py:738
  17.0 1.3 %collective-permute-done.5.refs_3_.refs_1_ = f32[232,128]{1,0:T(8,128)S(1)} collective-permute-done((f32[232,128]{1,0:T(8,128)S(1)}, f32[232,128]{1,0:T(8,128)S(1)}, u32[]{:S(2)}, u32[]{:S(2)}) %collective-permute-start.5) | collective-permute-done | bytes 118816 | tf_op jit(solution)/shard_map/ppermute | solution.py:826
  18.3 0.9 shard_map.116
  19.3 14.0 %collective-permute-start.9 = (f32[224,128]{1,0:T(8,128)S(1)}, f32[224,128]{1,0:T(8,128)S(1)}, u32[]{:S(2)}, u32[]{:S(2)}) collective-permute-start(f32[224,128]{1,0:T(8,128)S(1)} %get-tuple-element.59), channel_id=1, source_target_pairs={{1,2},{2,1},{3,4},{4,3},{5,6},{6,5},{9,10},{10,9},{11,12},{12,11},... | collective-permute-start | bytes 344072 | tf_op jit(solution)/shard_map/ppermute | solution.py:764
  33.4 0.7 collective-permute-start.7
  34.0 0.7 collective-permute-start.10
  34.7 2.2 %collective-permute-done.6.refs_8_.refs_6_ = f32[216,128]{1,0:T(8,128)S(1)} collective-permute-done((f32[216,128]{1,0:T(8,128)S(1)}, f32[216,128]{1,0:T(8,128)S(1)}, u32[]{:S(2)}, u32[]{:S(2)}) %collective-permute-start.6) | collective-permute-done | bytes 110624 | tf_op jit(solution)/shard_map/ppermute | solution.py:764
  37.0 3.3 %shard_map.117 = (f32[6,16,64,128]{3,2,1,0:T(8,128)S(1)}, f32[3,16,64,128]{3,2,1,0:T(8,128)S(1)}, f32[200,128]{1,0:T(8,128)S(1)}, f32[200,128]{1,0:T(8,128)S(1)}...) custom-call(f32[3,16,64,128]{3,2,1,0:T(8,128)S(1)} %get-tuple-element.53.refs_0_, f32[9,16,64,128]{3,2,1,0:T(8,128)S(1)} %copy-done, ...), custom_call_target="tpu_custom_call" | custom-call | flops 52428800 | bytes 14987264 | tf_op jit(solution)/shard_map/pallas_call | solution.py:738
  40.2 6.5 %collective-permute-start.15 = (f32[208,128]{1,0:T(8,128)S(1)}, f32[208,128]{1,0:T(8,128)S(1)}, u32[]{:S(2)}, u32[]{:S(2)}) collective-permute-start(f32[208,128]{1,0:T(8,128)S(1)} %get-tuple-element.68), channel_id=1, source_target_pairs={{1,2},{2,1},{3,4},{4,3},{5,6},{6,5},{9,10},{10,9},{11,12},{12,11},... | collective-permute-start | bytes 319496 | tf_op jit(solution)/shard_map/ppermute | solution.py:764
  46.8 2.5 %collective-permute-start.12 = (f32[200,128]{1,0:T(8,128)S(1)}, f32[200,128]{1,0:T(8,128)S(1)}, u32[]{:S(2)}, u32[]{:S(2)}) collective-permute-start(f32[200,128]{1,0:T(8,128)S(1)} %get-tuple-element.65), channel_id=1, source_target_pairs={{0,8},{8,0},{16,24},{24,16},{1,9},{9,1},{17,25},{25,17},{2,10},{10... | collective-permute-start | bytes 307208 | tf_op jit(solution)/shard_map/ppermute | solution.py:764
  50.0 1.3 %collective-permute-done.11.refs_5_ = f32[192,128]{1,0:T(8,128)S(1)} collective-permute-done((f32[192,128]{1,0:T(8,128)S(1)}, f32[192,128]{1,0:T(8,128)S(1)}, u32[]{:S(2)}, u32[]{:S(2)}) %collective-permute-start.11) | collective-permute-done | bytes 98336 | tf_op jit(solution)/shard_map/ppermute | solution.py:851
  51.9 3.5 %shard_map.119 = (f32[3,16,64,128]{3,2,1,0:T(8,128)S(1)}, f32[200,128]{1,0:T(8,128)S(1)}, f32[200,128]{1,0:T(8,128)S(1)}, f32[216,128]{1,0:T(8,128)S(1)}, f32[20...) custom-call(f32[3,16,64,128]{3,2,1,0:T(8,128)S(1)} %get-tuple-element.60.refs_0_, ...), custom_call_target="tpu_custom_call" | custom-call | flops 52428800 | bytes 14835712 | tf_op jit(solution)/shard_map/pallas_call | solution.py:738
  55.6 3.9 %collective-permute-start.19 = (f32[208,128]{1,0:T(8,128)S(1)}, f32[208,128]{1,0:T(8,128)S(1)}, u32[]{:S(2)}, u32[]{:S(2)}) collective-permute-start(f32[208,128]{1,0:T(8,128)S(1)} %get-tuple-element.73), channel_id=1, source_target_pairs={{1,2},{2,1},{3,4},{4,3},{5,6},{6,5},{9,10},{10,9},{11,12},{12,11},... | collective-permute-start | bytes 319496 | tf_op jit(solution)/shard_map/ppermute | solution.py:764
  59.5 3.8 %collective-permute-start.16 = (f32[200,128]{1,0:T(8,128)S(1)}, f32[200,128]{1,0:T(8,128)S(1)}, u32[]{:S(2)}, u32[]{:S(2)}) collective-permute-start(f32[200,128]{1,0:T(8,128)S(1)} %get-tuple-element.70), channel_id=1, source_target_pairs={{0,8},{8,0},{16,24},{24,16},{1,9},{9,1},{17,25},{25,17},{2,10},{10... | collective-permute-start | bytes 307208 | tf_op jit(solution)/shard_map/ppermute | solution.py:764
  64.0 0.7 collective-permute-start.21
  64.7 0.7 collective-permute-done.16.refs_5_.refs_4_
  65.4 1.7 %shard_map.120 = (f32[6,8,64,128]{3,2,1,0:T(8,128)S(1)}, f32[176,128]{1,0:T(8,128)S(1)}) custom-call(f32[3,16,64,128]{3,2,1,0:T(8,128)S(1)} %get-tuple-element.69.refs_0_.refs_1_, f32[6,16,64,128]{3,2,1,0:T(8,128)S(1)} %get-tuple-element.63.refs_1_.refs_2_, f32[3,16,64,128]{3,2,1,0:T(8,128)S(1)} %copy-done.1, f32[12,64,128]{2,1,0:T(8,128)S(1)} %shard_map.118.refs_3_, ...), custom_call_target="tpu_custom_call" | custom-call | bytes 1024 | tf_op jit(solution)/shard_map/pallas_call | solution.py:738
  67.1 0.8 collective-permute-start.20
  67.9 3.8 %shard_map.121 = (f32[9,16,64,128]{3,2,1,0:T(8,128)}, f32[8,128]{1,0:T(8,128)S(1)}) custom-call(f32[6,8,64,128]{3,2,1,0:T(8,128)S(1)} %get-tuple-element.74.refs_0_, f32[3,16,64,128]{3,2,1,0:T(8,128)S(1)} %get-tuple-element.69.refs_0_.refs_1_, f32[6,16,64,128]{3,2,1,0:T(8,128)S(1)} %get-tuple-element.63.refs_1_.refs_2_, f32[3,16,64,128]{3,2,1,0:T(8,128)S(1)} %copy-done.1, ...), custom_call_target="tpu_custom_call" | custom-call | flops 26214400 | bytes 13664256 | tf_op jit(solution)/shard_map/pallas_call | solution.py:738
  72.2 0.8 collective-permute-done.22.refs_3_
  73.7 12.6 %collective-permute-start.27 = (f32[96,128]{1,0:T(8,128)S(1)}, f32[96,128]{1,0:T(8,128)S(1)}, u32[]{:S(2)}, u32[]{:S(2)}) collective-permute-start(f32[96,128]{1,0:T(8,128)S(1)} %get-tuple-element.85), channel_id=1, source_target_pairs={{1,2},{2,1},{3,4},{4,3},{5,6},{6,5},{9,10},{10,9},{11,12},{12,11},... | collective-permute-start | bytes 147464 | tf_op jit(solution)/shard_map/ppermute | solution.py:764
  86.3 0.7 collective-permute-start.25
  87.0 2.8 %collective-permute-start.24 = (f32[24,128]{1,0:T(8,128)S(1)}, f32[24,128]{1,0:T(8,128)S(1)}, u32[]{:S(2)}, u32[]{:S(2)}) collective-permute-start(f32[24,128]{1,0:T(8,128)S(1)} %get-tuple-element.83), channel_id=1, source_target_pairs={{0,8},{8,0},{16,24},{24,16},{1,9},{9,1},{17,25},{25,17},{2,10},{10... | collective-permute-start | bytes 36872 | tf_op jit(solution)/shard_map/ppermute | solution.py:764
  89.8 1.1 %collective-permute-done.24.refs_5_ = f32[24,128]{1,0:T(8,128)S(1)} collective-permute-done((f32[24,128]{1,0:T(8,128)S(1)}, f32[24,128]{1,0:T(8,128)S(1)}, u32[]{:S(2)}, u32[]{:S(2)}) %collective-permute-start.24) | collective-permute-done | bytes 12320 | tf_op jit(solution)/shard_map/ppermute | solution.py:764
  90.8 1.3 %shard_map.123 = f32[9,8,16,128]{3,2,1,0:T(8,128)} custom-call(f32[9,8,16,128]{3,2,1,0:T(8,128)S(1)} %copy-done.3, f32[3,8,16,128]{3,2,1,0:T(8,128)S(1)} %copy-done.5, f32[3,8,16,128]{3,2,1,0:T(8,128)S(1)} %get-tuple-element.81.refs_2_, f32[192,128]{1,0:T(8,128)S(1)} %collective-permute-done.21.refs_3_, f32[192,128]{1,0:T(8,128)S(1)} %collective-permute-done.23.refs_4_, ...), custom_call_target="tpu_custom_call" | custom-call | bytes 2547712 | tf_op jit(solution)/shard_map/pallas_call | solution.py:738
  (57 shorter events, 3.9 us)
Async XLA Ops:
  0.6 13.6 %copy-start.2 = (bf16[2,256,256]{2,1,0:T(8,128)(2,1)S(1)}, bf16[2,256,256]{2,1,0:T(8,128)(2,1)}, u32[]{:S(2)}) copy-start(bf16[2,256,256]{2,1,0:T(8,128)(2,1)} %constant.6.clone.refs_6_.refs_12_.refs_9_.refs_8_) | copy-start | bytes 786436
  0.6 13.6 %copy-start.4 = (bf16[2,2,32,256]{3,2,1,0:T(8,128)(2,1)S(1)}, bf16[2,2,32,256]{3,2,1,0:T(8,128)(2,1)}, u32[]{:S(2)}) copy-start(bf16[2,2,32,256]{3,2,1,0:T(8,128)(2,1)} %constant.7.clone.refs_7_.refs_13_.refs_10_.refs_9_) | copy-start | bytes 196612
  3.9 8.7 %collective-permute-start.2 = (f32[328,128]{1,0:T(8,128)}, f32[328,128]{1,0:T(8,128)S(1)}, u32[]{:S(2)}, u32[]{:S(2)}) collective-permute-start(f32[328,128]{1,0:T(8,128)} %get-tuple-element.48), channel_id=1, source_target_pairs={{1,2},{2,1},{3,4},{4,3},{5,6},{6,5},{9,10},{10,9},{11,12},{12,11},... | collective-permute-start | bytes 503816 | tf_op jit(solution)/shard_map/ppermute | solution.py:764
  8.4 4.1 %collective-permute-start = (f32[256,128]{1,0:T(8,128)}, f32[256,128]{1,0:T(8,128)S(1)}, u32[]{:S(2)}, u32[]{:S(2)}) collective-permute-start(f32[256,128]{1,0:T(8,128)} %get-tuple-element.46), channel_id=1, source_target_pairs={{0,8},{8,0},{16,24},{24,16},{1,9},{9,1},{17,25},{25,17},{2,10},{10... | collective-permute-start | bytes 393224 | tf_op jit(solution)/shard_map/ppermute | solution.py:764
  9.8 2.7 %collective-permute-start.1 = (f32[256,128]{1,0:T(8,128)}, f32[256,128]{1,0:T(8,128)S(1)}, u32[]{:S(2)}, u32[]{:S(2)}) collective-permute-start(f32[256,128]{1,0:T(8,128)} %get-tuple-element.47), channel_id=1, source_target_pairs={{8,16},{16,8},{9,17},{17,9},{10,18},{18,10},{11,19},{19,11},{12,20... | collective-permute-start | bytes 393224 | tf_op jit(solution)/shard_map/ppermute | solution.py:764
  10.4 3.7 %collective-permute-start.4 = (f32[344,128]{1,0:T(8,128)}, f32[344,128]{1,0:T(8,128)S(1)}, u32[]{:S(2)}, u32[]{:S(2)}) collective-permute-start(f32[344,128]{1,0:T(8,128)} %get-tuple-element.49), channel_id=1, source_target_pairs={{0,1},{1,0},{2,3},{3,2},{4,5},{5,4},{6,7},{7,6},{8,9},{9,8},{10,11... | collective-permute-start | bytes 528392 | tf_op jit(solution)/shard_map/ppermute | solution.py:764
  13.5 3.4 %collective-permute-start.3 = (f32[232,128]{1,0:T(8,128)S(1)}, f32[232,128]{1,0:T(8,128)S(1)}, u32[]{:S(2)}, u32[]{:S(2)}) collective-permute-start(f32[232,128]{1,0:T(8,128)S(1)} %shard_map.114), channel_id=1, source_target_pairs={{0,0},{1,1},{2,8},{3,9},{4,16},{5,17},{6,24},{7,25},{8,2},{9,3},{1... | collective-permute-start | bytes 356360 | tf_op jit(solution)/shard_map/ppermute | solution.py:807
  16.9 1.4 %collective-permute-start.5 = (f32[232,128]{1,0:T(8,128)S(1)}, f32[232,128]{1,0:T(8,128)S(1)}, u32[]{:S(2)}, u32[]{:S(2)}) collective-permute-start(f32[232,128]{1,0:T(8,128)S(1)} %collective-permute-done.3.refs_2_.refs_0_), channel_id=1, source_target_pairs={{0,1},{1,0},{2,3},{3,2},{4,5},{5,4},{6,7},{7,6},{8,9},{9,8},{10,11... | collective-permute-start | bytes 356360 | tf_op jit(solution)/shard_map/ppermute | solution.py:826
  18.3 15.7 %copy-start.10 = (f32[192,128]{1,0:T(8,128)S(1)}, f32[192,128]{1,0:T(8,128)}, u32[]{:S(2)}) copy-start(f32[192,128]{1,0:T(8,128)} %get-tuple-element.61) | copy-start | bytes 294916
  19.1 17.8 %collective-permute-start.8 = (f32[232,128]{1,0:T(8,128)S(1)}, f32[232,128]{1,0:T(8,128)S(1)}, u32[]{:S(2)}, u32[]{:S(2)}) collective-permute-start(f32[232,128]{1,0:T(8,128)S(1)} %get-tuple-element.58), channel_id=1, source_target_pairs={{0,1},{1,0},{2,3},{3,2},{4,5},{5,4},{6,7},{7,6},{8,9},{9,8},{10,11... | collective-permute-start | bytes 356360 | tf_op jit(solution)/shard_map/ppermute | solution.py:764
  19.3 17.6 %collective-permute-start.9 = (f32[224,128]{1,0:T(8,128)S(1)}, f32[224,128]{1,0:T(8,128)S(1)}, u32[]{:S(2)}, u32[]{:S(2)}) collective-permute-start(f32[224,128]{1,0:T(8,128)S(1)} %get-tuple-element.59), channel_id=1, source_target_pairs={{1,2},{2,1},{3,4},{4,3},{5,6},{6,5},{9,10},{10,9},{11,12},{12,11},... | collective-permute-start | bytes 344072 | tf_op jit(solution)/shard_map/ppermute | solution.py:764
  33.3 3.7 %collective-permute-start.6 = (f32[216,128]{1,0:T(8,128)S(1)}, f32[216,128]{1,0:T(8,128)S(1)}, u32[]{:S(2)}, u32[]{:S(2)}) collective-permute-start(f32[216,128]{1,0:T(8,128)S(1)} %get-tuple-element.56), channel_id=1, source_target_pairs={{0,8},{8,0},{16,24},{24,16},{1,9},{9,1},{17,25},{25,17},{2,10},{10... | collective-permute-start | bytes 331784 | tf_op jit(solution)/shard_map/ppermute | solution.py:764
  33.4 3.6 %collective-permute-start.7 = (f32[216,128]{1,0:T(8,128)S(1)}, f32[216,128]{1,0:T(8,128)S(1)}, u32[]{:S(2)}, u32[]{:S(2)}) collective-permute-start(f32[216,128]{1,0:T(8,128)S(1)} %get-tuple-element.57), channel_id=1, source_target_pairs={{8,16},{16,8},{9,17},{17,9},{10,18},{18,10},{11,19},{19,11},{12,20... | collective-permute-start | bytes 331784 | tf_op jit(solution)/shard_map/ppermute | solution.py:764
  34.0 15.9 %collective-permute-start.10 = (f32[192,128]{1,0:T(8,128)S(1)}, f32[192,128]{1,0:T(8,128)S(1)}, u32[]{:S(2)}, u32[]{:S(2)}) collective-permute-start(f32[192,128]{1,0:T(8,128)S(1)} %copy-done.10), channel_id=1, source_target_pairs={{0,0},{1,1},{2,8},{3,9},{4,16},{5,17},{6,24},{7,25},{8,2},{9,3},{1... | collective-permute-start | bytes 294920 | tf_op jit(solution)/shard_map/ppermute | solution.py:836
  36.9 14.9 %copy-start.6 = (bf16[2,256,128]{2,1,0:T(8,128)(2,1)S(1)}, bf16[2,256,128]{2,1,0:T(8,128)(2,1)}, u32[]{:S(2)}) copy-start(bf16[2,256,128]{2,1,0:T(8,128)(2,1)} %constant.8.clone.refs_11_) | copy-start | bytes 393220
  40.2 11.6 %collective-permute-start.14 = (f32[216,128]{1,0:T(8,128)S(1)}, f32[216,128]{1,0:T(8,128)S(1)}, u32[]{:S(2)}, u32[]{:S(2)}) collective-permute-start(f32[216,128]{1,0:T(8,128)S(1)} %get-tuple-element.67), channel_id=1, source_target_pairs={{0,1},{1,0},{2,3},{3,2},{4,5},{5,4},{6,7},{7,6},{8,9},{9,8},{10,11... | collective-permute-start | bytes 331784 | tf_op jit(solution)/shard_map/ppermute | solution.py:764
  40.2 11.6 %collective-permute-start.15 = (f32[208,128]{1,0:T(8,128)S(1)}, f32[208,128]{1,0:T(8,128)S(1)}, u32[]{:S(2)}, u32[]{:S(2)}) collective-permute-start(f32[208,128]{1,0:T(8,128)S(1)} %get-tuple-element.68), channel_id=1, source_target_pairs={{1,2},{2,1},{3,4},{4,3},{5,6},{6,5},{9,10},{10,9},{11,12},{12,11},... | collective-permute-start | bytes 319496 | tf_op jit(solution)/shard_map/ppermute | solution.py:764
  46.8 5.0 %collective-permute-start.12 = (f32[200,128]{1,0:T(8,128)S(1)}, f32[200,128]{1,0:T(8,128)S(1)}, u32[]{:S(2)}, u32[]{:S(2)}) collective-permute-start(f32[200,128]{1,0:T(8,128)S(1)} %get-tuple-element.65), channel_id=1, source_target_pairs={{0,8},{8,0},{16,24},{24,16},{1,9},{9,1},{17,25},{25,17},{2,10},{10... | collective-permute-start | bytes 307208 | tf_op jit(solution)/shard_map/ppermute | solution.py:764
  49.3 2.6 %collective-permute-start.13 = (f32[200,128]{1,0:T(8,128)S(1)}, f32[200,128]{1,0:T(8,128)S(1)}, u32[]{:S(2)}, u32[]{:S(2)}) collective-permute-start(f32[200,128]{1,0:T(8,128)S(1)} %get-tuple-element.66), channel_id=1, source_target_pairs={{8,16},{16,8},{9,17},{17,9},{10,18},{18,10},{11,19},{19,11},{12,20... | collective-permute-start | bytes 307208 | tf_op jit(solution)/shard_map/ppermute | solution.py:764
  49.9 1.4 %collective-permute-start.11 = (f32[192,128]{1,0:T(8,128)S(1)}, f32[192,128]{1,0:T(8,128)S(1)}, u32[]{:S(2)}, u32[]{:S(2)}) collective-permute-start(f32[192,128]{1,0:T(8,128)S(1)} %collective-permute-done.10.refs_4_), channel_id=1, source_target_pairs={{0,1},{1,0},{2,3},{3,2},{4,5},{5,4},{6,7},{7,6},{8,9},{9,8},{10,11... | collective-permute-start | bytes 294920 | tf_op jit(solution)/shard_map/ppermute | solution.py:851
  55.4 10.0 %collective-permute-start.18 = (f32[216,128]{1,0:T(8,128)S(1)}, f32[216,128]{1,0:T(8,128)S(1)}, u32[]{:S(2)}, u32[]{:S(2)}) collective-permute-start(f32[216,128]{1,0:T(8,128)S(1)} %get-tuple-element.72), channel_id=1, source_target_pairs={{0,1},{1,0},{2,3},{3,2},{4,5},{5,4},{6,7},{7,6},{8,9},{9,8},{10,11... | collective-permute-start | bytes 331784 | tf_op jit(solution)/shard_map/ppermute | solution.py:764
  55.6 9.8 %collective-permute-start.19 = (f32[208,128]{1,0:T(8,128)S(1)}, f32[208,128]{1,0:T(8,128)S(1)}, u32[]{:S(2)}, u32[]{:S(2)}) collective-permute-start(f32[208,128]{1,0:T(8,128)S(1)} %get-tuple-element.73), channel_id=1, source_target_pairs={{1,2},{2,1},{3,4},{4,3},{5,6},{6,5},{9,10},{10,9},{11,12},{12,11},... | collective-permute-start | bytes 319496 | tf_op jit(solution)/shard_map/ppermute | solution.py:764
  59.5 5.8 %collective-permute-start.16 = (f32[200,128]{1,0:T(8,128)S(1)}, f32[200,128]{1,0:T(8,128)S(1)}, u32[]{:S(2)}, u32[]{:S(2)}) collective-permute-start(f32[200,128]{1,0:T(8,128)S(1)} %get-tuple-element.70), channel_id=1, source_target_pairs={{0,8},{8,0},{16,24},{24,16},{1,9},{9,1},{17,25},{25,17},{2,10},{10... | collective-permute-start | bytes 307208 | tf_op jit(solution)/shard_map/ppermute | solution.py:764
  63.3 2.1 %collective-permute-start.17 = (f32[200,128]{1,0:T(8,128)S(1)}, f32[200,128]{1,0:T(8,128)S(1)}, u32[]{:S(2)}, u32[]{:S(2)}) collective-permute-start(f32[200,128]{1,0:T(8,128)S(1)} %get-tuple-element.71), channel_id=1, source_target_pairs={{8,16},{16,8},{9,17},{17,9},{10,18},{18,10},{11,19},{19,11},{12,20... | collective-permute-start | bytes 307208 | tf_op jit(solution)/shard_map/ppermute | solution.py:764
  64.0 7.7 %collective-permute-start.21 = (f32[192,128]{1,0:T(8,128)S(1)}, f32[192,128]{1,0:T(8,128)S(1)}, u32[]{:S(2)}, u32[]{:S(2)}) collective-permute-start(f32[192,128]{1,0:T(8,128)S(1)} %get-tuple-element.78), channel_id=1, source_target_pairs={{0,0},{1,1},{2,8},{3,9},{4,16},{5,17},{6,24},{7,25},{8,2},{9,3},{1... | collective-permute-start | bytes 294920 | tf_op jit(solution)/shard_map/ppermute | solution.py:867
  67.1 4.6 %collective-permute-start.20 = (f32[176,128]{1,0:T(8,128)S(1)}, f32[176,128]{1,0:T(8,128)S(1)}, u32[]{:S(2)}, u32[]{:S(2)}) collective-permute-start(f32[176,128]{1,0:T(8,128)S(1)} %get-tuple-element.76), channel_id=1, source_target_pairs={{0,0},{1,1},{2,8},{3,9},{4,16},{5,17},{6,24},{7,25},{8,2},{9,3},{1... | collective-permute-start | bytes 270344 | tf_op jit(solution)/shard_map/ppermute | solution.py:875
  71.7 1.3 %collective-permute-start.22 = (f32[176,128]{1,0:T(8,128)S(1)}, f32[176,128]{1,0:T(8,128)S(1)}, u32[]{:S(2)}, u32[]{:S(2)}) collective-permute-start(f32[176,128]{1,0:T(8,128)S(1)} %collective-permute-done.20.refs_2_), channel_id=1, source_target_pairs={{0,1},{1,0},{2,3},{3,2},{4,5},{5,4},{6,7},{7,6},{8,9},{9,8},{10,11... | collective-permute-start | bytes 270344 | tf_op jit(solution)/shard_map/ppermute | solution.py:884
  71.7 18.0 %collective-permute-start.23 = (f32[192,128]{1,0:T(8,128)S(1)}, f32[192,128]{1,0:T(8,128)S(1)}, u32[]{:S(2)}, u32[]{:S(2)}) collective-permute-start(f32[192,128]{1,0:T(8,128)S(1)} %collective-permute-done.21.refs_3_), channel_id=1, source_target_pairs={{0,1},{1,0},{2,3},{3,2},{4,5},{5,4},{6,7},{7,6},{8,9},{9,8},{10,11... | collective-permute-start | bytes 294920 | tf_op jit(solution)/shard_map/ppermute | solution.py:885
  73.5 17.3 %collective-permute-start.26 = (f32[96,128]{1,0:T(8,128)S(1)}, f32[96,128]{1,0:T(8,128)S(1)}, u32[]{:S(2)}, u32[]{:S(2)}) collective-permute-start(f32[96,128]{1,0:T(8,128)S(1)} %get-tuple-element.84), channel_id=1, source_target_pairs={{0,1},{1,0},{2,3},{3,2},{4,5},{5,4},{6,7},{7,6},{8,9},{9,8},{10,11... | collective-permute-start | bytes 147464 | tf_op jit(solution)/shard_map/ppermute | solution.py:764
  73.7 17.2 %collective-permute-start.27 = (f32[96,128]{1,0:T(8,128)S(1)}, f32[96,128]{1,0:T(8,128)S(1)}, u32[]{:S(2)}, u32[]{:S(2)}) collective-permute-start(f32[96,128]{1,0:T(8,128)S(1)} %get-tuple-element.85), channel_id=1, source_target_pairs={{1,2},{2,1},{3,4},{4,3},{5,6},{6,5},{9,10},{10,9},{11,12},{12,11},... | collective-permute-start | bytes 147464 | tf_op jit(solution)/shard_map/ppermute | solution.py:764
  86.3 3.5 %collective-permute-start.25 = (f32[24,128]{1,0:T(8,128)S(1)}, f32[24,128]{1,0:T(8,128)S(1)}, u32[]{:S(2)}, u32[]{:S(2)}) collective-permute-start(f32[24,128]{1,0:T(8,128)S(1)} %get-tuple-element.83), channel_id=1, source_target_pairs={{8,16},{16,8},{9,17},{17,9},{10,18},{18,10},{11,19},{19,11},{12,20... | collective-permute-start | bytes 36872 | tf_op jit(solution)/shard_map/ppermute | solution.py:764
  87.0 3.9 %collective-permute-start.24 = (f32[24,128]{1,0:T(8,128)S(1)}, f32[24,128]{1,0:T(8,128)S(1)}, u32[]{:S(2)}, u32[]{:S(2)}) collective-permute-start(f32[24,128]{1,0:T(8,128)S(1)} %get-tuple-element.83), channel_id=1, source_target_pairs={{0,8},{8,0},{16,24},{24,16},{1,9},{9,1},{17,25},{25,17},{2,10},{10... | collective-permute-start | bytes 36872 | tf_op jit(solution)/shard_map/ppermute | solution.py:764
  (7 other events, 47.8 us)
